TPU v7x, 32 devices: a whole 2x2x4 slice. The times are simulated.
32 devices in a mesh: section: 4 (over z), tensor: 2 (over x), dp: 4 (over y, core).
Axes of the slice: x: 2, y: 2, z: 4, core: 2. Of those that a mesh axis runs over, the one named last changes fastest.
Arguments:
- parked: bfloat16 [4, 2, 128, 6144], P('section', None, 'tensor', 'dp'), may hold values from -6 to 6
- arriving: bfloat16 [4, 128, 6144], P('section', 'tensor', 'dp'), may hold values from -6 to 6
- slot_table: int32 [4, 2], replicated, may hold values from 0 to 1, each once within a row
- value_weight: bfloat16 [4, 6144, 8192], P('section', 'dp', 'tensor'), may hold values from -0.078125 to 0.078125
- output_weight: bfloat16 [4, 8192, 6144], P('section', 'tensor', 'dp'), may hold values from -0.0625 to 0.0625
- slopes: float32 [64], P('tensor'), may hold values from 0.004 to 0.12
Outputs:
- sent: bfloat16 [4, 128, 6144], P('section', 'tensor', 'dp')
- value_grad: bfloat16 [4, 6144, 8192], P('section', 'dp', 'tensor')
Inputs may be any that keep to these rules, and one draw needn't show every extreme that they name: `slot_table`: each row is a permutation of 0 to 1.
All inputs are finite; a program needn't handle non-finite values.
Results may differ from a plain program's by a relative error of at most 0.0065.
The roundings to bfloat16 on the way count: a program that leaves them out, or rounds other values in their place, can miss the bound.
Values may be sent and summed in bfloat16 or wider, within the bound.
No kernel may reach another device: no remote copies, remote signals or barrier semaphores. Data moves between devices by JAX's collectives and lax.ppermute only.
A program may use at most 192 MiB of HBM per device.

v0:
```python
import jax
import jax.numpy as jnp
from jax import lax
from jax.sharding import PartitionSpec as P

EPSILON = 1e-05


def partner(array, axis, bit):
    return lax.ppermute(array, axis, [(i, i ^ 1 << bit) for i in range(lax.axis_size(axis))])


def passed_along(array, axis, by):
    count = lax.axis_size(axis)
    pairs = [(i, i + by) for i in range(count) if 0 <= i + by < count]
    return lax.ppermute(array, axis, pairs)


def mixing_weights(slopes, length):
    places = jnp.arange(length)
    distance = (places[:, None] - places[None, :]).astype(jnp.float32)
    causal = distance >= 0
    logits = -slopes[:, None, None] * jnp.where(causal, distance, 0.0)[None, :, :]
    weights = jnp.where(causal[None, :, :], jnp.exp(logits), 0.0)
    return (weights / jnp.sum(weights, axis=-1, keepdims=True)).astype(jnp.bfloat16)


def across_width(parts):
    return lax.psum(parts, "dp")


def to_mirror(block):
    for bit_index in range(lax.axis_size("section").bit_length() - 1):
        block = partner(block, "section", bit_index)
    return block


def unmix_heads(mixing, grads):
    length = grads.shape[0]
    shaped = grads.reshape(length, mixing.shape[0], -1)
    result = jnp.einsum("hij,ihd->jhd", mixing, shaped, preferred_element_type=jnp.float32)
    return result.astype(jnp.bfloat16).reshape(length, -1)


def backward_slot(inputs, upstream, w_value, w_output, mixing, value_total):
    width = inputs.shape[1] * lax.axis_size("dp")
    floats = inputs.astype(jnp.float32)
    row_sums, row_squares = across_width(
        (jnp.sum(floats, axis=1, keepdims=True), jnp.sum(floats * floats, axis=1, keepdims=True))
    )
    center = row_sums / width
    inverse = lax.rsqrt(row_squares / width - center * center + EPSILON)
    scaled = (floats - center) * inverse
    normed = scaled.astype(jnp.bfloat16)
    normed_all, upstream_all = (
        lax.all_gather(normed, "tensor", axis=0, tiled=True),
        lax.all_gather(upstream, "tensor", axis=0, tiled=True),
    )
    grad_part = lax.dot_general(
        upstream_all, w_output, (((1,), (1,)), ((), ())), preferred_element_type=jnp.float32
    )
    grad_sum = across_width(grad_part)
    grad_value = unmix_heads(mixing, grad_sum.astype(jnp.bfloat16))
    grad_normed = lax.psum_scatter(
        lax.dot_general(
            grad_value, w_value, (((1,), (1,)), ((), ())), preferred_element_type=jnp.float32
        ),
        "tensor",
        scatter_dimension=0,
        tiled=True,
    )
    first_sum, second_sum = across_width(
        (
            jnp.sum(grad_normed, axis=1, keepdims=True),
            jnp.sum(grad_normed * scaled, axis=1, keepdims=True),
        )
    )
    grad_input = (
        upstream.astype(jnp.float32)
        + inverse * (grad_normed - first_sum / width - scaled * (second_sum / width))
    ).astype(jnp.bfloat16)
    value_total = value_total + lax.dot_general(
        normed_all, grad_value, (((0,), (0,)), ((), ())), preferred_element_type=jnp.float32
    )
    return (grad_input, value_total)


def on_device(parked, arriving, slot_table, value_weight, output_weight, slopes):
    parked_store = parked[0]
    w_value = value_weight[0]
    w_output = output_weight[0]
    slots_count = parked_store.shape[0]
    length = parked_store.shape[1] * lax.axis_size("tensor")
    mixing = mixing_weights(slopes, length)
    section_here = lax.axis_index("section")
    mirror_slots = lax.dynamic_index_in_dim(
        slot_table, lax.axis_size("section") - 1 - section_here, 0, keepdims=False
    )
    value_total = jnp.zeros(w_value.shape, jnp.float32)
    upstream = arriving[0]
    for window_slot in range(slots_count):
        inputs = to_mirror(
            lax.dynamic_index_in_dim(parked_store, mirror_slots[window_slot], 0, keepdims=False)
        )
        if window_slot > 0:
            upstream = passed_along(upstream, "section", -1)
        upstream, value_total = backward_slot(
            inputs, upstream, w_value, w_output, mixing, value_total
        )
    return (upstream[None], value_total.astype(jnp.bfloat16)[None])


def solution(mesh):
    in_specs = (
        P("section", None, "tensor", "dp"),
        P("section", "tensor", "dp"),
        P(),
        P("section", "dp", "tensor"),
        P("section", "tensor", "dp"),
        P("tensor"),
    )
    out_specs = (P("section", "tensor", "dp"), P("section", "dp", "tensor"))
    return jax.shard_map(
        on_device, mesh=mesh, in_specs=in_specs, out_specs=out_specs, check_vma=False
    )
```

profile of v0, /device:TPU:0, one launch (start us, length us, event | category | flops | bytes accessed | tf_op | source)
XLA Modules:
  0.0 258.2 jit_solution(6117093599336147)
XLA Ops:
  7.2 0.0 copy-start
  7.2 0.0 reduce-scatter.3.cloned.1.call-start
  7.2 0.6 copy-done
  7.9 0.1 constant_dynamic-slice_fusion
  7.9 0.5 fusion.36
  12.3 1.7 dynamic-slice_bitcast_fusion.1
  14.1 3.0 %collective-permute-start = (bf16[64,1536]{1,0:T(8,128)(2,1)S(1)}, bf16[64,1536]{1,0:T(8,128)(2,1)S(1)}, u32[]{:S(2)}, u32[]{:S(2)}) collective-permute-start(bf16[64,1536]{1,0:T(8,128)(2,1)S(1)} %get-tuple-element.20), channel_id=1, source_target_pairs={{0,8},{8,0},{16,24},{24,16},{1,9},{9,1},{17,25},{25,17},{2,10},{10... | collective-permute-start | bytes 589832 | tf_op jit(solution)/shard_map/ppermute | solution.py:10
  17.1 7.2 %all-gather = bf16[1,128,1536]{2,1,0:T(8,128)(2,1)S(1)} all-gather(bf16[1,64,1536]{2,1,0:T(8,128)(2,1)} %param.7), channel_id=2, replica_groups=mesh['section'=4,'tensor'=2,'dp'=4] {'tensor'}, dimensions={1}, use_global_device_ids=true | all-gather | bytes 589824 | tf_op jit(solution)/shard_map/all_gather | solution.py:57
  24.3 8.7 %fusion.7 = f32[128,4096]{1,0:T(8,128)S(1)} fusion(bf16[1,4096,1536]{2,1,0:T(8,128)(2,1)} %param.10, bf16[1,128,1536]{2,1,0:T(8,128)(2,1)S(1)} %all-gather), kind=kOutput, calls=%fused_computation.8 | convolution fusion | flops 1610612736 | bytes 15073280 | tf_op jit(solution)/shard_map/dot_general | solution.py:59
  33.0 0.0 collective-permute-done
  33.0 2.6 %collective-permute-start.1 = (bf16[64,1536]{1,0:T(8,128)(2,1)S(1)}, bf16[64,1536]{1,0:T(8,128)(2,1)S(1)}, u32[]{:S(2)}, u32[]{:S(2)}) collective-permute-start(bf16[64,1536]{1,0:T(8,128)(2,1)S(1)} %collective-permute-done), channel_id=1, source_target_pairs={{0,16},{8,24},{16,0},{24,8},{1,17},{9,25},{17,1},{25,9},{2,18},{10... | collective-permute-start | bytes 589832 | tf_op jit(solution)/shard_map/ppermute | solution.py:10
  35.7 1.3 fusion.9
  37.0 6.6 %collective-permute-done.1 = bf16[64,1536]{1,0:T(8,128)(2,1)S(1)} collective-permute-done((bf16[64,1536]{1,0:T(8,128)(2,1)S(1)}, bf16[64,1536]{1,0:T(8,128)(2,1)S(1)}, u32[]{:S(2)}, u32[]{:S(2)}) %collective-permute-start.1) | collective-permute-done | bytes 196640 | tf_op jit(solution)/shard_map/ppermute | solution.py:10
  43.6 0.2 fusion.10
  43.8 42.1 %all-reduce.6 = (bf16[128,4096]{1,0:T(8,128)(2,1)S(1)}, f32[64,1]{0,1:T(1,128)S(1)}, f32[64,1]{0,1:T(1,128)S(1)}) all-reduce(f32[128,4096]{1,0:T(8,128)S(1)} %fusion.7, f32[64,1]{0,1:T(1,128)S(1)} %bitcast.75, f32[64,1]{0,1:T(1,128)S(1)} %bitcast.76), channel_id=1, replica_groups=mesh['section'=4,'tensor'=2,'dp'=4] {'dp'}, use_global_device_ids=true, to_apply=%region_4.5 | all-reduce | flops 524416 | bytes 3146752 | tf_op jit(solution)/shard_map/psum | solution.py:29
  86.0 0.7 copy.10
  86.6 0.1 copy-done.6
  86.8 1.2 convolution_convert_fusion.1
  88.0 0.0 copy-start.4
  88.0 0.0 copy-start.3
  88.0 9.9 %fusion.3 = f32[128,1536]{1,0:T(8,128)} fusion(bf16[128,4096]{0,1:T(8,128)(2,1)S(1)} %bitcast.67, bf16[1,1536,4096]{2,1,0:T(8,128)(2,1)} %param.9), kind=kOutput, calls=%fused_computation.4 | convolution fusion | flops 1610612736 | bytes 14417920 | tf_op jit(solution)/shard_map/dot_general | solution.py:65
  97.9 0.0 reduce-scatter.3.cloned.1.call-update
  97.9 0.0 reduce-scatter.5.cloned.1.call-start
  98.0 0.1 collective-permute-start.3
  98.0 7.0 %collective-permute-done.3 = bf16[64,1536]{1,0:T(8,128)(2,1)S(1)} collective-permute-done((bf16[64,1536]{1,0:T(8,128)(2,1)S(1)}, bf16[64,1536]{1,0:T(8,128)(2,1)S(1)}, u32[]{:S(2)}, u32[]{:S(2)}) %collective-permute-start.3) | collective-permute-done | bytes 196640 | tf_op jit(solution)/shard_map/ppermute | solution.py:10
  105.0 0.6 collective-permute-start.4
  105.6 8.9 %reduce-scatter.3.cloned.1.call-done = f32[64,1536]{1,0:T(8,128)} async-done(((f32[128,1536]{1,0:T(8,128)}), f32[64,1536]{1,0:T(8,128)}) %reduce-scatter.3.cloned.1.call-update) | async-done | bytes 393232 | tf_op jit(solution)/shard_map/reduce_scatter | solution.py:64
  114.5 1.3 fusion.35
  115.8 6.9 %all-reduce.2 = (f32[64,1]{0,1:T(1,128)S(1)}, f32[64,1]{0,1:T(1,128)S(1)}) all-reduce(f32[64,1]{0,1:T(1,128)S(1)} %bitcast.78, f32[64,1]{0,1:T(1,128)S(1)} %bitcast.77), channel_id=1, replica_groups=mesh['section'=4,'tensor'=2,'dp'=4] {'dp'}, use_global_device_ids=true, to_apply=%region_10.11 | all-reduce | flops 128 | bytes 1024 | tf_op jit(solution)/shard_map/psum | solution.py:29
  122.6 1.2 fusion.12
  123.9 1.3 collective-permute-start.2
  125.2 0.0 collective-permute-done.4
  125.2 0.2 fusion.20
  125.3 6.5 %all_gather.14 = bf16[128,1536]{1,0:T(8,128)(2,1)} all-gather(bf16[64,1536]{1,0:T(8,128)(2,1)S(1)} %get-tuple-element.24), channel_id=1, replica_groups=mesh['section'=4,'tensor'=2,'dp'=4] {'tensor'}, dimensions={0}, use_global_device_ids=true | all-gather | bytes 589824 | tf_op jit(solution)/shard_map/all_gather | solution.py:56
  131.8 6.3 %all_gather.13 = bf16[128,1536]{1,0:T(8,128)(2,1)S(1)} all-gather(bf16[64,1536]{1,0:T(8,128)(2,1)S(1)} %collective-permute-done.2), channel_id=1, replica_groups=mesh['section'=4,'tensor'=2,'dp'=4] {'tensor'}, dimensions={0}, use_global_device_ids=true | all-gather | bytes 589824 | tf_op jit(solution)/shard_map/all_gather | solution.py:57
  138.1 8.6 %fusion.5 = f32[128,4096]{1,0:T(8,128)S(1)} fusion(bf16[128,1536]{1,0:T(8,128)(2,1)S(1)} %all_gather.13, bf16[1,4096,1536]{2,1,0:T(8,128)(2,1)} %param.10), kind=kOutput, calls=%fused_computation.6 | convolution fusion | flops 1610612736 | bytes 15073280 | tf_op jit(solution)/shard_map/dot_general | solution.py:59
  146.8 42.1 %all-reduce.7 = (bf16[128,4096]{1,0:T(8,128)(2,1)}, f32[64,1]{0,1:T(1,128)S(1)}, f32[64,1]{0,1:T(1,128)S(1)}) all-reduce(f32[128,4096]{1,0:T(8,128)S(1)} %fusion.5, f32[64,1]{0,1:T(1,128)S(1)} %bitcast.73, f32[64,1]{0,1:T(1,128)S(1)} %bitcast.74), channel_id=1, replica_groups=mesh['section'=4,'tensor'=2,'dp'=4] {'dp'}, use_global_device_ids=true, to_apply=%region_15.16 | all-reduce | flops 524416 | bytes 3146752 | tf_op jit(solution)/shard_map/psum | solution.py:29
  188.8 1.6 copy.11
  190.4 2.1 convolution_convert_fusion
  192.6 9.9 %fusion.1 = f32[128,1536]{1,0:T(8,128)} fusion(bf16[128,4096]{0,1:T(8,128)(2,1)S(1)} %bitcast.69, bf16[1,1536,4096]{2,1,0:T(8,128)(2,1)} %param.9), kind=kOutput, calls=%fused_computation.2 | convolution fusion | flops 1610612736 | bytes 14417920 | tf_op jit(solution)/shard_map/dot_general | solution.py:65
  202.4 0.0 reduce-scatter.5.cloned.1.call-update
  202.5 10.4 %fusion.37 = f32[1536,4096]{1,0:T(8,128)} fusion(bf16[128,1536]{1,0:T(8,128)(2,1)S(1)} %copy-done.2, bf16[128,4096]{0,1:T(8,128)(2,1)S(1)} %bitcast.68), kind=kOutput, calls=%fused_computation.62 | convolution fusion | flops 1610612736 | bytes 26607616 | tf_op jit(solution)/shard_map/dot_general | solution.py:82
  212.9 7.6 %reduce-scatter.5.cloned.1.call-done = f32[64,1536]{1,0:T(8,128)} async-done(((f32[128,1536]{1,0:T(8,128)}), f32[64,1536]{1,0:T(8,128)}) %reduce-scatter.5.cloned.1.call-update) | async-done | bytes 393232 | tf_op jit(solution)/shard_map/reduce_scatter | solution.py:64
  220.5 1.3 fusion.34
  221.7 6.9 %all-reduce = (f32[64,1]{0,1:T(1,128)S(1)}, f32[64,1]{0,1:T(1,128)S(1)}) all-reduce(f32[64,1]{0,1:T(1,128)S(1)} %bitcast.80, f32[64,1]{0,1:T(1,128)S(1)} %bitcast.79), channel_id=1, replica_groups=mesh['section'=4,'tensor'=2,'dp'=4] {'dp'}, use_global_device_ids=true, to_apply=%region_20.21 | all-reduce | flops 128 | bytes 1024 | tf_op jit(solution)/shard_map/psum | solution.py:29
  228.6 1.9 fusion.22
  230.5 6.3 %all_gather.15 = bf16[128,1536]{1,0:T(8,128)(2,1)S(1)} all-gather(bf16[64,1536]{1,0:T(8,128)(2,1)S(1)} %get-tuple-element.22), channel_id=1, replica_groups=mesh['section'=4,'tensor'=2,'dp'=4] {'tensor'}, dimensions={0}, use_global_device_ids=true | all-gather | bytes 589824 | tf_op jit(solution)/shard_map/all_gather | solution.py:56
  236.8 14.5 %fusion = bf16[1,1536,4096]{2,1,0:T(8,128)(2,1)} fusion(f32[1536,4096]{1,0:T(8,128)} %fusion.37, bf16[128,1536]{1,0:T(8,128)(2,1)S(1)} %all_gather.15, bf16[128,4096]{0,1:T(8,128)(2,1)S(1)} %bitcast.70), kind=kOutput, calls=%fused_computation.1 | convolution fusion | flops 1623195648 | bytes 39190528 | tf_op jit(solution)/shard_map/dot_general | solution.py:82
  (30 shorter events, 0.1 us)
Async XLA Ops:
  7.2 0.7 copy-start
  7.2 107.3 %reduce-scatter.3.cloned.1.call-start = ((), (), s32[]{:S(2)}) async-start(), calls=%async_computation.2 | async-start | bytes 1179648 | tf_op jit(solution)/shard_map/reduce_scatter | solution.py:64
  14.1 19.0 %collective-permute-start = (bf16[64,1536]{1,0:T(8,128)(2,1)S(1)}, bf16[64,1536]{1,0:T(8,128)(2,1)S(1)}, u32[]{:S(2)}, u32[]{:S(2)}) collective-permute-start(bf16[64,1536]{1,0:T(8,128)(2,1)S(1)} %get-tuple-element.20), channel_id=1, source_target_pairs={{0,8},{8,0},{16,24},{24,16},{1,9},{9,1},{17,25},{25,17},{2,10},{10... | collective-permute-start | bytes 589832 | tf_op jit(solution)/shard_map/ppermute | solution.py:10
  24.3 11.4 %copy-start.9 = (f32[32]{0:T(128)S(1)}, f32[32]{0:T(128)}, u32[]{:S(2)}) copy-start(f32[32]{0:T(128)} %param.11) | copy-start | bytes 388
  33.0 10.8 %copy-start.5 = (f32[128,128]{1,0:T(8,128)}, f32[128,128]{1,0:T(8,128)S(1)}, u32[]{:S(2)}) copy-start(f32[128,128]{1,0:T(8,128)S(1)} %convert_select_fusion) | copy-start | bytes 196612
  33.0 10.6 %collective-permute-start.1 = (bf16[64,1536]{1,0:T(8,128)(2,1)S(1)}, bf16[64,1536]{1,0:T(8,128)(2,1)S(1)}, u32[]{:S(2)}, u32[]{:S(2)}) collective-permute-start(bf16[64,1536]{1,0:T(8,128)(2,1)S(1)} %collective-permute-done), channel_id=1, source_target_pairs={{0,16},{8,24},{16,0},{24,8},{1,17},{9,25},{17,1},{25,9},{2,18},{10... | collective-permute-start | bytes 589832 | tf_op jit(solution)/shard_map/ppermute | solution.py:10
  35.7 8.1 %copy-start.7 = (pred[128,128]{1,0:T(8,128)(4,1)}, pred[128,128]{1,0:T(8,128)(4,1)S(1)}, u32[]{:S(2)}) copy-start(pred[128,128]{1,0:T(8,128)(4,1)S(1)} %convert_compare_fusion) | copy-start | bytes 49156
  35.7 50.9 %copy-start.10 = (f32[32]{0:T(128)}, f32[32]{0:T(128)S(1)}, u32[]{:S(2)}) copy-start(f32[32]{0:T(128)S(1)} %neg.4) | copy-start | bytes 388
  85.9 0.8 copy-start.6
  85.9 0.8 copy-start.8
  85.9 0.8 copy-start.12
  88.0 10.0 %copy-start.4 = (bf16[64,1536]{1,0:T(8,128)(2,1)S(1)}, bf16[64,1536]{1,0:T(8,128)(2,1)}, u32[]{:S(2)}) copy-start(bf16[64,1536]{1,0:T(8,128)(2,1)} %get-tuple-element.21) | copy-start | bytes 589828
  88.0 34.6 %copy-start.3 = (bf16[1,64,1536]{2,1,0:T(8,128)(2,1)S(1)}, bf16[1,64,1536]{2,1,0:T(8,128)(2,1)}, u32[]{:S(2)}) copy-start(bf16[1,64,1536]{2,1,0:T(8,128)(2,1)} %param.7) | copy-start | bytes 589828
  97.9 122.6 %reduce-scatter.5.cloned.1.call-start = ((), (), s32[]{:S(2)}) async-start(), calls=%async_computation.3 | async-start | bytes 1179648 | tf_op jit(solution)/shard_map/reduce_scatter | solution.py:64
  98.0 7.1 %collective-permute-start.3 = (bf16[64,1536]{1,0:T(8,128)(2,1)S(1)}, bf16[64,1536]{1,0:T(8,128)(2,1)S(1)}, u32[]{:S(2)}, u32[]{:S(2)}) collective-permute-start(bf16[64,1536]{1,0:T(8,128)(2,1)S(1)} %copy-done.4), channel_id=1, source_target_pairs={{0,8},{8,0},{16,24},{24,16},{1,9},{9,1},{17,25},{25,17},{2,10},{10... | collective-permute-start | bytes 589832 | tf_op jit(solution)/shard_map/ppermute | solution.py:10
  105.0 20.1 %collective-permute-start.4 = (bf16[64,1536]{1,0:T(8,128)(2,1)S(1)}, bf16[64,1536]{1,0:T(8,128)(2,1)S(1)}, u32[]{:S(2)}, u32[]{:S(2)}) collective-permute-start(bf16[64,1536]{1,0:T(8,128)(2,1)S(1)} %collective-permute-done.3), channel_id=1, source_target_pairs={{0,16},{8,24},{16,0},{24,8},{1,17},{9,25},{17,1},{25,9},{2,18},{10... | collective-permute-start | bytes 589832 | tf_op jit(solution)/shard_map/ppermute | solution.py:10
  123.9 7.9 %collective-permute-start.2 = (bf16[64,1536]{1,0:T(8,128)(2,1)S(1)}, bf16[64,1536]{1,0:T(8,128)(2,1)S(1)}, u32[]{:S(2)}, u32[]{:S(2)}) collective-permute-start(bf16[64,1536]{1,0:T(8,128)(2,1)S(1)} %get-tuple-element.25), channel_id=1, source_target_pairs={{8,0},{16,8},{24,16},{9,1},{17,9},{25,17},{10,2},{18,10},{26,18},{... | collective-permute-start | bytes 589832 | tf_op jit(solution)/shard_map/ppermute | solution.py:16
  188.8 1.6 copy-start.11
  192.6 9.9 %copy-start.2 = (bf16[128,1536]{1,0:T(8,128)(2,1)S(1)}, bf16[128,1536]{1,0:T(8,128)(2,1)}, u32[]{:S(2)}) copy-start(bf16[128,1536]{1,0:T(8,128)(2,1)} %all_gather.14) | copy-start | bytes 1179652
  236.8 14.5 %copy-start.1 = (s32[4,2]{0,1:T(2,128)S(1)}, s32[4,2]{0,1:T(2,128)}, u32[]{:S(2)}) copy-start(s32[4,2]{0,1:T(2,128)} %param.8) | copy-start | bytes 100
Sparse Core Ops, SparseCore 0:
  98.0 16.4 reduce-scatter.2
  202.6 17.8 reduce-scatter.4
where the time goes:
time: 259 us; the launch traced here: 258 us
  blocking collectives  124 us (48%)
  matrix products  65.2 us (25%)
  waiting for transfers between devices  30.1 us (12%)
  between operations  18.2 us (7%)
  starting transfers between devices  7.7 us (3%)
  other arithmetic  7.26 us (3%)
  local copies, waits for them, and re-layouts  5.4 us (2%)
    psum x4, blocking collectives, across_width(): return lax.psum(parts, 'dp')  97.9 us
    dot_general x2, matrix products, backward_slot(): lax.dot_general(normed_all, grad_value, (((0,), (0,)), ((), ())), preferr...  24.9 us
    dot_general x2, matrix products, backward_slot(): lax.dot_general(grad_value, w_value, (((1,), (1,)), ((), ())), preferred_...  19.7 us
    dot_general x2, matrix products, backward_slot(): lax.dot_general(upstream_all, w_output, (((1,), (1,)), ((), ())), preferr...  17.3 us
    reduce_scatter x2, waiting for transfers between devices, backward_slot(): lax.psum_scatter(lax.dot_general(grad_value, w_value, (((1,), (1,)), ((),...  16.4 us
    ppermute x4, waiting for transfers between devices, partner(): lax.ppermute(array, axis, [(i, i ^ 1 << bit) for i in range(lax.axis_size...  13.6 us
    all_gather x2, blocking collectives, backward_slot(): lax.all_gather(upstream, 'tensor', axis=0, tiled=True)  13.6 us
    all_gather x2, blocking collectives, backward_slot(): lax.all_gather(normed, 'tensor', axis=0, tiled=True)  12.8 us
  transfers between devices with their start and end apart: 7, of which 4 were waited for; matrix products, arithmetic and copies ran while one was open for 9% of the time, Pallas kernels for 0%

commit v1 on v0

v1 whole, which is shorter than its diff:
```python
import jax
import jax.numpy as jnp
from jax import lax
from jax.experimental import pallas as pl
from jax.experimental.pallas import tpu as pltpu
from jax.sharding import PartitionSpec as P

EPSILON = 1e-05
F32, BF16 = jnp.float32, jnp.bfloat16
NT = (((1,), (1,)), ((), ()))
TN = (((0,), (0,)), ((), ()))
NN = (((1,), (0,)), ((), ()))
SCOPED = 20 << 20
SMEM = pl.BlockSpec(memory_space=pltpu.SMEM)
VMEM = pl.BlockSpec(memory_space=pltpu.VMEM)


def call(body, out_shape, operands, flops=0, aliases=None):
    size = lambda a: a.size * a.dtype.itemsize
    single = not isinstance(out_shape, (list, tuple))
    outs = [out_shape] if single else list(out_shape)
    moved = sum(size(a) for a in operands) + sum(size(a) for a in outs)
    return pl.pallas_call(
        body,
        in_specs=[SMEM] + [VMEM] * (len(operands) - 1),
        out_specs=VMEM if single else [VMEM] * len(outs),
        out_shape=out_shape,
        input_output_aliases=aliases or {},
        compiler_params=pltpu.CompilerParams(vmem_limit_bytes=SCOPED),
        cost_estimate=pl.CostEstimate(flops=flops, bytes_accessed=moved, transcendentals=0),
    )(*operands)


def shape(dims, dtype):
    return jax.ShapeDtypeStruct(tuple(dims), dtype)


def grad_mixed_part(scalars, pieces, w_output, other, offset, size, received=None):
    rows = sum(p.shape[0] for p in pieces)
    half = w_output.shape[0] // 2
    count = len(pieces)

    def body(s, *refs):
        ups = jnp.concatenate([r[...] for r in refs[:count]], axis=0)
        w = refs[count]
        core = 1 - s[0] if other else s[0]
        start = pl.multiple_of(core * half + offset, 128)
        part = lax.dot_general(ups, w[pl.ds(start, size), :], NT, preferred_element_type=F32)
        if other:
            refs[count + 1][...] = part.astype(BF16)
        else:
            part = part + refs[count + 1][...].astype(F32)
            refs[count + 2][...] = part
            refs[count + 3][...] = part.astype(BF16)

    flops = 2 * rows * size * w_output.shape[1]
    if other:
        return call(body, shape((rows, size), BF16), [scalars, *pieces, w_output], flops)
    outs = [shape((rows, size), F32), shape((rows, size), BF16)]
    return call(body, outs, [scalars, *pieces, w_output, received], flops)


def unmix(scalars, kept, received, mixing, first_head):
    rows, size = kept.shape
    count = len(received)
    heads = mixing.shape[0] * size // (mixing.shape[0] * 128)

    def body(s, *refs):
        mix, out = refs[count + 1], refs[count + 2]
        for h in range(size // 128):
            cols = slice(h * 128, (h + 1) * 128)
            total = refs[0][:, cols]
            for r in refs[1 : count + 1]:
                total = total + r[:, cols].astype(F32)
            out[:, cols] = lax.dot_general(
                mix[first_head + h], total.astype(BF16), TN, preferred_element_type=F32
            ).astype(BF16)

    return call(
        body, shape((rows, size), BF16), [scalars, kept, *received, mixing], 2 * heads * rows * rows * 128
    )


def grad_normed_part(scalars, grads, w_value, other, offset, total=None):
    rows, size = grads.shape
    half = w_value.shape[1] // 2
    width = w_value.shape[0]

    def body(s, v, w, *refs):
        core = 1 - s[0] if other else s[0]
        start = pl.multiple_of(core * half + offset, 128)
        term = lax.dot_general(v[...], w[:, pl.ds(start, size)], NT, preferred_element_type=F32)
        if total is not None:
            term = term + refs[0][...]
        refs[-1][...] = term

    operands = [scalars, grads, w_value] + ([] if total is None else [total])
    return call(body, shape((rows, width), F32), operands, 2 * rows * size * width)


def grad_normed_last(scalars, grads, w_value, other, offset, total, inputs, pieces):
    rows, size = grads.shape
    half = w_value.shape[1] // 2
    width = w_value.shape[0]
    own = rows // pieces

    def body(s, v, w, total_ref, in_ref, keep, stats, *sends):
        core = 1 - s[0] if other else s[0]
        start = pl.multiple_of(core * half + offset, 128)
        term = lax.dot_general(v[...], w[:, pl.ds(start, size)], NT, preferred_element_type=F32)
        term = term + total_ref[...]
        keep[...] = term[:own]
        for t, ref in enumerate(sends):
            ref[...] = term[(t + 1) * own : (t + 2) * own].astype(BF16)
        stats[...] = stacked(
            [
                jnp.sum(term, axis=1, keepdims=True),
                jnp.sum(term * in_ref[...].astype(F32), axis=1, keepdims=True),
            ]
        )

    outs = [shape((own, width), F32), shape((8, rows), F32)]
    outs += [shape((own, width), BF16)] * (pieces - 1)
    operands = [scalars, grads, w_value, total, inputs]
    return call(body, outs, operands, 2 * rows * size * width)


def stacked(columns):
    rows = columns[0].shape[0]
    lane = lax.broadcasted_iota(jnp.int32, (rows, 128), 1)
    wide = jnp.zeros((rows, 128), F32)
    for k, column in enumerate(columns):
        wide = jnp.where(lane == k, column, wide)
    return wide.T[:8]


def as_columns(stats):
    rows = stats.shape[1]
    return jnp.concatenate([stats, jnp.zeros((120, rows), F32)], axis=0).T


def order_inputs(scalars, stores):
    slots, own, width = stores[0].shape
    count = len(stores)
    rows = own * count

    def body(s, *refs):
        outs, stats = refs[count : count + slots], refs[count + slots]
        columns = []
        for k in range(slots):
            picked = jnp.concatenate([r[s[1 + k]] for r in refs[:count]], axis=0)
            outs[k][...] = picked
            floats = picked.astype(F32)
            columns += [
                jnp.sum(floats, axis=1, keepdims=True),
                jnp.sum(floats * floats, axis=1, keepdims=True),
            ]
        stats[...] = stacked(columns)

    outs = [shape((rows, width), BF16)] * slots + [shape((8, rows), F32)]
    return call(body, outs, [scalars, *stores])


def normalize(scalars, inputs, stats, width):
    slots, (rows, part) = len(inputs), inputs[0].shape
    count = len(stats)

    def body(s, *refs):
        total = refs[slots][...]
        for r in refs[slots + 1 : slots + count]:
            total = total + r[...]
        columns = as_columns(total)
        for k in range(slots):
            center = columns[:, 2 * k : 2 * k + 1] / width
            inverse = lax.rsqrt(columns[:, 2 * k + 1 : 2 * k + 2] / width - center * center + EPSILON)
            floats = refs[k][...].astype(F32)
            refs[slots + count][k * rows : (k + 1) * rows, :] = ((floats - center) * inverse).astype(BF16)

    return call(body, shape((slots * rows, part), BF16), [scalars, *inputs, *stats])


def finish(scalars, keep, received, upstream, inputs, slot, input_stats, grad_stats, crossed, width):
    own, part = keep.shape
    rows = inputs.shape[0]
    n_in, n_grad, n_recv = len(input_stats), len(grad_stats), len(received)

    def body(s, keep_ref, ups_ref, in_ref, *refs):
        recv = refs[:n_recv]
        ins = refs[n_recv : n_recv + n_in]
        grads = refs[n_recv + n_in : n_recv + n_in + n_grad]
        out = refs[-1]
        total_in = ins[0][...]
        for r in ins[1:]:
            total_in = total_in + r[...]
        total = grads[0][...]
        for r, t in zip(grads[1:], crossed[1:], strict=True):
            got = r[...]
            if t:
                got = jnp.concatenate(
                    [got[:, (b ^ t) * own : ((b ^ t) + 1) * own] for b in range(rows // own)], axis=1
                )
            total = total + got
        in_columns = as_columns(total_in)[:own]
        columns = as_columns(total)[:own]
        center = in_columns[:, 2 * slot : 2 * slot + 1] / width
        inverse = lax.rsqrt(in_columns[:, 2 * slot + 1 : 2 * slot + 2] / width - center * center + EPSILON)
        first = columns[:, 0:1]
        second = (columns[:, 1:2] - center * first) * inverse
        grad = keep_ref[...]
        for r in recv:
            grad = grad + r[...].astype(F32)
        scaled = (in_ref[:own].astype(F32) - center) * inverse
        out[...] = (
            ups_ref[...].astype(F32) + inverse * (grad - first / width - scaled * (second / width))
        ).astype(BF16)

    operands = [scalars, keep, upstream, inputs, *received, *input_stats, *grad_stats]
    return call(body, shape((own, part), BF16), operands)


def value_grad_part(scalars, normed, grads, result, dims, other, offset):
    depth, width = normed.shape
    size = grads[0].shape[1]
    half = dims[1] // 2
    block = width // 3 if width % 3 == 0 and width // 3 % 128 == 0 else width // 2
    count = len(grads)

    def body(s, n, *refs):
        v = jnp.concatenate([r[...] for r in refs[:count]], axis=0)
        refs[-1][...] = lax.dot_general(n[...], v, TN, preferred_element_type=F32).astype(BF16)

    def place(i, s):
        core = 1 - s[0] if other else s[0]
        return (i, core * (half // size) + offset // size)

    in_specs = [pl.BlockSpec((depth, block), lambda i, s: (0, i))]
    in_specs += [pl.BlockSpec(g.shape, lambda i, s: (0, 0)) for g in grads]
    operands = [scalars, normed, *grads]
    aliases = {}
    if result is not None:
        in_specs.append(pl.BlockSpec(memory_space=pl.ANY))
        aliases = {len(operands): 0}
        operands.append(result)
    return pl.pallas_call(
        body,
        grid_spec=pltpu.PrefetchScalarGridSpec(
            num_scalar_prefetch=1,
            grid=(width // block,),
            in_specs=in_specs,
            out_specs=pl.BlockSpec((block, size), place),
        ),
        out_shape=shape(dims, BF16),
        input_output_aliases=aliases,
        compiler_params=pltpu.CompilerParams(vmem_limit_bytes=SCOPED),
        cost_estimate=pl.CostEstimate(
            flops=2 * depth * width * size, bytes_accessed=2 * width * size, transcendentals=0
        ),
    )(*operands)


def mixing_weights(slopes, places):
    distance = (places[:, None] - places[None, :]).astype(F32)
    causal = distance >= 0
    logits = -slopes[:, None, None] * jnp.where(causal, distance, 0.0)[None, :, :]
    weights = jnp.where(causal[None, :, :], jnp.exp(logits), 0.0)
    return (weights / jnp.sum(weights, axis=-1, keepdims=True)).astype(BF16)


def flipped(array, axis, mask):
    return lax.ppermute(array, axis, [(i, i ^ mask) for i in range(lax.axis_size(axis))])


def on_device(parked, arriving, slot_table, value_weight, output_weight, slopes):
    sections, tensors, parts = (lax.axis_size(a) for a in ("section", "tensor", "dp"))
    section, tensor, part = (lax.axis_index(a) for a in ("section", "tensor", "dp"))
    core = part % 2
    w_value = pltpu.with_memory_space_constraint(value_weight[0], pltpu.VMEM)
    w_output = pltpu.with_memory_space_constraint(output_weight[0], pltpu.VMEM)
    slots, own, part_width = parked.shape[1:]
    width = part_width * parts
    half = w_output.shape[0] // 2
    others = range(1, tensors)
    chips = range(2, parts, 2)
    bounds = [0, half // 2, half]
    chunks = [(a, b - a) for a, b in zip(bounds[:-1], bounds[1:], strict=True)]

    table = lax.dynamic_index_in_dim(slot_table, section, 0, keepdims=False)
    scalars = jnp.concatenate([core[None], table]).astype(jnp.int32)

    upstream = arriving[0]
    pieces = [upstream] + [flipped(upstream, "tensor", t) for t in others]
    store = lax.ppermute(parked[0], "section", [(i, sections - 1 - i) for i in range(sections)])
    stores = [store] + [flipped(store, "tensor", t) for t in others]

    blocks = jnp.arange(tensors) ^ tensor
    places = (blocks[:, None] * own + jnp.arange(own)[None, :]).reshape(-1)
    heads = slopes.shape[0] // 2
    mixing = mixing_weights(lax.dynamic_slice_in_dim(slopes, core * heads, heads), places)

    ordered = order_inputs(scalars, stores)
    inputs, stats = ordered[:slots], ordered[slots]
    stats = stats + flipped(stats, "dp", 1)
    input_stats = [stats] + [flipped(stats, "dp", m) for m in chips]

    values = []
    for slot in range(slots):
        if slot > 0:
            pieces = [
                lax.ppermute(
                    upstream,
                    ("section", "tensor"),
                    [(i * tensors + j, (i - 1) * tensors + (j ^ t)) for i in range(1, sections) for j in range(tensors)],
                )
                for t in range(tensors)
            ]
            upstream = pieces[0]
        sends = [grad_mixed_part(scalars, pieces, w_output, True, a, n) for a, n in chunks]
        halves = [flipped(x, "dp", 1) for x in sends]
        kept = [
            grad_mixed_part(scalars, pieces, w_output, False, a, n, x)
            for (a, n), x in zip(chunks, halves, strict=True)
        ]
        across = [[flipped(x, "dp", m) for m in chips] for _, x in kept]
        mine = [
            unmix(scalars, k, x, mixing, a // 128)
            for (k, _), x, (a, n) in zip(kept, across, chunks, strict=True)
        ]
        theirs = [flipped(x, "dp", 1) for x in mine]
        values.append([mine, theirs])
        total = None
        for j, (a, n) in enumerate(chunks):
            total = grad_normed_part(scalars, mine[j], w_value, False, a, total)
            if j + 1 < len(chunks):
                total = grad_normed_part(scalars, theirs[j], w_value, True, a, total)
        keep, stats, *sends = grad_normed_last(
            scalars, theirs[-1], w_value, True, chunks[-1][0], total, inputs[slot], tensors
        )
        received = [flipped(x, "tensor", t) for t, x in zip(others, sends, strict=True)]
        stats = stats + flipped(stats, "dp", 1)
        routes = [(t, m) for t in range(tensors) for m in range(0, parts, 2) if t or m]
        grad_stats = [stats] + [flipped(stats, ("tensor", "dp"), t * parts + m) for t, m in routes]
        upstream = finish(
            scalars, keep, received, upstream, inputs[slot], slot, input_stats, grad_stats,
            [0] + [t for t, _ in routes], width,
        )

    normed = normalize(scalars, inputs, input_stats, width)
    result = None
    for j, (a, n) in enumerate(chunks):
        for side in range(2):
            result = value_grad_part(
                scalars, normed, [v[side][j] for v in values], result, w_value.shape, side == 1, a
            )
    return (upstream[None], result[None])


def solution(mesh):
    in_specs = (
        P("section", None, "tensor", "dp"),
        P("section", "tensor", "dp"),
        P(),
        P("section", "dp", "tensor"),
        P("section", "tensor", "dp"),
        P("tensor"),
    )
    out_specs = (P("section", "tensor", "dp"), P("section", "dp", "tensor"))
    return jax.shard_map(
        on_device, mesh=mesh, in_specs=in_specs, out_specs=out_specs, check_vma=False
    )
```

time: 259 us -> 118 us (0.46)
  blocking collectives: 124 us -> 0 us
  matrix products: 65.2 us -> 0 us
  Pallas kernels: 0 us -> 49 us
  starting transfers between devices: 7.7 us -> 28.3 us
  between operations: 18.2 us -> 1.05 us
  other arithmetic: 7.26 us -> 2.58 us
    psum x4 -> x0, blocking collectives: 97.9 us -> none  [across_width(): return lax.psum(parts, 'dp')]
    dot_general x8 -> x0, matrix products: 65.2 us -> none  [the longest x2 24.9 us: backward_slot(): lax.dot_general(normed_all, grad_value, (((0,), (0,)), ((), ())), preferr...]
    pallas_call x0 -> x28, Pallas kernels: none -> 49 us  [the longest x24 35.1 us: call(): pl.pallas_call(body, in_specs=[SMEM] + [VMEM] * (len(operands) - 1), out_...]
    all_gather x4 -> x0, blocking collectives: 26.4 us -> none  [the longest x2 13.6 us: backward_slot(): lax.all_gather(upstream, 'tensor', axis=0, tiled=True)]
    ppermute x5 -> x29, starting transfers between devices: 7.62 us -> 28.3 us  [the longest x26 22 us: flipped(): lax.ppermute(array, axis, [(i, i ^ mask) for i in range(lax.axis_size(axi...]
    ppermute x5 -> x29, waiting for transfers between devices: 13.6 us -> 31.1 us  [the longest x26 19.4 us: flipped(): lax.ppermute(array, axis, [(i, i ^ mask) for i in range(lax.axis_size(axi...]
    reduce_scatter x2 -> x0, waiting for transfers between devices: 16.4 us -> none  [backward_slot(): lax.psum_scatter(lax.dot_general(grad_value, w_value, (((1,), (1,)), ((),...]
    unnamed x26 -> x20, local copies, waits for them, and re-layouts: 0.81 us -> 5.55 us
  transfers between devices with their start and end apart: 7 -> 29, of which waited for: 4 -> 10; matrix products, arithmetic and copies ran while one was open for 9% -> 2% of each run, Pallas kernels for 0% -> 35%
where the time goes in v1:
time: 118 us
  Pallas kernels  49 us (42%)
  waiting for transfers between devices  31.1 us (26%)
  starting transfers between devices  28.3 us (24%)
  local copies, waits for them, and re-layouts  5.83 us (5%)
  other arithmetic  2.58 us (2%)
    pallas_call x24, Pallas kernels, call(): pl.pallas_call(body, in_specs=[SMEM] + [VMEM] * (len(operands) - 1), out_...  35.1 us
    ppermute x26, starting transfers between devices, flipped(): lax.ppermute(array, axis, [(i, i ^ mask) for i in range(lax.axis_size(axi...  22 us
    ppermute x26, waiting for transfers between devices, flipped(): lax.ppermute(array, axis, [(i, i ^ mask) for i in range(lax.axis_size(axi...  19.4 us
    pallas_call x4, Pallas kernels, value_grad_part(): pl.pallas_call(body, grid_spec=pltpu.PrefetchScalarGridSpec(num_scalar_pr...  13.9 us
    ppermute x2, waiting for transfers between devices, on_device(): lax.ppermute(upstream, ('section', 'tensor'), [(i * tensors + j, (i - 1)...  11.7 us
    unnamed x20, local copies, waits for them, and re-layouts  5.55 us
    ppermute x1, starting transfers between devices, on_device(): lax.ppermute(parked[0], 'section', [(i, sections - 1 - i) for i in range(...  3.6 us
    ppermute x2, starting transfers between devices, on_device(): lax.ppermute(upstream, ('section', 'tensor'), [(i * tensors + j, (i - 1)...  2.76 us
  transfers between devices with their start and end apart: 29, of which 10 were waited for; matrix products, arithmetic and copies ran while one was open for 2% of the time, Pallas kernels for 35%

profile of v1, /device:TPU:0, one launch (start us, length us, event | category | flops | bytes accessed | tf_op | source)
XLA Modules:
  0.0 117.9 jit_solution(4112273585094290036)
XLA Ops:
  0.6 3.0 %collective-permute-start = (bf16[64,1536]{1,0:T(8,128)(2,1)}, bf16[64,1536]{1,0:T(8,128)(2,1)S(1)}, u32[]{:S(2)}, u32[]{:S(2)}) collective-permute-start(bf16[64,1536]{1,0:T(8,128)(2,1)} %bitcast.27), channel_id=1, source_target_pairs={{0,4},{4,0},{1,5},{5,1},{2,6},{6,2},{3,7},{7,3},{8,12},{12,8},{9,1... | collective-permute-start | bytes 589832 | tf_op jit(solution)/shard_map/ppermute | solution.py:270
  3.6 3.6 %collective-permute-start.7 = (bf16[2,64,1536]{2,1,0:T(8,128)(2,1)}, bf16[2,64,1536]{2,1,0:T(8,128)(2,1)S(1)}, u32[]{:S(2)}, u32[]{:S(2)}) collective-permute-start(bf16[2,64,1536]{2,1,0:T(8,128)(2,1)} %bitcast.35), channel_id=1, source_target_pairs={{0,24},{8,16},{16,8},{24,0},{1,25},{9,17},{17,9},{25,1},{2,26},{10... | collective-permute-start | bytes 1179656 | tf_op jit(solution)/shard_map/ppermute | solution.py:292
  8.8 4.6 %copy-done.1 = bf16[1,4096,1536]{2,1,0:T(8,128)(2,1)S(1)} copy-done((bf16[1,4096,1536]{2,1,0:T(8,128)(2,1)S(1)}, bf16[1,4096,1536]{2,1,0:T(8,128)(2,1)}, u32[]{:S(2)}) %copy-start.1) | copy-done | bytes 12582936
  13.3 0.9 copy-done.2
  14.3 1.7 %shard_map.80 = bf16[128,1024]{1,0:T(8,128)(2,1)S(1)} custom-call(s32[3]{0:T(128)S(1)} %pad_add_fusion.s, bf16[64,1536]{1,0:T(8,128)(2,1)S(1)} %bitcast.28, bf16[64,1536]{1,0:T(8,128)(2,1)S(1)} %collective-permute-done.refs_1_, bf16[4096,1536]{1,0:T(8,128)(2,1)S(1)} %bitcast.7), custom_call_target="tpu_custom_call" | custom-call | flops 402653184 | bytes 13238284 | tf_op jit(solution)/shard_map/pallas_call | solution.py:23
  16.0 1.7 %shard_map.77 = bf16[128,1024]{1,0:T(8,128)(2,1)S(1)} custom-call(s32[3]{0:T(128)S(1)} %pad_add_fusion.s, bf16[64,1536]{1,0:T(8,128)(2,1)S(1)} %bitcast.29, bf16[64,1536]{1,0:T(8,128)(2,1)S(1)} %collective-permute-done.refs_1_, bf16[4096,1536]{1,0:T(8,128)(2,1)S(1)} %bitcast.8), custom_call_target="tpu_custom_call" | custom-call | flops 402653184 | bytes 13238284 | tf_op jit(solution)/shard_map/pallas_call | solution.py:23
  18.4 1.8 %collective-permute-start.8 = (bf16[2,64,1536]{2,1,0:T(8,128)(2,1)S(1)}, bf16[2,64,1536]{2,1,0:T(8,128)(2,1)S(1)}, u32[]{:S(2)}, u32[]{:S(2)}) collective-permute-start(bf16[2,64,1536]{2,1,0:T(8,128)(2,1)S(1)} %collective-permute-done.7.refs_0_), channel_id=1, source_target_pairs={{0,4},{4,0},{1,5},{5,1},{2,6},{6,2},{3,7},{7,3},{8,12},{12,8},{9,1... | collective-permute-start | bytes 1179656 | tf_op jit(solution)/shard_map/ppermute | solution.py:270
  20.2 1.7 %shard_map.81 = (f32[128,1024]{1,0:T(8,128)S(1)}, bf16[128,1024]{1,0:T(8,128)(2,1)S(1)}) custom-call(s32[3]{0:T(128)S(1)} %pad_add_fusion.s, bf16[64,1536]{1,0:T(8,128)(2,1)S(1)} %bitcast.30, bf16[64,1536]{1,0:T(8,128)(2,1)S(1)} %collective-permute-done.refs_1_, bf16[4096,1536]{1,0:T(8,128)(2,1)S(1)} %bitcast.9, ...), custom_call_target="tpu_custom_call" | custom-call | flops 402653184 | bytes 14024716 | tf_op jit(solution)/shard_map/pallas_call | solution.py:23
  21.9 1.6 %collective-permute-start.5 = (bf16[128,1024]{1,0:T(8,128)(2,1)S(1)}, bf16[128,1024]{1,0:T(8,128)(2,1)S(1)}, u32[]{:S(2)}, u32[]{:S(2)}) collective-permute-start(bf16[128,1024]{1,0:T(8,128)(2,1)S(1)} %get-tuple-element.22), channel_id=1, source_target_pairs={{0,2},{1,3},{2,0},{3,1},{4,6},{5,7},{6,4},{7,5},{8,10},{9,11},{10,... | collective-permute-start | bytes 786440 | tf_op jit(solution)/shard_map/ppermute | solution.py:270
  23.5 1.7 %shard_map.78 = (f32[128,1024]{1,0:T(8,128)S(1)}, bf16[128,1024]{1,0:T(8,128)(2,1)S(1)}) custom-call(s32[3]{0:T(128)S(1)} %pad_add_fusion.s, bf16[64,1536]{1,0:T(8,128)(2,1)S(1)} %bitcast.31, bf16[64,1536]{1,0:T(8,128)(2,1)S(1)} %collective-permute-done.refs_1_, bf16[4096,1536]{1,0:T(8,128)(2,1)S(1)} %bitcast.10, ...), custom_call_target="tpu_custom_call" | custom-call | flops 402653184 | bytes 14024716 | tf_op jit(solution)/shard_map/pallas_call | solution.py:23
  25.7 1.5 %fusion.2.refs_2_ = bf16[16,128,128]{2,1,0:T(8,128)(2,1)S(1)} fusion(f32[128,128]{1,0:T(8,128)S(1)} %convert_select_fusion, f32[16]{0:T(128)S(1)} %dynamic-slice_negate_fusion, pred[128,128]{1,0:T(8,128)(4,1)S(1)} %convert_compare_fusion), kind=kOutput, calls=%fused_computation.2 | output fusion | flops 1050751 | bytes 606272 | tf_op jit(solution)/shard_map/div | solution.py:266
  27.3 3.9 %collective-permute-done.5.refs_1_ = bf16[128,1024]{1,0:T(8,128)(2,1)S(1)} collective-permute-done((bf16[128,1024]{1,0:T(8,128)(2,1)S(1)}, bf16[128,1024]{1,0:T(8,128)(2,1)S(1)}, u32[]{:S(2)}, u32[]{:S(2)}) %collective-permute-start.5) | collective-permute-done | bytes 262176 | tf_op jit(solution)/shard_map/ppermute | solution.py:270
  32.1 3.5 %collective-permute-done.2.refs_1_ = bf16[128,1024]{1,0:T(8,128)(2,1)S(1)} collective-permute-done((bf16[128,1024]{1,0:T(8,128)(2,1)S(1)}, bf16[128,1024]{1,0:T(8,128)(2,1)S(1)}, u32[]{:S(2)}, u32[]{:S(2)}) %collective-permute-start.2) | collective-permute-done | bytes 262176 | tf_op jit(solution)/shard_map/ppermute | solution.py:270
  36.5 1.7 %shard_map.83.refs_0_ = f32[128,1536]{1,0:T(8,128)S(1)} custom-call(s32[3]{0:T(128)S(1)} %pad_add_fusion.s, bf16[128,1024]{1,0:T(8,128)(2,1)S(1)} %shard_map.82.v.refs_0_, bf16[1536,4096]{1,0:T(8,128)(2,1)S(1)} %bitcast.19), custom_call_target="tpu_custom_call" | custom-call | flops 402653184 | bytes 13631500 | tf_op jit(solution)/shard_map/pallas_call | solution.py:23
  38.2 0.9 shard_map.86
  39.1 1.7 %shard_map.84.refs_0_ = f32[128,1536]{1,0:T(8,128)S(1)} custom-call(s32[3]{0:T(128)S(1)} %pad_add_fusion.s, bf16[128,1024]{1,0:T(8,128)(2,1)S(1)} %collective-permute-done.6.v.refs_0_, bf16[1536,4096]{1,0:T(8,128)(2,1)S(1)} %bitcast.20, f32[128,1536]{1,0:T(8,128)S(1)} %shard_map.83.refs_0_), custom_call_target="tpu_custom_call" | custom-call | flops 402653184 | bytes 14417932 | tf_op jit(solution)/shard_map/pallas_call | solution.py:23
  40.8 1.7 %shard_map.85.total_ref = f32[128,1536]{1,0:T(8,128)S(1)} custom-call(s32[3]{0:T(128)S(1)} %pad_add_fusion.s, bf16[128,1024]{1,0:T(8,128)(2,1)S(1)} %shard_map.79.v.refs_0_, bf16[1536,4096]{1,0:T(8,128)(2,1)S(1)} %bitcast.21, f32[128,1536]{1,0:T(8,128)S(1)} %shard_map.84.refs_0_), custom_call_target="tpu_custom_call" | custom-call | flops 402653184 | bytes 14417932 | tf_op jit(solution)/shard_map/pallas_call | solution.py:23
  42.6 1.9 %shard_map.87 = (f32[64,1536]{1,0:T(8,128)S(1)}, f32[8,128]{1,0:T(8,128)S(1)}, bf16[64,1536]{1,0:T(8,128)(2,1)S(1)}) custom-call(s32[3]{0:T(128)S(1)} %pad_add_fusion.s, bf16[128,1024]{1,0:T(8,128)(2,1)S(1)} %collective-permute-done.3.v.refs_0_, bf16[1536,4096]{1,0:T(8,128)(2,1)S(1)} %bitcast.22, f32[128,1536]{1,0:T(8,128)S(1)} %shard_map.85.total_ref, ...), custom_call_target="tpu_custom_call" | custom-call | flops 402653184 | bytes 14618636 | tf_op jit(solution)/shard_map/pallas_call | solution.py:23
  46.0 1.7 %collective-permute-start.11 = (f32[8,128]{1,0:T(8,128)S(1)}, f32[8,128]{1,0:T(8,128)S(1)}, u32[]{:S(2)}, u32[]{:S(2)}) collective-permute-start(f32[8,128]{1,0:T(8,128)S(1)} %add.51.refs_1_.refs_2_), channel_id=1, source_target_pairs={{0,2},{1,3},{2,0},{3,1},{4,6},{5,7},{6,4},{7,5},{8,10},{9,11},{10,... | collective-permute-start | bytes 12296 | tf_op jit(solution)/shard_map/ppermute | solution.py:270
  47.7 1.4 %collective-permute-start.15 = (f32[8,128]{1,0:T(8,128)S(1)}, f32[8,128]{1,0:T(8,128)S(1)}, u32[]{:S(2)}, u32[]{:S(2)}) collective-permute-start(f32[8,128]{1,0:T(8,128)S(1)} %add.52.refs_3_), channel_id=1, source_target_pairs={{0,6},{1,7},{2,4},{3,5},{4,2},{5,3},{6,0},{7,1},{8,14},{9,15},{10,... | collective-permute-start | bytes 12296 | tf_op jit(solution)/shard_map/ppermute | solution.py:270
  49.5 1.7 %collective-permute-start.13 = (f32[8,128]{1,0:T(8,128)S(1)}, f32[8,128]{1,0:T(8,128)S(1)}, u32[]{:S(2)}, u32[]{:S(2)}) collective-permute-start(f32[8,128]{1,0:T(8,128)S(1)} %add.52.refs_3_), channel_id=1, source_target_pairs={{0,2},{1,3},{2,0},{3,1},{4,6},{5,7},{6,4},{7,5},{8,10},{9,11},{10,... | collective-permute-start | bytes 12296 | tf_op jit(solution)/shard_map/ppermute | solution.py:270
  51.2 1.6 %collective-permute-done.15.refs_6_ = f32[8,128]{1,0:T(8,128)S(1)} collective-permute-done((f32[8,128]{1,0:T(8,128)S(1)}, f32[8,128]{1,0:T(8,128)S(1)}, u32[]{:S(2)}, u32[]{:S(2)}) %collective-permute-start.15) | collective-permute-done | bytes 4128 | tf_op jit(solution)/shard_map/ppermute | solution.py:270
  53.1 0.9 shard_map.88
  54.0 1.3 %collective-permute-start.17 = (bf16[64,1536]{1,0:T(8,128)(2,1)S(1)}, bf16[64,1536]{1,0:T(8,128)(2,1)S(1)}, u32[]{:S(2)}, u32[]{:S(2)}) collective-permute-start(bf16[64,1536]{1,0:T(8,128)(2,1)S(1)} %shard_map.88), channel_id=1, source_target_pairs={{8,4},{12,0},{16,12},{20,8},{24,20},{28,16},{9,5},{13,1},{17,13},{... | collective-permute-start | bytes 589832 | tf_op jit(solution)/shard_map/ppermute | solution.py:309
  55.3 1.5 %collective-permute-start.16 = (bf16[64,1536]{1,0:T(8,128)(2,1)S(1)}, bf16[64,1536]{1,0:T(8,128)(2,1)S(1)}, u32[]{:S(2)}, u32[]{:S(2)}) collective-permute-start(bf16[64,1536]{1,0:T(8,128)(2,1)S(1)} %shard_map.88), channel_id=1, source_target_pairs={{8,0},{12,4},{16,8},{20,12},{24,16},{28,20},{9,1},{13,5},{17,9},{2... | collective-permute-start | bytes 589832 | tf_op jit(solution)/shard_map/ppermute | solution.py:309
  56.8 9.9 %collective-permute-done.17.refs_1_ = bf16[64,1536]{1,0:T(8,128)(2,1)S(1)} collective-permute-done((bf16[64,1536]{1,0:T(8,128)(2,1)S(1)}, bf16[64,1536]{1,0:T(8,128)(2,1)S(1)}, u32[]{:S(2)}, u32[]{:S(2)}) %collective-permute-start.17) | collective-permute-done | bytes 196640 | tf_op jit(solution)/shard_map/ppermute | solution.py:309
  66.7 1.8 %collective-permute-done.16.refs_0_.ups_ref = bf16[64,1536]{1,0:T(8,128)(2,1)S(1)} collective-permute-done((bf16[64,1536]{1,0:T(8,128)(2,1)S(1)}, bf16[64,1536]{1,0:T(8,128)(2,1)S(1)}, u32[]{:S(2)}, u32[]{:S(2)}) %collective-permute-start.16) | collective-permute-done | bytes 196640 | tf_op jit(solution)/shard_map/ppermute | solution.py:309
  68.5 1.7 %shard_map.92 = bf16[128,1024]{1,0:T(8,128)(2,1)S(1)} custom-call(s32[3]{0:T(128)S(1)} %pad_add_fusion.s, bf16[64,1536]{1,0:T(8,128)(2,1)S(1)} %collective-permute-done.16.refs_0_.ups_ref, bf16[64,1536]{1,0:T(8,128)(2,1)S(1)} %collective-permute-done.17.refs_1_, bf16[4096,1536]{1,0:T(8,128)(2,1)S(1)} %bitcast.13), custom_call_target="tpu_custom_call" | custom-call | flops 402653184 | bytes 13238284 | tf_op jit(solution)/shard_map/pallas_call | solution.py:23
  70.3 1.7 %shard_map.89 = bf16[128,1024]{1,0:T(8,128)(2,1)S(1)} custom-call(s32[3]{0:T(128)S(1)} %pad_add_fusion.s, bf16[64,1536]{1,0:T(8,128)(2,1)S(1)} %collective-permute-done.16.refs_0_.ups_ref, bf16[64,1536]{1,0:T(8,128)(2,1)S(1)} %collective-permute-done.17.refs_1_, bf16[4096,1536]{1,0:T(8,128)(2,1)S(1)} %bitcast.14), custom_call_target="tpu_custom_call" | custom-call | flops 402653184 | bytes 13238284 | tf_op jit(solution)/shard_map/pallas_call | solution.py:23
  72.5 1.7 %shard_map.93 = (f32[128,1024]{1,0:T(8,128)S(1)}, bf16[128,1024]{1,0:T(8,128)(2,1)S(1)}) custom-call(s32[3]{0:T(128)S(1)} %pad_add_fusion.s, bf16[64,1536]{1,0:T(8,128)(2,1)S(1)} %collective-permute-done.16.refs_0_.ups_ref, bf16[64,1536]{1,0:T(8,128)(2,1)S(1)} %collective-permute-done.17.refs_1_, bf16[4096,1536]{1,0:T(8,128)(2,1)S(1)} %bitcast.15, ...), custom_call_target="tpu_custom_call" | custom-call | flops 402653184 | bytes 14024716 | tf_op jit(solution)/shard_map/pallas_call | solution.py:23
  74.2 1.5 %collective-permute-start.22 = (bf16[128,1024]{1,0:T(8,128)(2,1)S(1)}, bf16[128,1024]{1,0:T(8,128)(2,1)S(1)}, u32[]{:S(2)}, u32[]{:S(2)}) collective-permute-start(bf16[128,1024]{1,0:T(8,128)(2,1)S(1)} %get-tuple-element.31), channel_id=1, source_target_pairs={{0,2},{1,3},{2,0},{3,1},{4,6},{5,7},{6,4},{7,5},{8,10},{9,11},{10,... | collective-permute-start | bytes 786440 | tf_op jit(solution)/shard_map/ppermute | solution.py:270
  75.8 1.7 %shard_map.90 = (f32[128,1024]{1,0:T(8,128)S(1)}, bf16[128,1024]{1,0:T(8,128)(2,1)S(1)}) custom-call(s32[3]{0:T(128)S(1)} %pad_add_fusion.s, bf16[64,1536]{1,0:T(8,128)(2,1)S(1)} %collective-permute-done.16.refs_0_.ups_ref, bf16[64,1536]{1,0:T(8,128)(2,1)S(1)} %collective-permute-done.17.refs_1_, bf16[4096,1536]{1,0:T(8,128)(2,1)S(1)} %bitcast.16, ...), custom_call_target="tpu_custom_call" | custom-call | flops 402653184 | bytes 14024716 | tf_op jit(solution)/shard_map/pallas_call | solution.py:23
  78.1 5.4 %collective-permute-done.22.refs_1_ = bf16[128,1024]{1,0:T(8,128)(2,1)S(1)} collective-permute-done((bf16[128,1024]{1,0:T(8,128)(2,1)S(1)}, bf16[128,1024]{1,0:T(8,128)(2,1)S(1)}, u32[]{:S(2)}, u32[]{:S(2)}) %collective-permute-start.22) | collective-permute-done | bytes 262176 | tf_op jit(solution)/shard_map/ppermute | solution.py:270
  84.4 3.8 %collective-permute-done.19.refs_1_ = bf16[128,1024]{1,0:T(8,128)(2,1)S(1)} collective-permute-done((bf16[128,1024]{1,0:T(8,128)(2,1)S(1)}, bf16[128,1024]{1,0:T(8,128)(2,1)S(1)}, u32[]{:S(2)}, u32[]{:S(2)}) %collective-permute-start.19) | collective-permute-done | bytes 262176 | tf_op jit(solution)/shard_map/ppermute | solution.py:270
  89.0 0.9 shard_map.100.n
  90.0 1.7 %shard_map.95.refs_0_ = f32[128,1536]{1,0:T(8,128)S(1)} custom-call(s32[3]{0:T(128)S(1)} %pad_add_fusion.s, bf16[128,1024]{1,0:T(8,128)(2,1)S(1)} %shard_map.94.v.refs_1_, bf16[1536,4096]{1,0:T(8,128)(2,1)S(1)} %bitcast.23), custom_call_target="tpu_custom_call" | custom-call | flops 402653184 | bytes 13631500 | tf_op jit(solution)/shard_map/pallas_call | solution.py:23
  91.7 3.5 %shard_map.101.refs_2_ = bf16[1536,4096]{1,0:T(8,128)(2,1)} custom-call(s32[3]{0:T(128)S(1)} %pad_add_fusion.s, bf16[256,1536]{1,0:T(8,128)(2,1)S(1)} %shard_map.100.n, bf16[128,1024]{1,0:T(8,128)(2,1)S(1)} %shard_map.82.v.refs_0_, bf16[128,1024]{1,0:T(8,128)(2,1)S(1)} %shard_map.94.v.refs_1_), custom_call_target="tpu_custom_call" | custom-call | flops 805306368 | bytes 3145728 | tf_op jit(solution)/shard_map/pallas_call | solution.py:244
  95.2 1.7 %shard_map.96.refs_0_ = f32[128,1536]{1,0:T(8,128)S(1)} custom-call(s32[3]{0:T(128)S(1)} %pad_add_fusion.s, bf16[128,1024]{1,0:T(8,128)(2,1)S(1)} %collective-permute-done.23.v.refs_1_, bf16[1536,4096]{1,0:T(8,128)(2,1)S(1)} %bitcast.24, f32[128,1536]{1,0:T(8,128)S(1)} %shard_map.95.refs_0_), custom_call_target="tpu_custom_call" | custom-call | flops 402653184 | bytes 14417932 | tf_op jit(solution)/shard_map/pallas_call | solution.py:23
  96.9 1.7 %shard_map.97.total_ref = f32[128,1536]{1,0:T(8,128)S(1)} custom-call(s32[3]{0:T(128)S(1)} %pad_add_fusion.s, bf16[128,1024]{1,0:T(8,128)(2,1)S(1)} %shard_map.91.v.refs_1_, bf16[1536,4096]{1,0:T(8,128)(2,1)S(1)} %bitcast.25, f32[128,1536]{1,0:T(8,128)S(1)} %shard_map.96.refs_0_), custom_call_target="tpu_custom_call" | custom-call | flops 402653184 | bytes 14417932 | tf_op jit(solution)/shard_map/pallas_call | solution.py:23
  98.6 1.9 %shard_map.98 = (f32[64,1536]{1,0:T(8,128)S(1)}, f32[8,128]{1,0:T(8,128)S(1)}, bf16[64,1536]{1,0:T(8,128)(2,1)S(1)}) custom-call(s32[3]{0:T(128)S(1)} %pad_add_fusion.s, bf16[128,1024]{1,0:T(8,128)(2,1)S(1)} %collective-permute-done.20.v.refs_1_, bf16[1536,4096]{1,0:T(8,128)(2,1)S(1)} %bitcast.26, f32[128,1536]{1,0:T(8,128)S(1)} %shard_map.97.total_ref, ...), custom_call_target="tpu_custom_call" | custom-call | flops 402653184 | bytes 14618636 | tf_op jit(solution)/shard_map/pallas_call | solution.py:23
  101.1 1.2 %collective-permute-start.24 = (bf16[64,1536]{1,0:T(8,128)(2,1)S(1)}, bf16[64,1536]{1,0:T(8,128)(2,1)S(1)}, u32[]{:S(2)}, u32[]{:S(2)}) collective-permute-start(bf16[64,1536]{1,0:T(8,128)(2,1)S(1)} %get-tuple-element.34), channel_id=1, source_target_pairs={{0,4},{4,0},{1,5},{5,1},{2,6},{6,2},{3,7},{7,3},{8,12},{12,8},{9,1... | collective-permute-start | bytes 589832 | tf_op jit(solution)/shard_map/ppermute | solution.py:270
  102.2 3.5 %shard_map.102.refs_2_ = bf16[1536,4096]{1,0:T(8,128)(2,1)} custom-call(s32[3]{0:T(128)S(1)} %pad_add_fusion.s, bf16[256,1536]{1,0:T(8,128)(2,1)S(1)} %shard_map.100.n, bf16[128,1024]{1,0:T(8,128)(2,1)S(1)} %collective-permute-done.6.v.refs_0_, bf16[128,1024]{1,0:T(8,128)(2,1)S(1)} %collective-permute-done.23.v.refs_1_, ...), custom_call_target="tpu_custom_call", output_to_operand_aliasing={{}: (4, {})} | custom-call | flops 805306368 | bytes 3145728 | tf_op jit(solution)/shard_map/pallas_call | solution.py:244
  105.7 3.5 %shard_map.103.refs_2_ = bf16[1536,4096]{1,0:T(8,128)(2,1)} custom-call(s32[3]{0:T(128)S(1)} %pad_add_fusion.s, bf16[256,1536]{1,0:T(8,128)(2,1)S(1)} %shard_map.100.n, bf16[128,1024]{1,0:T(8,128)(2,1)S(1)} %shard_map.79.v.refs_0_, bf16[128,1024]{1,0:T(8,128)(2,1)S(1)} %shard_map.91.v.refs_1_, ...), custom_call_target="tpu_custom_call", output_to_operand_aliasing={{}: (4, {})} | custom-call | flops 805306368 | bytes 3145728 | tf_op jit(solution)/shard_map/pallas_call | solution.py:244
  109.2 1.7 %collective-permute-start.28 = (f32[8,128]{1,0:T(8,128)S(1)}, f32[8,128]{1,0:T(8,128)S(1)}, u32[]{:S(2)}, u32[]{:S(2)}) collective-permute-start(f32[8,128]{1,0:T(8,128)S(1)} %add.53.refs_3_), channel_id=1, source_target_pairs={{0,6},{1,7},{2,4},{3,5},{4,2},{5,3},{6,0},{7,1},{8,14},{9,15},{10,... | collective-permute-start | bytes 12296 | tf_op jit(solution)/shard_map/ppermute | solution.py:270
  111.0 0.8 collective-permute-start.27
  111.8 0.9 collective-permute-start.26
  112.7 3.5 %shard_map.104 = bf16[1536,4096]{1,0:T(8,128)(2,1)} custom-call(s32[3]{0:T(128)S(1)} %pad_add_fusion.s, bf16[256,1536]{1,0:T(8,128)(2,1)S(1)} %shard_map.100.n, bf16[128,1024]{1,0:T(8,128)(2,1)S(1)} %collective-permute-done.3.v.refs_0_, bf16[128,1024]{1,0:T(8,128)(2,1)S(1)} %collective-permute-done.20.v.refs_1_, ...), custom_call_target="tpu_custom_call", output_to_operand_aliasing={{}: (4, {})} | custom-call | flops 805306368 | bytes 3145728 | tf_op jit(solution)/shard_map/pallas_call | solution.py:244
  116.2 1.7 %shard_map.99 = bf16[64,1536]{1,0:T(8,128)(2,1)} custom-call(s32[3]{0:T(128)S(1)} %pad_add_fusion.s, f32[64,1536]{1,0:T(8,128)S(1)} %get-tuple-element.33.keep_ref, bf16[64,1536]{1,0:T(8,128)(2,1)S(1)} %collective-permute-done.16.refs_0_.ups_ref, bf16[128,1536]{1,0:T(8,128)(2,1)S(1)} %get-tuple-element.32.in_ref.refs_1_, ...), custom_call_target="tpu_custom_call" | custom-call | bytes 1400844 | tf_op jit(solution)/shard_map/pallas_call | solution.py:23
  (72 shorter events, 10.3 us)
Async XLA Ops:
  0.6 6.9 %copy-start = (s32[4,2]{0,1:T(2,128)S(1)}, s32[4,2]{0,1:T(2,128)}, u32[]{:S(2)}) copy-start(s32[4,2]{0,1:T(2,128)} %param.8) | copy-start | bytes 100
  0.6 8.1 %collective-permute-start = (bf16[64,1536]{1,0:T(8,128)(2,1)}, bf16[64,1536]{1,0:T(8,128)(2,1)S(1)}, u32[]{:S(2)}, u32[]{:S(2)}) collective-permute-start(bf16[64,1536]{1,0:T(8,128)(2,1)} %bitcast.27), channel_id=1, source_target_pairs={{0,4},{4,0},{1,5},{5,1},{2,6},{6,2},{3,7},{7,3},{8,12},{12,8},{9,1... | collective-permute-start | bytes 589832 | tf_op jit(solution)/shard_map/ppermute | solution.py:270
  3.6 14.7 %collective-permute-start.7 = (bf16[2,64,1536]{2,1,0:T(8,128)(2,1)}, bf16[2,64,1536]{2,1,0:T(8,128)(2,1)S(1)}, u32[]{:S(2)}, u32[]{:S(2)}) collective-permute-start(bf16[2,64,1536]{2,1,0:T(8,128)(2,1)} %bitcast.35), channel_id=1, source_target_pairs={{0,24},{8,16},{16,8},{24,0},{1,25},{9,17},{17,9},{25,1},{2,26},{10... | collective-permute-start | bytes 1179656 | tf_op jit(solution)/shard_map/ppermute | solution.py:292
  8.8 4.6 %copy-start.1 = (bf16[1,4096,1536]{2,1,0:T(8,128)(2,1)S(1)}, bf16[1,4096,1536]{2,1,0:T(8,128)(2,1)}, u32[]{:S(2)}) copy-start(bf16[1,4096,1536]{2,1,0:T(8,128)(2,1)} %param.10) | copy-start | bytes 37748740
  13.3 0.9 copy-start.2
  16.0 4.2 %collective-permute-start.4 = (bf16[128,1024]{1,0:T(8,128)(2,1)S(1)}, bf16[128,1024]{1,0:T(8,128)(2,1)S(1)}, u32[]{:S(2)}, u32[]{:S(2)}) collective-permute-start(bf16[128,1024]{1,0:T(8,128)(2,1)S(1)} %shard_map.80), channel_id=1, source_target_pairs={{0,1},{1,0},{2,3},{3,2},{4,5},{5,4},{6,7},{7,6},{8,9},{9,8},{10,11... | collective-permute-start | bytes 786440 | tf_op jit(solution)/shard_map/ppermute | solution.py:270
  17.7 5.8 %collective-permute-start.1 = (bf16[128,1024]{1,0:T(8,128)(2,1)S(1)}, bf16[128,1024]{1,0:T(8,128)(2,1)S(1)}, u32[]{:S(2)}, u32[]{:S(2)}) collective-permute-start(bf16[128,1024]{1,0:T(8,128)(2,1)S(1)} %shard_map.77), channel_id=1, source_target_pairs={{0,1},{1,0},{2,3},{3,2},{4,5},{5,4},{6,7},{7,6},{8,9},{9,8},{10,11... | collective-permute-start | bytes 786440 | tf_op jit(solution)/shard_map/ppermute | solution.py:270
  18.4 19.8 %collective-permute-start.8 = (bf16[2,64,1536]{2,1,0:T(8,128)(2,1)S(1)}, bf16[2,64,1536]{2,1,0:T(8,128)(2,1)S(1)}, u32[]{:S(2)}, u32[]{:S(2)}) collective-permute-start(bf16[2,64,1536]{2,1,0:T(8,128)(2,1)S(1)} %collective-permute-done.7.refs_0_), channel_id=1, source_target_pairs={{0,4},{4,0},{1,5},{5,1},{2,6},{6,2},{3,7},{7,3},{8,12},{12,8},{9,1... | collective-permute-start | bytes 1179656 | tf_op jit(solution)/shard_map/ppermute | solution.py:270
  20.2 16.2 %slice-start.3 = ((s8[12582912]{0:T(1024)(128)(4,1)}), s8[4194304]{0:T(1024)(128)(4,1)S(1)}, s32[]{:S(2)}) async-start(s8[12582912]{0:T(1024)(128)(4,1)} %bitcast.17), calls=%async_computation.3 | async-start | bytes 8388608
  20.2 16.3 %slice-start.4 = ((s8[12582912]{0:T(1024)(128)(4,1)}), s8[4194304]{0:T(1024)(128)(4,1)S(1)}, s32[]{:S(2)}) async-start(s8[12582912]{0:T(1024)(128)(4,1)} %bitcast.17), calls=%async_computation.4 | async-start | bytes 8388608
  21.9 14.6 %slice-start.5 = ((s8[12582912]{0:T(1024)(128)(4,1)}), s8[4194304]{0:T(1024)(128)(4,1)S(1)}, s32[]{:S(2)}) async-start(s8[12582912]{0:T(1024)(128)(4,1)} %bitcast.17), calls=%async_computation.5 | async-start | bytes 8388608
  21.9 9.3 %collective-permute-start.5 = (bf16[128,1024]{1,0:T(8,128)(2,1)S(1)}, bf16[128,1024]{1,0:T(8,128)(2,1)S(1)}, u32[]{:S(2)}, u32[]{:S(2)}) collective-permute-start(bf16[128,1024]{1,0:T(8,128)(2,1)S(1)} %get-tuple-element.22), channel_id=1, source_target_pairs={{0,2},{1,3},{2,0},{3,1},{4,6},{5,7},{6,4},{7,5},{8,10},{9,11},{10,... | collective-permute-start | bytes 786440 | tf_op jit(solution)/shard_map/ppermute | solution.py:270
  25.2 10.4 %collective-permute-start.2 = (bf16[128,1024]{1,0:T(8,128)(2,1)S(1)}, bf16[128,1024]{1,0:T(8,128)(2,1)S(1)}, u32[]{:S(2)}, u32[]{:S(2)}) collective-permute-start(bf16[128,1024]{1,0:T(8,128)(2,1)S(1)} %get-tuple-element.20), channel_id=1, source_target_pairs={{0,2},{1,3},{2,0},{3,1},{4,6},{5,7},{6,4},{7,5},{8,10},{9,11},{10,... | collective-permute-start | bytes 786440 | tf_op jit(solution)/shard_map/ppermute | solution.py:270
  32.0 7.1 %collective-permute-start.6 = (bf16[128,1024]{1,0:T(8,128)(2,1)S(1)}, bf16[128,1024]{1,0:T(8,128)(2,1)S(1)}, u32[]{:S(2)}, u32[]{:S(2)}) collective-permute-start(bf16[128,1024]{1,0:T(8,128)(2,1)S(1)} %shard_map.82.v.refs_0_), channel_id=1, source_target_pairs={{0,1},{1,0},{2,3},{3,2},{4,5},{5,4},{6,7},{7,6},{8,9},{9,8},{10,11... | collective-permute-start | bytes 786440 | tf_op jit(solution)/shard_map/ppermute | solution.py:270
  36.3 6.2 %collective-permute-start.3 = (bf16[128,1024]{1,0:T(8,128)(2,1)S(1)}, bf16[128,1024]{1,0:T(8,128)(2,1)S(1)}, u32[]{:S(2)}, u32[]{:S(2)}) collective-permute-start(bf16[128,1024]{1,0:T(8,128)(2,1)S(1)} %shard_map.79.v.refs_0_), channel_id=1, source_target_pairs={{0,1},{1,0},{2,3},{3,2},{4,5},{5,4},{6,7},{7,6},{8,9},{9,8},{10,11... | collective-permute-start | bytes 786440 | tf_op jit(solution)/shard_map/ppermute | solution.py:270
  40.8 12.3 %copy-start.3 = (bf16[1,64,1536]{2,1,0:T(8,128)(2,1)S(1)}, bf16[1,64,1536]{2,1,0:T(8,128)(2,1)}, u32[]{:S(2)}) copy-start(bf16[1,64,1536]{2,1,0:T(8,128)(2,1)} %param.7) | copy-start | bytes 589828
  40.8 27.7 %slice-start = ((s8[12582912]{0:T(1024)(128)(4,1)}), s8[4194304]{0:T(1024)(128)(4,1)S(1)}, s32[]{:S(2)}) async-start(s8[12582912]{0:T(1024)(128)(4,1)} %bitcast.11), calls=%async_computation | async-start | bytes 8388608
  40.8 27.7 %slice-start.1 = ((s8[12582912]{0:T(1024)(128)(4,1)}), s8[4194304]{0:T(1024)(128)(4,1)S(1)}, s32[]{:S(2)}) async-start(s8[12582912]{0:T(1024)(128)(4,1)} %bitcast.11), calls=%async_computation.1 | async-start | bytes 8388608
  42.5 26.0 %slice-start.2 = ((s8[12582912]{0:T(1024)(128)(4,1)}), s8[4194304]{0:T(1024)(128)(4,1)S(1)}, s32[]{:S(2)}) async-start(s8[12582912]{0:T(1024)(128)(4,1)} %bitcast.11), calls=%async_computation.2 | async-start | bytes 8388608
  44.4 8.6 %collective-permute-start.9 = (bf16[64,1536]{1,0:T(8,128)(2,1)S(1)}, bf16[64,1536]{1,0:T(8,128)(2,1)S(1)}, u32[]{:S(2)}, u32[]{:S(2)}) collective-permute-start(bf16[64,1536]{1,0:T(8,128)(2,1)S(1)} %get-tuple-element.25), channel_id=1, source_target_pairs={{0,4},{4,0},{1,5},{5,1},{2,6},{6,2},{3,7},{7,3},{8,12},{12,8},{9,1... | collective-permute-start | bytes 589832 | tf_op jit(solution)/shard_map/ppermute | solution.py:270
  44.8 1.2 collective-permute-start.10
  45.0 2.7 %collective-permute-start.12 = (f32[8,128]{1,0:T(8,128)S(1)}, f32[8,128]{1,0:T(8,128)S(1)}, u32[]{:S(2)}, u32[]{:S(2)}) collective-permute-start(f32[8,128]{1,0:T(8,128)S(1)} %get-tuple-element.27), channel_id=1, source_target_pairs={{0,1},{1,0},{2,3},{3,2},{4,5},{5,4},{6,7},{7,6},{8,9},{9,8},{10,11... | collective-permute-start | bytes 12296 | tf_op jit(solution)/shard_map/ppermute | solution.py:270
  46.0 5.2 %collective-permute-start.11 = (f32[8,128]{1,0:T(8,128)S(1)}, f32[8,128]{1,0:T(8,128)S(1)}, u32[]{:S(2)}, u32[]{:S(2)}) collective-permute-start(f32[8,128]{1,0:T(8,128)S(1)} %add.51.refs_1_.refs_2_), channel_id=1, source_target_pairs={{0,2},{1,3},{2,0},{3,1},{4,6},{5,7},{6,4},{7,5},{8,10},{9,11},{10,... | collective-permute-start | bytes 12296 | tf_op jit(solution)/shard_map/ppermute | solution.py:270
  47.7 5.1 %collective-permute-start.15 = (f32[8,128]{1,0:T(8,128)S(1)}, f32[8,128]{1,0:T(8,128)S(1)}, u32[]{:S(2)}, u32[]{:S(2)}) collective-permute-start(f32[8,128]{1,0:T(8,128)S(1)} %add.52.refs_3_), channel_id=1, source_target_pairs={{0,6},{1,7},{2,4},{3,5},{4,2},{5,3},{6,0},{7,1},{8,14},{9,15},{10,... | collective-permute-start | bytes 12296 | tf_op jit(solution)/shard_map/ppermute | solution.py:270
  49.1 3.7 %collective-permute-start.14 = (f32[8,128]{1,0:T(8,128)S(1)}, f32[8,128]{1,0:T(8,128)S(1)}, u32[]{:S(2)}, u32[]{:S(2)}) collective-permute-start(f32[8,128]{1,0:T(8,128)S(1)} %add.52.refs_3_), channel_id=1, source_target_pairs={{0,4},{1,5},{2,6},{3,7},{4,0},{5,1},{6,2},{7,3},{8,12},{9,13},{10,... | collective-permute-start | bytes 12296 | tf_op jit(solution)/shard_map/ppermute | solution.py:270
  49.5 3.6 %collective-permute-start.13 = (f32[8,128]{1,0:T(8,128)S(1)}, f32[8,128]{1,0:T(8,128)S(1)}, u32[]{:S(2)}, u32[]{:S(2)}) collective-permute-start(f32[8,128]{1,0:T(8,128)S(1)} %add.52.refs_3_), channel_id=1, source_target_pairs={{0,2},{1,3},{2,0},{3,1},{4,6},{5,7},{6,4},{7,5},{8,10},{9,11},{10,... | collective-permute-start | bytes 12296 | tf_op jit(solution)/shard_map/ppermute | solution.py:270
  54.0 12.7 %collective-permute-start.17 = (bf16[64,1536]{1,0:T(8,128)(2,1)S(1)}, bf16[64,1536]{1,0:T(8,128)(2,1)S(1)}, u32[]{:S(2)}, u32[]{:S(2)}) collective-permute-start(bf16[64,1536]{1,0:T(8,128)(2,1)S(1)} %shard_map.88), channel_id=1, source_target_pairs={{8,4},{12,0},{16,12},{20,8},{24,20},{28,16},{9,5},{13,1},{17,13},{... | collective-permute-start | bytes 589832 | tf_op jit(solution)/shard_map/ppermute | solution.py:309
  55.3 13.2 %collective-permute-start.16 = (bf16[64,1536]{1,0:T(8,128)(2,1)S(1)}, bf16[64,1536]{1,0:T(8,128)(2,1)S(1)}, u32[]{:S(2)}, u32[]{:S(2)}) collective-permute-start(bf16[64,1536]{1,0:T(8,128)(2,1)S(1)} %shard_map.88), channel_id=1, source_target_pairs={{8,0},{12,4},{16,8},{20,12},{24,16},{28,20},{9,1},{13,5},{17,9},{2... | collective-permute-start | bytes 589832 | tf_op jit(solution)/shard_map/ppermute | solution.py:309
  70.2 2.3 %collective-permute-start.21 = (bf16[128,1024]{1,0:T(8,128)(2,1)S(1)}, bf16[128,1024]{1,0:T(8,128)(2,1)S(1)}, u32[]{:S(2)}, u32[]{:S(2)}) collective-permute-start(bf16[128,1024]{1,0:T(8,128)(2,1)S(1)} %shard_map.92), channel_id=1, source_target_pairs={{0,1},{1,0},{2,3},{3,2},{4,5},{5,4},{6,7},{7,6},{8,9},{9,8},{10,11... | collective-permute-start | bytes 786440 | tf_op jit(solution)/shard_map/ppermute | solution.py:270
  72.0 3.8 %collective-permute-start.18 = (bf16[128,1024]{1,0:T(8,128)(2,1)S(1)}, bf16[128,1024]{1,0:T(8,128)(2,1)S(1)}, u32[]{:S(2)}, u32[]{:S(2)}) collective-permute-start(bf16[128,1024]{1,0:T(8,128)(2,1)S(1)} %shard_map.89), channel_id=1, source_target_pairs={{0,1},{1,0},{2,3},{3,2},{4,5},{5,4},{6,7},{7,6},{8,9},{9,8},{10,11... | collective-permute-start | bytes 786440 | tf_op jit(solution)/shard_map/ppermute | solution.py:270
  74.2 9.2 %collective-permute-start.22 = (bf16[128,1024]{1,0:T(8,128)(2,1)S(1)}, bf16[128,1024]{1,0:T(8,128)(2,1)S(1)}, u32[]{:S(2)}, u32[]{:S(2)}) collective-permute-start(bf16[128,1024]{1,0:T(8,128)(2,1)S(1)} %get-tuple-element.31), channel_id=1, source_target_pairs={{0,2},{1,3},{2,0},{3,1},{4,6},{5,7},{6,4},{7,5},{8,10},{9,11},{10,... | collective-permute-start | bytes 786440 | tf_op jit(solution)/shard_map/ppermute | solution.py:270
  77.5 10.7 %collective-permute-start.19 = (bf16[128,1024]{1,0:T(8,128)(2,1)S(1)}, bf16[128,1024]{1,0:T(8,128)(2,1)S(1)}, u32[]{:S(2)}, u32[]{:S(2)}) collective-permute-start(bf16[128,1024]{1,0:T(8,128)(2,1)S(1)} %get-tuple-element.29), channel_id=1, source_target_pairs={{0,2},{1,3},{2,0},{3,1},{4,6},{5,7},{6,4},{7,5},{8,10},{9,11},{10,... | collective-permute-start | bytes 786440 | tf_op jit(solution)/shard_map/ppermute | solution.py:270
  84.3 10.9 %collective-permute-start.23 = (bf16[128,1024]{1,0:T(8,128)(2,1)S(1)}, bf16[128,1024]{1,0:T(8,128)(2,1)S(1)}, u32[]{:S(2)}, u32[]{:S(2)}) collective-permute-start(bf16[128,1024]{1,0:T(8,128)(2,1)S(1)} %shard_map.94.v.refs_1_), channel_id=1, source_target_pairs={{0,1},{1,0},{2,3},{3,2},{4,5},{5,4},{6,7},{7,6},{8,9},{9,8},{10,11... | collective-permute-start | bytes 786440 | tf_op jit(solution)/shard_map/ppermute | solution.py:270
  89.0 9.7 %collective-permute-start.20 = (bf16[128,1024]{1,0:T(8,128)(2,1)S(1)}, bf16[128,1024]{1,0:T(8,128)(2,1)S(1)}, u32[]{:S(2)}, u32[]{:S(2)}) collective-permute-start(bf16[128,1024]{1,0:T(8,128)(2,1)S(1)} %shard_map.91.v.refs_1_), channel_id=1, source_target_pairs={{0,1},{1,0},{2,3},{3,2},{4,5},{5,4},{6,7},{7,6},{8,9},{9,8},{10,11... | collective-permute-start | bytes 786440 | tf_op jit(solution)/shard_map/ppermute | solution.py:270
  100.5 8.7 %collective-permute-start.25 = (f32[8,128]{1,0:T(8,128)S(1)}, f32[8,128]{1,0:T(8,128)S(1)}, u32[]{:S(2)}, u32[]{:S(2)}) collective-permute-start(f32[8,128]{1,0:T(8,128)S(1)} %get-tuple-element.35), channel_id=1, source_target_pairs={{0,1},{1,0},{2,3},{3,2},{4,5},{5,4},{6,7},{7,6},{8,9},{9,8},{10,11... | collective-permute-start | bytes 12296 | tf_op jit(solution)/shard_map/ppermute | solution.py:270
  101.1 15.1 %collective-permute-start.24 = (bf16[64,1536]{1,0:T(8,128)(2,1)S(1)}, bf16[64,1536]{1,0:T(8,128)(2,1)S(1)}, u32[]{:S(2)}, u32[]{:S(2)}) collective-permute-start(bf16[64,1536]{1,0:T(8,128)(2,1)S(1)} %get-tuple-element.34), channel_id=1, source_target_pairs={{0,4},{4,0},{1,5},{5,1},{2,6},{6,2},{3,7},{7,3},{8,12},{12,8},{9,1... | collective-permute-start | bytes 589832 | tf_op jit(solution)/shard_map/ppermute | solution.py:270
  109.2 7.0 %collective-permute-start.28 = (f32[8,128]{1,0:T(8,128)S(1)}, f32[8,128]{1,0:T(8,128)S(1)}, u32[]{:S(2)}, u32[]{:S(2)}) collective-permute-start(f32[8,128]{1,0:T(8,128)S(1)} %add.53.refs_3_), channel_id=1, source_target_pairs={{0,6},{1,7},{2,4},{3,5},{4,2},{5,3},{6,0},{7,1},{8,14},{9,15},{10,... | collective-permute-start | bytes 12296 | tf_op jit(solution)/shard_map/ppermute | solution.py:270
  111.0 5.2 %collective-permute-start.27 = (f32[8,128]{1,0:T(8,128)S(1)}, f32[8,128]{1,0:T(8,128)S(1)}, u32[]{:S(2)}, u32[]{:S(2)}) collective-permute-start(f32[8,128]{1,0:T(8,128)S(1)} %add.53.refs_3_), channel_id=1, source_target_pairs={{0,4},{1,5},{2,6},{3,7},{4,0},{5,1},{6,2},{7,3},{8,12},{9,13},{10,... | collective-permute-start | bytes 12296 | tf_op jit(solution)/shard_map/ppermute | solution.py:270
  111.8 4.4 %collective-permute-start.26 = (f32[8,128]{1,0:T(8,128)S(1)}, f32[8,128]{1,0:T(8,128)S(1)}, u32[]{:S(2)}, u32[]{:S(2)}) collective-permute-start(f32[8,128]{1,0:T(8,128)S(1)} %add.53.refs_3_), channel_id=1, source_target_pairs={{0,2},{1,3},{2,0},{3,1},{4,6},{5,7},{6,4},{7,5},{8,10},{9,11},{10,... | collective-permute-start | bytes 12296 | tf_op jit(solution)/shard_map/ppermute | solution.py:270

commit v2 on v0

v2 whole, which is shorter than its diff:
```python
import jax
import jax.numpy as jnp
from jax import lax
from jax.experimental import pallas as pl
from jax.experimental.pallas import tpu as pltpu
from jax.sharding import PartitionSpec as P

EPSILON = 1e-05
F32, BF16 = jnp.float32, jnp.bfloat16
NT = (((1,), (1,)), ((), ()))
TN = (((0,), (0,)), ((), ()))
SCOPED = 14 << 20
SMEM = pl.BlockSpec(memory_space=pltpu.SMEM)
VMEM = pl.BlockSpec(memory_space=pltpu.VMEM)
ANY = pl.BlockSpec(memory_space=pl.ANY)
HEAD = 128
STEPS = 8
COST = pl.CostEstimate(flops=10**10, bytes_accessed=10**8, transcendentals=0)


def call(body, outs, operands, held=(), first_spec=VMEM, carry=()):
    operands = list(operands)
    held = [h for h in held if not any(h is a for a in operands)]
    n_in, n_held, n_out, n_carry = len(operands), len(held), len(outs), len(carry)
    sources = [pltpu.with_memory_space_constraint(w, pltpu.HBM) for w, _, _, _ in carry]
    rows = carry[0][0].shape[0] if carry else 0
    block = rows // STEPS

    def kernel(*refs):
        ins, refs = refs[:n_in], refs[n_in + n_held :]
        weights, refs = refs[:n_carry], refs[n_carry:]
        made, refs = refs[:n_out], refs[n_out:]
        copies = []
        for k, (w, (_, other, offset, size)) in enumerate(zip(weights, carry, strict=True)):
            columns = w.shape[1]
            start = 0 if size == columns else half_start(columns, other, offset)
            for i in range(STEPS):
                part = pl.ds(i * block, block)
                source = w.at[part] if size == columns else w.at[part, pl.ds(start, size)]
                copies.append(pltpu.make_async_copy(source, refs[k].at[part], refs[n_carry].at[k, i]))
        for copy in copies:
            copy.start()
        if body is not None:
            body(*ins, *made)
        for copy in copies:
            copy.wait()

    more = [pltpu.VMEM((rows, size), w.dtype) for w, _, _, size in carry]
    return pl.pallas_call(
        kernel,
        in_specs=([first_spec] + [VMEM] * (n_in - 1) if n_in else [])
        + [VMEM] * n_held
        + [pl.BlockSpec(memory_space=pltpu.HBM)] * n_carry,
        out_specs=[VMEM] * (n_out + n_carry),
        out_shape=[*outs, *more],
        scratch_shapes=[pltpu.SemaphoreType.DMA((n_carry, STEPS))] if carry else [],
        compiler_params=pltpu.CompilerParams(vmem_limit_bytes=SCOPED),
        cost_estimate=COST,
    )(*operands, *held, *sources)


def shape(dims, dtype):
    return jax.ShapeDtypeStruct(tuple(dims), dtype)


def after(array, *earlier):
    return lax.optimization_barrier((array, *earlier))[0]


def half_start(extent, other, offset):
    core = lax.axis_index("dp") % 2
    core = 1 - core if other else core
    return pl.multiple_of(core * (extent // 2) + offset, HEAD)


def grad_mixed_part(pieces, w_output, other, offset, size, received=None, held=(), carry=()):
    counts = [len(p) for p in pieces]
    flat = [a for p in pieces for a in p]
    rows = sum(p[0].shape[0] for p in pieces)

    def body(*refs):
        blocks, at = [], 0
        for n in counts:
            blocks.append(jnp.concatenate([r[...] for r in refs[at : at + n]], axis=1))
            at += n
        ups = jnp.concatenate(blocks, axis=0)
        w = refs[at]
        start = half_start(w_output.shape[0], other, offset)
        part = lax.dot_general(ups, w[pl.ds(start, size), :], NT, preferred_element_type=F32)
        if other:
            refs[at + 1][...] = part.astype(BF16)
        else:
            part = part + refs[at + 1][...].astype(F32)
            refs[at + 2][...] = part
            refs[at + 3][...] = part.astype(BF16)

    if other:
        return call(body, [shape((rows, size), BF16)], [*flat, w_output], held, carry=carry)
    outs = [shape((rows, size), F32), shape((rows, size), BF16)]
    return call(body, outs, [*flat, w_output, received], held, carry=carry)


def unmix(kept, received, mixing, first_head, held=()):
    rows, size = kept.shape
    count = len(received)

    def body(*refs):
        mix, out = refs[count + 1], refs[count + 2]
        for h in range(size // HEAD):
            cols = slice(h * HEAD, (h + 1) * HEAD)
            total = refs[0][:, cols]
            for r in refs[1 : count + 1]:
                total = total + r[:, cols].astype(F32)
            out[:, cols] = lax.dot_general(
                mix[first_head + h], total.astype(BF16), TN, preferred_element_type=F32
            ).astype(BF16)

    return call(body, [shape((rows, size), BF16)], [kept, *received, mixing], held)


def grad_normed_part(grads, weights, total=None, pieces=0, held=(), carry=()):
    rows, width = grads[0].shape[0], weights[0].shape[0]
    count = len(grads)

    def body(*refs):
        sums = None if total is None else refs[2 * count][...]
        for g, w in zip(refs[:count], refs[count : 2 * count], strict=True):
            term = lax.dot_general(g[...], w[...], NT, preferred_element_type=F32)
            sums = term if sums is None else sums + term
        if not pieces:
            refs[-1][...] = sums
            return
        keep, *sends = refs[-pieces:]
        own = rows // pieces
        keep[...] = sums[:own]
        for t, ref in enumerate(sends):
            ref[...] = sums[(t + 1) * own : (t + 2) * own].astype(BF16)

    if pieces:
        outs = [shape((rows // pieces, width), F32)] + [shape((rows // pieces, width), BF16)] * (pieces - 1)
    else:
        outs = [shape((rows, width), F32)]
    operands = [*grads, *weights] + ([] if total is None else [total])
    return call(body, outs, operands, held, carry=carry)


def stacked(columns):
    rows = columns[0].shape[0]
    lane = lax.broadcasted_iota(jnp.int32, (rows, 128), 1)
    wide = jnp.zeros((rows, 128), F32)
    for k, column in enumerate(columns):
        wide = jnp.where(lane == k, column, wide)
    if rows % 128:
        wide = jnp.concatenate([wide, jnp.zeros((-rows % 128, 128), F32)], axis=0)
    return wide.T[:8]


def as_columns(stats, rows):
    return jnp.concatenate([stats, jnp.zeros((120, stats.shape[1]), F32)], axis=0).T[:rows]


def added(one, other, held=()):
    def body(a, b, out):
        out[...] = a[...] + b[...]

    return call(body, [shape(one.shape, one.dtype)], [one, other], held)


def ordered(store, table, held=()):
    slots = store.shape[0]

    def body(s, store_ref, *outs):
        for k, out in enumerate(outs):
            out[...] = store_ref[s[k]]

    return call(body, [shape(store.shape[1:], BF16)] * slots, [table, store], held, SMEM)


def width_sums(keep, received, inputs, slot, held=()):
    own, width = keep.shape
    slots = len(inputs)

    def body(keep_ref, *refs):
        ins, refs = refs[:slots], refs[slots:]
        grad_ref, stats = refs[-2:]
        grad = keep_ref[...]
        for r in refs[:-2]:
            grad = grad + r[...].astype(F32)
        grad_ref[...] = grad
        floats = [r[...].astype(F32) for r in ins]
        columns = [jnp.sum(grad, axis=1, keepdims=True), jnp.sum(grad * floats[slot], axis=1, keepdims=True)]
        if slot == 0:
            for x in floats:
                columns += [jnp.sum(x, axis=1, keepdims=True), jnp.sum(x * x, axis=1, keepdims=True)]
        stats[...] = stacked(columns)

    outs = [shape((own, width), F32), shape((8, -(-own // 128) * 128), F32)]
    return call(body, outs, [keep, *inputs, *received], held)


def finish(grad, upstream, inputs, slot, input_stats, grad_stats, width, parts, held=()):
    own, part = grad.shape
    slots = len(inputs)
    n_up, n_in, n_grad = len(upstream), len(input_stats), len(grad_stats)

    def body(grad_ref, *refs):
        x_refs, refs = refs[:slots], refs[slots:]
        ups, refs = refs[:n_up], refs[n_up:]
        ins, refs = refs[:n_in], refs[n_in:]
        grads, outs = refs[:n_grad], refs[n_grad:]
        total_in = ins[0][...]
        for r in ins[1:]:
            total_in = total_in + r[...]
        total = grads[0][...]
        for r in grads[1:]:
            total = total + r[...]
        in_columns = as_columns(total_in, own)
        columns = as_columns(total, own)

        def normal(k):
            center = in_columns[:, 2 * k + 2 : 2 * k + 3] / width
            inverse = lax.rsqrt(in_columns[:, 2 * k + 3 : 2 * k + 4] / width - center * center + EPSILON)
            return center, inverse, (x_refs[k][...].astype(F32) - center) * inverse

        center, inverse, scaled = normal(slot)
        first = columns[:, 0:1]
        second = (columns[:, 1:2] - center * first) * inverse
        above = jnp.concatenate([r[...] for r in ups], axis=1).astype(F32)
        made = (above + inverse * (grad_ref[...] - first / width - scaled * (second / width))).astype(BF16)
        for k in range(parts):
            outs[k][...] = made[:, k * (part // parts) : (k + 1) * (part // parts)]
        if slot == 0:
            for k in range(slots):
                outs[parts + k][...] = (scaled if k == slot else normal(k)[2]).astype(BF16)

    operands = [grad, *inputs, *upstream, *input_stats, *grad_stats]
    outs = [shape((own, part // parts), BF16)] * parts
    if slot == 0:
        outs += [shape((own, part), BF16)] * slots
    return call(body, outs, operands, held)


def value_grad_part(normed, grads, result, dims, other, offset):
    depth, width = sum(a.shape[0] for a in normed), normed[0].shape[1]
    blocks = len(normed)
    size = grads[0].shape[1]
    count = len(grads)
    block = 256 if width % 256 == 0 else 128
    steps = width // block
    given = [] if result is None else [result]

    def body(*refs):
        norms, refs = refs[:blocks], refs[blocks:]
        out, made, sems = refs[count + len(given) :]
        v = jnp.concatenate([r[...] for r in refs[:count]], axis=0)
        start = half_start(dims[1], other, offset)
        copies = []
        for i in range(steps):
            rows = pl.ds(i * block, block)
            made[rows, :] = lax.dot_general(
                jnp.concatenate([n[:, i * block : (i + 1) * block] for n in norms], axis=0),
                v,
                TN,
                preferred_element_type=F32,
            ).astype(BF16)
            copies.append(
                pltpu.make_async_copy(made.at[rows], out.at[rows, pl.ds(start, size)], sems.at[i])
            )
            copies[-1].start()
        for copy in copies:
            copy.wait()

    return pl.pallas_call(
        body,
        in_specs=[VMEM] * (blocks + count) + [ANY] * len(given),
        out_specs=ANY,
        out_shape=pltpu.HBM(dims, BF16),
        scratch_shapes=[pltpu.VMEM((width, size), BF16), pltpu.SemaphoreType.DMA((steps,))],
        input_output_aliases={blocks + count: 0} if given else {},
        compiler_params=pltpu.CompilerParams(vmem_limit_bytes=SCOPED),
        cost_estimate=COST,
    )(*normed, *grads, *given)


def mixing_weights(slopes, length, own, held=()):
    heads = slopes.shape[0] // 2

    def body(slopes_ref, out):
        tensor = lax.axis_index("tensor")
        first = (lax.axis_index("dp") % 2) * heads

        def place(dim):
            local = lax.broadcasted_iota(jnp.int32, (length, length), dim)
            return ((local // own) ^ tensor) * own + local % own

        distance = (place(0) - place(1)).astype(F32)
        causal = distance >= 0
        distance = jnp.where(causal, distance, 0.0)
        for h in range(heads):
            logits = -slopes_ref[pl.ds(first + h, 1), :] * distance
            weights = jnp.where(causal, jnp.exp(logits), 0.0)
            out[h] = (weights / jnp.sum(weights, axis=-1, keepdims=True)).astype(BF16)

    wide = jnp.broadcast_to(slopes[:, None], (slopes.shape[0], length))
    return call(body, [shape((heads, length, length), BF16)], [wide], held)


def flipped(array, axis, mask):
    return lax.ppermute(array, axis, [(i, i ^ mask) for i in range(lax.axis_size(axis))])


def on_device(parked, arriving, slot_table, value_weight, output_weight, slopes):
    sections, tensors, parts = (lax.axis_size(a) for a in ("section", "tensor", "dp"))
    slots, own, part_width = parked.shape[1:]
    width = part_width * parts
    half = output_weight.shape[1] // 2
    others = range(1, tensors)
    chips = range(2, parts, 2)
    bounds = [0, half // 2, half]
    chunks = [(a, b - a) for a, b in zip(bounds[:-1], bounds[1:], strict=True)]
    final = len(chunks) - 1

    def others_of(array):
        return [flipped(array, "tensor", t) for t in others]

    token, held = [None], []

    def run(kernel, first, *rest, **more):
        if token[0] is not None:
            if isinstance(first, list):
                first = [after(first[0], token[0]), *first[1:]]
            else:
                first = after(first, token[0])
        outs = kernel(first, *rest, held=held, **more)
        token[0] = outs[0]
        return outs

    upstream = [arriving[0]]
    pieces = [[a] for a in [upstream[0], *others_of(upstream[0])]]
    table = lax.dynamic_index_in_dim(slot_table, lax.axis_index("section"), 0, keepdims=False)
    mixing, = run(mixing_weights, after(slopes, table), own * tensors, own)
    w_output, = run(
        lambda w, held: call(None, [], [], held, carry=[(w, False, 0, w.shape[1])]), output_weight[0]
    )
    held.append(w_output)
    w_value = [[None, None] for _ in chunks]

    def spans(j, sides):
        return [(value_weight[0], side == 1, *chunks[j]) for side in sides]

    values, input_stats, result = [], None, None
    for slot in range(slots):
        last = slot == slots - 1
        if slot > 0:
            upstream = [lax.ppermute(a, "section", [(i, i - 1) for i in range(1, sections)]) for a in upstream]
            pieces = [list(p) for p in zip(*[[a, *others_of(a)] for a in upstream], strict=True)]

        def product(j, other, received=None, carry=()):
            a, n = chunks[j]
            mixed = lambda first, *rest, held: grad_mixed_part([first, *pieces[1:]], *rest, held, carry)
            return run(mixed, pieces[0], w_output, other, a, n, received)

        halves, kept, across = [], [], []
        for j in range(len(chunks) + 1):
            if j <= final:
                halves.append(flipped(product(j, True)[0], "dp", 1))
            if j > 0:
                bring = slot == 0 and j - 1 == final
                outs = product(j - 1, False, halves[j - 1], spans(0, (0, 1)) if bring else ())
                if bring:
                    w_value[0] = outs[2:]
                    held.extend(outs[2:])
                kept.append(outs[:2])
                across.append([flipped(outs[1], "dp", m) for m in chips])
        if slot == 0:
            store = lax.ppermute(
                after(parked[0], kept[-1][1]), "section", [(i, sections - 1 - i) for i in range(sections)]
            )
        mine, theirs, total = [], [], None
        for j, (a, n) in enumerate(chunks):
            mine += run(unmix, kept[j][0], across[j], mixing, a // HEAD)
            theirs.append(flipped(mine[j], "dp", 1))
            for side, grads in enumerate((mine[j], theirs[j])):
                end = j == final and side == 1
                bring = slot == 0 and j < final
                outs = run(
                    grad_normed_part, [grads], [w_value[j][side]], total, tensors if end else 0,
                    carry=spans(j + 1, (side,)) if bring else (),
                )
                if bring:
                    w_value[j + 1][side] = outs[-1]
                    held.append(outs[-1])
                if end:
                    keep, *sends = outs
                else:
                    total = outs[0]
        values.append([mine, theirs])
        received = [flipped(x, "tensor", t) for t, x in zip(others, sends, strict=True)]
        if last:
            held.clear()
        if slot == 0:
            inputs = run(ordered, store, table)
        grad, sums = run(width_sums, keep, received, inputs, slot)
        sums, = run(added, sums, flipped(sums, "dp", 1))
        grad_stats = [sums] + [flipped(sums, "dp", m) for m in chips]
        if slot == 0:
            input_stats = grad_stats
        outs = run(finish, grad, upstream, inputs, slot, input_stats, grad_stats, width, 1 if last else 2)
        if slot == 0:
            normed = outs[-slots:]
            outs = outs[:-slots]
        upstream = outs

    normed = [b for a in normed for b in [a, *others_of(a)]]
    result = None
    for j, (a, n) in enumerate(chunks):
        for side in range(2):
            result = value_grad_part(
                normed, [v[side][j] for v in values], result, value_weight.shape[1:], side == 1, a
            )
    return (upstream[0][None], result[None])


def solution(mesh):
    in_specs = (
        P("section", None, "tensor", "dp"),
        P("section", "tensor", "dp"),
        P(),
        P("section", "dp", "tensor"),
        P("section", "tensor", "dp"),
        P("tensor"),
    )
    out_specs = (P("section", "tensor", "dp"), P("section", "dp", "tensor"))
    return jax.shard_map(
        on_device, mesh=mesh, in_specs=in_specs, out_specs=out_specs, check_vma=False
    )
```

time: 259 us -> 101 us (0.39)
  blocking collectives: 124 us -> 0 us
  matrix products: 65.2 us -> 0 us
  Pallas kernels: 0 us -> 41.6 us
  between operations: 18.2 us -> 1.13 us
  starting transfers between devices: 7.7 us -> 24.5 us
  other arithmetic: 7.26 us -> 0 us
  local copies, waits for them, and re-layouts: 5.4 us -> 1.08 us
    psum x4 -> x0, blocking collectives: 97.9 us -> none  [across_width(): return lax.psum(parts, 'dp')]
    dot_general x8 -> x0, matrix products: 65.2 us -> none  [the longest x2 24.9 us: backward_slot(): lax.dot_general(normed_all, grad_value, (((0,), (0,)), ((), ())), preferr...]
    pallas_call x0 -> x33, Pallas kernels: none -> 41.6 us  [the longest x29 33.4 us: call(): pl.pallas_call(kernel, in_specs=([first_spec] + [VMEM] * (n_in - 1) if n_...]
    all_gather x4 -> x0, blocking collectives: 26.4 us -> none  [the longest x2 13.6 us: backward_slot(): lax.all_gather(upstream, 'tensor', axis=0, tiled=True)]
    ppermute x5 -> x26, waiting for transfers between devices: 13.6 us -> 32.3 us  [the longest x23 23 us: flipped(): lax.ppermute(array, axis, [(i, i ^ mask) for i in range(lax.axis_size(axi...]
    ppermute x5 -> x26, starting transfers between devices: 7.62 us -> 24.5 us  [the longest x23 18.1 us: flipped(): lax.ppermute(array, axis, [(i, i ^ mask) for i in range(lax.axis_size(axi...]
    reduce_scatter x2 -> x0, waiting for transfers between devices: 16.4 us -> none  [backward_slot(): lax.psum_scatter(lax.dot_general(grad_value, w_value, (((1,), (1,)), ((),...]
    reduce_sum x5 -> x0, other arithmetic: 4.1 us -> none  [the longest x2 2.51 us: backward_slot(): jnp.sum(grad_normed, axis=1, keepdims=True)]
  transfers between devices with their start and end apart: 7 -> 26, of which waited for: 4 -> 10; matrix products, arithmetic and copies ran while one was open for 9% -> 1% of each run, Pallas kernels for 0% -> 37%
where the time goes in v2:
time: 101 us
  Pallas kernels  41.6 us (41%)
  waiting for transfers between devices  32.3 us (32%)
  starting transfers between devices  24.5 us (24%)
  between operations  1.13 us (1%)
  local copies, waits for them, and re-layouts  1.08 us (1%)
    pallas_call x29, Pallas kernels, call(): pl.pallas_call(kernel, in_specs=([first_spec] + [VMEM] * (n_in - 1) if n_...  33.4 us
    ppermute x23, waiting for transfers between devices, flipped(): lax.ppermute(array, axis, [(i, i ^ mask) for i in range(lax.axis_size(axi...  23 us
    ppermute x23, starting transfers between devices, flipped(): lax.ppermute(array, axis, [(i, i ^ mask) for i in range(lax.axis_size(axi...  18.1 us
    ppermute x2, waiting for transfers between devices, on_device(): lax.ppermute(a, 'section', [(i, i - 1) for i in range(1, sections)])  9.29 us
    pallas_call x4, Pallas kernels, value_grad_part(): pl.pallas_call(body, in_specs=[VMEM] * (blocks + count) + [ANY] * len(giv...  8.15 us
    ppermute x1, starting transfers between devices, on_device(): lax.ppermute(after(parked[0], kept[-1][1]), 'section', [(i, sections - 1...  3.6 us
    ppermute x2, starting transfers between devices, on_device(): lax.ppermute(a, 'section', [(i, i - 1) for i in range(1, sections)])  2.75 us
  transfers between devices with their start and end apart: 26, of which 10 were waited for; matrix products, arithmetic and copies ran while one was open for 1% of the time, Pallas kernels for 37%

profile of v2, /device:TPU:0, one launch (start us, length us, event | category | flops | bytes accessed | tf_op | source)
XLA Modules:
  0.0 100.6 jit_solution(1860441259126616780)
XLA Ops:
  0.6 3.0 %collective-permute-start = (bf16[64,1536]{1,0:T(8,128)(2,1)}, bf16[64,1536]{1,0:T(8,128)(2,1)S(1)}, u32[]{:S(2)}, u32[]{:S(2)}) collective-permute-start(bf16[64,1536]{1,0:T(8,128)(2,1)} %bitcast.6), channel_id=1, source_target_pairs={{0,4},{4,0},{1,5},{5,1},{2,6},{6,2},{3,7},{7,3},{8,12},{12,8},{9,1... | collective-permute-start | bytes 589832 | tf_op jit(solution)/shard_map/ppermute | solution.py:309
  3.8 0.7 broadcast_in_dim.12.refs_0_
  5.0 4.7 %shard_map.78.refs_2_.refs_3_.refs_4_.refs_8_ = bf16[4096,1536]{1,0:T(8,128)(2,1)S(1)} custom-call(bf16[4096,1536]{1,0:T(8,128)(2,1)} %bitcast.16), custom_call_target="tpu_custom_call" | custom-call | flops 10000000000 | bytes 100000000 | tf_op jit(solution)/shard_map/pallas_call | solution.py:49
  9.7 1.2 %shard_map.79 = bf16[128,1024]{1,0:T(8,128)(2,1)S(1)} custom-call(bf16[64,1536]{1,0:T(8,128)(2,1)S(1)} %bitcast.7, bf16[64,1536]{1,0:T(8,128)(2,1)S(1)} %collective-permute-done.refs_1_, bf16[4096,1536]{1,0:T(8,128)(2,1)S(1)} %shard_map.78.refs_2_.refs_3_.refs_4_.refs_8_), custom_call_target="tpu_custom_call" | custom-call | flops 10000000000 | bytes 100000000 | tf_op jit(solution)/shard_map/pallas_call | solution.py:49
  11.0 1.2 %shard_map.80 = bf16[128,1024]{1,0:T(8,128)(2,1)S(1)} custom-call(bf16[64,1536]{1,0:T(8,128)(2,1)S(1)} %bitcast.8, bf16[64,1536]{1,0:T(8,128)(2,1)S(1)} %collective-permute-done.refs_1_, bf16[4096,1536]{1,0:T(8,128)(2,1)S(1)} %shard_map.78.refs_2_.refs_3_.refs_4_.refs_8_), custom_call_target="tpu_custom_call" | custom-call | flops 10000000000 | bytes 100000000 | tf_op jit(solution)/shard_map/pallas_call | solution.py:49
  12.7 1.1 %shard_map.81 = (f32[128,1024]{1,0:T(8,128)S(1)}, bf16[128,1024]{1,0:T(8,128)(2,1)S(1)}) custom-call(bf16[64,1536]{1,0:T(8,128)(2,1)S(1)} %bitcast.9, bf16[64,1536]{1,0:T(8,128)(2,1)S(1)} %collective-permute-done.refs_1_, bf16[4096,1536]{1,0:T(8,128)(2,1)S(1)} %shard_map.78.refs_2_.refs_3_.refs_4_.refs_8_, bf16[128,1024]{1,0:T(8,128)(2,1)S(1)} %collective-permute-done.1.refs_3_), custom_call_target="tpu_custom_call" | custom-call | flops 10000000000 | bytes 100000000 | tf_op jit(solution)/shard_map/pallas_call | solution.py:49
  13.8 1.6 %collective-permute-start.3 = (bf16[128,1024]{1,0:T(8,128)(2,1)S(1)}, bf16[128,1024]{1,0:T(8,128)(2,1)S(1)}, u32[]{:S(2)}, u32[]{:S(2)}) collective-permute-start(bf16[128,1024]{1,0:T(8,128)(2,1)S(1)} %get-tuple-element.68), channel_id=1, source_target_pairs={{0,2},{1,3},{2,0},{3,1},{4,6},{5,7},{6,4},{7,5},{8,10},{9,11},{10,... | collective-permute-start | bytes 786440 | tf_op jit(solution)/shard_map/ppermute | solution.py:309
  15.4 3.9 %shard_map.82 = (f32[128,1024]{1,0:T(8,128)S(1)}, bf16[128,1024]{1,0:T(8,128)(2,1)S(1)}, bf16[1536,1024]{1,0:T(8,128)(2,1)S(1)}, bf16[1536,1024]{1,0:T(8,128)(2,1)S(1)}) custom-call(bf16[64,1536]{1,0:T(8,128)(2,1)S(1)} %bitcast.10, bf16[64,1536]{1,0:T(8,128)(2,1)S(1)} %collective-permute-done.refs_1_, ...), custom_call_target="tpu_custom_call" | custom-call | flops 10000000000 | bytes 100000000 | tf_op jit(solution)/shard_map/pallas_call | solution.py:49
  19.3 0.6 collective-permute-start.5
  19.8 3.6 %collective-permute-start.7 = (bf16[2,64,1536]{2,1,0:T(8,128)(2,1)S(1)}, bf16[2,64,1536]{2,1,0:T(8,128)(2,1)S(1)}, u32[]{:S(2)}, u32[]{:S(2)}) collective-permute-start(bf16[2,64,1536]{2,1,0:T(8,128)(2,1)S(1)} %bitcast.17), channel_id=1, source_target_pairs={{0,24},{8,16},{16,8},{24,0},{1,25},{9,17},{17,9},{25,1},{2,26},{10... | collective-permute-start | bytes 1179656 | tf_op jit(solution)/shard_map/ppermute | solution.py:376
  23.8 2.9 %shard_map.84 = (f32[128,1536]{1,0:T(8,128)S(1)}, bf16[1536,1024]{1,0:T(8,128)(2,1)S(1)}) custom-call(bf16[128,1024]{1,0:T(8,128)(2,1)S(1)} %shard_map.83.refs_0_.refs_4_, bf16[1536,1024]{1,0:T(8,128)(2,1)S(1)} %get-tuple-element.69.refs_4_.refs_1_.refs_3_.refs_5_.refs_9_.refs_6_, bf16[4096,1536]{1,0:T(8,128)(2,1)S(1)} %shard_map.78.refs_2_.refs_3_.refs_4_.refs_8_, ...), custom_call_target="tpu_custom_call" | custom-call | flops 10000000000 | bytes 100000000 | tf_op jit(solution)/shard_map/pallas_call | solution.py:49
  26.7 2.9 %shard_map.85 = (f32[128,1536]{1,0:T(8,128)S(1)}, bf16[1536,1024]{1,0:T(8,128)(2,1)S(1)}) custom-call(bf16[128,1024]{1,0:T(8,128)(2,1)S(1)} %collective-permute-done.4.refs_0_.refs_4_, bf16[1536,1024]{1,0:T(8,128)(2,1)S(1)} %get-tuple-element.70.refs_5_.refs_3_.refs_1_.refs_4_.refs_6_.refs_10_.refs_7_, f32[128,1536]{1,0:T(8,128)S(1)} %get-tuple-element.72.refs_2_, ...), custom_call_target="tpu_custom_call" | custom-call | flops 10000000000 | bytes 100000000 | tf_op jit(solution)/shard_map/pallas_call | solution.py:49
  30.5 1.2 %shard_map.87.refs_2_ = f32[128,1536]{1,0:T(8,128)S(1)} custom-call(bf16[128,1024]{1,0:T(8,128)(2,1)S(1)} %shard_map.86.refs_0_.refs_4_, bf16[1536,1024]{1,0:T(8,128)(2,1)S(1)} %get-tuple-element.74.refs_5_.refs_6_.refs_1_.refs_7_.refs_11_.refs_8_.refs_4_, f32[128,1536]{1,0:T(8,128)S(1)} %get-tuple-element.75.refs_2_, ...), custom_call_target="tpu_custom_call" | custom-call | flops 10000000000 | bytes 100000000 | tf_op jit(solution)/shard_map/pallas_call | solution.py:49
  31.7 1.2 %shard_map.88 = (f32[64,1536]{1,0:T(8,128)S(1)}, bf16[64,1536]{1,0:T(8,128)(2,1)S(1)}) custom-call(bf16[128,1024]{1,0:T(8,128)(2,1)S(1)} %collective-permute-done.6.refs_0_.refs_4_, bf16[1536,1024]{1,0:T(8,128)(2,1)S(1)} %get-tuple-element.78.refs_7_.refs_6_.refs_1_.refs_8_.refs_12_.refs_9_.refs_5_, f32[128,1536]{1,0:T(8,128)S(1)} %shard_map.87.refs_2_, ...), custom_call_target="tpu_custom_call" | custom-call | flops 10000000000 | bytes 100000000 | tf_op jit(solution)/shard_map/pallas_call | solution.py:49
  32.9 0.8 collective-permute-start.8
  33.7 0.6 shard_map.89
  34.3 5.8 %collective-permute-done.8.refs_3_ = bf16[64,1536]{1,0:T(8,128)(2,1)S(1)} collective-permute-done((bf16[64,1536]{1,0:T(8,128)(2,1)S(1)}, bf16[64,1536]{1,0:T(8,128)(2,1)S(1)}, u32[]{:S(2)}, u32[]{:S(2)}) %collective-permute-start.8) | collective-permute-done | bytes 196640 | tf_op jit(solution)/shard_map/ppermute | solution.py:309
  40.4 1.2 %collective-permute-done.9.refs_1_ = f32[8,128]{1,0:T(8,128)S(1)} collective-permute-done((f32[8,128]{1,0:T(8,128)S(1)}, f32[8,128]{1,0:T(8,128)S(1)}, u32[]{:S(2)}, u32[]{:S(2)}) %collective-permute-start.9) | collective-permute-done | bytes 4128 | tf_op jit(solution)/shard_map/ppermute | solution.py:309
  41.5 1.5 %collective-permute-start.10 = (f32[8,128]{1,0:T(8,128)S(1)}, f32[8,128]{1,0:T(8,128)S(1)}, u32[]{:S(2)}, u32[]{:S(2)}) collective-permute-start(f32[8,128]{1,0:T(8,128)S(1)} %shard_map.91.refs_4_.refs_6_.refs_5_), channel_id=1, source_target_pairs={{0,2},{1,3},{2,0},{3,1},{4,6},{5,7},{6,4},{7,5},{8,10},{9,11},{10,... | collective-permute-start | bytes 12296 | tf_op jit(solution)/shard_map/ppermute | solution.py:309
  43.1 2.1 %collective-permute-done.10.refs_5_.refs_7_.refs_6_ = f32[8,128]{1,0:T(8,128)S(1)} collective-permute-done((f32[8,128]{1,0:T(8,128)S(1)}, f32[8,128]{1,0:T(8,128)S(1)}, u32[]{:S(2)}, u32[]{:S(2)}) %collective-permute-start.10) | collective-permute-done | bytes 4128 | tf_op jit(solution)/shard_map/ppermute | solution.py:309
  45.7 1.3 %collective-permute-start.11 = (bf16[64,768]{1,0:T(8,128)(2,1)S(1)}, bf16[64,768]{1,0:T(8,128)(2,1)S(1)}, u32[]{:S(2)}, u32[]{:S(2)}) collective-permute-start(bf16[64,768]{1,0:T(8,128)(2,1)S(1)} %get-tuple-element.92), channel_id=1, source_target_pairs={{8,0},{16,8},{24,16},{9,1},{17,9},{25,17},{10,2},{18,10},{26,18},{... | collective-permute-start | bytes 294920 | tf_op jit(solution)/shard_map/ppermute | solution.py:355
  47.0 1.5 %collective-permute-start.12 = (bf16[64,768]{1,0:T(8,128)(2,1)S(1)}, bf16[64,768]{1,0:T(8,128)(2,1)S(1)}, u32[]{:S(2)}, u32[]{:S(2)}) collective-permute-start(bf16[64,768]{1,0:T(8,128)(2,1)S(1)} %get-tuple-element.94), channel_id=1, source_target_pairs={{8,0},{16,8},{24,16},{9,1},{17,9},{25,17},{10,2},{18,10},{26,18},{... | collective-permute-start | bytes 294920 | tf_op jit(solution)/shard_map/ppermute | solution.py:355
  48.5 8.7 %collective-permute-done.11.refs_0_.refs_3_ = bf16[64,768]{1,0:T(8,128)(2,1)S(1)} collective-permute-done((bf16[64,768]{1,0:T(8,128)(2,1)S(1)}, bf16[64,768]{1,0:T(8,128)(2,1)S(1)}, u32[]{:S(2)}, u32[]{:S(2)}) %collective-permute-start.11) | collective-permute-done | bytes 98336 | tf_op jit(solution)/shard_map/ppermute | solution.py:355
  57.3 0.8 collective-permute-start.13
  58.6 0.8 collective-permute-start.14
  59.4 1.3 %collective-permute-start.24 = (bf16[64,1536]{1,0:T(8,128)(2,1)S(1)}, bf16[64,1536]{1,0:T(8,128)(2,1)S(1)}, u32[]{:S(2)}, u32[]{:S(2)}) collective-permute-start(bf16[64,1536]{1,0:T(8,128)(2,1)S(1)} %get-tuple-element.114.refs_0_), channel_id=1, source_target_pairs={{0,4},{4,0},{1,5},{5,1},{2,6},{6,2},{3,7},{7,3},{8,12},{12,8},{9,1... | collective-permute-start | bytes 589832 | tf_op jit(solution)/shard_map/ppermute | solution.py:309
  60.6 0.8 collective-permute-start.25
  61.4 1.5 %collective-permute-done.13.refs_2_ = bf16[64,768]{1,0:T(8,128)(2,1)S(1)} collective-permute-done((bf16[64,768]{1,0:T(8,128)(2,1)S(1)}, bf16[64,768]{1,0:T(8,128)(2,1)S(1)}, u32[]{:S(2)}, u32[]{:S(2)}) %collective-permute-start.13) | collective-permute-done | bytes 98336 | tf_op jit(solution)/shard_map/ppermute | solution.py:309
  62.9 2.1 %collective-permute-done.14.refs_3_ = bf16[64,768]{1,0:T(8,128)(2,1)S(1)} collective-permute-done((bf16[64,768]{1,0:T(8,128)(2,1)S(1)}, bf16[64,768]{1,0:T(8,128)(2,1)S(1)}, u32[]{:S(2)}, u32[]{:S(2)}) %collective-permute-start.14) | collective-permute-done | bytes 98336 | tf_op jit(solution)/shard_map/ppermute | solution.py:309
  65.0 1.1 %shard_map.93 = bf16[128,1024]{1,0:T(8,128)(2,1)S(1)} custom-call(bf16[64,768]{1,0:T(8,128)(2,1)S(1)} %collective-permute-done.11.refs_0_.refs_3_, bf16[64,768]{1,0:T(8,128)(2,1)S(1)} %collective-permute-done.12.refs_1_.refs_4_, bf16[64,768]{1,0:T(8,128)(2,1)S(1)} %collective-permute-done.13.refs_2_, bf16[64,768]{1,0:T(8,128)(2,1)S(1)} %collective-permute-done.14.refs_3_, ...), custom_call_target="tpu_custom_call" | custom-call | flops 10000000000 | bytes 100000000 | tf_op jit(solution)/shard_map/pallas_call | solution.py:49
  66.2 1.2 %shard_map.94 = bf16[128,1024]{1,0:T(8,128)(2,1)S(1)} custom-call(bf16[64,768]{1,0:T(8,128)(2,1)S(1)} %collective-permute-done.11.refs_0_.refs_3_, bf16[64,768]{1,0:T(8,128)(2,1)S(1)} %collective-permute-done.12.refs_1_.refs_4_, bf16[64,768]{1,0:T(8,128)(2,1)S(1)} %collective-permute-done.13.refs_2_, bf16[64,768]{1,0:T(8,128)(2,1)S(1)} %collective-permute-done.14.refs_3_, ...), custom_call_target="tpu_custom_call" | custom-call | flops 10000000000 | bytes 100000000 | tf_op jit(solution)/shard_map/pallas_call | solution.py:49
  67.9 1.1 %shard_map.95 = (f32[128,1024]{1,0:T(8,128)S(1)}, bf16[128,1024]{1,0:T(8,128)(2,1)S(1)}) custom-call(bf16[64,768]{1,0:T(8,128)(2,1)S(1)} %collective-permute-done.11.refs_0_.refs_3_, bf16[64,768]{1,0:T(8,128)(2,1)S(1)} %collective-permute-done.12.refs_1_.refs_4_, bf16[64,768]{1,0:T(8,128)(2,1)S(1)} %collective-permute-done.13.refs_2_, ...), custom_call_target="tpu_custom_call" | custom-call | flops 10000000000 | bytes 100000000 | tf_op jit(solution)/shard_map/pallas_call | solution.py:49
  69.0 1.5 %collective-permute-start.17 = (bf16[128,1024]{1,0:T(8,128)(2,1)S(1)}, bf16[128,1024]{1,0:T(8,128)(2,1)S(1)}, u32[]{:S(2)}, u32[]{:S(2)}) collective-permute-start(bf16[128,1024]{1,0:T(8,128)(2,1)S(1)} %get-tuple-element.101), channel_id=1, source_target_pairs={{0,2},{1,3},{2,0},{3,1},{4,6},{5,7},{6,4},{7,5},{8,10},{9,11},{10,... | collective-permute-start | bytes 786440 | tf_op jit(solution)/shard_map/ppermute | solution.py:309
  70.6 1.1 %shard_map.96 = (f32[128,1024]{1,0:T(8,128)S(1)}, bf16[128,1024]{1,0:T(8,128)(2,1)S(1)}) custom-call(bf16[64,768]{1,0:T(8,128)(2,1)S(1)} %collective-permute-done.11.refs_0_.refs_3_, bf16[64,768]{1,0:T(8,128)(2,1)S(1)} %collective-permute-done.12.refs_1_.refs_4_, bf16[64,768]{1,0:T(8,128)(2,1)S(1)} %collective-permute-done.13.refs_2_, ...), custom_call_target="tpu_custom_call" | custom-call | flops 10000000000 | bytes 100000000 | tf_op jit(solution)/shard_map/pallas_call | solution.py:49
  71.7 0.6 collective-permute-start.19
  72.3 5.9 %collective-permute-done.17.refs_1_ = bf16[128,1024]{1,0:T(8,128)(2,1)S(1)} collective-permute-done((bf16[128,1024]{1,0:T(8,128)(2,1)S(1)}, bf16[128,1024]{1,0:T(8,128)(2,1)S(1)}, u32[]{:S(2)}, u32[]{:S(2)}) %collective-permute-start.17) | collective-permute-done | bytes 262176 | tf_op jit(solution)/shard_map/ppermute | solution.py:309
  78.6 1.1 %shard_map.98.refs_2_ = f32[128,1536]{1,0:T(8,128)S(1)} custom-call(bf16[128,1024]{1,0:T(8,128)(2,1)S(1)} %shard_map.97.refs_0_.refs_5_, bf16[1536,1024]{1,0:T(8,128)(2,1)S(1)} %get-tuple-element.69.refs_4_.refs_1_.refs_3_.refs_5_.refs_9_.refs_6_, bf16[4096,1536]{1,0:T(8,128)(2,1)S(1)} %shard_map.78.refs_2_.refs_3_.refs_4_.refs_8_, ...), custom_call_target="tpu_custom_call" | custom-call | flops 10000000000 | bytes 100000000 | tf_op jit(solution)/shard_map/pallas_call | solution.py:49
  79.8 2.0 %shard_map.106.refs_6_ = bf16[1536,4096]{1,0:T(8,128)(2,1)} custom-call(bf16[64,1536]{1,0:T(8,128)(2,1)S(1)} %get-tuple-element.114.refs_0_, bf16[64,1536]{1,0:T(8,128)(2,1)S(1)} %collective-permute-done.24.refs_1_, bf16[64,1536]{1,0:T(8,128)(2,1)S(1)} %get-tuple-element.115.refs_2_, bf16[64,1536]{1,0:T(8,128)(2,1)S(1)} %collective-permute-done.25.refs_3_, ...), custom_call_target="tpu_custom_call" | custom-call | flops 10000000000 | bytes 100000000 | tf_op jit(solution)/shard_map/pallas_call | solution.py:273
  81.9 1.2 %shard_map.99.refs_2_ = f32[128,1536]{1,0:T(8,128)S(1)} custom-call(bf16[128,1024]{1,0:T(8,128)(2,1)S(1)} %collective-permute-done.18.refs_0_.refs_5_, bf16[1536,1024]{1,0:T(8,128)(2,1)S(1)} %get-tuple-element.70.refs_5_.refs_3_.refs_1_.refs_4_.refs_6_.refs_10_.refs_7_, f32[128,1536]{1,0:T(8,128)S(1)} %shard_map.98.refs_2_, ...), custom_call_target="tpu_custom_call" | custom-call | flops 10000000000 | bytes 100000000 | tf_op jit(solution)/shard_map/pallas_call | solution.py:49
  83.9 1.2 %shard_map.101.refs_2_ = f32[128,1536]{1,0:T(8,128)S(1)} custom-call(bf16[128,1024]{1,0:T(8,128)(2,1)S(1)} %shard_map.100.refs_0_.refs_5_, bf16[1536,1024]{1,0:T(8,128)(2,1)S(1)} %get-tuple-element.74.refs_5_.refs_6_.refs_1_.refs_7_.refs_11_.refs_8_.refs_4_, f32[128,1536]{1,0:T(8,128)S(1)} %shard_map.99.refs_2_, ...), custom_call_target="tpu_custom_call" | custom-call | flops 10000000000 | bytes 100000000 | tf_op jit(solution)/shard_map/pallas_call | solution.py:49
  85.1 1.2 %shard_map.102 = (f32[64,1536]{1,0:T(8,128)S(1)}, bf16[64,1536]{1,0:T(8,128)(2,1)S(1)}) custom-call(bf16[128,1024]{1,0:T(8,128)(2,1)S(1)} %collective-permute-done.20.refs_0_.refs_5_, bf16[1536,1024]{1,0:T(8,128)(2,1)S(1)} %get-tuple-element.78.refs_7_.refs_6_.refs_1_.refs_8_.refs_12_.refs_9_.refs_5_, f32[128,1536]{1,0:T(8,128)S(1)} %shard_map.101.refs_2_, ...), custom_call_target="tpu_custom_call" | custom-call | flops 10000000000 | bytes 100000000 | tf_op jit(solution)/shard_map/pallas_call | solution.py:49
  86.2 0.9 collective-permute-start.21
  87.1 2.0 %shard_map.107.refs_6_ = bf16[1536,4096]{1,0:T(8,128)(2,1)} custom-call(bf16[64,1536]{1,0:T(8,128)(2,1)S(1)} %get-tuple-element.114.refs_0_, bf16[64,1536]{1,0:T(8,128)(2,1)S(1)} %collective-permute-done.24.refs_1_, bf16[64,1536]{1,0:T(8,128)(2,1)S(1)} %get-tuple-element.115.refs_2_, ...), custom_call_target="tpu_custom_call", output_to_operand_aliasing={{}: (6, {})} | custom-call | flops 10000000000 | bytes 100000000 | tf_op jit(solution)/shard_map/pallas_call | solution.py:273
  89.1 4.3 %collective-permute-done.21.refs_3_ = bf16[64,1536]{1,0:T(8,128)(2,1)S(1)} collective-permute-done((bf16[64,1536]{1,0:T(8,128)(2,1)S(1)}, bf16[64,1536]{1,0:T(8,128)(2,1)S(1)}, u32[]{:S(2)}, u32[]{:S(2)}) %collective-permute-start.21) | collective-permute-done | bytes 196640 | tf_op jit(solution)/shard_map/ppermute | solution.py:309
  93.7 2.0 %shard_map.108.refs_6_ = bf16[1536,4096]{1,0:T(8,128)(2,1)} custom-call(bf16[64,1536]{1,0:T(8,128)(2,1)S(1)} %get-tuple-element.114.refs_0_, bf16[64,1536]{1,0:T(8,128)(2,1)S(1)} %collective-permute-done.24.refs_1_, bf16[64,1536]{1,0:T(8,128)(2,1)S(1)} %get-tuple-element.115.refs_2_, ...), custom_call_target="tpu_custom_call", output_to_operand_aliasing={{}: (6, {})} | custom-call | flops 10000000000 | bytes 100000000 | tf_op jit(solution)/shard_map/pallas_call | solution.py:273
  95.8 1.5 %collective-permute-start.23 = (f32[8,128]{1,0:T(8,128)S(1)}, f32[8,128]{1,0:T(8,128)S(1)}, u32[]{:S(2)}, u32[]{:S(2)}) collective-permute-start(f32[8,128]{1,0:T(8,128)S(1)} %shard_map.104.refs_7_), channel_id=1, source_target_pairs={{0,2},{1,3},{2,0},{3,1},{4,6},{5,7},{6,4},{7,5},{8,10},{9,11},{10,... | collective-permute-start | bytes 12296 | tf_op jit(solution)/shard_map/ppermute | solution.py:309
  97.3 2.0 %shard_map.109 = bf16[1536,4096]{1,0:T(8,128)(2,1)} custom-call(bf16[64,1536]{1,0:T(8,128)(2,1)S(1)} %get-tuple-element.114.refs_0_, bf16[64,1536]{1,0:T(8,128)(2,1)S(1)} %collective-permute-done.24.refs_1_, bf16[64,1536]{1,0:T(8,128)(2,1)S(1)} %get-tuple-element.115.refs_2_, ...), custom_call_target="tpu_custom_call", output_to_operand_aliasing={{}: (6, {})} | custom-call | flops 10000000000 | bytes 100000000 | tf_op jit(solution)/shard_map/pallas_call | solution.py:273
  99.5 1.1 %shard_map.105 = bf16[64,1536]{1,0:T(8,128)(2,1)} custom-call(f32[64,1536]{1,0:T(8,128)S(1)} %get-tuple-element.113.refs_0_, bf16[64,1536]{1,0:T(8,128)(2,1)S(1)} %get-tuple-element.84.refs_1_, bf16[64,1536]{1,0:T(8,128)(2,1)S(1)} %get-tuple-element.86.refs_2_, bf16[64,768]{1,0:T(8,128)(2,1)S(1)} %collective-permute-done.11.refs_0_.refs_3_, ...), custom_call_target="tpu_custom_call" | custom-call | flops 10000000000 | bytes 100000000 | tf_op jit(solution)/shard_map/pallas_call | solution.py:49
  (63 shorter events, 6.0 us)
Async XLA Ops:
  0.6 3.0 %copy-start = (s32[4,2]{0,1:T(2,128)S(1)}, s32[4,2]{0,1:T(2,128)}, u32[]{:S(2)}) copy-start(s32[4,2]{0,1:T(2,128)} %param.8) | copy-start | bytes 100
  0.6 9.1 %collective-permute-start = (bf16[64,1536]{1,0:T(8,128)(2,1)}, bf16[64,1536]{1,0:T(8,128)(2,1)S(1)}, u32[]{:S(2)}, u32[]{:S(2)}) collective-permute-start(bf16[64,1536]{1,0:T(8,128)(2,1)} %bitcast.6), channel_id=1, source_target_pairs={{0,4},{4,0},{1,5},{5,1},{2,6},{6,2},{3,7},{7,3},{8,12},{12,8},{9,1... | collective-permute-start | bytes 589832 | tf_op jit(solution)/shard_map/ppermute | solution.py:309
  4.9 4.8 %copy-start.2 = (bf16[1,64,1536]{2,1,0:T(8,128)(2,1)S(1)}, bf16[1,64,1536]{2,1,0:T(8,128)(2,1)}, u32[]{:S(2)}) copy-start(bf16[1,64,1536]{2,1,0:T(8,128)(2,1)} %param.7) | copy-start | bytes 589828
  10.9 1.8 %collective-permute-start.1 = (bf16[128,1024]{1,0:T(8,128)(2,1)S(1)}, bf16[128,1024]{1,0:T(8,128)(2,1)S(1)}, u32[]{:S(2)}, u32[]{:S(2)}) collective-permute-start(bf16[128,1024]{1,0:T(8,128)(2,1)S(1)} %shard_map.79), channel_id=1, source_target_pairs={{0,1},{1,0},{2,3},{3,2},{4,5},{5,4},{6,7},{7,6},{8,9},{9,8},{10,11... | collective-permute-start | bytes 786440 | tf_op jit(solution)/shard_map/ppermute | solution.py:309
  12.1 3.3 %collective-permute-start.2 = (bf16[128,1024]{1,0:T(8,128)(2,1)S(1)}, bf16[128,1024]{1,0:T(8,128)(2,1)S(1)}, u32[]{:S(2)}, u32[]{:S(2)}) collective-permute-start(bf16[128,1024]{1,0:T(8,128)(2,1)S(1)} %shard_map.80), channel_id=1, source_target_pairs={{0,1},{1,0},{2,3},{3,2},{4,5},{5,4},{6,7},{7,6},{8,9},{9,8},{10,11... | collective-permute-start | bytes 786440 | tf_op jit(solution)/shard_map/ppermute | solution.py:309
  13.8 9.6 %collective-permute-start.3 = (bf16[128,1024]{1,0:T(8,128)(2,1)S(1)}, bf16[128,1024]{1,0:T(8,128)(2,1)S(1)}, u32[]{:S(2)}, u32[]{:S(2)}) collective-permute-start(bf16[128,1024]{1,0:T(8,128)(2,1)S(1)} %get-tuple-element.68), channel_id=1, source_target_pairs={{0,2},{1,3},{2,0},{3,1},{4,6},{5,7},{6,4},{7,5},{8,10},{9,11},{10,... | collective-permute-start | bytes 786440 | tf_op jit(solution)/shard_map/ppermute | solution.py:309
  15.4 4.4 %copy-start.11 = (bf16[1,2,64,1536]{3,2,1,0:T(8,128)(2,1)S(1)}, bf16[1,2,64,1536]{3,2,1,0:T(8,128)(2,1)}, u32[]{:S(2)}) copy-start(bf16[1,2,64,1536]{3,2,1,0:T(8,128)(2,1)} %param.6) | copy-start | bytes 1179652
  19.3 10.4 %collective-permute-start.5 = (bf16[128,1024]{1,0:T(8,128)(2,1)S(1)}, bf16[128,1024]{1,0:T(8,128)(2,1)S(1)}, u32[]{:S(2)}, u32[]{:S(2)}) collective-permute-start(bf16[128,1024]{1,0:T(8,128)(2,1)S(1)} %get-tuple-element.77), channel_id=1, source_target_pairs={{0,2},{1,3},{2,0},{3,1},{4,6},{5,7},{6,4},{7,5},{8,10},{9,11},{10,... | collective-permute-start | bytes 786440 | tf_op jit(solution)/shard_map/ppermute | solution.py:309
  19.8 13.0 %collective-permute-start.7 = (bf16[2,64,1536]{2,1,0:T(8,128)(2,1)S(1)}, bf16[2,64,1536]{2,1,0:T(8,128)(2,1)S(1)}, u32[]{:S(2)}, u32[]{:S(2)}) collective-permute-start(bf16[2,64,1536]{2,1,0:T(8,128)(2,1)S(1)} %bitcast.17), channel_id=1, source_target_pairs={{0,24},{8,16},{16,8},{24,0},{1,25},{9,17},{17,9},{25,1},{2,26},{10... | collective-permute-start | bytes 1179656 | tf_op jit(solution)/shard_map/ppermute | solution.py:376
  23.7 3.0 %collective-permute-start.4 = (bf16[128,1024]{1,0:T(8,128)(2,1)S(1)}, bf16[128,1024]{1,0:T(8,128)(2,1)S(1)}, u32[]{:S(2)}, u32[]{:S(2)}) collective-permute-start(bf16[128,1024]{1,0:T(8,128)(2,1)S(1)} %shard_map.83.refs_0_.refs_4_), channel_id=1, source_target_pairs={{0,1},{1,0},{2,3},{3,2},{4,5},{5,4},{6,7},{7,6},{8,9},{9,8},{10,11... | collective-permute-start | bytes 786440 | tf_op jit(solution)/shard_map/ppermute | solution.py:309
  26.7 2.9 %copy-start.7 = (bf16[128,1024]{1,0:T(8,128)(2,1)}, bf16[128,1024]{1,0:T(8,128)(2,1)S(1)}, u32[]{:S(2)}) copy-start(bf16[128,1024]{1,0:T(8,128)(2,1)S(1)} %collective-permute-done.4.refs_0_.refs_4_) | copy-start | bytes 786436
  29.9 1.7 %copy-start.5 = (bf16[128,1024]{1,0:T(8,128)(2,1)}, bf16[128,1024]{1,0:T(8,128)(2,1)S(1)}, u32[]{:S(2)}) copy-start(bf16[128,1024]{1,0:T(8,128)(2,1)S(1)} %shard_map.86.refs_0_.refs_4_) | copy-start | bytes 786436
  29.9 1.7 %collective-permute-start.6 = (bf16[128,1024]{1,0:T(8,128)(2,1)S(1)}, bf16[128,1024]{1,0:T(8,128)(2,1)S(1)}, u32[]{:S(2)}, u32[]{:S(2)}) collective-permute-start(bf16[128,1024]{1,0:T(8,128)(2,1)S(1)} %shard_map.86.refs_0_.refs_4_), channel_id=1, source_target_pairs={{0,1},{1,0},{2,3},{3,2},{4,5},{5,4},{6,7},{7,6},{8,9},{9,8},{10,11... | collective-permute-start | bytes 786440 | tf_op jit(solution)/shard_map/ppermute | solution.py:309
  31.7 1.2 %copy-start.3 = (bf16[128,1024]{1,0:T(8,128)(2,1)}, bf16[128,1024]{1,0:T(8,128)(2,1)S(1)}, u32[]{:S(2)}) copy-start(bf16[128,1024]{1,0:T(8,128)(2,1)S(1)} %collective-permute-done.6.refs_0_.refs_4_) | copy-start | bytes 786436
  32.9 7.2 %collective-permute-start.8 = (bf16[64,1536]{1,0:T(8,128)(2,1)S(1)}, bf16[64,1536]{1,0:T(8,128)(2,1)S(1)}, u32[]{:S(2)}, u32[]{:S(2)}) collective-permute-start(bf16[64,1536]{1,0:T(8,128)(2,1)S(1)} %get-tuple-element.87), channel_id=1, source_target_pairs={{0,4},{4,0},{1,5},{5,1},{2,6},{6,2},{3,7},{7,3},{8,12},{12,8},{9,1... | collective-permute-start | bytes 589832 | tf_op jit(solution)/shard_map/ppermute | solution.py:309
  40.4 1.2 %collective-permute-start.9 = (f32[8,128]{1,0:T(8,128)S(1)}, f32[8,128]{1,0:T(8,128)S(1)}, u32[]{:S(2)}, u32[]{:S(2)}) collective-permute-start(f32[8,128]{1,0:T(8,128)S(1)} %get-tuple-element.90.refs_0_), channel_id=1, source_target_pairs={{0,1},{1,0},{2,3},{3,2},{4,5},{5,4},{6,7},{7,6},{8,9},{9,8},{10,11... | collective-permute-start | bytes 12296 | tf_op jit(solution)/shard_map/ppermute | solution.py:309
  41.5 3.6 %collective-permute-start.10 = (f32[8,128]{1,0:T(8,128)S(1)}, f32[8,128]{1,0:T(8,128)S(1)}, u32[]{:S(2)}, u32[]{:S(2)}) collective-permute-start(f32[8,128]{1,0:T(8,128)S(1)} %shard_map.91.refs_4_.refs_6_.refs_5_), channel_id=1, source_target_pairs={{0,2},{1,3},{2,0},{3,1},{4,6},{5,7},{6,4},{7,5},{8,10},{9,11},{10,... | collective-permute-start | bytes 12296 | tf_op jit(solution)/shard_map/ppermute | solution.py:309
  45.2 0.6 copy-start.9
  45.7 11.5 %collective-permute-start.11 = (bf16[64,768]{1,0:T(8,128)(2,1)S(1)}, bf16[64,768]{1,0:T(8,128)(2,1)S(1)}, u32[]{:S(2)}, u32[]{:S(2)}) collective-permute-start(bf16[64,768]{1,0:T(8,128)(2,1)S(1)} %get-tuple-element.92), channel_id=1, source_target_pairs={{8,0},{16,8},{24,16},{9,1},{17,9},{25,17},{10,2},{18,10},{26,18},{... | collective-permute-start | bytes 294920 | tf_op jit(solution)/shard_map/ppermute | solution.py:355
  47.0 11.5 %collective-permute-start.12 = (bf16[64,768]{1,0:T(8,128)(2,1)S(1)}, bf16[64,768]{1,0:T(8,128)(2,1)S(1)}, u32[]{:S(2)}, u32[]{:S(2)}) collective-permute-start(bf16[64,768]{1,0:T(8,128)(2,1)S(1)} %get-tuple-element.94), channel_id=1, source_target_pairs={{8,0},{16,8},{24,16},{9,1},{17,9},{25,17},{10,2},{18,10},{26,18},{... | collective-permute-start | bytes 294920 | tf_op jit(solution)/shard_map/ppermute | solution.py:355
  57.3 5.6 %collective-permute-start.13 = (bf16[64,768]{1,0:T(8,128)(2,1)S(1)}, bf16[64,768]{1,0:T(8,128)(2,1)S(1)}, u32[]{:S(2)}, u32[]{:S(2)}) collective-permute-start(bf16[64,768]{1,0:T(8,128)(2,1)S(1)} %collective-permute-done.11.refs_0_.refs_3_), channel_id=1, source_target_pairs={{0,4},{4,0},{1,5},{5,1},{2,6},{6,2},{3,7},{7,3},{8,12},{12,8},{9,1... | collective-permute-start | bytes 294920 | tf_op jit(solution)/shard_map/ppermute | solution.py:309
  58.6 6.4 %collective-permute-start.14 = (bf16[64,768]{1,0:T(8,128)(2,1)S(1)}, bf16[64,768]{1,0:T(8,128)(2,1)S(1)}, u32[]{:S(2)}, u32[]{:S(2)}) collective-permute-start(bf16[64,768]{1,0:T(8,128)(2,1)S(1)} %collective-permute-done.12.refs_1_.refs_4_), channel_id=1, source_target_pairs={{0,4},{4,0},{1,5},{5,1},{2,6},{6,2},{3,7},{7,3},{8,12},{12,8},{9,1... | collective-permute-start | bytes 294920 | tf_op jit(solution)/shard_map/ppermute | solution.py:309
  59.4 20.4 %collective-permute-start.24 = (bf16[64,1536]{1,0:T(8,128)(2,1)S(1)}, bf16[64,1536]{1,0:T(8,128)(2,1)S(1)}, u32[]{:S(2)}, u32[]{:S(2)}) collective-permute-start(bf16[64,1536]{1,0:T(8,128)(2,1)S(1)} %get-tuple-element.114.refs_0_), channel_id=1, source_target_pairs={{0,4},{4,0},{1,5},{5,1},{2,6},{6,2},{3,7},{7,3},{8,12},{12,8},{9,1... | collective-permute-start | bytes 589832 | tf_op jit(solution)/shard_map/ppermute | solution.py:309
  60.6 19.2 %collective-permute-start.25 = (bf16[64,1536]{1,0:T(8,128)(2,1)S(1)}, bf16[64,1536]{1,0:T(8,128)(2,1)S(1)}, u32[]{:S(2)}, u32[]{:S(2)}) collective-permute-start(bf16[64,1536]{1,0:T(8,128)(2,1)S(1)} %get-tuple-element.115.refs_2_), channel_id=1, source_target_pairs={{0,4},{4,0},{1,5},{5,1},{2,6},{6,2},{3,7},{7,3},{8,12},{12,8},{9,1... | collective-permute-start | bytes 589832 | tf_op jit(solution)/shard_map/ppermute | solution.py:309
  66.1 1.8 %collective-permute-start.15 = (bf16[128,1024]{1,0:T(8,128)(2,1)S(1)}, bf16[128,1024]{1,0:T(8,128)(2,1)S(1)}, u32[]{:S(2)}, u32[]{:S(2)}) collective-permute-start(bf16[128,1024]{1,0:T(8,128)(2,1)S(1)} %shard_map.93), channel_id=1, source_target_pairs={{0,1},{1,0},{2,3},{3,2},{4,5},{5,4},{6,7},{7,6},{8,9},{9,8},{10,11... | collective-permute-start | bytes 786440 | tf_op jit(solution)/shard_map/ppermute | solution.py:309
  67.4 3.2 %collective-permute-start.16 = (bf16[128,1024]{1,0:T(8,128)(2,1)S(1)}, bf16[128,1024]{1,0:T(8,128)(2,1)S(1)}, u32[]{:S(2)}, u32[]{:S(2)}) collective-permute-start(bf16[128,1024]{1,0:T(8,128)(2,1)S(1)} %shard_map.94), channel_id=1, source_target_pairs={{0,1},{1,0},{2,3},{3,2},{4,5},{5,4},{6,7},{7,6},{8,9},{9,8},{10,11... | collective-permute-start | bytes 786440 | tf_op jit(solution)/shard_map/ppermute | solution.py:309
  69.0 9.2 %collective-permute-start.17 = (bf16[128,1024]{1,0:T(8,128)(2,1)S(1)}, bf16[128,1024]{1,0:T(8,128)(2,1)S(1)}, u32[]{:S(2)}, u32[]{:S(2)}) collective-permute-start(bf16[128,1024]{1,0:T(8,128)(2,1)S(1)} %get-tuple-element.101), channel_id=1, source_target_pairs={{0,2},{1,3},{2,0},{3,1},{4,6},{5,7},{6,4},{7,5},{8,10},{9,11},{10,... | collective-permute-start | bytes 786440 | tf_op jit(solution)/shard_map/ppermute | solution.py:309
  71.7 11.3 %collective-permute-start.19 = (bf16[128,1024]{1,0:T(8,128)(2,1)S(1)}, bf16[128,1024]{1,0:T(8,128)(2,1)S(1)}, u32[]{:S(2)}, u32[]{:S(2)}) collective-permute-start(bf16[128,1024]{1,0:T(8,128)(2,1)S(1)} %get-tuple-element.105), channel_id=1, source_target_pairs={{0,2},{1,3},{2,0},{3,1},{4,6},{5,7},{6,4},{7,5},{8,10},{9,11},{10,... | collective-permute-start | bytes 786440 | tf_op jit(solution)/shard_map/ppermute | solution.py:309
  78.5 3.3 %collective-permute-start.18 = (bf16[128,1024]{1,0:T(8,128)(2,1)S(1)}, bf16[128,1024]{1,0:T(8,128)(2,1)S(1)}, u32[]{:S(2)}, u32[]{:S(2)}) collective-permute-start(bf16[128,1024]{1,0:T(8,128)(2,1)S(1)} %shard_map.97.refs_0_.refs_5_), channel_id=1, source_target_pairs={{0,1},{1,0},{2,3},{3,2},{4,5},{5,4},{6,7},{7,6},{8,9},{9,8},{10,11... | collective-permute-start | bytes 786440 | tf_op jit(solution)/shard_map/ppermute | solution.py:309
  83.3 1.7 %collective-permute-start.20 = (bf16[128,1024]{1,0:T(8,128)(2,1)S(1)}, bf16[128,1024]{1,0:T(8,128)(2,1)S(1)}, u32[]{:S(2)}, u32[]{:S(2)}) collective-permute-start(bf16[128,1024]{1,0:T(8,128)(2,1)S(1)} %shard_map.100.refs_0_.refs_5_), channel_id=1, source_target_pairs={{0,1},{1,0},{2,3},{3,2},{4,5},{5,4},{6,7},{7,6},{8,9},{9,8},{10,11... | collective-permute-start | bytes 786440 | tf_op jit(solution)/shard_map/ppermute | solution.py:309
  85.0 2.0 %copy-start.8 = (bf16[128,1024]{1,0:T(8,128)(2,1)S(1)}, bf16[128,1024]{1,0:T(8,128)(2,1)}, u32[]{:S(2)}) copy-start(bf16[128,1024]{1,0:T(8,128)(2,1)} %copy-done.7) | copy-start | bytes 786436
  86.2 7.2 %collective-permute-start.21 = (bf16[64,1536]{1,0:T(8,128)(2,1)S(1)}, bf16[64,1536]{1,0:T(8,128)(2,1)S(1)}, u32[]{:S(2)}, u32[]{:S(2)}) collective-permute-start(bf16[64,1536]{1,0:T(8,128)(2,1)S(1)} %get-tuple-element.109), channel_id=1, source_target_pairs={{0,4},{4,0},{1,5},{5,1},{2,6},{6,2},{3,7},{7,3},{8,12},{12,8},{9,1... | collective-permute-start | bytes 589832 | tf_op jit(solution)/shard_map/ppermute | solution.py:309
  89.1 4.6 %copy-start.6 = (bf16[128,1024]{1,0:T(8,128)(2,1)S(1)}, bf16[128,1024]{1,0:T(8,128)(2,1)}, u32[]{:S(2)}) copy-start(bf16[128,1024]{1,0:T(8,128)(2,1)} %copy-done.5) | copy-start | bytes 786436
  93.7 2.1 %collective-permute-start.22 = (f32[8,128]{1,0:T(8,128)S(1)}, f32[8,128]{1,0:T(8,128)S(1)}, u32[]{:S(2)}, u32[]{:S(2)}) collective-permute-start(f32[8,128]{1,0:T(8,128)S(1)} %get-tuple-element.112.refs_0_), channel_id=1, source_target_pairs={{0,1},{1,0},{2,3},{3,2},{4,5},{5,4},{6,7},{7,6},{8,9},{9,8},{10,11... | collective-permute-start | bytes 12296 | tf_op jit(solution)/shard_map/ppermute | solution.py:309
  95.7 1.6 %copy-start.4 = (bf16[128,1024]{1,0:T(8,128)(2,1)S(1)}, bf16[128,1024]{1,0:T(8,128)(2,1)}, u32[]{:S(2)}) copy-start(bf16[128,1024]{1,0:T(8,128)(2,1)} %copy-done.3) | copy-start | bytes 786436
  95.8 3.7 %copy-start.10 = (f32[8,128]{1,0:T(8,128)S(1)}, f32[8,128]{1,0:T(8,128)}, u32[]{:S(2)}) copy-start(f32[8,128]{1,0:T(8,128)} %copy-done.9) | copy-start | bytes 12292
  95.8 3.7 %collective-permute-start.23 = (f32[8,128]{1,0:T(8,128)S(1)}, f32[8,128]{1,0:T(8,128)S(1)}, u32[]{:S(2)}, u32[]{:S(2)}) collective-permute-start(f32[8,128]{1,0:T(8,128)S(1)} %shard_map.104.refs_7_), channel_id=1, source_target_pairs={{0,2},{1,3},{2,0},{3,1},{4,6},{5,7},{6,4},{7,5},{8,10},{9,11},{10,... | collective-permute-start | bytes 12296 | tf_op jit(solution)/shard_map/ppermute | solution.py:309
  97.3 3.2 %copy-start.1 = (s32[4,2]{0,1:T(2,128)S(1)}, s32[4,2]{0,1:T(2,128)}, u32[]{:S(2)}) copy-start(s32[4,2]{0,1:T(2,128)} %param.8) | copy-start | bytes 100

commit v3 on v2

--- a/solution.py
+++ b/solution.py
@@ -15,10 +15,11 @@
 ANY = pl.BlockSpec(memory_space=pl.ANY)
 HEAD = 128
 STEPS = 8
-COST = pl.CostEstimate(flops=10**10, bytes_accessed=10**8, transcendentals=0)
-
-
-def call(body, outs, operands, held=(), first_spec=VMEM, carry=()):
+COST = pl.CostEstimate(flops=4 * 10**9, bytes_accessed=10**8, transcendentals=0)
+LIGHT = pl.CostEstimate(flops=1, bytes_accessed=1, transcendentals=0)
+
+
+def call(body, outs, operands, held=(), first_spec=VMEM, carry=(), light=False):
     operands = list(operands)
     held = [h for h in held if not any(h is a for a in operands)]
     n_in, n_held, n_out, n_carry = len(operands), len(held), len(outs), len(carry)
@@ -55,7 +56,7 @@
         out_shape=[*outs, *more],
         scratch_shapes=[pltpu.SemaphoreType.DMA((n_carry, STEPS))] if carry else [],
         compiler_params=pltpu.CompilerParams(vmem_limit_bytes=SCOPED),
-        cost_estimate=COST,
+        cost_estimate=LIGHT if light else COST,
     )(*operands, *held, *sources)
 
 
@@ -118,15 +119,14 @@
     return call(body, [shape((rows, size), BF16)], [kept, *received, mixing], held)
 
 
-def grad_normed_part(grads, weights, total=None, pieces=0, held=(), carry=()):
-    rows, width = grads[0].shape[0], weights[0].shape[0]
-    count = len(grads)
-
-    def body(*refs):
-        sums = None if total is None else refs[2 * count][...]
-        for g, w in zip(refs[:count], refs[count : 2 * count], strict=True):
-            term = lax.dot_general(g[...], w[...], NT, preferred_element_type=F32)
-            sums = term if sums is None else sums + term
+def grad_normed_part(grads, w_value, other, offset, total=None, pieces=0, held=()):
+    (rows, size), width = grads.shape, w_value.shape[0]
+
+    def body(v, w, *refs):
+        start = half_start(w_value.shape[1], other, offset)
+        sums = lax.dot_general(v[...], w[:, pl.ds(start, size)], NT, preferred_element_type=F32)
+        if total is not None:
+            sums = sums + refs[0][...]
         if not pieces:
             refs[-1][...] = sums
             return
@@ -140,8 +140,8 @@
         outs = [shape((rows // pieces, width), F32)] + [shape((rows // pieces, width), BF16)] * (pieces - 1)
     else:
         outs = [shape((rows, width), F32)]
-    operands = [*grads, *weights] + ([] if total is None else [total])
-    return call(body, outs, operands, held, carry=carry)
+    operands = [grads, pltpu.with_memory_space_constraint(w_value, pltpu.VMEM)] + ([] if total is None else [total])
+    return call(body, outs, operands, held)
 
 
 def stacked(columns):
@@ -170,10 +170,11 @@
     slots = store.shape[0]
 
     def body(s, store_ref, *outs):
+        section = lax.axis_index("section")
         for k, out in enumerate(outs):
-            out[...] = store_ref[s[k]]
-
-    return call(body, [shape(store.shape[1:], BF16)] * slots, [table, store], held, SMEM)
+            out[...] = store_ref[s[k, section]]
+
+    return call(body, [shape(store.shape[1:], BF16)] * slots, [table, store], held, SMEM, light=True)
 
 
 def width_sums(keep, received, inputs, slot, held=()):
@@ -240,7 +241,7 @@
     return call(body, outs, operands, held)
 
 
-def value_grad_part(normed, grads, result, dims, other, offset):
+def value_grad_part(normed, grads, result, dims, other, offset, held=()):
     depth, width = sum(a.shape[0] for a in normed), normed[0].shape[1]
     blocks = len(normed)
     size = grads[0].shape[1]
@@ -273,8 +274,8 @@
     return pl.pallas_call(
         body,
         in_specs=[VMEM] * (blocks + count) + [ANY] * len(given),
-        out_specs=ANY,
-        out_shape=pltpu.HBM(dims, BF16),
+        out_specs=[ANY],
+        out_shape=[pltpu.HBM(dims, BF16)],
         scratch_shapes=[pltpu.VMEM((width, size), BF16), pltpu.SemaphoreType.DMA((steps,))],
         input_output_aliases={blocks + count: 0} if given else {},
         compiler_params=pltpu.CompilerParams(vmem_limit_bytes=SCOPED),
@@ -282,8 +283,8 @@
     )(*normed, *grads, *given)
 
 
-def mixing_weights(slopes, length, own, held=()):
-    heads = slopes.shape[0] // 2
+def mixing_and_weight(slopes, weight, length, own, held=()):
+    heads = slopes.shape[1] // 2
 
     def body(slopes_ref, out):
         tensor = lax.axis_index("tensor")
@@ -296,13 +297,14 @@
         distance = (place(0) - place(1)).astype(F32)
         causal = distance >= 0
         distance = jnp.where(causal, distance, 0.0)
+        lane = lax.broadcasted_iota(jnp.int32, slopes.shape, 1)
         for h in range(heads):
-            logits = -slopes_ref[pl.ds(first + h, 1), :] * distance
-            weights = jnp.where(causal, jnp.exp(logits), 0.0)
+            slope = jnp.sum(jnp.where(lane == first + h, slopes_ref[...], 0.0), axis=1, keepdims=True)
+            weights = jnp.where(causal, jnp.exp(-slope * distance), 0.0)
             out[h] = (weights / jnp.sum(weights, axis=-1, keepdims=True)).astype(BF16)
 
-    wide = jnp.broadcast_to(slopes[:, None], (slopes.shape[0], length))
-    return call(body, [shape((heads, length, length), BF16)], [wide], held)
+    carry = [(weight, False, 0, weight.shape[1])]
+    return call(body, [shape((heads, length, length), BF16)], [slopes], held, carry=carry)
 
 
 def flipped(array, axis, mask):
@@ -337,18 +339,9 @@
 
     upstream = [arriving[0]]
     pieces = [[a] for a in [upstream[0], *others_of(upstream[0])]]
-    table = lax.dynamic_index_in_dim(slot_table, lax.axis_index("section"), 0, keepdims=False)
-    mixing, = run(mixing_weights, after(slopes, table), own * tensors, own)
-    w_output, = run(
-        lambda w, held: call(None, [], [], held, carry=[(w, False, 0, w.shape[1])]), output_weight[0]
-    )
+    mixing, w_output = run(mixing_and_weight, slopes[None], output_weight[0], own * tensors, own)
     held.append(w_output)
-    w_value = [[None, None] for _ in chunks]
-
-    def spans(j, sides):
-        return [(value_weight[0], side == 1, *chunks[j]) for side in sides]
-
-    values, input_stats, result = [], None, None
+    values = []
     for slot in range(slots):
         last = slot == slots - 1
         if slot > 0:
@@ -365,12 +358,11 @@
             if j <= final:
                 halves.append(flipped(product(j, True)[0], "dp", 1))
             if j > 0:
-                bring = slot == 0 and j - 1 == final
-                outs = product(j - 1, False, halves[j - 1], spans(0, (0, 1)) if bring else ())
-                if bring:
-                    w_value[0] = outs[2:]
-                    held.extend(outs[2:])
+                outs = product(j - 1, False, halves[j - 1])
                 kept.append(outs[:2])
+                if last and j == len(chunks):
+                    normed = [after(a, outs[0]) for a in normed]
+                    blocks = [b for a in normed for b in [a, *others_of(a)]]
                 across.append([flipped(outs[1], "dp", m) for m in chips])
         if slot == 0:
             store = lax.ppermute(
@@ -382,42 +374,40 @@
             theirs.append(flipped(mine[j], "dp", 1))
             for side, grads in enumerate((mine[j], theirs[j])):
                 end = j == final and side == 1
-                bring = slot == 0 and j < final
-                outs = run(
-                    grad_normed_part, [grads], [w_value[j][side]], total, tensors if end else 0,
-                    carry=spans(j + 1, (side,)) if bring else (),
-                )
-                if bring:
-                    w_value[j + 1][side] = outs[-1]
-                    held.append(outs[-1])
+                outs = run(grad_normed_part, grads, value_weight[0], side == 1, a, total, tensors if end else 0)
                 if end:
                     keep, *sends = outs
                 else:
                     total = outs[0]
         values.append([mine, theirs])
         received = [flipped(x, "tensor", t) for t, x in zip(others, sends, strict=True)]
+        if slot == 0:
+            inputs = run(ordered, store, slot_table.T)
         if last:
             held.clear()
-        if slot == 0:
-            inputs = run(ordered, store, table)
+            result = None
+            todo = [(j, side) for j in range(len(chunks)) for side in range(2)]
+
+            def write(j, side):
+                terms = [v[side][j] for v in values]
+                return run(value_grad_part, blocks, terms, result, value_weight.shape[1:], side == 1, chunks[j][0])[0]
+
+            for piece in todo[: len(todo) * 3 // 4]:
+                result = write(*piece)
         grad, sums = run(width_sums, keep, received, inputs, slot)
         sums, = run(added, sums, flipped(sums, "dp", 1))
         grad_stats = [sums] + [flipped(sums, "dp", m) for m in chips]
+        if last:
+            for piece in todo[len(todo) * 3 // 4 :]:
+                result = write(*piece)
         if slot == 0:
             input_stats = grad_stats
-        outs = run(finish, grad, upstream, inputs, slot, input_stats, grad_stats, width, 1 if last else 2)
+        outs = run(finish, grad, upstream, inputs, slot, input_stats, grad_stats, width, 1)
         if slot == 0:
             normed = outs[-slots:]
             outs = outs[:-slots]
         upstream = outs
 
-    normed = [b for a in normed for b in [a, *others_of(a)]]
-    result = None
-    for j, (a, n) in enumerate(chunks):
-        for side in range(2):
-            result = value_grad_part(
-                normed, [v[side][j] for v in values], result, value_weight.shape[1:], side == 1, a
-            )
     return (upstream[0][None], result[None])
 
 

time: 101 us -> 91.1 us (0.902)
  Pallas kernels: 41.6 us -> 35.2 us
  starting transfers between devices: 24.5 us -> 22.9 us
  waiting for transfers between devices: 32.3 us -> 31.1 us
    pallas_call x29 -> x28, Pallas kernels: 33.4 us -> 27 us  [call(): pl.pallas_call(kernel, in_specs=([first_spec] + [VMEM] * (n_in - 1) if n_...]
    ppermute x2 -> x1, waiting for transfers between devices: 9.29 us -> 6.24 us  [on_device(): lax.ppermute(a, 'section', [(i, i - 1) for i in range(1, sections)])]
    ppermute x23 -> x22, waiting for transfers between devices: 23 us -> 24.9 us  [flipped(): lax.ppermute(array, axis, [(i, i ^ mask) for i in range(lax.axis_size(axi...]
    ppermute x2 -> x1, starting transfers between devices: 2.75 us -> 1.47 us  [on_device(): lax.ppermute(a, 'section', [(i, i - 1) for i in range(1, sections)])]
    ppermute x23 -> x22, starting transfers between devices: 18.1 us -> 17.8 us  [flipped(): lax.ppermute(array, axis, [(i, i ^ mask) for i in range(lax.axis_size(axi...]
  transfers between devices with their start and end apart: 26 -> 24, of which waited for: 10 -> 15; matrix products, arithmetic and copies ran while one was open for 1% -> 0% of each run, Pallas kernels for 37% -> 34%
where the time goes in v3:
time: 91.1 us; the launch traced here: 90.9 us
  Pallas kernels  35.2 us (39%)
  waiting for transfers between devices  31.1 us (34%)
  starting transfers between devices  22.9 us (25%)
  between operations  1.03 us (1%)
    pallas_call x28, Pallas kernels, call(): pl.pallas_call(kernel, in_specs=([first_spec] + [VMEM] * (n_in - 1) if n_...  27 us
    ppermute x22, waiting for transfers between devices, flipped(): lax.ppermute(array, axis, [(i, i ^ mask) for i in range(lax.axis_size(axi...  24.9 us
    ppermute x22, starting transfers between devices, flipped(): lax.ppermute(array, axis, [(i, i ^ mask) for i in range(lax.axis_size(axi...  17.8 us
    pallas_call x4, Pallas kernels, value_grad_part(): pl.pallas_call(body, in_specs=[VMEM] * (blocks + count) + [ANY] * len(giv...  8.13 us
    ppermute x1, waiting for transfers between devices, on_device(): lax.ppermute(a, 'section', [(i, i - 1) for i in range(1, sections)])  6.24 us
    ppermute x1, starting transfers between devices, on_device(): lax.ppermute(after(parked[0], kept[-1][1]), 'section', [(i, sections - 1...  3.59 us
  transfers between devices with their start and end apart: 24, of which 15 were waited for; matrix products, arithmetic and copies ran while one was open for 0% of the time, Pallas kernels for 34%

profile of v3, /device:TPU:0, one launch (start us, length us, event | category | flops | bytes accessed | tf_op | source)
XLA Modules:
  0.0 90.9 jit_solution(16984384640978928548)
XLA Ops:
  0.6 3.0 %collective-permute-start = (bf16[64,1536]{1,0:T(8,128)(2,1)}, bf16[64,1536]{1,0:T(8,128)(2,1)S(1)}, u32[]{:S(2)}, u32[]{:S(2)}) collective-permute-start(bf16[64,1536]{1,0:T(8,128)(2,1)} %bitcast.19), channel_id=1, source_target_pairs={{0,4},{4,0},{1,5},{5,1},{2,6},{6,2},{3,7},{7,3},{8,12},{12,8},{9,1... | collective-permute-start | bytes 589832 | tf_op jit(solution)/shard_map/ppermute | solution.py:311
  3.6 0.7 copy-done.2
  4.3 4.9 %shard_map.77 = (bf16[16,128,128]{2,1,0:T(8,128)(2,1)S(1)}, bf16[4096,1536]{1,0:T(8,128)(2,1)S(1)}) custom-call(f32[1,32]{1,0:T(1,128)S(1)} %bitcast.25, bf16[4096,1536]{1,0:T(8,128)(2,1)} %bitcast.27), custom_call_target="tpu_custom_call" | custom-call | flops 4000000000 | bytes 100000000 | tf_op jit(solution)/shard_map/pallas_call | solution.py:50
  9.2 1.2 %shard_map.78 = bf16[128,1024]{1,0:T(8,128)(2,1)S(1)} custom-call(bf16[64,1536]{1,0:T(8,128)(2,1)S(1)} %bitcast.20, bf16[64,1536]{1,0:T(8,128)(2,1)S(1)} %collective-permute-done.refs_1_, bf16[4096,1536]{1,0:T(8,128)(2,1)S(1)} %get-tuple-element.61.refs_2_.refs_3_.refs_4_.refs_8_), custom_call_target="tpu_custom_call" | custom-call | flops 4000000000 | bytes 100000000 | tf_op jit(solution)/shard_map/pallas_call | solution.py:50
  10.5 1.1 %shard_map.79 = bf16[128,1024]{1,0:T(8,128)(2,1)S(1)} custom-call(bf16[64,1536]{1,0:T(8,128)(2,1)S(1)} %bitcast.21, bf16[64,1536]{1,0:T(8,128)(2,1)S(1)} %collective-permute-done.refs_1_, bf16[4096,1536]{1,0:T(8,128)(2,1)S(1)} %get-tuple-element.61.refs_2_.refs_3_.refs_4_.refs_8_), custom_call_target="tpu_custom_call" | custom-call | flops 4000000000 | bytes 100000000 | tf_op jit(solution)/shard_map/pallas_call | solution.py:50
  11.6 0.6 collective-permute-start.2
  12.2 1.1 %shard_map.80 = (f32[128,1024]{1,0:T(8,128)S(1)}, bf16[128,1024]{1,0:T(8,128)(2,1)S(1)}) custom-call(bf16[64,1536]{1,0:T(8,128)(2,1)S(1)} %bitcast.22, bf16[64,1536]{1,0:T(8,128)(2,1)S(1)} %collective-permute-done.refs_1_, bf16[4096,1536]{1,0:T(8,128)(2,1)S(1)} %get-tuple-element.61.refs_2_.refs_3_.refs_4_.refs_8_, ...), custom_call_target="tpu_custom_call" | custom-call | flops 4000000000 | bytes 100000000 | tf_op jit(solution)/shard_map/pallas_call | solution.py:50
  13.3 1.6 %collective-permute-start.3 = (bf16[128,1024]{1,0:T(8,128)(2,1)S(1)}, bf16[128,1024]{1,0:T(8,128)(2,1)S(1)}, u32[]{:S(2)}, u32[]{:S(2)}) collective-permute-start(bf16[128,1024]{1,0:T(8,128)(2,1)S(1)} %get-tuple-element.68), channel_id=1, source_target_pairs={{0,2},{1,3},{2,0},{3,1},{4,6},{5,7},{6,4},{7,5},{8,10},{9,11},{10,... | collective-permute-start | bytes 786440 | tf_op jit(solution)/shard_map/ppermute | solution.py:311
  14.9 1.1 %shard_map.81 = (f32[128,1024]{1,0:T(8,128)S(1)}, bf16[128,1024]{1,0:T(8,128)(2,1)S(1)}) custom-call(bf16[64,1536]{1,0:T(8,128)(2,1)S(1)} %bitcast.23, bf16[64,1536]{1,0:T(8,128)(2,1)S(1)} %collective-permute-done.refs_1_, bf16[4096,1536]{1,0:T(8,128)(2,1)S(1)} %get-tuple-element.61.refs_2_.refs_3_.refs_4_.refs_8_, ...), custom_call_target="tpu_custom_call" | custom-call | flops 4000000000 | bytes 100000000 | tf_op jit(solution)/shard_map/pallas_call | solution.py:50
  16.1 0.6 collective-permute-start.5
  16.7 3.6 %collective-permute-start.7 = (bf16[2,64,1536]{2,1,0:T(8,128)(2,1)S(1)}, bf16[2,64,1536]{2,1,0:T(8,128)(2,1)S(1)}, u32[]{:S(2)}, u32[]{:S(2)}) collective-permute-start(bf16[2,64,1536]{2,1,0:T(8,128)(2,1)S(1)} %bitcast.28), channel_id=1, source_target_pairs={{0,24},{8,16},{16,8},{24,0},{1,25},{9,17},{17,9},{25,1},{2,26},{10... | collective-permute-start | bytes 1179656 | tf_op jit(solution)/shard_map/ppermute | solution.py:368
  20.2 2.3 %collective-permute-done.3.refs_1_ = bf16[128,1024]{1,0:T(8,128)(2,1)S(1)} collective-permute-done((bf16[128,1024]{1,0:T(8,128)(2,1)S(1)}, bf16[128,1024]{1,0:T(8,128)(2,1)S(1)}, u32[]{:S(2)}, u32[]{:S(2)}) %collective-permute-start.3) | collective-permute-done | bytes 262176 | tf_op jit(solution)/shard_map/ppermute | solution.py:311
  23.0 1.2 %shard_map.83.refs_2_ = f32[128,1536]{1,0:T(8,128)S(1)} custom-call(bf16[128,1024]{1,0:T(8,128)(2,1)S(1)} %shard_map.82.refs_0_.refs_4_, bf16[1536,4096]{1,0:T(8,128)(2,1)S(1)} %bitcast.10, bf16[4096,1536]{1,0:T(8,128)(2,1)S(1)} %get-tuple-element.61.refs_2_.refs_3_.refs_4_.refs_8_), custom_call_target="tpu_custom_call" | custom-call | flops 4000000000 | bytes 100000000 | tf_op jit(solution)/shard_map/pallas_call | solution.py:50
  24.4 1.2 %shard_map.84.refs_2_ = f32[128,1536]{1,0:T(8,128)S(1)} custom-call(bf16[128,1024]{1,0:T(8,128)(2,1)S(1)} %collective-permute-done.4.refs_0_.refs_4_, bf16[1536,4096]{1,0:T(8,128)(2,1)S(1)} %bitcast.11, f32[128,1536]{1,0:T(8,128)S(1)} %shard_map.83.refs_2_, bf16[4096,1536]{1,0:T(8,128)(2,1)S(1)} %get-tuple-element.61.refs_2_.refs_3_.refs_4_.refs_8_), custom_call_target="tpu_custom_call" | custom-call | flops 4000000000 | bytes 100000000 | tf_op jit(solution)/shard_map/pallas_call | solution.py:50
  25.6 1.6 %collective-permute-done.5.refs_1_ = bf16[128,1024]{1,0:T(8,128)(2,1)S(1)} collective-permute-done((bf16[128,1024]{1,0:T(8,128)(2,1)S(1)}, bf16[128,1024]{1,0:T(8,128)(2,1)S(1)}, u32[]{:S(2)}, u32[]{:S(2)}) %collective-permute-start.5) | collective-permute-done | bytes 262176 | tf_op jit(solution)/shard_map/ppermute | solution.py:311
  27.6 1.2 %shard_map.86.refs_2_ = f32[128,1536]{1,0:T(8,128)S(1)} custom-call(bf16[128,1024]{1,0:T(8,128)(2,1)S(1)} %shard_map.85.refs_0_.refs_4_, bf16[1536,4096]{1,0:T(8,128)(2,1)S(1)} %bitcast.12, f32[128,1536]{1,0:T(8,128)S(1)} %shard_map.84.refs_2_, bf16[4096,1536]{1,0:T(8,128)(2,1)S(1)} %get-tuple-element.61.refs_2_.refs_3_.refs_4_.refs_8_), custom_call_target="tpu_custom_call" | custom-call | flops 4000000000 | bytes 100000000 | tf_op jit(solution)/shard_map/pallas_call | solution.py:50
  29.1 1.2 %shard_map.87 = (f32[64,1536]{1,0:T(8,128)S(1)}, bf16[64,1536]{1,0:T(8,128)(2,1)S(1)}) custom-call(bf16[128,1024]{1,0:T(8,128)(2,1)S(1)} %collective-permute-done.6.refs_0_.refs_4_, bf16[1536,4096]{1,0:T(8,128)(2,1)S(1)} %bitcast.13, f32[128,1536]{1,0:T(8,128)S(1)} %shard_map.86.refs_2_, bf16[4096,1536]{1,0:T(8,128)(2,1)S(1)} %get-tuple-element.61.refs_2_.refs_3_.refs_4_.refs_8_), custom_call_target="tpu_custom_call" | custom-call | flops 4000000000 | bytes 100000000 | tf_op jit(solution)/shard_map/pallas_call | solution.py:50
  30.3 1.3 %collective-permute-start.8 = (bf16[64,1536]{1,0:T(8,128)(2,1)S(1)}, bf16[64,1536]{1,0:T(8,128)(2,1)S(1)}, u32[]{:S(2)}, u32[]{:S(2)}) collective-permute-start(bf16[64,1536]{1,0:T(8,128)(2,1)S(1)} %get-tuple-element.81), channel_id=1, source_target_pairs={{0,4},{4,0},{1,5},{5,1},{2,6},{6,2},{3,7},{7,3},{8,12},{12,8},{9,1... | collective-permute-start | bytes 589832 | tf_op jit(solution)/shard_map/ppermute | solution.py:311
  31.6 0.6 shard_map.88
  32.2 5.1 %collective-permute-done.8.refs_3_ = bf16[64,1536]{1,0:T(8,128)(2,1)S(1)} collective-permute-done((bf16[64,1536]{1,0:T(8,128)(2,1)S(1)}, bf16[64,1536]{1,0:T(8,128)(2,1)S(1)}, u32[]{:S(2)}, u32[]{:S(2)}) %collective-permute-start.8) | collective-permute-done | bytes 196640 | tf_op jit(solution)/shard_map/ppermute | solution.py:311
  37.7 1.2 %collective-permute-done.9.refs_1_ = f32[8,128]{1,0:T(8,128)S(1)} collective-permute-done((f32[8,128]{1,0:T(8,128)S(1)}, f32[8,128]{1,0:T(8,128)S(1)}, u32[]{:S(2)}, u32[]{:S(2)}) %collective-permute-start.9) | collective-permute-done | bytes 4128 | tf_op jit(solution)/shard_map/ppermute | solution.py:311
  38.8 1.5 %collective-permute-start.10 = (f32[8,128]{1,0:T(8,128)S(1)}, f32[8,128]{1,0:T(8,128)S(1)}, u32[]{:S(2)}, u32[]{:S(2)}) collective-permute-start(f32[8,128]{1,0:T(8,128)S(1)} %shard_map.90.refs_4_.refs_6_), channel_id=1, source_target_pairs={{0,2},{1,3},{2,0},{3,1},{4,6},{5,7},{6,4},{7,5},{8,10},{9,11},{10,... | collective-permute-start | bytes 12296 | tf_op jit(solution)/shard_map/ppermute | solution.py:311
  40.3 2.1 %collective-permute-done.10.refs_5_.refs_7_ = f32[8,128]{1,0:T(8,128)S(1)} collective-permute-done((f32[8,128]{1,0:T(8,128)S(1)}, f32[8,128]{1,0:T(8,128)S(1)}, u32[]{:S(2)}, u32[]{:S(2)}) %collective-permute-start.10) | collective-permute-done | bytes 4128 | tf_op jit(solution)/shard_map/ppermute | solution.py:311
  42.9 1.5 %collective-permute-start.11 = (bf16[64,1536]{1,0:T(8,128)(2,1)S(1)}, bf16[64,1536]{1,0:T(8,128)(2,1)S(1)}, u32[]{:S(2)}, u32[]{:S(2)}) collective-permute-start(bf16[64,1536]{1,0:T(8,128)(2,1)S(1)} %get-tuple-element.86), channel_id=1, source_target_pairs={{8,0},{16,8},{24,16},{9,1},{17,9},{25,17},{10,2},{18,10},{26,18},{... | collective-permute-start | bytes 589832 | tf_op jit(solution)/shard_map/ppermute | solution.py:348
  44.4 6.2 %collective-permute-done.11.refs_0_.refs_3_ = bf16[64,1536]{1,0:T(8,128)(2,1)S(1)} collective-permute-done((bf16[64,1536]{1,0:T(8,128)(2,1)S(1)}, bf16[64,1536]{1,0:T(8,128)(2,1)S(1)}, u32[]{:S(2)}, u32[]{:S(2)}) %collective-permute-start.11) | collective-permute-done | bytes 196640 | tf_op jit(solution)/shard_map/ppermute | solution.py:348
  50.6 1.3 %collective-permute-start.12 = (bf16[64,1536]{1,0:T(8,128)(2,1)S(1)}, bf16[64,1536]{1,0:T(8,128)(2,1)S(1)}, u32[]{:S(2)}, u32[]{:S(2)}) collective-permute-start(bf16[64,1536]{1,0:T(8,128)(2,1)S(1)} %collective-permute-done.11.refs_0_.refs_3_), channel_id=1, source_target_pairs={{0,4},{4,0},{1,5},{5,1},{2,6},{6,2},{3,7},{7,3},{8,12},{12,8},{9,1... | collective-permute-start | bytes 589832 | tf_op jit(solution)/shard_map/ppermute | solution.py:311
  51.9 4.4 %collective-permute-done.12.refs_1_ = bf16[64,1536]{1,0:T(8,128)(2,1)S(1)} collective-permute-done((bf16[64,1536]{1,0:T(8,128)(2,1)S(1)}, bf16[64,1536]{1,0:T(8,128)(2,1)S(1)}, u32[]{:S(2)}, u32[]{:S(2)}) %collective-permute-start.12) | collective-permute-done | bytes 196640 | tf_op jit(solution)/shard_map/ppermute | solution.py:311
  56.3 1.1 %shard_map.92 = bf16[128,1024]{1,0:T(8,128)(2,1)S(1)} custom-call(bf16[64,1536]{1,0:T(8,128)(2,1)S(1)} %collective-permute-done.11.refs_0_.refs_3_, bf16[64,1536]{1,0:T(8,128)(2,1)S(1)} %collective-permute-done.12.refs_1_, bf16[4096,1536]{1,0:T(8,128)(2,1)S(1)} %get-tuple-element.61.refs_2_.refs_3_.refs_4_.refs_8_), custom_call_target="tpu_custom_call" | custom-call | flops 4000000000 | bytes 100000000 | tf_op jit(solution)/shard_map/pallas_call | solution.py:50
  57.5 1.1 %shard_map.93 = bf16[128,1024]{1,0:T(8,128)(2,1)S(1)} custom-call(bf16[64,1536]{1,0:T(8,128)(2,1)S(1)} %collective-permute-done.11.refs_0_.refs_3_, bf16[64,1536]{1,0:T(8,128)(2,1)S(1)} %collective-permute-done.12.refs_1_, bf16[4096,1536]{1,0:T(8,128)(2,1)S(1)} %get-tuple-element.61.refs_2_.refs_3_.refs_4_.refs_8_), custom_call_target="tpu_custom_call" | custom-call | flops 4000000000 | bytes 100000000 | tf_op jit(solution)/shard_map/pallas_call | solution.py:50
  59.2 1.1 %shard_map.94 = (f32[128,1024]{1,0:T(8,128)S(1)}, bf16[128,1024]{1,0:T(8,128)(2,1)S(1)}) custom-call(bf16[64,1536]{1,0:T(8,128)(2,1)S(1)} %collective-permute-done.11.refs_0_.refs_3_, bf16[64,1536]{1,0:T(8,128)(2,1)S(1)} %collective-permute-done.12.refs_1_, bf16[4096,1536]{1,0:T(8,128)(2,1)S(1)} %get-tuple-element.61.refs_2_.refs_3_.refs_4_.refs_8_, ...), custom_call_target="tpu_custom_call" | custom-call | flops 4000000000 | bytes 100000000 | tf_op jit(solution)/shard_map/pallas_call | solution.py:50
  60.4 1.6 %collective-permute-start.15 = (bf16[128,1024]{1,0:T(8,128)(2,1)S(1)}, bf16[128,1024]{1,0:T(8,128)(2,1)S(1)}, u32[]{:S(2)}, u32[]{:S(2)}) collective-permute-start(bf16[128,1024]{1,0:T(8,128)(2,1)S(1)} %get-tuple-element.94), channel_id=1, source_target_pairs={{0,2},{1,3},{2,0},{3,1},{4,6},{5,7},{6,4},{7,5},{8,10},{9,11},{10,... | collective-permute-start | bytes 786440 | tf_op jit(solution)/shard_map/ppermute | solution.py:311
  62.0 1.1 %shard_map.95 = (f32[128,1024]{1,0:T(8,128)S(1)}, bf16[128,1024]{1,0:T(8,128)(2,1)S(1)}) custom-call(bf16[64,1536]{1,0:T(8,128)(2,1)S(1)} %collective-permute-done.11.refs_0_.refs_3_, bf16[64,1536]{1,0:T(8,128)(2,1)S(1)} %collective-permute-done.12.refs_1_, bf16[4096,1536]{1,0:T(8,128)(2,1)S(1)} %get-tuple-element.61.refs_2_.refs_3_.refs_4_.refs_8_, ...), custom_call_target="tpu_custom_call" | custom-call | flops 4000000000 | bytes 100000000 | tf_op jit(solution)/shard_map/pallas_call | solution.py:50
  63.1 1.3 %collective-permute-start.19 = (bf16[64,1536]{1,0:T(8,128)(2,1)S(1)}, bf16[64,1536]{1,0:T(8,128)(2,1)S(1)}, u32[]{:S(2)}, u32[]{:S(2)}) collective-permute-start(bf16[64,1536]{1,0:T(8,128)(2,1)S(1)} %get-tuple-element.114.refs_0_), channel_id=1, source_target_pairs={{0,4},{4,0},{1,5},{5,1},{2,6},{6,2},{3,7},{7,3},{8,12},{12,8},{9,1... | collective-permute-start | bytes 589832 | tf_op jit(solution)/shard_map/ppermute | solution.py:311
  64.4 0.8 collective-permute-start.20
  65.7 3.9 %collective-permute-done.15.refs_1_ = bf16[128,1024]{1,0:T(8,128)(2,1)S(1)} collective-permute-done((bf16[128,1024]{1,0:T(8,128)(2,1)S(1)}, bf16[128,1024]{1,0:T(8,128)(2,1)S(1)}, u32[]{:S(2)}, u32[]{:S(2)}) %collective-permute-start.15) | collective-permute-done | bytes 262176 | tf_op jit(solution)/shard_map/ppermute | solution.py:311
  70.0 1.2 %shard_map.97.refs_2_ = f32[128,1536]{1,0:T(8,128)S(1)} custom-call(bf16[128,1024]{1,0:T(8,128)(2,1)S(1)} %shard_map.96.refs_0_.refs_5_, bf16[1536,4096]{1,0:T(8,128)(2,1)S(1)} %bitcast.14, bf16[4096,1536]{1,0:T(8,128)(2,1)S(1)} %get-tuple-element.61.refs_2_.refs_3_.refs_4_.refs_8_), custom_call_target="tpu_custom_call" | custom-call | flops 4000000000 | bytes 100000000 | tf_op jit(solution)/shard_map/pallas_call | solution.py:50
  71.5 1.2 %shard_map.98.refs_2_ = f32[128,1536]{1,0:T(8,128)S(1)} custom-call(bf16[128,1024]{1,0:T(8,128)(2,1)S(1)} %collective-permute-done.16.refs_0_.refs_5_, bf16[1536,4096]{1,0:T(8,128)(2,1)S(1)} %bitcast.15, f32[128,1536]{1,0:T(8,128)S(1)} %shard_map.97.refs_2_, bf16[4096,1536]{1,0:T(8,128)(2,1)S(1)} %get-tuple-element.61.refs_2_.refs_3_.refs_4_.refs_8_), custom_call_target="tpu_custom_call" | custom-call | flops 4000000000 | bytes 100000000 | tf_op jit(solution)/shard_map/pallas_call | solution.py:50
  72.7 1.7 %collective-permute-done.17.refs_1_ = bf16[128,1024]{1,0:T(8,128)(2,1)S(1)} collective-permute-done((bf16[128,1024]{1,0:T(8,128)(2,1)S(1)}, bf16[128,1024]{1,0:T(8,128)(2,1)S(1)}, u32[]{:S(2)}, u32[]{:S(2)}) %collective-permute-start.17) | collective-permute-done | bytes 262176 | tf_op jit(solution)/shard_map/ppermute | solution.py:311
  74.7 1.2 %shard_map.100.refs_2_ = f32[128,1536]{1,0:T(8,128)S(1)} custom-call(bf16[128,1024]{1,0:T(8,128)(2,1)S(1)} %shard_map.99.refs_0_.refs_5_, bf16[1536,4096]{1,0:T(8,128)(2,1)S(1)} %bitcast.16, f32[128,1536]{1,0:T(8,128)S(1)} %shard_map.98.refs_2_, bf16[4096,1536]{1,0:T(8,128)(2,1)S(1)} %get-tuple-element.61.refs_2_.refs_3_.refs_4_.refs_8_), custom_call_target="tpu_custom_call" | custom-call | flops 4000000000 | bytes 100000000 | tf_op jit(solution)/shard_map/pallas_call | solution.py:50
  76.2 1.2 %shard_map.101 = (f32[64,1536]{1,0:T(8,128)S(1)}, bf16[64,1536]{1,0:T(8,128)(2,1)S(1)}) custom-call(bf16[128,1024]{1,0:T(8,128)(2,1)S(1)} %collective-permute-done.18.refs_0_.refs_5_, bf16[1536,4096]{1,0:T(8,128)(2,1)S(1)} %bitcast.17, f32[128,1536]{1,0:T(8,128)S(1)} %shard_map.100.refs_2_, ...), custom_call_target="tpu_custom_call" | custom-call | flops 4000000000 | bytes 100000000 | tf_op jit(solution)/shard_map/pallas_call | solution.py:50
  77.3 1.3 %collective-permute-start.21 = (bf16[64,1536]{1,0:T(8,128)(2,1)S(1)}, bf16[64,1536]{1,0:T(8,128)(2,1)S(1)}, u32[]{:S(2)}, u32[]{:S(2)}) collective-permute-start(bf16[64,1536]{1,0:T(8,128)(2,1)S(1)} %get-tuple-element.110), channel_id=1, source_target_pairs={{0,4},{4,0},{1,5},{5,1},{2,6},{6,2},{3,7},{7,3},{8,12},{12,8},{9,1... | collective-permute-start | bytes 589832 | tf_op jit(solution)/shard_map/ppermute | solution.py:311
  78.7 2.0 %shard_map.102.refs_6_ = bf16[1536,4096]{1,0:T(8,128)(2,1)} custom-call(bf16[64,1536]{1,0:T(8,128)(2,1)S(1)} %get-tuple-element.114.refs_0_, bf16[64,1536]{1,0:T(8,128)(2,1)S(1)} %collective-permute-done.19.refs_1_, bf16[64,1536]{1,0:T(8,128)(2,1)S(1)} %get-tuple-element.106.refs_2_, bf16[64,1536]{1,0:T(8,128)(2,1)S(1)} %collective-permute-done.20.refs_3_, ...), custom_call_target="tpu_custom_call" | custom-call | flops 4000000000 | bytes 100000000 | tf_op jit(solution)/shard_map/pallas_call | solution.py:274
  80.7 2.0 %shard_map.103.refs_6_ = bf16[1536,4096]{1,0:T(8,128)(2,1)} custom-call(bf16[64,1536]{1,0:T(8,128)(2,1)S(1)} %get-tuple-element.114.refs_0_, bf16[64,1536]{1,0:T(8,128)(2,1)S(1)} %collective-permute-done.19.refs_1_, bf16[64,1536]{1,0:T(8,128)(2,1)S(1)} %get-tuple-element.106.refs_2_, ...), custom_call_target="tpu_custom_call", output_to_operand_aliasing={{}: (6, {})} | custom-call | flops 4000000000 | bytes 100000000 | tf_op jit(solution)/shard_map/pallas_call | solution.py:274
  82.8 2.0 %shard_map.104.refs_6_ = bf16[1536,4096]{1,0:T(8,128)(2,1)} custom-call(bf16[64,1536]{1,0:T(8,128)(2,1)S(1)} %get-tuple-element.114.refs_0_, bf16[64,1536]{1,0:T(8,128)(2,1)S(1)} %collective-permute-done.19.refs_1_, bf16[64,1536]{1,0:T(8,128)(2,1)S(1)} %get-tuple-element.106.refs_2_, ...), custom_call_target="tpu_custom_call", output_to_operand_aliasing={{}: (6, {})} | custom-call | flops 4000000000 | bytes 100000000 | tf_op jit(solution)/shard_map/pallas_call | solution.py:274
  85.0 1.2 %collective-permute-done.22.refs_1_ = f32[8,128]{1,0:T(8,128)S(1)} collective-permute-done((f32[8,128]{1,0:T(8,128)S(1)}, f32[8,128]{1,0:T(8,128)S(1)}, u32[]{:S(2)}, u32[]{:S(2)}) %collective-permute-start.22) | collective-permute-done | bytes 4128 | tf_op jit(solution)/shard_map/ppermute | solution.py:311
  86.2 1.5 %collective-permute-start.23 = (f32[8,128]{1,0:T(8,128)S(1)}, f32[8,128]{1,0:T(8,128)S(1)}, u32[]{:S(2)}, u32[]{:S(2)}) collective-permute-start(f32[8,128]{1,0:T(8,128)S(1)} %shard_map.106.refs_6_), channel_id=1, source_target_pairs={{0,2},{1,3},{2,0},{3,1},{4,6},{5,7},{6,4},{7,5},{8,10},{9,11},{10,... | collective-permute-start | bytes 12296 | tf_op jit(solution)/shard_map/ppermute | solution.py:311
  87.7 2.0 %shard_map.107 = bf16[1536,4096]{1,0:T(8,128)(2,1)} custom-call(bf16[64,1536]{1,0:T(8,128)(2,1)S(1)} %get-tuple-element.114.refs_0_, bf16[64,1536]{1,0:T(8,128)(2,1)S(1)} %collective-permute-done.19.refs_1_, bf16[64,1536]{1,0:T(8,128)(2,1)S(1)} %get-tuple-element.106.refs_2_, ...), custom_call_target="tpu_custom_call", output_to_operand_aliasing={{}: (6, {})} | custom-call | flops 4000000000 | bytes 100000000 | tf_op jit(solution)/shard_map/pallas_call | solution.py:274
  89.8 1.1 %shard_map.108 = bf16[64,1536]{1,0:T(8,128)(2,1)} custom-call(f32[64,1536]{1,0:T(8,128)S(1)} %get-tuple-element.115.refs_0_, bf16[64,1536]{1,0:T(8,128)(2,1)S(1)} %get-tuple-element.78.refs_1_, bf16[64,1536]{1,0:T(8,128)(2,1)S(1)} %get-tuple-element.80.refs_2_, bf16[64,1536]{1,0:T(8,128)(2,1)S(1)} %collective-permute-done.11.refs_0_.refs_3_, ...), custom_call_target="tpu_custom_call" | custom-call | flops 4000000000 | bytes 100000000 | tf_op jit(solution)/shard_map/pallas_call | solution.py:50
  (47 shorter events, 5.0 us)
Async XLA Ops:
  0.6 8.6 %copy-start.1 = (bf16[1,64,1536]{2,1,0:T(8,128)(2,1)S(1)}, bf16[1,64,1536]{2,1,0:T(8,128)(2,1)}, u32[]{:S(2)}) copy-start(bf16[1,64,1536]{2,1,0:T(8,128)(2,1)} %param.7) | copy-start | bytes 589828
  0.6 8.6 %collective-permute-start = (bf16[64,1536]{1,0:T(8,128)(2,1)}, bf16[64,1536]{1,0:T(8,128)(2,1)S(1)}, u32[]{:S(2)}, u32[]{:S(2)}) collective-permute-start(bf16[64,1536]{1,0:T(8,128)(2,1)} %bitcast.19), channel_id=1, source_target_pairs={{0,4},{4,0},{1,5},{5,1},{2,6},{6,2},{3,7},{7,3},{8,12},{12,8},{9,1... | collective-permute-start | bytes 589832 | tf_op jit(solution)/shard_map/ppermute | solution.py:311
  3.6 0.7 copy-start.2
  10.4 1.8 %collective-permute-start.1 = (bf16[128,1024]{1,0:T(8,128)(2,1)S(1)}, bf16[128,1024]{1,0:T(8,128)(2,1)S(1)}, u32[]{:S(2)}, u32[]{:S(2)}) collective-permute-start(bf16[128,1024]{1,0:T(8,128)(2,1)S(1)} %shard_map.78), channel_id=1, source_target_pairs={{0,1},{1,0},{2,3},{3,2},{4,5},{5,4},{6,7},{7,6},{8,9},{9,8},{10,11... | collective-permute-start | bytes 786440 | tf_op jit(solution)/shard_map/ppermute | solution.py:311
  11.6 5.0 %copy-start.3 = (bf16[1,2,64,1536]{3,2,1,0:T(8,128)(2,1)S(1)}, bf16[1,2,64,1536]{3,2,1,0:T(8,128)(2,1)}, u32[]{:S(2)}) copy-start(bf16[1,2,64,1536]{3,2,1,0:T(8,128)(2,1)} %param.6) | copy-start | bytes 1179652
  11.6 3.3 %collective-permute-start.2 = (bf16[128,1024]{1,0:T(8,128)(2,1)S(1)}, bf16[128,1024]{1,0:T(8,128)(2,1)S(1)}, u32[]{:S(2)}, u32[]{:S(2)}) collective-permute-start(bf16[128,1024]{1,0:T(8,128)(2,1)S(1)} %shard_map.79), channel_id=1, source_target_pairs={{0,1},{1,0},{2,3},{3,2},{4,5},{5,4},{6,7},{7,6},{8,9},{9,8},{10,11... | collective-permute-start | bytes 786440 | tf_op jit(solution)/shard_map/ppermute | solution.py:311
  13.3 9.6 %slice-start = ((s8[12582912]{0:T(1024)(128)(4,1)}), s8[4194304]{0:T(1024)(128)(4,1)S(1)}, s32[]{:S(2)}) async-start(s8[12582912]{0:T(1024)(128)(4,1)} %bitcast.8), calls=%async_computation | async-start | bytes 8388608
  13.3 9.6 %slice-start.1 = ((s8[12582912]{0:T(1024)(128)(4,1)}), s8[4194304]{0:T(1024)(128)(4,1)S(1)}, s32[]{:S(2)}) async-start(s8[12582912]{0:T(1024)(128)(4,1)} %bitcast.8), calls=%async_computation.1 | async-start | bytes 8388608
  13.3 9.2 %collective-permute-start.3 = (bf16[128,1024]{1,0:T(8,128)(2,1)S(1)}, bf16[128,1024]{1,0:T(8,128)(2,1)S(1)}, u32[]{:S(2)}, u32[]{:S(2)}) collective-permute-start(bf16[128,1024]{1,0:T(8,128)(2,1)S(1)} %get-tuple-element.68), channel_id=1, source_target_pairs={{0,2},{1,3},{2,0},{3,1},{4,6},{5,7},{6,4},{7,5},{8,10},{9,11},{10,... | collective-permute-start | bytes 786440 | tf_op jit(solution)/shard_map/ppermute | solution.py:311
  16.1 11.2 %collective-permute-start.5 = (bf16[128,1024]{1,0:T(8,128)(2,1)S(1)}, bf16[128,1024]{1,0:T(8,128)(2,1)S(1)}, u32[]{:S(2)}, u32[]{:S(2)}) collective-permute-start(bf16[128,1024]{1,0:T(8,128)(2,1)S(1)} %get-tuple-element.72), channel_id=1, source_target_pairs={{0,2},{1,3},{2,0},{3,1},{4,6},{5,7},{6,4},{7,5},{8,10},{9,11},{10,... | collective-permute-start | bytes 786440 | tf_op jit(solution)/shard_map/ppermute | solution.py:311
  16.7 6.3 %slice-start.2 = ((s8[12582912]{0:T(1024)(128)(4,1)}), s8[4194304]{0:T(1024)(128)(4,1)S(1)}, s32[]{:S(2)}) async-start(s8[12582912]{0:T(1024)(128)(4,1)} %bitcast.8), calls=%async_computation.2 | async-start | bytes 8388608
  16.7 15.0 %collective-permute-start.7 = (bf16[2,64,1536]{2,1,0:T(8,128)(2,1)S(1)}, bf16[2,64,1536]{2,1,0:T(8,128)(2,1)S(1)}, u32[]{:S(2)}, u32[]{:S(2)}) collective-permute-start(bf16[2,64,1536]{2,1,0:T(8,128)(2,1)S(1)} %bitcast.28), channel_id=1, source_target_pairs={{0,24},{8,16},{16,8},{24,0},{1,25},{9,17},{17,9},{25,1},{2,26},{10... | collective-permute-start | bytes 1179656 | tf_op jit(solution)/shard_map/ppermute | solution.py:368
  22.8 1.6 %collective-permute-start.4 = (bf16[128,1024]{1,0:T(8,128)(2,1)S(1)}, bf16[128,1024]{1,0:T(8,128)(2,1)S(1)}, u32[]{:S(2)}, u32[]{:S(2)}) collective-permute-start(bf16[128,1024]{1,0:T(8,128)(2,1)S(1)} %shard_map.82.refs_0_.refs_4_), channel_id=1, source_target_pairs={{0,1},{1,0},{2,3},{3,2},{4,5},{5,4},{6,7},{7,6},{8,9},{9,8},{10,11... | collective-permute-start | bytes 786440 | tf_op jit(solution)/shard_map/ppermute | solution.py:311
  27.5 1.6 %collective-permute-start.6 = (bf16[128,1024]{1,0:T(8,128)(2,1)S(1)}, bf16[128,1024]{1,0:T(8,128)(2,1)S(1)}, u32[]{:S(2)}, u32[]{:S(2)}) collective-permute-start(bf16[128,1024]{1,0:T(8,128)(2,1)S(1)} %shard_map.85.refs_0_.refs_4_), channel_id=1, source_target_pairs={{0,1},{1,0},{2,3},{3,2},{4,5},{5,4},{6,7},{7,6},{8,9},{9,8},{10,11... | collective-permute-start | bytes 786440 | tf_op jit(solution)/shard_map/ppermute | solution.py:311
  28.8 2.8 %copy-start = (s32[4,2]{0,1:T(2,128)S(1)}, s32[4,2]{0,1:T(2,128)}, u32[]{:S(2)}) copy-start(s32[4,2]{0,1:T(2,128)} %param.8) | copy-start | bytes 100
  30.3 7.1 %collective-permute-start.8 = (bf16[64,1536]{1,0:T(8,128)(2,1)S(1)}, bf16[64,1536]{1,0:T(8,128)(2,1)S(1)}, u32[]{:S(2)}, u32[]{:S(2)}) collective-permute-start(bf16[64,1536]{1,0:T(8,128)(2,1)S(1)} %get-tuple-element.81), channel_id=1, source_target_pairs={{0,4},{4,0},{1,5},{5,1},{2,6},{6,2},{3,7},{7,3},{8,12},{12,8},{9,1... | collective-permute-start | bytes 589832 | tf_op jit(solution)/shard_map/ppermute | solution.py:311
  37.7 1.2 %collective-permute-start.9 = (f32[8,128]{1,0:T(8,128)S(1)}, f32[8,128]{1,0:T(8,128)S(1)}, u32[]{:S(2)}, u32[]{:S(2)}) collective-permute-start(f32[8,128]{1,0:T(8,128)S(1)} %get-tuple-element.84.refs_0_), channel_id=1, source_target_pairs={{0,1},{1,0},{2,3},{3,2},{4,5},{5,4},{6,7},{7,6},{8,9},{9,8},{10,11... | collective-permute-start | bytes 12296 | tf_op jit(solution)/shard_map/ppermute | solution.py:311
  38.8 3.6 %collective-permute-start.10 = (f32[8,128]{1,0:T(8,128)S(1)}, f32[8,128]{1,0:T(8,128)S(1)}, u32[]{:S(2)}, u32[]{:S(2)}) collective-permute-start(f32[8,128]{1,0:T(8,128)S(1)} %shard_map.90.refs_4_.refs_6_), channel_id=1, source_target_pairs={{0,2},{1,3},{2,0},{3,1},{4,6},{5,7},{6,4},{7,5},{8,10},{9,11},{10,... | collective-permute-start | bytes 12296 | tf_op jit(solution)/shard_map/ppermute | solution.py:311
  42.9 7.7 %collective-permute-start.11 = (bf16[64,1536]{1,0:T(8,128)(2,1)S(1)}, bf16[64,1536]{1,0:T(8,128)(2,1)S(1)}, u32[]{:S(2)}, u32[]{:S(2)}) collective-permute-start(bf16[64,1536]{1,0:T(8,128)(2,1)S(1)} %get-tuple-element.86), channel_id=1, source_target_pairs={{8,0},{16,8},{24,16},{9,1},{17,9},{25,17},{10,2},{18,10},{26,18},{... | collective-permute-start | bytes 589832 | tf_op jit(solution)/shard_map/ppermute | solution.py:348
  50.6 5.7 %collective-permute-start.12 = (bf16[64,1536]{1,0:T(8,128)(2,1)S(1)}, bf16[64,1536]{1,0:T(8,128)(2,1)S(1)}, u32[]{:S(2)}, u32[]{:S(2)}) collective-permute-start(bf16[64,1536]{1,0:T(8,128)(2,1)S(1)} %collective-permute-done.11.refs_0_.refs_3_), channel_id=1, source_target_pairs={{0,4},{4,0},{1,5},{5,1},{2,6},{6,2},{3,7},{7,3},{8,12},{12,8},{9,1... | collective-permute-start | bytes 589832 | tf_op jit(solution)/shard_map/ppermute | solution.py:311
  57.4 1.8 %collective-permute-start.13 = (bf16[128,1024]{1,0:T(8,128)(2,1)S(1)}, bf16[128,1024]{1,0:T(8,128)(2,1)S(1)}, u32[]{:S(2)}, u32[]{:S(2)}) collective-permute-start(bf16[128,1024]{1,0:T(8,128)(2,1)S(1)} %shard_map.92), channel_id=1, source_target_pairs={{0,1},{1,0},{2,3},{3,2},{4,5},{5,4},{6,7},{7,6},{8,9},{9,8},{10,11... | collective-permute-start | bytes 786440 | tf_op jit(solution)/shard_map/ppermute | solution.py:311
  58.7 3.3 %collective-permute-start.14 = (bf16[128,1024]{1,0:T(8,128)(2,1)S(1)}, bf16[128,1024]{1,0:T(8,128)(2,1)S(1)}, u32[]{:S(2)}, u32[]{:S(2)}) collective-permute-start(bf16[128,1024]{1,0:T(8,128)(2,1)S(1)} %shard_map.93), channel_id=1, source_target_pairs={{0,1},{1,0},{2,3},{3,2},{4,5},{5,4},{6,7},{7,6},{8,9},{9,8},{10,11... | collective-permute-start | bytes 786440 | tf_op jit(solution)/shard_map/ppermute | solution.py:311
  60.4 9.2 %collective-permute-start.15 = (bf16[128,1024]{1,0:T(8,128)(2,1)S(1)}, bf16[128,1024]{1,0:T(8,128)(2,1)S(1)}, u32[]{:S(2)}, u32[]{:S(2)}) collective-permute-start(bf16[128,1024]{1,0:T(8,128)(2,1)S(1)} %get-tuple-element.94), channel_id=1, source_target_pairs={{0,2},{1,3},{2,0},{3,1},{4,6},{5,7},{6,4},{7,5},{8,10},{9,11},{10,... | collective-permute-start | bytes 786440 | tf_op jit(solution)/shard_map/ppermute | solution.py:311
  63.1 15.6 %collective-permute-start.19 = (bf16[64,1536]{1,0:T(8,128)(2,1)S(1)}, bf16[64,1536]{1,0:T(8,128)(2,1)S(1)}, u32[]{:S(2)}, u32[]{:S(2)}) collective-permute-start(bf16[64,1536]{1,0:T(8,128)(2,1)S(1)} %get-tuple-element.114.refs_0_), channel_id=1, source_target_pairs={{0,4},{4,0},{1,5},{5,1},{2,6},{6,2},{3,7},{7,3},{8,12},{12,8},{9,1... | collective-permute-start | bytes 589832 | tf_op jit(solution)/shard_map/ppermute | solution.py:311
  64.4 14.2 %collective-permute-start.20 = (bf16[64,1536]{1,0:T(8,128)(2,1)S(1)}, bf16[64,1536]{1,0:T(8,128)(2,1)S(1)}, u32[]{:S(2)}, u32[]{:S(2)}) collective-permute-start(bf16[64,1536]{1,0:T(8,128)(2,1)S(1)} %get-tuple-element.106.refs_2_), channel_id=1, source_target_pairs={{0,4},{4,0},{1,5},{5,1},{2,6},{6,2},{3,7},{7,3},{8,12},{12,8},{9,1... | collective-permute-start | bytes 589832 | tf_op jit(solution)/shard_map/ppermute | solution.py:311
  65.2 9.1 %collective-permute-start.17 = (bf16[128,1024]{1,0:T(8,128)(2,1)S(1)}, bf16[128,1024]{1,0:T(8,128)(2,1)S(1)}, u32[]{:S(2)}, u32[]{:S(2)}) collective-permute-start(bf16[128,1024]{1,0:T(8,128)(2,1)S(1)} %get-tuple-element.98), channel_id=1, source_target_pairs={{0,2},{1,3},{2,0},{3,1},{4,6},{5,7},{6,4},{7,5},{8,10},{9,11},{10,... | collective-permute-start | bytes 786440 | tf_op jit(solution)/shard_map/ppermute | solution.py:311
  69.9 1.6 %collective-permute-start.16 = (bf16[128,1024]{1,0:T(8,128)(2,1)S(1)}, bf16[128,1024]{1,0:T(8,128)(2,1)S(1)}, u32[]{:S(2)}, u32[]{:S(2)}) collective-permute-start(bf16[128,1024]{1,0:T(8,128)(2,1)S(1)} %shard_map.96.refs_0_.refs_5_), channel_id=1, source_target_pairs={{0,1},{1,0},{2,3},{3,2},{4,5},{5,4},{6,7},{7,6},{8,9},{9,8},{10,11... | collective-permute-start | bytes 786440 | tf_op jit(solution)/shard_map/ppermute | solution.py:311
  74.6 1.6 %collective-permute-start.18 = (bf16[128,1024]{1,0:T(8,128)(2,1)S(1)}, bf16[128,1024]{1,0:T(8,128)(2,1)S(1)}, u32[]{:S(2)}, u32[]{:S(2)}) collective-permute-start(bf16[128,1024]{1,0:T(8,128)(2,1)S(1)} %shard_map.99.refs_0_.refs_5_), channel_id=1, source_target_pairs={{0,1},{1,0},{2,3},{3,2},{4,5},{5,4},{6,7},{7,6},{8,9},{9,8},{10,11... | collective-permute-start | bytes 786440 | tf_op jit(solution)/shard_map/ppermute | solution.py:311
  77.3 7.5 %collective-permute-start.21 = (bf16[64,1536]{1,0:T(8,128)(2,1)S(1)}, bf16[64,1536]{1,0:T(8,128)(2,1)S(1)}, u32[]{:S(2)}, u32[]{:S(2)}) collective-permute-start(bf16[64,1536]{1,0:T(8,128)(2,1)S(1)} %get-tuple-element.110), channel_id=1, source_target_pairs={{0,4},{4,0},{1,5},{5,1},{2,6},{6,2},{3,7},{7,3},{8,12},{12,8},{9,1... | collective-permute-start | bytes 589832 | tf_op jit(solution)/shard_map/ppermute | solution.py:311
  85.0 1.2 %collective-permute-start.22 = (f32[8,128]{1,0:T(8,128)S(1)}, f32[8,128]{1,0:T(8,128)S(1)}, u32[]{:S(2)}, u32[]{:S(2)}) collective-permute-start(f32[8,128]{1,0:T(8,128)S(1)} %get-tuple-element.113.refs_0_), channel_id=1, source_target_pairs={{0,1},{1,0},{2,3},{3,2},{4,5},{5,4},{6,7},{7,6},{8,9},{9,8},{10,11... | collective-permute-start | bytes 12296 | tf_op jit(solution)/shard_map/ppermute | solution.py:311
  86.2 3.6 %collective-permute-start.23 = (f32[8,128]{1,0:T(8,128)S(1)}, f32[8,128]{1,0:T(8,128)S(1)}, u32[]{:S(2)}, u32[]{:S(2)}) collective-permute-start(f32[8,128]{1,0:T(8,128)S(1)} %shard_map.106.refs_6_), channel_id=1, source_target_pairs={{0,2},{1,3},{2,0},{3,1},{4,6},{5,7},{6,4},{7,5},{8,10},{9,11},{10,... | collective-permute-start | bytes 12296 | tf_op jit(solution)/shard_map/ppermute | solution.py:311

commit v4 on v3

--- a/solution.py
+++ b/solution.py
@@ -14,50 +14,19 @@
 VMEM = pl.BlockSpec(memory_space=pltpu.VMEM)
 ANY = pl.BlockSpec(memory_space=pl.ANY)
 HEAD = 128
-STEPS = 8
-COST = pl.CostEstimate(flops=4 * 10**9, bytes_accessed=10**8, transcendentals=0)
+COST = pl.CostEstimate(flops=8 * 10**9, bytes_accessed=10**8, transcendentals=0)
 LIGHT = pl.CostEstimate(flops=1, bytes_accessed=1, transcendentals=0)
 
 
-def call(body, outs, operands, held=(), first_spec=VMEM, carry=(), light=False):
-    operands = list(operands)
-    held = [h for h in held if not any(h is a for a in operands)]
-    n_in, n_held, n_out, n_carry = len(operands), len(held), len(outs), len(carry)
-    sources = [pltpu.with_memory_space_constraint(w, pltpu.HBM) for w, _, _, _ in carry]
-    rows = carry[0][0].shape[0] if carry else 0
-    block = rows // STEPS
-
-    def kernel(*refs):
-        ins, refs = refs[:n_in], refs[n_in + n_held :]
-        weights, refs = refs[:n_carry], refs[n_carry:]
-        made, refs = refs[:n_out], refs[n_out:]
-        copies = []
-        for k, (w, (_, other, offset, size)) in enumerate(zip(weights, carry, strict=True)):
-            columns = w.shape[1]
-            start = 0 if size == columns else half_start(columns, other, offset)
-            for i in range(STEPS):
-                part = pl.ds(i * block, block)
-                source = w.at[part] if size == columns else w.at[part, pl.ds(start, size)]
-                copies.append(pltpu.make_async_copy(source, refs[k].at[part], refs[n_carry].at[k, i]))
-        for copy in copies:
-            copy.start()
-        if body is not None:
-            body(*ins, *made)
-        for copy in copies:
-            copy.wait()
-
-    more = [pltpu.VMEM((rows, size), w.dtype) for w, _, _, size in carry]
+def call(body, outs, operands, first_spec=VMEM, light=False):
     return pl.pallas_call(
-        kernel,
-        in_specs=([first_spec] + [VMEM] * (n_in - 1) if n_in else [])
-        + [VMEM] * n_held
-        + [pl.BlockSpec(memory_space=pltpu.HBM)] * n_carry,
-        out_specs=[VMEM] * (n_out + n_carry),
-        out_shape=[*outs, *more],
-        scratch_shapes=[pltpu.SemaphoreType.DMA((n_carry, STEPS))] if carry else [],
+        body,
+        in_specs=[first_spec] + [VMEM] * (len(operands) - 1),
+        out_specs=[VMEM] * len(outs),
+        out_shape=outs,
         compiler_params=pltpu.CompilerParams(vmem_limit_bytes=SCOPED),
         cost_estimate=LIGHT if light else COST,
-    )(*operands, *held, *sources)
+    )(*operands)
 
 
 def shape(dims, dtype):
@@ -74,7 +43,7 @@
     return pl.multiple_of(core * (extent // 2) + offset, HEAD)
 
 
-def grad_mixed_part(pieces, w_output, other, offset, size, received=None, held=(), carry=()):
+def grad_mixed_part(pieces, w_output, other, offset, size, received=None):
     counts = [len(p) for p in pieces]
     flat = [a for p in pieces for a in p]
     rows = sum(p[0].shape[0] for p in pieces)
@@ -96,12 +65,12 @@
             refs[at + 3][...] = part.astype(BF16)
 
     if other:
-        return call(body, [shape((rows, size), BF16)], [*flat, w_output], held, carry=carry)
+        return call(body, [shape((rows, size), BF16)], [*flat, w_output])
     outs = [shape((rows, size), F32), shape((rows, size), BF16)]
-    return call(body, outs, [*flat, w_output, received], held, carry=carry)
-
-
-def unmix(kept, received, mixing, first_head, held=()):
+    return call(body, outs, [*flat, w_output, received])
+
+
+def unmix(kept, received, mixing, first_head):
     rows, size = kept.shape
     count = len(received)
 
@@ -116,10 +85,10 @@
                 mix[first_head + h], total.astype(BF16), TN, preferred_element_type=F32
             ).astype(BF16)
 
-    return call(body, [shape((rows, size), BF16)], [kept, *received, mixing], held)
-
-
-def grad_normed_part(grads, w_value, other, offset, total=None, pieces=0, held=()):
+    return call(body, [shape((rows, size), BF16)], [kept, *received, mixing])
+
+
+def grad_normed_part(grads, w_value, other, offset, total=None, pieces=0):
     (rows, size), width = grads.shape, w_value.shape[0]
 
     def body(v, w, *refs):
@@ -141,7 +110,7 @@
     else:
         outs = [shape((rows, width), F32)]
     operands = [grads, pltpu.with_memory_space_constraint(w_value, pltpu.VMEM)] + ([] if total is None else [total])
-    return call(body, outs, operands, held)
+    return call(body, outs, operands)
 
 
 def stacked(columns):
@@ -159,14 +128,14 @@
     return jnp.concatenate([stats, jnp.zeros((120, stats.shape[1]), F32)], axis=0).T[:rows]
 
 
-def added(one, other, held=()):
+def added(one, other):
     def body(a, b, out):
         out[...] = a[...] + b[...]
 
-    return call(body, [shape(one.shape, one.dtype)], [one, other], held)
-
-
-def ordered(store, table, held=()):
+    return call(body, [shape(one.shape, one.dtype)], [one, other])
+
+
+def ordered(store, table):
     slots = store.shape[0]
 
     def body(s, store_ref, *outs):
@@ -174,10 +143,10 @@
         for k, out in enumerate(outs):
             out[...] = store_ref[s[k, section]]
 
-    return call(body, [shape(store.shape[1:], BF16)] * slots, [table, store], held, SMEM, light=True)
-
-
-def width_sums(keep, received, inputs, slot, held=()):
+    return call(body, [shape(store.shape[1:], BF16)] * slots, [table, store], SMEM, light=True)
+
+
+def width_sums(keep, received, inputs, slot):
     own, width = keep.shape
     slots = len(inputs)
 
@@ -196,10 +165,10 @@
         stats[...] = stacked(columns)
 
     outs = [shape((own, width), F32), shape((8, -(-own // 128) * 128), F32)]
-    return call(body, outs, [keep, *inputs, *received], held)
-
-
-def finish(grad, upstream, inputs, slot, input_stats, grad_stats, width, parts, held=()):
+    return call(body, outs, [keep, *inputs, *received])
+
+
+def finish(grad, upstream, inputs, slot, input_stats, grad_stats, width, parts):
     own, part = grad.shape
     slots = len(inputs)
     n_up, n_in, n_grad = len(upstream), len(input_stats), len(grad_stats)
@@ -238,10 +207,10 @@
     outs = [shape((own, part // parts), BF16)] * parts
     if slot == 0:
         outs += [shape((own, part), BF16)] * slots
-    return call(body, outs, operands, held)
-
-
-def value_grad_part(normed, grads, result, dims, other, offset, held=()):
+    return call(body, outs, operands)
+
+
+def value_grad_part(normed, grads, result, dims, other, offset):
     depth, width = sum(a.shape[0] for a in normed), normed[0].shape[1]
     blocks = len(normed)
     size = grads[0].shape[1]
@@ -283,7 +252,7 @@
     )(*normed, *grads, *given)
 
 
-def mixing_and_weight(slopes, weight, length, own, held=()):
+def mixing_weights(slopes, length, own):
     heads = slopes.shape[1] // 2
 
     def body(slopes_ref, out):
@@ -303,8 +272,7 @@
             weights = jnp.where(causal, jnp.exp(-slope * distance), 0.0)
             out[h] = (weights / jnp.sum(weights, axis=-1, keepdims=True)).astype(BF16)
 
-    carry = [(weight, False, 0, weight.shape[1])]
-    return call(body, [shape((heads, length, length), BF16)], [slopes], held, carry=carry)
+    return call(body, [shape((heads, length, length), BF16)], [slopes])
 
 
 def flipped(array, axis, mask):
@@ -325,32 +293,42 @@
     def others_of(array):
         return [flipped(array, "tensor", t) for t in others]
 
-    token, held = [None], []
-
-    def run(kernel, first, *rest, **more):
+    token = [None]
+
+    def run(kernel, first, *rest):
         if token[0] is not None:
             if isinstance(first, list):
                 first = [after(first[0], token[0]), *first[1:]]
             else:
                 first = after(first, token[0])
-        outs = kernel(first, *rest, held=held, **more)
+        outs = kernel(first, *rest)
         token[0] = outs[0]
         return outs
 
     upstream = [arriving[0]]
     pieces = [[a] for a in [upstream[0], *others_of(upstream[0])]]
-    mixing, w_output = run(mixing_and_weight, slopes[None], output_weight[0], own * tensors, own)
-    held.append(w_output)
+    mixing, = run(mixing_weights, slopes[None], own * tensors, own)
+    pieces[0][0] = after(pieces[0][0], mixing)
+    w_output = pltpu.with_memory_space_constraint(output_weight[0], pltpu.VMEM)
     values = []
     for slot in range(slots):
         last = slot == slots - 1
         if slot > 0:
-            upstream = [lax.ppermute(a, "section", [(i, i - 1) for i in range(1, sections)]) for a in upstream]
-            pieces = [list(p) for p in zip(*[[a, *others_of(a)] for a in upstream], strict=True)]
-
-        def product(j, other, received=None, carry=()):
+            pieces = [
+                [
+                    lax.ppermute(
+                        upstream[0],
+                        ("section", "tensor"),
+                        [(i * tensors + k, (i - 1) * tensors + (k ^ t)) for i in range(1, sections) for k in range(tensors)],
+                    )
+                ]
+                for t in range(tensors)
+            ]
+            upstream = pieces[0]
+
+        def product(j, other, received=None):
             a, n = chunks[j]
-            mixed = lambda first, *rest, held: grad_mixed_part([first, *pieces[1:]], *rest, held, carry)
+            mixed = lambda first, *rest: grad_mixed_part([first, *pieces[1:]], *rest)
             return run(mixed, pieces[0], w_output, other, a, n, received)
 
         halves, kept, across = [], [], []
@@ -384,7 +362,6 @@
         if slot == 0:
             inputs = run(ordered, store, slot_table.T)
         if last:
-            held.clear()
             result = None
             todo = [(j, side) for j in range(len(chunks)) for side in range(2)]
 

time: 91.1 us -> 89.9 us (0.987)
  Pallas kernels: 35.2 us -> 31.3 us
  waiting for transfers between devices: 31.1 us -> 33.9 us
    ppermute x1 -> x2, waiting for transfers between devices: 6.24 us -> 10.2 us  [on_device(): lax.ppermute(upstream[0], ('section', 'tensor'), [(i * tensors + k, (i -...]
    pallas_call x28, Pallas kernels: 27 us -> 23.1 us  [call(): pl.pallas_call(body, in_specs=[first_spec] + [VMEM] * (len(operands) - 1)...]
    ppermute x22 -> x21, starting transfers between devices: 17.8 us -> 16.2 us  [flipped(): lax.ppermute(array, axis, [(i, i ^ mask) for i in range(lax.axis_size(axi...]
    ppermute x1 -> x2, starting transfers between devices: 1.47 us -> 2.76 us  [on_device(): lax.ppermute(upstream[0], ('section', 'tensor'), [(i * tensors + k, (i -...]
    ppermute x22 -> x21, waiting for transfers between devices: 24.9 us -> 23.7 us  [flipped(): lax.ppermute(array, axis, [(i, i ^ mask) for i in range(lax.axis_size(axi...]
  transfers between devices with their start and end apart: 24 -> 24, of which waited for: 15 -> 17; matrix products, arithmetic and copies ran while one was open for 0% -> 0% of each run, Pallas kernels for 34% -> 30%
where the time goes in v4:
time: 89.9 us; the launch traced here: 89.7 us
  waiting for transfers between devices  33.9 us (38%)
  Pallas kernels  31.3 us (35%)
  starting transfers between devices  22.8 us (25%)
  between operations  0.99 us (1%)
    ppermute x21, waiting for transfers between devices, flipped(): lax.ppermute(array, axis, [(i, i ^ mask) for i in range(lax.axis_size(axi...  23.7 us
    pallas_call x28, Pallas kernels, call(): pl.pallas_call(body, in_specs=[first_spec] + [VMEM] * (len(operands) - 1)...  23.1 us
    ppermute x21, starting transfers between devices, flipped(): lax.ppermute(array, axis, [(i, i ^ mask) for i in range(lax.axis_size(axi...  16.2 us
    ppermute x2, waiting for transfers between devices, on_device(): lax.ppermute(upstream[0], ('section', 'tensor'), [(i * tensors + k, (i -...  10.2 us
    pallas_call x4, Pallas kernels, value_grad_part(): pl.pallas_call(body, in_specs=[VMEM] * (blocks + count) + [ANY] * len(giv...  8.13 us
    ppermute x1, starting transfers between devices, on_device(): lax.ppermute(after(parked[0], kept[-1][1]), 'section', [(i, sections - 1...  3.81 us
    ppermute x2, starting transfers between devices, on_device(): lax.ppermute(upstream[0], ('section', 'tensor'), [(i * tensors + k, (i -...  2.76 us
  transfers between devices with their start and end apart: 24, of which 17 were waited for; matrix products, arithmetic and copies ran while one was open for 0% of the time, Pallas kernels for 30%

profile of v4, /device:TPU:0, one launch (start us, length us, event | category | flops | bytes accessed | tf_op | source)
XLA Modules:
  0.0 89.7 jit_solution(16146209826881920327)
XLA Ops:
  0.6 3.0 %collective-permute-start = (bf16[64,1536]{1,0:T(8,128)(2,1)}, bf16[64,1536]{1,0:T(8,128)(2,1)S(1)}, u32[]{:S(2)}, u32[]{:S(2)}) collective-permute-start(bf16[64,1536]{1,0:T(8,128)(2,1)} %bitcast.27), channel_id=1, source_target_pairs={{0,4},{4,0},{1,5},{5,1},{2,6},{6,2},{3,7},{7,3},{8,12},{12,8},{9,1... | collective-permute-start | bytes 589832 | tf_op jit(solution)/shard_map/ppermute | solution.py:279
  3.6 0.7 copy-done.3
  4.3 1.0 %shard_map.77.refs_2_ = bf16[16,128,128]{2,1,0:T(8,128)(2,1)S(1)} custom-call(f32[1,32]{1,0:T(1,128)S(1)} %bitcast.33), custom_call_target="tpu_custom_call" | custom-call | flops 8000000000 | bytes 100000000 | tf_op jit(solution)/shard_map/pallas_call | solution.py:22
  5.3 3.5 %collective-permute-done.refs_1_ = bf16[64,1536]{1,0:T(8,128)(2,1)S(1)} collective-permute-done((bf16[64,1536]{1,0:T(8,128)(2,1)}, bf16[64,1536]{1,0:T(8,128)(2,1)S(1)}, u32[]{:S(2)}, u32[]{:S(2)}) %collective-permute-start) | collective-permute-done | bytes 196640 | tf_op jit(solution)/shard_map/ppermute | solution.py:279
  8.9 1.1 %shard_map.78 = bf16[128,1024]{1,0:T(8,128)(2,1)S(1)} custom-call(bf16[64,1536]{1,0:T(8,128)(2,1)S(1)} %bitcast.28, bf16[64,1536]{1,0:T(8,128)(2,1)S(1)} %collective-permute-done.refs_1_, bf16[4096,1536]{1,0:T(8,128)(2,1)S(1)} %bitcast.9), custom_call_target="tpu_custom_call" | custom-call | flops 8000000000 | bytes 100000000 | tf_op jit(solution)/shard_map/pallas_call | solution.py:22
  10.1 1.1 %shard_map.79 = bf16[128,1024]{1,0:T(8,128)(2,1)S(1)} custom-call(bf16[64,1536]{1,0:T(8,128)(2,1)S(1)} %bitcast.29, bf16[64,1536]{1,0:T(8,128)(2,1)S(1)} %collective-permute-done.refs_1_, bf16[4096,1536]{1,0:T(8,128)(2,1)S(1)} %bitcast.10), custom_call_target="tpu_custom_call" | custom-call | flops 8000000000 | bytes 100000000 | tf_op jit(solution)/shard_map/pallas_call | solution.py:22
  11.2 0.6 collective-permute-start.2
  11.8 1.1 %shard_map.80 = (f32[128,1024]{1,0:T(8,128)S(1)}, bf16[128,1024]{1,0:T(8,128)(2,1)S(1)}) custom-call(bf16[64,1536]{1,0:T(8,128)(2,1)S(1)} %bitcast.30, bf16[64,1536]{1,0:T(8,128)(2,1)S(1)} %collective-permute-done.refs_1_, bf16[4096,1536]{1,0:T(8,128)(2,1)S(1)} %bitcast.11, bf16[128,1024]{1,0:T(8,128)(2,1)S(1)} %collective-permute-done.1.refs_3_), custom_call_target="tpu_custom_call" | custom-call | flops 8000000000 | bytes 100000000 | tf_op jit(solution)/shard_map/pallas_call | solution.py:22
  12.9 1.7 %collective-permute-start.3 = (bf16[128,1024]{1,0:T(8,128)(2,1)S(1)}, bf16[128,1024]{1,0:T(8,128)(2,1)S(1)}, u32[]{:S(2)}, u32[]{:S(2)}) collective-permute-start(bf16[128,1024]{1,0:T(8,128)(2,1)S(1)} %get-tuple-element.66), channel_id=1, source_target_pairs={{0,2},{1,3},{2,0},{3,1},{4,6},{5,7},{6,4},{7,5},{8,10},{9,11},{10,... | collective-permute-start | bytes 786440 | tf_op jit(solution)/shard_map/ppermute | solution.py:279
  14.7 1.1 %shard_map.81 = (f32[128,1024]{1,0:T(8,128)S(1)}, bf16[128,1024]{1,0:T(8,128)(2,1)S(1)}) custom-call(bf16[64,1536]{1,0:T(8,128)(2,1)S(1)} %bitcast.31, bf16[64,1536]{1,0:T(8,128)(2,1)S(1)} %collective-permute-done.refs_1_, bf16[4096,1536]{1,0:T(8,128)(2,1)S(1)} %bitcast.12, bf16[128,1024]{1,0:T(8,128)(2,1)S(1)} %collective-permute-done.2.refs_3_), custom_call_target="tpu_custom_call" | custom-call | flops 8000000000 | bytes 100000000 | tf_op jit(solution)/shard_map/pallas_call | solution.py:22
  16.3 3.8 %collective-permute-start.7 = (bf16[2,64,1536]{2,1,0:T(8,128)(2,1)S(1)}, bf16[2,64,1536]{2,1,0:T(8,128)(2,1)S(1)}, u32[]{:S(2)}, u32[]{:S(2)}) collective-permute-start(bf16[2,64,1536]{2,1,0:T(8,128)(2,1)S(1)} %bitcast.34), channel_id=1, source_target_pairs={{0,24},{8,16},{16,8},{24,0},{1,25},{9,17},{17,9},{25,1},{2,26},{10... | collective-permute-start | bytes 1179656 | tf_op jit(solution)/shard_map/ppermute | solution.py:346
  20.1 2.1 %collective-permute-done.3.refs_1_ = bf16[128,1024]{1,0:T(8,128)(2,1)S(1)} collective-permute-done((bf16[128,1024]{1,0:T(8,128)(2,1)S(1)}, bf16[128,1024]{1,0:T(8,128)(2,1)S(1)}, u32[]{:S(2)}, u32[]{:S(2)}) %collective-permute-start.3) | collective-permute-done | bytes 262176 | tf_op jit(solution)/shard_map/ppermute | solution.py:279
  22.6 1.2 %shard_map.83.refs_0_ = f32[128,1536]{1,0:T(8,128)S(1)} custom-call(bf16[128,1024]{1,0:T(8,128)(2,1)S(1)} %shard_map.82.v.refs_4_, bf16[1536,4096]{1,0:T(8,128)(2,1)S(1)} %bitcast.19), custom_call_target="tpu_custom_call" | custom-call | flops 8000000000 | bytes 100000000 | tf_op jit(solution)/shard_map/pallas_call | solution.py:22
  24.1 1.2 %shard_map.84.refs_0_ = f32[128,1536]{1,0:T(8,128)S(1)} custom-call(bf16[128,1024]{1,0:T(8,128)(2,1)S(1)} %collective-permute-done.4.v.refs_4_, bf16[1536,4096]{1,0:T(8,128)(2,1)S(1)} %bitcast.20, f32[128,1536]{1,0:T(8,128)S(1)} %shard_map.83.refs_0_), custom_call_target="tpu_custom_call" | custom-call | flops 8000000000 | bytes 100000000 | tf_op jit(solution)/shard_map/pallas_call | solution.py:22
  25.2 1.6 %collective-permute-done.5.refs_1_ = bf16[128,1024]{1,0:T(8,128)(2,1)S(1)} collective-permute-done((bf16[128,1024]{1,0:T(8,128)(2,1)S(1)}, bf16[128,1024]{1,0:T(8,128)(2,1)S(1)}, u32[]{:S(2)}, u32[]{:S(2)}) %collective-permute-start.5) | collective-permute-done | bytes 262176 | tf_op jit(solution)/shard_map/ppermute | solution.py:279
  27.2 1.2 %shard_map.86.refs_0_ = f32[128,1536]{1,0:T(8,128)S(1)} custom-call(bf16[128,1024]{1,0:T(8,128)(2,1)S(1)} %shard_map.85.v.refs_4_, bf16[1536,4096]{1,0:T(8,128)(2,1)S(1)} %bitcast.21, f32[128,1536]{1,0:T(8,128)S(1)} %shard_map.84.refs_0_), custom_call_target="tpu_custom_call" | custom-call | flops 8000000000 | bytes 100000000 | tf_op jit(solution)/shard_map/pallas_call | solution.py:22
  28.8 1.2 %shard_map.87 = (f32[64,1536]{1,0:T(8,128)S(1)}, bf16[64,1536]{1,0:T(8,128)(2,1)S(1)}) custom-call(bf16[128,1024]{1,0:T(8,128)(2,1)S(1)} %collective-permute-done.6.v.refs_4_, bf16[1536,4096]{1,0:T(8,128)(2,1)S(1)} %bitcast.22, f32[128,1536]{1,0:T(8,128)S(1)} %shard_map.86.refs_0_), custom_call_target="tpu_custom_call" | custom-call | flops 8000000000 | bytes 100000000 | tf_op jit(solution)/shard_map/pallas_call | solution.py:22
  29.9 1.7 %collective-permute-start.8 = (bf16[64,1536]{1,0:T(8,128)(2,1)S(1)}, bf16[64,1536]{1,0:T(8,128)(2,1)S(1)}, u32[]{:S(2)}, u32[]{:S(2)}) collective-permute-start(bf16[64,1536]{1,0:T(8,128)(2,1)S(1)} %get-tuple-element.79), channel_id=1, source_target_pairs={{0,4},{4,0},{1,5},{5,1},{2,6},{6,2},{3,7},{7,3},{8,12},{12,8},{9,1... | collective-permute-start | bytes 589832 | tf_op jit(solution)/shard_map/ppermute | solution.py:279
  31.6 0.6 shard_map.88
  32.2 4.8 %collective-permute-done.8.refs_2_ = bf16[64,1536]{1,0:T(8,128)(2,1)S(1)} collective-permute-done((bf16[64,1536]{1,0:T(8,128)(2,1)S(1)}, bf16[64,1536]{1,0:T(8,128)(2,1)S(1)}, u32[]{:S(2)}, u32[]{:S(2)}) %collective-permute-start.8) | collective-permute-done | bytes 196640 | tf_op jit(solution)/shard_map/ppermute | solution.py:279
  37.3 1.2 %collective-permute-done.9.b = f32[8,128]{1,0:T(8,128)S(1)} collective-permute-done((f32[8,128]{1,0:T(8,128)S(1)}, f32[8,128]{1,0:T(8,128)S(1)}, u32[]{:S(2)}, u32[]{:S(2)}) %collective-permute-start.9) | collective-permute-done | bytes 4128 | tf_op jit(solution)/shard_map/ppermute | solution.py:279
  38.5 1.7 %collective-permute-start.10 = (f32[8,128]{1,0:T(8,128)S(1)}, f32[8,128]{1,0:T(8,128)S(1)}, u32[]{:S(2)}, u32[]{:S(2)}) collective-permute-start(f32[8,128]{1,0:T(8,128)S(1)} %shard_map.90.refs_3_.refs_5_), channel_id=1, source_target_pairs={{0,2},{1,3},{2,0},{3,1},{4,6},{5,7},{6,4},{7,5},{8,10},{9,11},{10,... | collective-permute-start | bytes 12296 | tf_op jit(solution)/shard_map/ppermute | solution.py:279
  40.1 2.0 %collective-permute-done.10.refs_4_.refs_6_ = f32[8,128]{1,0:T(8,128)S(1)} collective-permute-done((f32[8,128]{1,0:T(8,128)S(1)}, f32[8,128]{1,0:T(8,128)S(1)}, u32[]{:S(2)}, u32[]{:S(2)}) %collective-permute-start.10) | collective-permute-done | bytes 4128 | tf_op jit(solution)/shard_map/ppermute | solution.py:279
  42.5 1.3 %collective-permute-start.11 = (bf16[64,1536]{1,0:T(8,128)(2,1)S(1)}, bf16[64,1536]{1,0:T(8,128)(2,1)S(1)}, u32[]{:S(2)}, u32[]{:S(2)}) collective-permute-start(bf16[64,1536]{1,0:T(8,128)(2,1)S(1)} %get-tuple-element.84), channel_id=1, source_target_pairs={{8,0},{12,4},{16,8},{20,12},{24,16},{28,20},{9,1},{13,5},{17,9},{2... | collective-permute-start | bytes 589832 | tf_op jit(solution)/shard_map/ppermute | solution.py:319
  43.8 1.5 %collective-permute-start.12 = (bf16[64,1536]{1,0:T(8,128)(2,1)S(1)}, bf16[64,1536]{1,0:T(8,128)(2,1)S(1)}, u32[]{:S(2)}, u32[]{:S(2)}) collective-permute-start(bf16[64,1536]{1,0:T(8,128)(2,1)S(1)} %get-tuple-element.84), channel_id=1, source_target_pairs={{8,4},{12,0},{16,12},{20,8},{24,20},{28,16},{9,5},{13,1},{17,13},{... | collective-permute-start | bytes 589832 | tf_op jit(solution)/shard_map/ppermute | solution.py:319
  45.3 6.8 %collective-permute-done.11.refs_0_.refs_2_ = bf16[64,1536]{1,0:T(8,128)(2,1)S(1)} collective-permute-done((bf16[64,1536]{1,0:T(8,128)(2,1)S(1)}, bf16[64,1536]{1,0:T(8,128)(2,1)S(1)}, u32[]{:S(2)}, u32[]{:S(2)}) %collective-permute-start.11) | collective-permute-done | bytes 196640 | tf_op jit(solution)/shard_map/ppermute | solution.py:319
  52.1 3.4 %collective-permute-done.12.refs_1_ = bf16[64,1536]{1,0:T(8,128)(2,1)S(1)} collective-permute-done((bf16[64,1536]{1,0:T(8,128)(2,1)S(1)}, bf16[64,1536]{1,0:T(8,128)(2,1)S(1)}, u32[]{:S(2)}, u32[]{:S(2)}) %collective-permute-start.12) | collective-permute-done | bytes 196640 | tf_op jit(solution)/shard_map/ppermute | solution.py:319
  55.5 1.1 %shard_map.92 = bf16[128,1024]{1,0:T(8,128)(2,1)S(1)} custom-call(bf16[64,1536]{1,0:T(8,128)(2,1)S(1)} %collective-permute-done.11.refs_0_.refs_2_, bf16[64,1536]{1,0:T(8,128)(2,1)S(1)} %collective-permute-done.12.refs_1_, bf16[4096,1536]{1,0:T(8,128)(2,1)S(1)} %bitcast.13), custom_call_target="tpu_custom_call" | custom-call | flops 8000000000 | bytes 100000000 | tf_op jit(solution)/shard_map/pallas_call | solution.py:22
  56.8 1.1 %shard_map.93 = bf16[128,1024]{1,0:T(8,128)(2,1)S(1)} custom-call(bf16[64,1536]{1,0:T(8,128)(2,1)S(1)} %collective-permute-done.11.refs_0_.refs_2_, bf16[64,1536]{1,0:T(8,128)(2,1)S(1)} %collective-permute-done.12.refs_1_, bf16[4096,1536]{1,0:T(8,128)(2,1)S(1)} %bitcast.14), custom_call_target="tpu_custom_call" | custom-call | flops 8000000000 | bytes 100000000 | tf_op jit(solution)/shard_map/pallas_call | solution.py:22
  57.9 0.6 collective-permute-start.14
  58.5 1.1 %shard_map.94 = (f32[128,1024]{1,0:T(8,128)S(1)}, bf16[128,1024]{1,0:T(8,128)(2,1)S(1)}) custom-call(bf16[64,1536]{1,0:T(8,128)(2,1)S(1)} %collective-permute-done.11.refs_0_.refs_2_, bf16[64,1536]{1,0:T(8,128)(2,1)S(1)} %collective-permute-done.12.refs_1_, bf16[4096,1536]{1,0:T(8,128)(2,1)S(1)} %bitcast.15, ...), custom_call_target="tpu_custom_call" | custom-call | flops 8000000000 | bytes 100000000 | tf_op jit(solution)/shard_map/pallas_call | solution.py:22
  59.6 1.6 %collective-permute-start.15 = (bf16[128,1024]{1,0:T(8,128)(2,1)S(1)}, bf16[128,1024]{1,0:T(8,128)(2,1)S(1)}, u32[]{:S(2)}, u32[]{:S(2)}) collective-permute-start(bf16[128,1024]{1,0:T(8,128)(2,1)S(1)} %get-tuple-element.92), channel_id=1, source_target_pairs={{0,2},{1,3},{2,0},{3,1},{4,6},{5,7},{6,4},{7,5},{8,10},{9,11},{10,... | collective-permute-start | bytes 786440 | tf_op jit(solution)/shard_map/ppermute | solution.py:279
  61.2 1.1 %shard_map.95 = (f32[128,1024]{1,0:T(8,128)S(1)}, bf16[128,1024]{1,0:T(8,128)(2,1)S(1)}) custom-call(bf16[64,1536]{1,0:T(8,128)(2,1)S(1)} %collective-permute-done.11.refs_0_.refs_2_, bf16[64,1536]{1,0:T(8,128)(2,1)S(1)} %collective-permute-done.12.refs_1_, bf16[4096,1536]{1,0:T(8,128)(2,1)S(1)} %bitcast.16, ...), custom_call_target="tpu_custom_call" | custom-call | flops 8000000000 | bytes 100000000 | tf_op jit(solution)/shard_map/pallas_call | solution.py:22
  62.4 0.6 collective-permute-start.19
  63.0 1.5 %collective-permute-start.20 = (bf16[64,1536]{1,0:T(8,128)(2,1)S(1)}, bf16[64,1536]{1,0:T(8,128)(2,1)S(1)}, u32[]{:S(2)}, u32[]{:S(2)}) collective-permute-start(bf16[64,1536]{1,0:T(8,128)(2,1)S(1)} %get-tuple-element.104.refs_2_), channel_id=1, source_target_pairs={{0,4},{4,0},{1,5},{5,1},{2,6},{6,2},{3,7},{7,3},{8,12},{12,8},{9,1... | collective-permute-start | bytes 589832 | tf_op jit(solution)/shard_map/ppermute | solution.py:279
  65.0 3.9 %collective-permute-done.15.refs_1_ = bf16[128,1024]{1,0:T(8,128)(2,1)S(1)} collective-permute-done((bf16[128,1024]{1,0:T(8,128)(2,1)S(1)}, bf16[128,1024]{1,0:T(8,128)(2,1)S(1)}, u32[]{:S(2)}, u32[]{:S(2)}) %collective-permute-start.15) | collective-permute-done | bytes 262176 | tf_op jit(solution)/shard_map/ppermute | solution.py:279
  69.2 1.2 %shard_map.97.refs_0_ = f32[128,1536]{1,0:T(8,128)S(1)} custom-call(bf16[128,1024]{1,0:T(8,128)(2,1)S(1)} %shard_map.96.v.refs_5_, bf16[1536,4096]{1,0:T(8,128)(2,1)S(1)} %bitcast.23), custom_call_target="tpu_custom_call" | custom-call | flops 8000000000 | bytes 100000000 | tf_op jit(solution)/shard_map/pallas_call | solution.py:22
  70.7 1.2 %shard_map.98.refs_0_ = f32[128,1536]{1,0:T(8,128)S(1)} custom-call(bf16[128,1024]{1,0:T(8,128)(2,1)S(1)} %collective-permute-done.16.v.refs_5_, bf16[1536,4096]{1,0:T(8,128)(2,1)S(1)} %bitcast.24, f32[128,1536]{1,0:T(8,128)S(1)} %shard_map.97.refs_0_), custom_call_target="tpu_custom_call" | custom-call | flops 8000000000 | bytes 100000000 | tf_op jit(solution)/shard_map/pallas_call | solution.py:22
  71.9 1.7 %collective-permute-done.17.refs_1_ = bf16[128,1024]{1,0:T(8,128)(2,1)S(1)} collective-permute-done((bf16[128,1024]{1,0:T(8,128)(2,1)S(1)}, bf16[128,1024]{1,0:T(8,128)(2,1)S(1)}, u32[]{:S(2)}, u32[]{:S(2)}) %collective-permute-start.17) | collective-permute-done | bytes 262176 | tf_op jit(solution)/shard_map/ppermute | solution.py:279
  73.9 1.2 %shard_map.100.refs_0_ = f32[128,1536]{1,0:T(8,128)S(1)} custom-call(bf16[128,1024]{1,0:T(8,128)(2,1)S(1)} %shard_map.99.v.refs_5_, bf16[1536,4096]{1,0:T(8,128)(2,1)S(1)} %bitcast.25, f32[128,1536]{1,0:T(8,128)S(1)} %shard_map.98.refs_0_), custom_call_target="tpu_custom_call" | custom-call | flops 8000000000 | bytes 100000000 | tf_op jit(solution)/shard_map/pallas_call | solution.py:22
  75.4 1.2 %shard_map.101 = (f32[64,1536]{1,0:T(8,128)S(1)}, bf16[64,1536]{1,0:T(8,128)(2,1)S(1)}) custom-call(bf16[128,1024]{1,0:T(8,128)(2,1)S(1)} %collective-permute-done.18.v.refs_5_, bf16[1536,4096]{1,0:T(8,128)(2,1)S(1)} %bitcast.26, f32[128,1536]{1,0:T(8,128)S(1)} %shard_map.100.refs_0_), custom_call_target="tpu_custom_call" | custom-call | flops 8000000000 | bytes 100000000 | tf_op jit(solution)/shard_map/pallas_call | solution.py:22
  77.1 2.0 %shard_map.102.refs_6_ = bf16[1536,4096]{1,0:T(8,128)(2,1)} custom-call(bf16[64,1536]{1,0:T(8,128)(2,1)S(1)} %get-tuple-element.112.refs_0_, bf16[64,1536]{1,0:T(8,128)(2,1)S(1)} %collective-permute-done.19.refs_1_, bf16[64,1536]{1,0:T(8,128)(2,1)S(1)} %get-tuple-element.104.refs_2_, bf16[64,1536]{1,0:T(8,128)(2,1)S(1)} %collective-permute-done.20.refs_3_, ...), custom_call_target="tpu_custom_call" | custom-call | flops 8000000000 | bytes 100000000 | tf_op jit(solution)/shard_map/pallas_call | solution.py:243
  79.1 2.0 %shard_map.103.refs_6_ = bf16[1536,4096]{1,0:T(8,128)(2,1)} custom-call(bf16[64,1536]{1,0:T(8,128)(2,1)S(1)} %get-tuple-element.112.refs_0_, bf16[64,1536]{1,0:T(8,128)(2,1)S(1)} %collective-permute-done.19.refs_1_, bf16[64,1536]{1,0:T(8,128)(2,1)S(1)} %get-tuple-element.104.refs_2_, ...), custom_call_target="tpu_custom_call", output_to_operand_aliasing={{}: (6, {})} | custom-call | flops 8000000000 | bytes 100000000 | tf_op jit(solution)/shard_map/pallas_call | solution.py:243
  81.2 2.0 %shard_map.104.refs_6_ = bf16[1536,4096]{1,0:T(8,128)(2,1)} custom-call(bf16[64,1536]{1,0:T(8,128)(2,1)S(1)} %get-tuple-element.112.refs_0_, bf16[64,1536]{1,0:T(8,128)(2,1)S(1)} %collective-permute-done.19.refs_1_, bf16[64,1536]{1,0:T(8,128)(2,1)S(1)} %get-tuple-element.104.refs_2_, ...), custom_call_target="tpu_custom_call", output_to_operand_aliasing={{}: (6, {})} | custom-call | flops 8000000000 | bytes 100000000 | tf_op jit(solution)/shard_map/pallas_call | solution.py:243
  83.9 1.2 %collective-permute-done.22.b = f32[8,128]{1,0:T(8,128)S(1)} collective-permute-done((f32[8,128]{1,0:T(8,128)S(1)}, f32[8,128]{1,0:T(8,128)S(1)}, u32[]{:S(2)}, u32[]{:S(2)}) %collective-permute-start.22) | collective-permute-done | bytes 4128 | tf_op jit(solution)/shard_map/ppermute | solution.py:279
  85.0 1.5 %collective-permute-start.23 = (f32[8,128]{1,0:T(8,128)S(1)}, f32[8,128]{1,0:T(8,128)S(1)}, u32[]{:S(2)}, u32[]{:S(2)}) collective-permute-start(f32[8,128]{1,0:T(8,128)S(1)} %shard_map.106.refs_5_), channel_id=1, source_target_pairs={{0,2},{1,3},{2,0},{3,1},{4,6},{5,7},{6,4},{7,5},{8,10},{9,11},{10,... | collective-permute-start | bytes 12296 | tf_op jit(solution)/shard_map/ppermute | solution.py:279
  86.5 2.0 %shard_map.107 = bf16[1536,4096]{1,0:T(8,128)(2,1)} custom-call(bf16[64,1536]{1,0:T(8,128)(2,1)S(1)} %get-tuple-element.112.refs_0_, bf16[64,1536]{1,0:T(8,128)(2,1)S(1)} %collective-permute-done.19.refs_1_, bf16[64,1536]{1,0:T(8,128)(2,1)S(1)} %get-tuple-element.104.refs_2_, ...), custom_call_target="tpu_custom_call", output_to_operand_aliasing={{}: (6, {})} | custom-call | flops 8000000000 | bytes 100000000 | tf_op jit(solution)/shard_map/pallas_call | solution.py:243
  88.6 1.1 %shard_map.108 = bf16[64,1536]{1,0:T(8,128)(2,1)} custom-call(f32[64,1536]{1,0:T(8,128)S(1)} %get-tuple-element.113.grad_ref, bf16[64,1536]{1,0:T(8,128)(2,1)S(1)} %get-tuple-element.76.refs_0_, bf16[64,1536]{1,0:T(8,128)(2,1)S(1)} %get-tuple-element.78.refs_1_, bf16[64,1536]{1,0:T(8,128)(2,1)S(1)} %collective-permute-done.11.refs_0_.refs_2_, ...), custom_call_target="tpu_custom_call" | custom-call | flops 8000000000 | bytes 100000000 | tf_op jit(solution)/shard_map/pallas_call | solution.py:22
  (49 shorter events, 5.9 us)
Async XLA Ops:
  0.6 8.1 %collective-permute-start = (bf16[64,1536]{1,0:T(8,128)(2,1)}, bf16[64,1536]{1,0:T(8,128)(2,1)S(1)}, u32[]{:S(2)}, u32[]{:S(2)}) collective-permute-start(bf16[64,1536]{1,0:T(8,128)(2,1)} %bitcast.27), channel_id=1, source_target_pairs={{0,4},{4,0},{1,5},{5,1},{2,6},{6,2},{3,7},{7,3},{8,12},{12,8},{9,1... | collective-permute-start | bytes 589832 | tf_op jit(solution)/shard_map/ppermute | solution.py:279
  3.6 0.7 copy-start.3
  4.3 4.6 %copy-start.1 = (bf16[1,4096,1536]{2,1,0:T(8,128)(2,1)S(1)}, bf16[1,4096,1536]{2,1,0:T(8,128)(2,1)}, u32[]{:S(2)}) copy-start(bf16[1,4096,1536]{2,1,0:T(8,128)(2,1)} %param.10) | copy-start | bytes 37748740
  4.3 4.6 %copy-start.2 = (bf16[1,64,1536]{2,1,0:T(8,128)(2,1)S(1)}, bf16[1,64,1536]{2,1,0:T(8,128)(2,1)}, u32[]{:S(2)}) copy-start(bf16[1,64,1536]{2,1,0:T(8,128)(2,1)} %param.7) | copy-start | bytes 589828
  10.0 1.8 %collective-permute-start.1 = (bf16[128,1024]{1,0:T(8,128)(2,1)S(1)}, bf16[128,1024]{1,0:T(8,128)(2,1)S(1)}, u32[]{:S(2)}, u32[]{:S(2)}) collective-permute-start(bf16[128,1024]{1,0:T(8,128)(2,1)S(1)} %shard_map.78), channel_id=1, source_target_pairs={{0,1},{1,0},{2,3},{3,2},{4,5},{5,4},{6,7},{7,6},{8,9},{9,8},{10,11... | collective-permute-start | bytes 786440 | tf_op jit(solution)/shard_map/ppermute | solution.py:279
  11.2 3.4 %collective-permute-start.2 = (bf16[128,1024]{1,0:T(8,128)(2,1)S(1)}, bf16[128,1024]{1,0:T(8,128)(2,1)S(1)}, u32[]{:S(2)}, u32[]{:S(2)}) collective-permute-start(bf16[128,1024]{1,0:T(8,128)(2,1)S(1)} %shard_map.79), channel_id=1, source_target_pairs={{0,1},{1,0},{2,3},{3,2},{4,5},{5,4},{6,7},{7,6},{8,9},{9,8},{10,11... | collective-permute-start | bytes 786440 | tf_op jit(solution)/shard_map/ppermute | solution.py:279
  12.9 3.3 %copy-start.4 = (bf16[1,2,64,1536]{3,2,1,0:T(8,128)(2,1)S(1)}, bf16[1,2,64,1536]{3,2,1,0:T(8,128)(2,1)}, u32[]{:S(2)}) copy-start(bf16[1,2,64,1536]{3,2,1,0:T(8,128)(2,1)} %param.6) | copy-start | bytes 1179652
  12.9 9.2 %collective-permute-start.3 = (bf16[128,1024]{1,0:T(8,128)(2,1)S(1)}, bf16[128,1024]{1,0:T(8,128)(2,1)S(1)}, u32[]{:S(2)}, u32[]{:S(2)}) collective-permute-start(bf16[128,1024]{1,0:T(8,128)(2,1)S(1)} %get-tuple-element.66), channel_id=1, source_target_pairs={{0,2},{1,3},{2,0},{3,1},{4,6},{5,7},{6,4},{7,5},{8,10},{9,11},{10,... | collective-permute-start | bytes 786440 | tf_op jit(solution)/shard_map/ppermute | solution.py:279
  15.8 11.1 %collective-permute-start.5 = (bf16[128,1024]{1,0:T(8,128)(2,1)S(1)}, bf16[128,1024]{1,0:T(8,128)(2,1)S(1)}, u32[]{:S(2)}, u32[]{:S(2)}) collective-permute-start(bf16[128,1024]{1,0:T(8,128)(2,1)S(1)} %get-tuple-element.70), channel_id=1, source_target_pairs={{0,2},{1,3},{2,0},{3,1},{4,6},{5,7},{6,4},{7,5},{8,10},{9,11},{10,... | collective-permute-start | bytes 786440 | tf_op jit(solution)/shard_map/ppermute | solution.py:279
  16.3 6.3 %slice-start = ((s8[12582912]{0:T(1024)(128)(4,1)}), s8[4194304]{0:T(1024)(128)(4,1)S(1)}, s32[]{:S(2)}) async-start(s8[12582912]{0:T(1024)(128)(4,1)} %bitcast.17), calls=%async_computation | async-start | bytes 8388608
  16.3 6.3 %slice-start.1 = ((s8[12582912]{0:T(1024)(128)(4,1)}), s8[4194304]{0:T(1024)(128)(4,1)S(1)}, s32[]{:S(2)}) async-start(s8[12582912]{0:T(1024)(128)(4,1)} %bitcast.17), calls=%async_computation.1 | async-start | bytes 8388608
  16.3 6.3 %slice-start.2 = ((s8[12582912]{0:T(1024)(128)(4,1)}), s8[4194304]{0:T(1024)(128)(4,1)S(1)}, s32[]{:S(2)}) async-start(s8[12582912]{0:T(1024)(128)(4,1)} %bitcast.17), calls=%async_computation.2 | async-start | bytes 8388608
  16.3 15.4 %collective-permute-start.7 = (bf16[2,64,1536]{2,1,0:T(8,128)(2,1)S(1)}, bf16[2,64,1536]{2,1,0:T(8,128)(2,1)S(1)}, u32[]{:S(2)}, u32[]{:S(2)}) collective-permute-start(bf16[2,64,1536]{2,1,0:T(8,128)(2,1)S(1)} %bitcast.34), channel_id=1, source_target_pairs={{0,24},{8,16},{16,8},{24,0},{1,25},{9,17},{17,9},{25,1},{2,26},{10... | collective-permute-start | bytes 1179656 | tf_op jit(solution)/shard_map/ppermute | solution.py:346
  22.5 1.6 %collective-permute-start.4 = (bf16[128,1024]{1,0:T(8,128)(2,1)S(1)}, bf16[128,1024]{1,0:T(8,128)(2,1)S(1)}, u32[]{:S(2)}, u32[]{:S(2)}) collective-permute-start(bf16[128,1024]{1,0:T(8,128)(2,1)S(1)} %shard_map.82.v.refs_4_), channel_id=1, source_target_pairs={{0,1},{1,0},{2,3},{3,2},{4,5},{5,4},{6,7},{7,6},{8,9},{9,8},{10,11... | collective-permute-start | bytes 786440 | tf_op jit(solution)/shard_map/ppermute | solution.py:279
  27.2 1.6 %collective-permute-start.6 = (bf16[128,1024]{1,0:T(8,128)(2,1)S(1)}, bf16[128,1024]{1,0:T(8,128)(2,1)S(1)}, u32[]{:S(2)}, u32[]{:S(2)}) collective-permute-start(bf16[128,1024]{1,0:T(8,128)(2,1)S(1)} %shard_map.85.v.refs_4_), channel_id=1, source_target_pairs={{0,1},{1,0},{2,3},{3,2},{4,5},{5,4},{6,7},{7,6},{8,9},{9,8},{10,11... | collective-permute-start | bytes 786440 | tf_op jit(solution)/shard_map/ppermute | solution.py:279
  28.4 3.2 %copy-start = (s32[4,2]{0,1:T(2,128)S(1)}, s32[4,2]{0,1:T(2,128)}, u32[]{:S(2)}) copy-start(s32[4,2]{0,1:T(2,128)} %param.8) | copy-start | bytes 100
  29.9 7.1 %collective-permute-start.8 = (bf16[64,1536]{1,0:T(8,128)(2,1)S(1)}, bf16[64,1536]{1,0:T(8,128)(2,1)S(1)}, u32[]{:S(2)}, u32[]{:S(2)}) collective-permute-start(bf16[64,1536]{1,0:T(8,128)(2,1)S(1)} %get-tuple-element.79), channel_id=1, source_target_pairs={{0,4},{4,0},{1,5},{5,1},{2,6},{6,2},{3,7},{7,3},{8,12},{12,8},{9,1... | collective-permute-start | bytes 589832 | tf_op jit(solution)/shard_map/ppermute | solution.py:279
  37.3 1.2 %collective-permute-start.9 = (f32[8,128]{1,0:T(8,128)S(1)}, f32[8,128]{1,0:T(8,128)S(1)}, u32[]{:S(2)}, u32[]{:S(2)}) collective-permute-start(f32[8,128]{1,0:T(8,128)S(1)} %get-tuple-element.82.a), channel_id=1, source_target_pairs={{0,1},{1,0},{2,3},{3,2},{4,5},{5,4},{6,7},{7,6},{8,9},{9,8},{10,11... | collective-permute-start | bytes 12296 | tf_op jit(solution)/shard_map/ppermute | solution.py:279
  38.5 3.6 %collective-permute-start.10 = (f32[8,128]{1,0:T(8,128)S(1)}, f32[8,128]{1,0:T(8,128)S(1)}, u32[]{:S(2)}, u32[]{:S(2)}) collective-permute-start(f32[8,128]{1,0:T(8,128)S(1)} %shard_map.90.refs_3_.refs_5_), channel_id=1, source_target_pairs={{0,2},{1,3},{2,0},{3,1},{4,6},{5,7},{6,4},{7,5},{8,10},{9,11},{10,... | collective-permute-start | bytes 12296 | tf_op jit(solution)/shard_map/ppermute | solution.py:279
  42.5 9.6 %collective-permute-start.11 = (bf16[64,1536]{1,0:T(8,128)(2,1)S(1)}, bf16[64,1536]{1,0:T(8,128)(2,1)S(1)}, u32[]{:S(2)}, u32[]{:S(2)}) collective-permute-start(bf16[64,1536]{1,0:T(8,128)(2,1)S(1)} %get-tuple-element.84), channel_id=1, source_target_pairs={{8,0},{12,4},{16,8},{20,12},{24,16},{28,20},{9,1},{13,5},{17,9},{2... | collective-permute-start | bytes 589832 | tf_op jit(solution)/shard_map/ppermute | solution.py:319
  43.8 11.7 %collective-permute-start.12 = (bf16[64,1536]{1,0:T(8,128)(2,1)S(1)}, bf16[64,1536]{1,0:T(8,128)(2,1)S(1)}, u32[]{:S(2)}, u32[]{:S(2)}) collective-permute-start(bf16[64,1536]{1,0:T(8,128)(2,1)S(1)} %get-tuple-element.84), channel_id=1, source_target_pairs={{8,4},{12,0},{16,12},{20,8},{24,20},{28,16},{9,5},{13,1},{17,13},{... | collective-permute-start | bytes 589832 | tf_op jit(solution)/shard_map/ppermute | solution.py:319
  56.7 1.8 %collective-permute-start.13 = (bf16[128,1024]{1,0:T(8,128)(2,1)S(1)}, bf16[128,1024]{1,0:T(8,128)(2,1)S(1)}, u32[]{:S(2)}, u32[]{:S(2)}) collective-permute-start(bf16[128,1024]{1,0:T(8,128)(2,1)S(1)} %shard_map.92), channel_id=1, source_target_pairs={{0,1},{1,0},{2,3},{3,2},{4,5},{5,4},{6,7},{7,6},{8,9},{9,8},{10,11... | collective-permute-start | bytes 786440 | tf_op jit(solution)/shard_map/ppermute | solution.py:279
  57.9 3.3 %collective-permute-start.14 = (bf16[128,1024]{1,0:T(8,128)(2,1)S(1)}, bf16[128,1024]{1,0:T(8,128)(2,1)S(1)}, u32[]{:S(2)}, u32[]{:S(2)}) collective-permute-start(bf16[128,1024]{1,0:T(8,128)(2,1)S(1)} %shard_map.93), channel_id=1, source_target_pairs={{0,1},{1,0},{2,3},{3,2},{4,5},{5,4},{6,7},{7,6},{8,9},{9,8},{10,11... | collective-permute-start | bytes 786440 | tf_op jit(solution)/shard_map/ppermute | solution.py:279
  59.6 9.2 %collective-permute-start.15 = (bf16[128,1024]{1,0:T(8,128)(2,1)S(1)}, bf16[128,1024]{1,0:T(8,128)(2,1)S(1)}, u32[]{:S(2)}, u32[]{:S(2)}) collective-permute-start(bf16[128,1024]{1,0:T(8,128)(2,1)S(1)} %get-tuple-element.92), channel_id=1, source_target_pairs={{0,2},{1,3},{2,0},{3,1},{4,6},{5,7},{6,4},{7,5},{8,10},{9,11},{10,... | collective-permute-start | bytes 786440 | tf_op jit(solution)/shard_map/ppermute | solution.py:279
  62.4 14.7 %collective-permute-start.19 = (bf16[64,1536]{1,0:T(8,128)(2,1)S(1)}, bf16[64,1536]{1,0:T(8,128)(2,1)S(1)}, u32[]{:S(2)}, u32[]{:S(2)}) collective-permute-start(bf16[64,1536]{1,0:T(8,128)(2,1)S(1)} %get-tuple-element.112.refs_0_), channel_id=1, source_target_pairs={{0,4},{4,0},{1,5},{5,1},{2,6},{6,2},{3,7},{7,3},{8,12},{12,8},{9,1... | collective-permute-start | bytes 589832 | tf_op jit(solution)/shard_map/ppermute | solution.py:279
  63.0 14.1 %collective-permute-start.20 = (bf16[64,1536]{1,0:T(8,128)(2,1)S(1)}, bf16[64,1536]{1,0:T(8,128)(2,1)S(1)}, u32[]{:S(2)}, u32[]{:S(2)}) collective-permute-start(bf16[64,1536]{1,0:T(8,128)(2,1)S(1)} %get-tuple-element.104.refs_2_), channel_id=1, source_target_pairs={{0,4},{4,0},{1,5},{5,1},{2,6},{6,2},{3,7},{7,3},{8,12},{12,8},{9,1... | collective-permute-start | bytes 589832 | tf_op jit(solution)/shard_map/ppermute | solution.py:279
  64.4 9.1 %collective-permute-start.17 = (bf16[128,1024]{1,0:T(8,128)(2,1)S(1)}, bf16[128,1024]{1,0:T(8,128)(2,1)S(1)}, u32[]{:S(2)}, u32[]{:S(2)}) collective-permute-start(bf16[128,1024]{1,0:T(8,128)(2,1)S(1)} %get-tuple-element.96), channel_id=1, source_target_pairs={{0,2},{1,3},{2,0},{3,1},{4,6},{5,7},{6,4},{7,5},{8,10},{9,11},{10,... | collective-permute-start | bytes 786440 | tf_op jit(solution)/shard_map/ppermute | solution.py:279
  69.1 1.6 %collective-permute-start.16 = (bf16[128,1024]{1,0:T(8,128)(2,1)S(1)}, bf16[128,1024]{1,0:T(8,128)(2,1)S(1)}, u32[]{:S(2)}, u32[]{:S(2)}) collective-permute-start(bf16[128,1024]{1,0:T(8,128)(2,1)S(1)} %shard_map.96.v.refs_5_), channel_id=1, source_target_pairs={{0,1},{1,0},{2,3},{3,2},{4,5},{5,4},{6,7},{7,6},{8,9},{9,8},{10,11... | collective-permute-start | bytes 786440 | tf_op jit(solution)/shard_map/ppermute | solution.py:279
  73.8 1.6 %collective-permute-start.18 = (bf16[128,1024]{1,0:T(8,128)(2,1)S(1)}, bf16[128,1024]{1,0:T(8,128)(2,1)S(1)}, u32[]{:S(2)}, u32[]{:S(2)}) collective-permute-start(bf16[128,1024]{1,0:T(8,128)(2,1)S(1)} %shard_map.99.v.refs_5_), channel_id=1, source_target_pairs={{0,1},{1,0},{2,3},{3,2},{4,5},{5,4},{6,7},{7,6},{8,9},{9,8},{10,11... | collective-permute-start | bytes 786440 | tf_op jit(solution)/shard_map/ppermute | solution.py:279
  76.6 7.0 %collective-permute-start.21 = (bf16[64,1536]{1,0:T(8,128)(2,1)S(1)}, bf16[64,1536]{1,0:T(8,128)(2,1)S(1)}, u32[]{:S(2)}, u32[]{:S(2)}) collective-permute-start(bf16[64,1536]{1,0:T(8,128)(2,1)S(1)} %get-tuple-element.108), channel_id=1, source_target_pairs={{0,4},{4,0},{1,5},{5,1},{2,6},{6,2},{3,7},{7,3},{8,12},{12,8},{9,1... | collective-permute-start | bytes 589832 | tf_op jit(solution)/shard_map/ppermute | solution.py:279
  83.9 1.2 %collective-permute-start.22 = (f32[8,128]{1,0:T(8,128)S(1)}, f32[8,128]{1,0:T(8,128)S(1)}, u32[]{:S(2)}, u32[]{:S(2)}) collective-permute-start(f32[8,128]{1,0:T(8,128)S(1)} %get-tuple-element.111.a), channel_id=1, source_target_pairs={{0,1},{1,0},{2,3},{3,2},{4,5},{5,4},{6,7},{7,6},{8,9},{9,8},{10,11... | collective-permute-start | bytes 12296 | tf_op jit(solution)/shard_map/ppermute | solution.py:279
  85.0 3.6 %collective-permute-start.23 = (f32[8,128]{1,0:T(8,128)S(1)}, f32[8,128]{1,0:T(8,128)S(1)}, u32[]{:S(2)}, u32[]{:S(2)}) collective-permute-start(f32[8,128]{1,0:T(8,128)S(1)} %shard_map.106.refs_5_), channel_id=1, source_target_pairs={{0,2},{1,3},{2,0},{3,1},{4,6},{5,7},{6,4},{7,5},{8,10},{9,11},{10,... | collective-permute-start | bytes 12296 | tf_op jit(solution)/shard_map/ppermute | solution.py:279

commit v5 on v4

--- a/solution.py
+++ b/solution.py
@@ -128,13 +128,6 @@
     return jnp.concatenate([stats, jnp.zeros((120, stats.shape[1]), F32)], axis=0).T[:rows]
 
 
-def added(one, other):
-    def body(a, b, out):
-        out[...] = a[...] + b[...]
-
-    return call(body, [shape(one.shape, one.dtype)], [one, other])
-
-
 def ordered(store, table):
     slots = store.shape[0]
 
@@ -210,46 +203,48 @@
     return call(body, outs, operands)
 
 
-def value_grad_part(normed, grads, result, dims, other, offset):
+def value_grad(normed, terms, dims):
     depth, width = sum(a.shape[0] for a in normed), normed[0].shape[1]
-    blocks = len(normed)
-    size = grads[0].shape[1]
-    count = len(grads)
+    blocks, count = len(normed), len(terms)
+    slots, size = len(terms[0][0]), terms[0][0][0].shape[1]
     block = 256 if width % 256 == 0 else 128
     steps = width // block
-    given = [] if result is None else [result]
 
     def body(*refs):
         norms, refs = refs[:blocks], refs[blocks:]
-        out, made, sems = refs[count + len(given) :]
-        v = jnp.concatenate([r[...] for r in refs[:count]], axis=0)
-        start = half_start(dims[1], other, offset)
+        grads, refs = refs[: count * slots], refs[count * slots :]
+        out, made, sems = refs
         copies = []
-        for i in range(steps):
-            rows = pl.ds(i * block, block)
-            made[rows, :] = lax.dot_general(
-                jnp.concatenate([n[:, i * block : (i + 1) * block] for n in norms], axis=0),
-                v,
-                TN,
-                preferred_element_type=F32,
-            ).astype(BF16)
-            copies.append(
-                pltpu.make_async_copy(made.at[rows], out.at[rows, pl.ds(start, size)], sems.at[i])
-            )
-            copies[-1].start()
+        for k, (_, other, offset) in enumerate(terms):
+            v = jnp.concatenate([r[...] for r in grads[k * slots : (k + 1) * slots]], axis=0)
+            start = half_start(dims[1], other, offset)
+            for i in range(steps):
+                rows = pl.ds(i * block, block)
+                made[k, rows, :] = lax.dot_general(
+                    jnp.concatenate([n[:, i * block : (i + 1) * block] for n in norms], axis=0),
+                    v,
+                    TN,
+                    preferred_element_type=F32,
+                ).astype(BF16)
+                copies.append(
+                    pltpu.make_async_copy(
+                        made.at[k, rows], out.at[rows, pl.ds(start, size)], sems.at[k, i]
+                    )
+                )
+                copies[-1].start()
         for copy in copies:
             copy.wait()
 
+    flat = [g for grads, _, _ in terms for g in grads]
     return pl.pallas_call(
         body,
-        in_specs=[VMEM] * (blocks + count) + [ANY] * len(given),
+        in_specs=[VMEM] * (blocks + len(flat)),
         out_specs=[ANY],
         out_shape=[pltpu.HBM(dims, BF16)],
-        scratch_shapes=[pltpu.VMEM((width, size), BF16), pltpu.SemaphoreType.DMA((steps,))],
-        input_output_aliases={blocks + count: 0} if given else {},
+        scratch_shapes=[pltpu.VMEM((count, width, size), BF16), pltpu.SemaphoreType.DMA((count, steps))],
         compiler_params=pltpu.CompilerParams(vmem_limit_bytes=SCOPED),
         cost_estimate=COST,
-    )(*normed, *grads, *given)
+    )(*normed, *flat)
 
 
 def mixing_weights(slopes, length, own):
@@ -362,21 +357,12 @@
         if slot == 0:
             inputs = run(ordered, store, slot_table.T)
         if last:
-            result = None
-            todo = [(j, side) for j in range(len(chunks)) for side in range(2)]
-
-            def write(j, side):
-                terms = [v[side][j] for v in values]
-                return run(value_grad_part, blocks, terms, result, value_weight.shape[1:], side == 1, chunks[j][0])[0]
-
-            for piece in todo[: len(todo) * 3 // 4]:
-                result = write(*piece)
+            terms = [
+                ([v[side][j] for v in values], side == 1, a) for j, (a, _) in enumerate(chunks) for side in range(2)
+            ]
+            result, = run(value_grad, blocks, terms, value_weight.shape[1:])
         grad, sums = run(width_sums, keep, received, inputs, slot)
-        sums, = run(added, sums, flipped(sums, "dp", 1))
-        grad_stats = [sums] + [flipped(sums, "dp", m) for m in chips]
-        if last:
-            for piece in todo[len(todo) * 3 // 4 :]:
-                result = write(*piece)
+        grad_stats = [sums] + [flipped(sums, "dp", m) for m in range(1, parts)]
         if slot == 0:
             input_stats = grad_stats
         outs = run(finish, grad, upstream, inputs, slot, input_stats, grad_stats, width, 1)

time: 89.9 us -> 89.2 us (level)
  Pallas kernels: 31.3 us -> 28.2 us
  waiting for transfers between devices: 33.9 us -> 35.6 us
    pallas_call x4 -> x1, Pallas kernels: 8.13 us -> 5.07 us  [value_grad(): pl.pallas_call(body, in_specs=[VMEM] * (blocks + len(flat)), out_specs=[A...]
    ppermute x2, waiting for transfers between devices: 10.2 us -> 11.2 us  [on_device(): lax.ppermute(upstream[0], ('section', 'tensor'), [(i * tensors + k, (i -...]
    ppermute x21 -> x23, waiting for transfers between devices: 23.7 us -> 24.4 us  [flipped(): lax.ppermute(array, axis, [(i, i ^ mask) for i in range(lax.axis_size(axi...]
    ppermute x21 -> x23, starting transfers between devices: 16.2 us -> 16.9 us  [flipped(): lax.ppermute(array, axis, [(i, i ^ mask) for i in range(lax.axis_size(axi...]
    pallas_call x28 -> x26, Pallas kernels: 23.1 us -> 23.1 us  [call(): pl.pallas_call(body, in_specs=[first_spec] + [VMEM] * (len(operands) - 1)...]
  transfers between devices with their start and end apart: 24 -> 26, of which waited for: 17 -> 17; matrix products, arithmetic and copies ran while one was open for 0% -> 0% of each run, Pallas kernels for 30% -> 27%
where the time goes in v5:
time: 89.2 us; the launch traced here: 89 us
  waiting for transfers between devices  35.6 us (40%)
  Pallas kernels  28.2 us (32%)
  starting transfers between devices  23.5 us (26%)
  between operations  0.96 us (1%)
    ppermute x23, waiting for transfers between devices, flipped(): lax.ppermute(array, axis, [(i, i ^ mask) for i in range(lax.axis_size(axi...  24.4 us
    pallas_call x26, Pallas kernels, call(): pl.pallas_call(body, in_specs=[first_spec] + [VMEM] * (len(operands) - 1)...  23.1 us
    ppermute x23, starting transfers between devices, flipped(): lax.ppermute(array, axis, [(i, i ^ mask) for i in range(lax.axis_size(axi...  16.9 us
    ppermute x2, waiting for transfers between devices, on_device(): lax.ppermute(upstream[0], ('section', 'tensor'), [(i * tensors + k, (i -...  11.2 us
    pallas_call x1, Pallas kernels, value_grad(): pl.pallas_call(body, in_specs=[VMEM] * (blocks + len(flat)), out_specs=[A...  5.07 us
    ppermute x1, starting transfers between devices, on_device(): lax.ppermute(after(parked[0], kept[-1][1]), 'section', [(i, sections - 1...  3.81 us
    ppermute x2, starting transfers between devices, on_device(): lax.ppermute(upstream[0], ('section', 'tensor'), [(i * tensors + k, (i -...  2.76 us
  transfers between devices with their start and end apart: 26, of which 17 were waited for; matrix products, arithmetic and copies ran while one was open for 0% of the time, Pallas kernels for 27%

profile of v5, /device:TPU:0, one launch (start us, length us, event | category | flops | bytes accessed | tf_op | source)
XLA Modules:
  0.0 89.0 jit_solution(10537595339032979912)
XLA Ops:
  0.6 3.0 %collective-permute-start = (bf16[64,1536]{1,0:T(8,128)(2,1)}, bf16[64,1536]{1,0:T(8,128)(2,1)S(1)}, u32[]{:S(2)}, u32[]{:S(2)}) collective-permute-start(bf16[64,1536]{1,0:T(8,128)(2,1)} %bitcast.27), channel_id=1, source_target_pairs={{0,4},{4,0},{1,5},{5,1},{2,6},{6,2},{3,7},{7,3},{8,12},{12,8},{9,1... | collective-permute-start | bytes 589832 | tf_op jit(solution)/shard_map/ppermute | solution.py:274
  3.6 0.7 copy-done.3
  4.3 1.0 %shard_map.77.refs_2_ = bf16[16,128,128]{2,1,0:T(8,128)(2,1)S(1)} custom-call(f32[1,32]{1,0:T(1,128)S(1)} %bitcast.33), custom_call_target="tpu_custom_call" | custom-call | flops 8000000000 | bytes 100000000 | tf_op jit(solution)/shard_map/pallas_call | solution.py:22
  5.3 3.5 %collective-permute-done.refs_1_ = bf16[64,1536]{1,0:T(8,128)(2,1)S(1)} collective-permute-done((bf16[64,1536]{1,0:T(8,128)(2,1)}, bf16[64,1536]{1,0:T(8,128)(2,1)S(1)}, u32[]{:S(2)}, u32[]{:S(2)}) %collective-permute-start) | collective-permute-done | bytes 196640 | tf_op jit(solution)/shard_map/ppermute | solution.py:274
  8.9 1.1 %shard_map.78 = bf16[128,1024]{1,0:T(8,128)(2,1)S(1)} custom-call(bf16[64,1536]{1,0:T(8,128)(2,1)S(1)} %bitcast.28, bf16[64,1536]{1,0:T(8,128)(2,1)S(1)} %collective-permute-done.refs_1_, bf16[4096,1536]{1,0:T(8,128)(2,1)S(1)} %bitcast.9), custom_call_target="tpu_custom_call" | custom-call | flops 8000000000 | bytes 100000000 | tf_op jit(solution)/shard_map/pallas_call | solution.py:22
  10.1 1.1 %shard_map.79 = bf16[128,1024]{1,0:T(8,128)(2,1)S(1)} custom-call(bf16[64,1536]{1,0:T(8,128)(2,1)S(1)} %bitcast.29, bf16[64,1536]{1,0:T(8,128)(2,1)S(1)} %collective-permute-done.refs_1_, bf16[4096,1536]{1,0:T(8,128)(2,1)S(1)} %bitcast.10), custom_call_target="tpu_custom_call" | custom-call | flops 8000000000 | bytes 100000000 | tf_op jit(solution)/shard_map/pallas_call | solution.py:22
  11.8 1.1 %shard_map.80 = (f32[128,1024]{1,0:T(8,128)S(1)}, bf16[128,1024]{1,0:T(8,128)(2,1)S(1)}) custom-call(bf16[64,1536]{1,0:T(8,128)(2,1)S(1)} %bitcast.30, bf16[64,1536]{1,0:T(8,128)(2,1)S(1)} %collective-permute-done.refs_1_, bf16[4096,1536]{1,0:T(8,128)(2,1)S(1)} %bitcast.11, bf16[128,1024]{1,0:T(8,128)(2,1)S(1)} %collective-permute-done.1.refs_3_), custom_call_target="tpu_custom_call" | custom-call | flops 8000000000 | bytes 100000000 | tf_op jit(solution)/shard_map/pallas_call | solution.py:22
  12.9 1.7 %collective-permute-start.3 = (bf16[128,1024]{1,0:T(8,128)(2,1)S(1)}, bf16[128,1024]{1,0:T(8,128)(2,1)S(1)}, u32[]{:S(2)}, u32[]{:S(2)}) collective-permute-start(bf16[128,1024]{1,0:T(8,128)(2,1)S(1)} %get-tuple-element.59), channel_id=1, source_target_pairs={{0,2},{1,3},{2,0},{3,1},{4,6},{5,7},{6,4},{7,5},{8,10},{9,11},{10,... | collective-permute-start | bytes 786440 | tf_op jit(solution)/shard_map/ppermute | solution.py:274
  14.7 1.1 %shard_map.81 = (f32[128,1024]{1,0:T(8,128)S(1)}, bf16[128,1024]{1,0:T(8,128)(2,1)S(1)}) custom-call(bf16[64,1536]{1,0:T(8,128)(2,1)S(1)} %bitcast.31, bf16[64,1536]{1,0:T(8,128)(2,1)S(1)} %collective-permute-done.refs_1_, bf16[4096,1536]{1,0:T(8,128)(2,1)S(1)} %bitcast.12, bf16[128,1024]{1,0:T(8,128)(2,1)S(1)} %collective-permute-done.2.refs_3_), custom_call_target="tpu_custom_call" | custom-call | flops 8000000000 | bytes 100000000 | tf_op jit(solution)/shard_map/pallas_call | solution.py:22
  16.3 3.8 %collective-permute-start.7 = (bf16[2,64,1536]{2,1,0:T(8,128)(2,1)S(1)}, bf16[2,64,1536]{2,1,0:T(8,128)(2,1)S(1)}, u32[]{:S(2)}, u32[]{:S(2)}) collective-permute-start(bf16[2,64,1536]{2,1,0:T(8,128)(2,1)S(1)} %bitcast.34), channel_id=1, source_target_pairs={{0,24},{8,16},{16,8},{24,0},{1,25},{9,17},{17,9},{25,1},{2,26},{10... | collective-permute-start | bytes 1179656 | tf_op jit(solution)/shard_map/ppermute | solution.py:341
  20.1 2.1 %collective-permute-done.3.refs_1_ = bf16[128,1024]{1,0:T(8,128)(2,1)S(1)} collective-permute-done((bf16[128,1024]{1,0:T(8,128)(2,1)S(1)}, bf16[128,1024]{1,0:T(8,128)(2,1)S(1)}, u32[]{:S(2)}, u32[]{:S(2)}) %collective-permute-start.3) | collective-permute-done | bytes 262176 | tf_op jit(solution)/shard_map/ppermute | solution.py:274
  22.6 1.2 %shard_map.83.refs_0_ = f32[128,1536]{1,0:T(8,128)S(1)} custom-call(bf16[128,1024]{1,0:T(8,128)(2,1)S(1)} %shard_map.82.v.refs_4_, bf16[1536,4096]{1,0:T(8,128)(2,1)S(1)} %bitcast.19), custom_call_target="tpu_custom_call" | custom-call | flops 8000000000 | bytes 100000000 | tf_op jit(solution)/shard_map/pallas_call | solution.py:22
  24.0 1.2 %shard_map.84.refs_0_ = f32[128,1536]{1,0:T(8,128)S(1)} custom-call(bf16[128,1024]{1,0:T(8,128)(2,1)S(1)} %collective-permute-done.4.v.refs_6_, bf16[1536,4096]{1,0:T(8,128)(2,1)S(1)} %bitcast.20, f32[128,1536]{1,0:T(8,128)S(1)} %shard_map.83.refs_0_), custom_call_target="tpu_custom_call" | custom-call | flops 8000000000 | bytes 100000000 | tf_op jit(solution)/shard_map/pallas_call | solution.py:22
  25.2 1.7 %collective-permute-done.5.refs_1_ = bf16[128,1024]{1,0:T(8,128)(2,1)S(1)} collective-permute-done((bf16[128,1024]{1,0:T(8,128)(2,1)S(1)}, bf16[128,1024]{1,0:T(8,128)(2,1)S(1)}, u32[]{:S(2)}, u32[]{:S(2)}) %collective-permute-start.5) | collective-permute-done | bytes 262176 | tf_op jit(solution)/shard_map/ppermute | solution.py:274
  27.2 1.2 %shard_map.86.refs_0_ = f32[128,1536]{1,0:T(8,128)S(1)} custom-call(bf16[128,1024]{1,0:T(8,128)(2,1)S(1)} %shard_map.85.v.refs_8_, bf16[1536,4096]{1,0:T(8,128)(2,1)S(1)} %bitcast.21, f32[128,1536]{1,0:T(8,128)S(1)} %shard_map.84.refs_0_), custom_call_target="tpu_custom_call" | custom-call | flops 8000000000 | bytes 100000000 | tf_op jit(solution)/shard_map/pallas_call | solution.py:22
  28.7 1.2 %shard_map.87 = (f32[64,1536]{1,0:T(8,128)S(1)}, bf16[64,1536]{1,0:T(8,128)(2,1)S(1)}) custom-call(bf16[128,1024]{1,0:T(8,128)(2,1)S(1)} %collective-permute-done.6.v.refs_10_, bf16[1536,4096]{1,0:T(8,128)(2,1)S(1)} %bitcast.22, f32[128,1536]{1,0:T(8,128)S(1)} %shard_map.86.refs_0_), custom_call_target="tpu_custom_call" | custom-call | flops 8000000000 | bytes 100000000 | tf_op jit(solution)/shard_map/pallas_call | solution.py:22
  29.9 1.7 %collective-permute-start.8 = (bf16[64,1536]{1,0:T(8,128)(2,1)S(1)}, bf16[64,1536]{1,0:T(8,128)(2,1)S(1)}, u32[]{:S(2)}, u32[]{:S(2)}) collective-permute-start(bf16[64,1536]{1,0:T(8,128)(2,1)S(1)} %get-tuple-element.72), channel_id=1, source_target_pairs={{0,4},{4,0},{1,5},{5,1},{2,6},{6,2},{3,7},{7,3},{8,12},{12,8},{9,1... | collective-permute-start | bytes 589832 | tf_op jit(solution)/shard_map/ppermute | solution.py:274
  31.6 0.6 shard_map.88
  32.2 4.8 %collective-permute-done.8.refs_2_ = bf16[64,1536]{1,0:T(8,128)(2,1)S(1)} collective-permute-done((bf16[64,1536]{1,0:T(8,128)(2,1)S(1)}, bf16[64,1536]{1,0:T(8,128)(2,1)S(1)}, u32[]{:S(2)}, u32[]{:S(2)}) %collective-permute-start.8) | collective-permute-done | bytes 196640 | tf_op jit(solution)/shard_map/ppermute | solution.py:274
  37.3 0.6 collective-permute-start.11
  37.9 1.1 %collective-permute-start.10 = (f32[8,128]{1,0:T(8,128)S(1)}, f32[8,128]{1,0:T(8,128)S(1)}, u32[]{:S(2)}, u32[]{:S(2)}) collective-permute-start(f32[8,128]{1,0:T(8,128)S(1)} %get-tuple-element.74.refs_3_.refs_7_), channel_id=1, source_target_pairs={{0,2},{1,3},{2,0},{3,1},{4,6},{5,7},{6,4},{7,5},{8,10},{9,11},{10,... | collective-permute-start | bytes 12296 | tf_op jit(solution)/shard_map/ppermute | solution.py:274
  39.2 1.2 %collective-permute-done.11.refs_6_.refs_10_ = f32[8,128]{1,0:T(8,128)S(1)} collective-permute-done((f32[8,128]{1,0:T(8,128)S(1)}, f32[8,128]{1,0:T(8,128)S(1)}, u32[]{:S(2)}, u32[]{:S(2)}) %collective-permute-start.11) | collective-permute-done | bytes 4128 | tf_op jit(solution)/shard_map/ppermute | solution.py:274
  40.3 1.2 %collective-permute-done.10.refs_5_.refs_9_ = f32[8,128]{1,0:T(8,128)S(1)} collective-permute-done((f32[8,128]{1,0:T(8,128)S(1)}, f32[8,128]{1,0:T(8,128)S(1)}, u32[]{:S(2)}, u32[]{:S(2)}) %collective-permute-start.10) | collective-permute-done | bytes 4128 | tf_op jit(solution)/shard_map/ppermute | solution.py:274
  42.0 1.3 %collective-permute-start.12 = (bf16[64,1536]{1,0:T(8,128)(2,1)S(1)}, bf16[64,1536]{1,0:T(8,128)(2,1)S(1)}, u32[]{:S(2)}, u32[]{:S(2)}) collective-permute-start(bf16[64,1536]{1,0:T(8,128)(2,1)S(1)} %get-tuple-element.75), channel_id=1, source_target_pairs={{8,0},{12,4},{16,8},{20,12},{24,16},{28,20},{9,1},{13,5},{17,9},{2... | collective-permute-start | bytes 589832 | tf_op jit(solution)/shard_map/ppermute | solution.py:314
  43.3 1.5 %collective-permute-start.13 = (bf16[64,1536]{1,0:T(8,128)(2,1)S(1)}, bf16[64,1536]{1,0:T(8,128)(2,1)S(1)}, u32[]{:S(2)}, u32[]{:S(2)}) collective-permute-start(bf16[64,1536]{1,0:T(8,128)(2,1)S(1)} %get-tuple-element.75), channel_id=1, source_target_pairs={{8,4},{12,0},{16,12},{20,8},{24,20},{28,16},{9,5},{13,1},{17,13},{... | collective-permute-start | bytes 589832 | tf_op jit(solution)/shard_map/ppermute | solution.py:314
  44.8 6.9 %collective-permute-done.12.refs_0_.refs_2_ = bf16[64,1536]{1,0:T(8,128)(2,1)S(1)} collective-permute-done((bf16[64,1536]{1,0:T(8,128)(2,1)S(1)}, bf16[64,1536]{1,0:T(8,128)(2,1)S(1)}, u32[]{:S(2)}, u32[]{:S(2)}) %collective-permute-start.12) | collective-permute-done | bytes 196640 | tf_op jit(solution)/shard_map/ppermute | solution.py:314
  51.6 4.3 %collective-permute-done.13.refs_1_ = bf16[64,1536]{1,0:T(8,128)(2,1)S(1)} collective-permute-done((bf16[64,1536]{1,0:T(8,128)(2,1)S(1)}, bf16[64,1536]{1,0:T(8,128)(2,1)S(1)}, u32[]{:S(2)}, u32[]{:S(2)}) %collective-permute-start.13) | collective-permute-done | bytes 196640 | tf_op jit(solution)/shard_map/ppermute | solution.py:314
  55.9 1.1 %shard_map.91 = bf16[128,1024]{1,0:T(8,128)(2,1)S(1)} custom-call(bf16[64,1536]{1,0:T(8,128)(2,1)S(1)} %collective-permute-done.12.refs_0_.refs_2_, bf16[64,1536]{1,0:T(8,128)(2,1)S(1)} %collective-permute-done.13.refs_1_, bf16[4096,1536]{1,0:T(8,128)(2,1)S(1)} %bitcast.13), custom_call_target="tpu_custom_call" | custom-call | flops 8000000000 | bytes 100000000 | tf_op jit(solution)/shard_map/pallas_call | solution.py:22
  57.2 1.1 %shard_map.92 = bf16[128,1024]{1,0:T(8,128)(2,1)S(1)} custom-call(bf16[64,1536]{1,0:T(8,128)(2,1)S(1)} %collective-permute-done.12.refs_0_.refs_2_, bf16[64,1536]{1,0:T(8,128)(2,1)S(1)} %collective-permute-done.13.refs_1_, bf16[4096,1536]{1,0:T(8,128)(2,1)S(1)} %bitcast.14), custom_call_target="tpu_custom_call" | custom-call | flops 8000000000 | bytes 100000000 | tf_op jit(solution)/shard_map/pallas_call | solution.py:22
  58.9 1.1 %shard_map.93 = (f32[128,1024]{1,0:T(8,128)S(1)}, bf16[128,1024]{1,0:T(8,128)(2,1)S(1)}) custom-call(bf16[64,1536]{1,0:T(8,128)(2,1)S(1)} %collective-permute-done.12.refs_0_.refs_2_, bf16[64,1536]{1,0:T(8,128)(2,1)S(1)} %collective-permute-done.13.refs_1_, bf16[4096,1536]{1,0:T(8,128)(2,1)S(1)} %bitcast.15, ...), custom_call_target="tpu_custom_call" | custom-call | flops 8000000000 | bytes 100000000 | tf_op jit(solution)/shard_map/pallas_call | solution.py:22
  60.5 1.1 %shard_map.94 = (f32[128,1024]{1,0:T(8,128)S(1)}, bf16[128,1024]{1,0:T(8,128)(2,1)S(1)}) custom-call(bf16[64,1536]{1,0:T(8,128)(2,1)S(1)} %collective-permute-done.12.refs_0_.refs_2_, bf16[64,1536]{1,0:T(8,128)(2,1)S(1)} %collective-permute-done.13.refs_1_, bf16[4096,1536]{1,0:T(8,128)(2,1)S(1)} %bitcast.16, ...), custom_call_target="tpu_custom_call" | custom-call | flops 8000000000 | bytes 100000000 | tf_op jit(solution)/shard_map/pallas_call | solution.py:22
  61.7 0.6 collective-permute-start.20
  62.3 1.5 %collective-permute-start.21 = (bf16[64,1536]{1,0:T(8,128)(2,1)S(1)}, bf16[64,1536]{1,0:T(8,128)(2,1)S(1)}, u32[]{:S(2)}, u32[]{:S(2)}) collective-permute-start(bf16[64,1536]{1,0:T(8,128)(2,1)S(1)} %get-tuple-element.95.refs_2_), channel_id=1, source_target_pairs={{0,4},{4,0},{1,5},{5,1},{2,6},{6,2},{3,7},{7,3},{8,12},{12,8},{9,1... | collective-permute-start | bytes 589832 | tf_op jit(solution)/shard_map/ppermute | solution.py:274
  63.8 1.6 %collective-permute-start.18 = (bf16[128,1024]{1,0:T(8,128)(2,1)S(1)}, bf16[128,1024]{1,0:T(8,128)(2,1)S(1)}, u32[]{:S(2)}, u32[]{:S(2)}) collective-permute-start(bf16[128,1024]{1,0:T(8,128)(2,1)S(1)} %get-tuple-element.87), channel_id=1, source_target_pairs={{0,2},{1,3},{2,0},{3,1},{4,6},{5,7},{6,4},{7,5},{8,10},{9,11},{10,... | collective-permute-start | bytes 786440 | tf_op jit(solution)/shard_map/ppermute | solution.py:274
  65.3 3.9 %collective-permute-done.16.refs_1_ = bf16[128,1024]{1,0:T(8,128)(2,1)S(1)} collective-permute-done((bf16[128,1024]{1,0:T(8,128)(2,1)S(1)}, bf16[128,1024]{1,0:T(8,128)(2,1)S(1)}, u32[]{:S(2)}, u32[]{:S(2)}) %collective-permute-start.16) | collective-permute-done | bytes 262176 | tf_op jit(solution)/shard_map/ppermute | solution.py:274
  69.6 1.2 %shard_map.96.refs_0_ = f32[128,1536]{1,0:T(8,128)S(1)} custom-call(bf16[128,1024]{1,0:T(8,128)(2,1)S(1)} %shard_map.95.v.refs_5_, bf16[1536,4096]{1,0:T(8,128)(2,1)S(1)} %bitcast.23), custom_call_target="tpu_custom_call" | custom-call | flops 8000000000 | bytes 100000000 | tf_op jit(solution)/shard_map/pallas_call | solution.py:22
  71.1 1.2 %shard_map.97.refs_0_ = f32[128,1536]{1,0:T(8,128)S(1)} custom-call(bf16[128,1024]{1,0:T(8,128)(2,1)S(1)} %collective-permute-done.17.v.refs_7_, bf16[1536,4096]{1,0:T(8,128)(2,1)S(1)} %bitcast.24, f32[128,1536]{1,0:T(8,128)S(1)} %shard_map.96.refs_0_), custom_call_target="tpu_custom_call" | custom-call | flops 8000000000 | bytes 100000000 | tf_op jit(solution)/shard_map/pallas_call | solution.py:22
  72.3 1.7 %collective-permute-done.18.refs_1_ = bf16[128,1024]{1,0:T(8,128)(2,1)S(1)} collective-permute-done((bf16[128,1024]{1,0:T(8,128)(2,1)S(1)}, bf16[128,1024]{1,0:T(8,128)(2,1)S(1)}, u32[]{:S(2)}, u32[]{:S(2)}) %collective-permute-start.18) | collective-permute-done | bytes 262176 | tf_op jit(solution)/shard_map/ppermute | solution.py:274
  74.3 1.2 %shard_map.99.refs_0_ = f32[128,1536]{1,0:T(8,128)S(1)} custom-call(bf16[128,1024]{1,0:T(8,128)(2,1)S(1)} %shard_map.98.v.refs_9_, bf16[1536,4096]{1,0:T(8,128)(2,1)S(1)} %bitcast.25, f32[128,1536]{1,0:T(8,128)S(1)} %shard_map.97.refs_0_), custom_call_target="tpu_custom_call" | custom-call | flops 8000000000 | bytes 100000000 | tf_op jit(solution)/shard_map/pallas_call | solution.py:22
  75.8 1.2 %shard_map.100 = (f32[64,1536]{1,0:T(8,128)S(1)}, bf16[64,1536]{1,0:T(8,128)(2,1)S(1)}) custom-call(bf16[128,1024]{1,0:T(8,128)(2,1)S(1)} %collective-permute-done.19.v.refs_11_, bf16[1536,4096]{1,0:T(8,128)(2,1)S(1)} %bitcast.26, f32[128,1536]{1,0:T(8,128)S(1)} %shard_map.99.refs_0_), custom_call_target="tpu_custom_call" | custom-call | flops 8000000000 | bytes 100000000 | tf_op jit(solution)/shard_map/pallas_call | solution.py:22
  77.0 0.6 collective-permute-start.22
  77.6 5.1 %shard_map.101 = bf16[1536,4096]{1,0:T(8,128)(2,1)} custom-call(bf16[64,1536]{1,0:T(8,128)(2,1)S(1)} %get-tuple-element.93.refs_0_, bf16[64,1536]{1,0:T(8,128)(2,1)S(1)} %collective-permute-done.20.refs_1_, bf16[64,1536]{1,0:T(8,128)(2,1)S(1)} %get-tuple-element.95.refs_2_, bf16[64,1536]{1,0:T(8,128)(2,1)S(1)} %collective-permute-done.21.refs_3_, ...), custom_call_target="tpu_custom_call" | custom-call | flops 8000000000 | bytes 100000000 | tf_op jit(solution)/shard_map/pallas_call | solution.py:239
  82.7 1.4 %collective-permute-done.22.refs_2_ = bf16[64,1536]{1,0:T(8,128)(2,1)S(1)} collective-permute-done((bf16[64,1536]{1,0:T(8,128)(2,1)S(1)}, bf16[64,1536]{1,0:T(8,128)(2,1)S(1)}, u32[]{:S(2)}, u32[]{:S(2)}) %collective-permute-start.22) | collective-permute-done | bytes 196640 | tf_op jit(solution)/shard_map/ppermute | solution.py:274
  84.2 1.0 %collective-permute-start.24 = (f32[8,128]{1,0:T(8,128)S(1)}, f32[8,128]{1,0:T(8,128)S(1)}, u32[]{:S(2)}, u32[]{:S(2)}) collective-permute-start(f32[8,128]{1,0:T(8,128)S(1)} %get-tuple-element.99.refs_7_), channel_id=1, source_target_pairs={{0,2},{1,3},{2,0},{3,1},{4,6},{5,7},{6,4},{7,5},{8,10},{9,11},{10,... | collective-permute-start | bytes 12296 | tf_op jit(solution)/shard_map/ppermute | solution.py:274
  85.2 0.9 collective-permute-start.23
  86.1 1.2 %collective-permute-done.25.refs_10_ = f32[8,128]{1,0:T(8,128)S(1)} collective-permute-done((f32[8,128]{1,0:T(8,128)S(1)}, f32[8,128]{1,0:T(8,128)S(1)}, u32[]{:S(2)}, u32[]{:S(2)}) %collective-permute-start.25) | collective-permute-done | bytes 4128 | tf_op jit(solution)/shard_map/ppermute | solution.py:274
  87.3 0.7 collective-permute-done.24.refs_9_
  87.9 1.1 %shard_map.103 = bf16[64,1536]{1,0:T(8,128)(2,1)} custom-call(f32[64,1536]{1,0:T(8,128)S(1)} %get-tuple-element.98.grad_ref, bf16[64,1536]{1,0:T(8,128)(2,1)S(1)} %get-tuple-element.69.refs_0_, bf16[64,1536]{1,0:T(8,128)(2,1)S(1)} %get-tuple-element.71.refs_1_, bf16[64,1536]{1,0:T(8,128)(2,1)S(1)} %collective-permute-done.12.refs_0_.refs_2_, ...), custom_call_target="tpu_custom_call" | custom-call | flops 8000000000 | bytes 100000000 | tf_op jit(solution)/shard_map/pallas_call | solution.py:22
  (48 shorter events, 6.1 us)
Async XLA Ops:
  0.6 8.1 %collective-permute-start = (bf16[64,1536]{1,0:T(8,128)(2,1)}, bf16[64,1536]{1,0:T(8,128)(2,1)S(1)}, u32[]{:S(2)}, u32[]{:S(2)}) collective-permute-start(bf16[64,1536]{1,0:T(8,128)(2,1)} %bitcast.27), channel_id=1, source_target_pairs={{0,4},{4,0},{1,5},{5,1},{2,6},{6,2},{3,7},{7,3},{8,12},{12,8},{9,1... | collective-permute-start | bytes 589832 | tf_op jit(solution)/shard_map/ppermute | solution.py:274
  3.6 0.7 copy-start.3
  4.3 4.6 %copy-start.1 = (bf16[1,4096,1536]{2,1,0:T(8,128)(2,1)S(1)}, bf16[1,4096,1536]{2,1,0:T(8,128)(2,1)}, u32[]{:S(2)}) copy-start(bf16[1,4096,1536]{2,1,0:T(8,128)(2,1)} %param.10) | copy-start | bytes 37748740
  4.3 4.6 %copy-start.2 = (bf16[1,64,1536]{2,1,0:T(8,128)(2,1)S(1)}, bf16[1,64,1536]{2,1,0:T(8,128)(2,1)}, u32[]{:S(2)}) copy-start(bf16[1,64,1536]{2,1,0:T(8,128)(2,1)} %param.7) | copy-start | bytes 589828
  10.0 1.8 %collective-permute-start.1 = (bf16[128,1024]{1,0:T(8,128)(2,1)S(1)}, bf16[128,1024]{1,0:T(8,128)(2,1)S(1)}, u32[]{:S(2)}, u32[]{:S(2)}) collective-permute-start(bf16[128,1024]{1,0:T(8,128)(2,1)S(1)} %shard_map.78), channel_id=1, source_target_pairs={{0,1},{1,0},{2,3},{3,2},{4,5},{5,4},{6,7},{7,6},{8,9},{9,8},{10,11... | collective-permute-start | bytes 786440 | tf_op jit(solution)/shard_map/ppermute | solution.py:274
  11.2 3.4 %collective-permute-start.2 = (bf16[128,1024]{1,0:T(8,128)(2,1)S(1)}, bf16[128,1024]{1,0:T(8,128)(2,1)S(1)}, u32[]{:S(2)}, u32[]{:S(2)}) collective-permute-start(bf16[128,1024]{1,0:T(8,128)(2,1)S(1)} %shard_map.79), channel_id=1, source_target_pairs={{0,1},{1,0},{2,3},{3,2},{4,5},{5,4},{6,7},{7,6},{8,9},{9,8},{10,11... | collective-permute-start | bytes 786440 | tf_op jit(solution)/shard_map/ppermute | solution.py:274
  12.9 3.3 %copy-start.4 = (bf16[1,2,64,1536]{3,2,1,0:T(8,128)(2,1)S(1)}, bf16[1,2,64,1536]{3,2,1,0:T(8,128)(2,1)}, u32[]{:S(2)}) copy-start(bf16[1,2,64,1536]{3,2,1,0:T(8,128)(2,1)} %param.6) | copy-start | bytes 1179652
  12.9 9.2 %collective-permute-start.3 = (bf16[128,1024]{1,0:T(8,128)(2,1)S(1)}, bf16[128,1024]{1,0:T(8,128)(2,1)S(1)}, u32[]{:S(2)}, u32[]{:S(2)}) collective-permute-start(bf16[128,1024]{1,0:T(8,128)(2,1)S(1)} %get-tuple-element.59), channel_id=1, source_target_pairs={{0,2},{1,3},{2,0},{3,1},{4,6},{5,7},{6,4},{7,5},{8,10},{9,11},{10,... | collective-permute-start | bytes 786440 | tf_op jit(solution)/shard_map/ppermute | solution.py:274
  15.8 11.1 %collective-permute-start.5 = (bf16[128,1024]{1,0:T(8,128)(2,1)S(1)}, bf16[128,1024]{1,0:T(8,128)(2,1)S(1)}, u32[]{:S(2)}, u32[]{:S(2)}) collective-permute-start(bf16[128,1024]{1,0:T(8,128)(2,1)S(1)} %get-tuple-element.63), channel_id=1, source_target_pairs={{0,2},{1,3},{2,0},{3,1},{4,6},{5,7},{6,4},{7,5},{8,10},{9,11},{10,... | collective-permute-start | bytes 786440 | tf_op jit(solution)/shard_map/ppermute | solution.py:274
  16.3 6.3 %slice-start = ((s8[12582912]{0:T(1024)(128)(4,1)}), s8[4194304]{0:T(1024)(128)(4,1)S(1)}, s32[]{:S(2)}) async-start(s8[12582912]{0:T(1024)(128)(4,1)} %bitcast.17), calls=%async_computation | async-start | bytes 8388608
  16.3 6.3 %slice-start.1 = ((s8[12582912]{0:T(1024)(128)(4,1)}), s8[4194304]{0:T(1024)(128)(4,1)S(1)}, s32[]{:S(2)}) async-start(s8[12582912]{0:T(1024)(128)(4,1)} %bitcast.17), calls=%async_computation.1 | async-start | bytes 8388608
  16.3 6.3 %slice-start.2 = ((s8[12582912]{0:T(1024)(128)(4,1)}), s8[4194304]{0:T(1024)(128)(4,1)S(1)}, s32[]{:S(2)}) async-start(s8[12582912]{0:T(1024)(128)(4,1)} %bitcast.17), calls=%async_computation.2 | async-start | bytes 8388608
  16.3 15.3 %collective-permute-start.7 = (bf16[2,64,1536]{2,1,0:T(8,128)(2,1)S(1)}, bf16[2,64,1536]{2,1,0:T(8,128)(2,1)S(1)}, u32[]{:S(2)}, u32[]{:S(2)}) collective-permute-start(bf16[2,64,1536]{2,1,0:T(8,128)(2,1)S(1)} %bitcast.34), channel_id=1, source_target_pairs={{0,24},{8,16},{16,8},{24,0},{1,25},{9,17},{17,9},{25,1},{2,26},{10... | collective-permute-start | bytes 1179656 | tf_op jit(solution)/shard_map/ppermute | solution.py:341
  22.4 1.6 %collective-permute-start.4 = (bf16[128,1024]{1,0:T(8,128)(2,1)S(1)}, bf16[128,1024]{1,0:T(8,128)(2,1)S(1)}, u32[]{:S(2)}, u32[]{:S(2)}) collective-permute-start(bf16[128,1024]{1,0:T(8,128)(2,1)S(1)} %shard_map.82.v.refs_4_), channel_id=1, source_target_pairs={{0,1},{1,0},{2,3},{3,2},{4,5},{5,4},{6,7},{7,6},{8,9},{9,8},{10,11... | collective-permute-start | bytes 786440 | tf_op jit(solution)/shard_map/ppermute | solution.py:274
  27.1 1.6 %collective-permute-start.6 = (bf16[128,1024]{1,0:T(8,128)(2,1)S(1)}, bf16[128,1024]{1,0:T(8,128)(2,1)S(1)}, u32[]{:S(2)}, u32[]{:S(2)}) collective-permute-start(bf16[128,1024]{1,0:T(8,128)(2,1)S(1)} %shard_map.85.v.refs_8_), channel_id=1, source_target_pairs={{0,1},{1,0},{2,3},{3,2},{4,5},{5,4},{6,7},{7,6},{8,9},{9,8},{10,11... | collective-permute-start | bytes 786440 | tf_op jit(solution)/shard_map/ppermute | solution.py:274
  28.4 3.2 %copy-start = (s32[4,2]{0,1:T(2,128)S(1)}, s32[4,2]{0,1:T(2,128)}, u32[]{:S(2)}) copy-start(s32[4,2]{0,1:T(2,128)} %param.8) | copy-start | bytes 100
  29.9 7.0 %collective-permute-start.8 = (bf16[64,1536]{1,0:T(8,128)(2,1)S(1)}, bf16[64,1536]{1,0:T(8,128)(2,1)S(1)}, u32[]{:S(2)}, u32[]{:S(2)}) collective-permute-start(bf16[64,1536]{1,0:T(8,128)(2,1)S(1)} %get-tuple-element.72), channel_id=1, source_target_pairs={{0,4},{4,0},{1,5},{5,1},{2,6},{6,2},{3,7},{7,3},{8,12},{12,8},{9,1... | collective-permute-start | bytes 589832 | tf_op jit(solution)/shard_map/ppermute | solution.py:274
  37.3 3.0 %collective-permute-start.11 = (f32[8,128]{1,0:T(8,128)S(1)}, f32[8,128]{1,0:T(8,128)S(1)}, u32[]{:S(2)}, u32[]{:S(2)}) collective-permute-start(f32[8,128]{1,0:T(8,128)S(1)} %get-tuple-element.74.refs_3_.refs_7_), channel_id=1, source_target_pairs={{0,3},{1,2},{2,1},{3,0},{4,7},{5,6},{6,5},{7,4},{8,11},{9,10},{10,... | collective-permute-start | bytes 12296 | tf_op jit(solution)/shard_map/ppermute | solution.py:274
  37.9 3.6 %collective-permute-start.10 = (f32[8,128]{1,0:T(8,128)S(1)}, f32[8,128]{1,0:T(8,128)S(1)}, u32[]{:S(2)}, u32[]{:S(2)}) collective-permute-start(f32[8,128]{1,0:T(8,128)S(1)} %get-tuple-element.74.refs_3_.refs_7_), channel_id=1, source_target_pairs={{0,2},{1,3},{2,0},{3,1},{4,6},{5,7},{6,4},{7,5},{8,10},{9,11},{10,... | collective-permute-start | bytes 12296 | tf_op jit(solution)/shard_map/ppermute | solution.py:274
  39.0 2.5 %collective-permute-start.9 = (f32[8,128]{1,0:T(8,128)S(1)}, f32[8,128]{1,0:T(8,128)S(1)}, u32[]{:S(2)}, u32[]{:S(2)}) collective-permute-start(f32[8,128]{1,0:T(8,128)S(1)} %get-tuple-element.74.refs_3_.refs_7_), channel_id=1, source_target_pairs={{0,1},{1,0},{2,3},{3,2},{4,5},{5,4},{6,7},{7,6},{8,9},{9,8},{10,11... | collective-permute-start | bytes 12296 | tf_op jit(solution)/shard_map/ppermute | solution.py:274
  42.0 9.6 %collective-permute-start.12 = (bf16[64,1536]{1,0:T(8,128)(2,1)S(1)}, bf16[64,1536]{1,0:T(8,128)(2,1)S(1)}, u32[]{:S(2)}, u32[]{:S(2)}) collective-permute-start(bf16[64,1536]{1,0:T(8,128)(2,1)S(1)} %get-tuple-element.75), channel_id=1, source_target_pairs={{8,0},{12,4},{16,8},{20,12},{24,16},{28,20},{9,1},{13,5},{17,9},{2... | collective-permute-start | bytes 589832 | tf_op jit(solution)/shard_map/ppermute | solution.py:314
  43.3 12.7 %collective-permute-start.13 = (bf16[64,1536]{1,0:T(8,128)(2,1)S(1)}, bf16[64,1536]{1,0:T(8,128)(2,1)S(1)}, u32[]{:S(2)}, u32[]{:S(2)}) collective-permute-start(bf16[64,1536]{1,0:T(8,128)(2,1)S(1)} %get-tuple-element.75), channel_id=1, source_target_pairs={{8,4},{12,0},{16,12},{20,8},{24,20},{28,16},{9,5},{13,1},{17,13},{... | collective-permute-start | bytes 589832 | tf_op jit(solution)/shard_map/ppermute | solution.py:314
  57.1 1.8 %collective-permute-start.14 = (bf16[128,1024]{1,0:T(8,128)(2,1)S(1)}, bf16[128,1024]{1,0:T(8,128)(2,1)S(1)}, u32[]{:S(2)}, u32[]{:S(2)}) collective-permute-start(bf16[128,1024]{1,0:T(8,128)(2,1)S(1)} %shard_map.91), channel_id=1, source_target_pairs={{0,1},{1,0},{2,3},{3,2},{4,5},{5,4},{6,7},{7,6},{8,9},{9,8},{10,11... | collective-permute-start | bytes 786440 | tf_op jit(solution)/shard_map/ppermute | solution.py:274
  58.3 2.2 %collective-permute-start.15 = (bf16[128,1024]{1,0:T(8,128)(2,1)S(1)}, bf16[128,1024]{1,0:T(8,128)(2,1)S(1)}, u32[]{:S(2)}, u32[]{:S(2)}) collective-permute-start(bf16[128,1024]{1,0:T(8,128)(2,1)S(1)} %shard_map.92), channel_id=1, source_target_pairs={{0,1},{1,0},{2,3},{3,2},{4,5},{5,4},{6,7},{7,6},{8,9},{9,8},{10,11... | collective-permute-start | bytes 786440 | tf_op jit(solution)/shard_map/ppermute | solution.py:274
  60.0 9.2 %collective-permute-start.16 = (bf16[128,1024]{1,0:T(8,128)(2,1)S(1)}, bf16[128,1024]{1,0:T(8,128)(2,1)S(1)}, u32[]{:S(2)}, u32[]{:S(2)}) collective-permute-start(bf16[128,1024]{1,0:T(8,128)(2,1)S(1)} %get-tuple-element.83), channel_id=1, source_target_pairs={{0,2},{1,3},{2,0},{3,1},{4,6},{5,7},{6,4},{7,5},{8,10},{9,11},{10,... | collective-permute-start | bytes 786440 | tf_op jit(solution)/shard_map/ppermute | solution.py:274
  61.7 15.9 %collective-permute-start.20 = (bf16[64,1536]{1,0:T(8,128)(2,1)S(1)}, bf16[64,1536]{1,0:T(8,128)(2,1)S(1)}, u32[]{:S(2)}, u32[]{:S(2)}) collective-permute-start(bf16[64,1536]{1,0:T(8,128)(2,1)S(1)} %get-tuple-element.93.refs_0_), channel_id=1, source_target_pairs={{0,4},{4,0},{1,5},{5,1},{2,6},{6,2},{3,7},{7,3},{8,12},{12,8},{9,1... | collective-permute-start | bytes 589832 | tf_op jit(solution)/shard_map/ppermute | solution.py:274
  62.3 15.3 %collective-permute-start.21 = (bf16[64,1536]{1,0:T(8,128)(2,1)S(1)}, bf16[64,1536]{1,0:T(8,128)(2,1)S(1)}, u32[]{:S(2)}, u32[]{:S(2)}) collective-permute-start(bf16[64,1536]{1,0:T(8,128)(2,1)S(1)} %get-tuple-element.95.refs_2_), channel_id=1, source_target_pairs={{0,4},{4,0},{1,5},{5,1},{2,6},{6,2},{3,7},{7,3},{8,12},{12,8},{9,1... | collective-permute-start | bytes 589832 | tf_op jit(solution)/shard_map/ppermute | solution.py:274
  63.8 10.2 %collective-permute-start.18 = (bf16[128,1024]{1,0:T(8,128)(2,1)S(1)}, bf16[128,1024]{1,0:T(8,128)(2,1)S(1)}, u32[]{:S(2)}, u32[]{:S(2)}) collective-permute-start(bf16[128,1024]{1,0:T(8,128)(2,1)S(1)} %get-tuple-element.87), channel_id=1, source_target_pairs={{0,2},{1,3},{2,0},{3,1},{4,6},{5,7},{6,4},{7,5},{8,10},{9,11},{10,... | collective-permute-start | bytes 786440 | tf_op jit(solution)/shard_map/ppermute | solution.py:274
  69.5 1.6 %collective-permute-start.17 = (bf16[128,1024]{1,0:T(8,128)(2,1)S(1)}, bf16[128,1024]{1,0:T(8,128)(2,1)S(1)}, u32[]{:S(2)}, u32[]{:S(2)}) collective-permute-start(bf16[128,1024]{1,0:T(8,128)(2,1)S(1)} %shard_map.95.v.refs_5_), channel_id=1, source_target_pairs={{0,1},{1,0},{2,3},{3,2},{4,5},{5,4},{6,7},{7,6},{8,9},{9,8},{10,11... | collective-permute-start | bytes 786440 | tf_op jit(solution)/shard_map/ppermute | solution.py:274
  74.2 1.6 %collective-permute-start.19 = (bf16[128,1024]{1,0:T(8,128)(2,1)S(1)}, bf16[128,1024]{1,0:T(8,128)(2,1)S(1)}, u32[]{:S(2)}, u32[]{:S(2)}) collective-permute-start(bf16[128,1024]{1,0:T(8,128)(2,1)S(1)} %shard_map.98.v.refs_9_), channel_id=1, source_target_pairs={{0,1},{1,0},{2,3},{3,2},{4,5},{5,4},{6,7},{7,6},{8,9},{9,8},{10,11... | collective-permute-start | bytes 786440 | tf_op jit(solution)/shard_map/ppermute | solution.py:274
  77.0 7.0 %collective-permute-start.22 = (bf16[64,1536]{1,0:T(8,128)(2,1)S(1)}, bf16[64,1536]{1,0:T(8,128)(2,1)S(1)}, u32[]{:S(2)}, u32[]{:S(2)}) collective-permute-start(bf16[64,1536]{1,0:T(8,128)(2,1)S(1)} %get-tuple-element.97), channel_id=1, source_target_pairs={{0,4},{4,0},{1,5},{5,1},{2,6},{6,2},{3,7},{7,3},{8,12},{12,8},{9,1... | collective-permute-start | bytes 589832 | tf_op jit(solution)/shard_map/ppermute | solution.py:274
  84.2 3.0 %collective-permute-start.25 = (f32[8,128]{1,0:T(8,128)S(1)}, f32[8,128]{1,0:T(8,128)S(1)}, u32[]{:S(2)}, u32[]{:S(2)}) collective-permute-start(f32[8,128]{1,0:T(8,128)S(1)} %get-tuple-element.99.refs_7_), channel_id=1, source_target_pairs={{0,3},{1,2},{2,1},{3,0},{4,7},{5,6},{6,5},{7,4},{8,11},{9,10},{10,... | collective-permute-start | bytes 12296 | tf_op jit(solution)/shard_map/ppermute | solution.py:274
  84.2 3.7 %collective-permute-start.24 = (f32[8,128]{1,0:T(8,128)S(1)}, f32[8,128]{1,0:T(8,128)S(1)}, u32[]{:S(2)}, u32[]{:S(2)}) collective-permute-start(f32[8,128]{1,0:T(8,128)S(1)} %get-tuple-element.99.refs_7_), channel_id=1, source_target_pairs={{0,2},{1,3},{2,0},{3,1},{4,6},{5,7},{6,4},{7,5},{8,10},{9,11},{10,... | collective-permute-start | bytes 12296 | tf_op jit(solution)/shard_map/ppermute | solution.py:274
  85.2 2.7 %collective-permute-start.23 = (f32[8,128]{1,0:T(8,128)S(1)}, f32[8,128]{1,0:T(8,128)S(1)}, u32[]{:S(2)}, u32[]{:S(2)}) collective-permute-start(f32[8,128]{1,0:T(8,128)S(1)} %get-tuple-element.99.refs_7_), channel_id=1, source_target_pairs={{0,1},{1,0},{2,3},{3,2},{4,5},{5,4},{6,7},{7,6},{8,9},{9,8},{10,11... | collective-permute-start | bytes 12296 | tf_op jit(solution)/shard_map/ppermute | solution.py:274

commit v6 on v5

--- a/solution.py
+++ b/solution.py
@@ -309,17 +309,15 @@
     for slot in range(slots):
         last = slot == slots - 1
         if slot > 0:
-            pieces = [
-                [
-                    lax.ppermute(
-                        upstream[0],
-                        ("section", "tensor"),
-                        [(i * tensors + k, (i - 1) * tensors + (k ^ t)) for i in range(1, sections) for k in range(tensors)],
-                    )
-                ]
-                for t in range(tensors)
-            ]
-            upstream = pieces[0]
+            def from_above(array, t):
+                return lax.ppermute(
+                    array,
+                    ("section", "tensor"),
+                    [(i * tensors + k, (i - 1) * tensors + (k ^ t)) for i in range(1, sections) for k in range(tensors)],
+                )
+
+            above, upstream = upstream, [from_above(a, 0) for a in upstream]
+            pieces = [upstream] + [[from_above(above[0], t), *(flipped(a, "tensor", t) for a in upstream[1:])] for t in others]
 
         def product(j, other, received=None):
             a, n = chunks[j]
@@ -365,7 +363,7 @@
         grad_stats = [sums] + [flipped(sums, "dp", m) for m in range(1, parts)]
         if slot == 0:
             input_stats = grad_stats
-        outs = run(finish, grad, upstream, inputs, slot, input_stats, grad_stats, width, 1)
+        outs = run(finish, grad, upstream, inputs, slot, input_stats, grad_stats, width, 1 if last else 2)
         if slot == 0:
             normed = outs[-slots:]
             outs = outs[:-slots]

time: 89.2 us -> 88.2 us (0.989)
  waiting for transfers between devices: 35.6 us -> 31 us
  starting transfers between devices: 23.5 us -> 27 us
    ppermute x2 -> x3, waiting for transfers between devices: 11.2 us -> 6.38 us  [from_above(): lax.ppermute(array, ('section', 'tensor'), [(i * tensors + k, (i - 1) * t...]
    ppermute x23 -> x24, starting transfers between devices: 16.9 us -> 19.2 us  [flipped(): lax.ppermute(array, axis, [(i, i ^ mask) for i in range(lax.axis_size(axi...]
    ppermute x2 -> x3, starting transfers between devices: 2.76 us -> 4.06 us  [from_above(): lax.ppermute(array, ('section', 'tensor'), [(i * tensors + k, (i - 1) * t...]
    ppermute x23 -> x24, waiting for transfers between devices: 24.4 us -> 24.6 us  [flipped(): lax.ppermute(array, axis, [(i, i ^ mask) for i in range(lax.axis_size(axi...]
  transfers between devices with their start and end apart: 26 -> 28, of which waited for: 17 -> 19; matrix products, arithmetic and copies ran while one was open for 0% -> 0% of each run, Pallas kernels for 27% -> 27%
where the time goes in v6:
time: 88.2 us; the launch traced here: 88 us
  waiting for transfers between devices  31 us (35%)
  Pallas kernels  28.2 us (32%)
  starting transfers between devices  27 us (31%)
  between operations  0.97 us (1%)
    ppermute x24, waiting for transfers between devices, flipped(): lax.ppermute(array, axis, [(i, i ^ mask) for i in range(lax.axis_size(axi...  24.6 us
    pallas_call x26, Pallas kernels, call(): pl.pallas_call(body, in_specs=[first_spec] + [VMEM] * (len(operands) - 1)...  23.1 us
    ppermute x24, starting transfers between devices, flipped(): lax.ppermute(array, axis, [(i, i ^ mask) for i in range(lax.axis_size(axi...  19.2 us
    ppermute x3, waiting for transfers between devices, from_above(): lax.ppermute(array, ('section', 'tensor'), [(i * tensors + k, (i - 1) * t...  6.38 us
    pallas_call x1, Pallas kernels, value_grad(): pl.pallas_call(body, in_specs=[VMEM] * (blocks + len(flat)), out_specs=[A...  5.07 us
    ppermute x3, starting transfers between devices, from_above(): lax.ppermute(array, ('section', 'tensor'), [(i * tensors + k, (i - 1) * t...  4.06 us
    ppermute x1, starting transfers between devices, on_device(): lax.ppermute(after(parked[0], kept[-1][1]), 'section', [(i, sections - 1...  3.81 us
  transfers between devices with their start and end apart: 28, of which 19 were waited for; matrix products, arithmetic and copies ran while one was open for 0% of the time, Pallas kernels for 27%

profile of v6, /device:TPU:0, one launch (start us, length us, event | category | flops | bytes accessed | tf_op | source)
XLA Modules:
  0.0 88.0 jit_solution(7054562027296168920)
XLA Ops:
  0.6 3.0 %collective-permute-start = (bf16[64,1536]{1,0:T(8,128)(2,1)}, bf16[64,1536]{1,0:T(8,128)(2,1)S(1)}, u32[]{:S(2)}, u32[]{:S(2)}) collective-permute-start(bf16[64,1536]{1,0:T(8,128)(2,1)} %bitcast.27), channel_id=1, source_target_pairs={{0,4},{4,0},{1,5},{5,1},{2,6},{6,2},{3,7},{7,3},{8,12},{12,8},{9,1... | collective-permute-start | bytes 589832 | tf_op jit(solution)/shard_map/ppermute | solution.py:274
  4.3 1.0 %shard_map.77.refs_2_ = bf16[16,128,128]{2,1,0:T(8,128)(2,1)S(1)} custom-call(f32[1,32]{1,0:T(1,128)S(1)} %bitcast.33), custom_call_target="tpu_custom_call" | custom-call | flops 8000000000 | bytes 100000000 | tf_op jit(solution)/shard_map/pallas_call | solution.py:22
  5.3 3.5 %collective-permute-done.refs_1_ = bf16[64,1536]{1,0:T(8,128)(2,1)S(1)} collective-permute-done((bf16[64,1536]{1,0:T(8,128)(2,1)}, bf16[64,1536]{1,0:T(8,128)(2,1)S(1)}, u32[]{:S(2)}, u32[]{:S(2)}) %collective-permute-start) | collective-permute-done | bytes 196640 | tf_op jit(solution)/shard_map/ppermute | solution.py:274
  8.9 1.1 %shard_map.78 = bf16[128,1024]{1,0:T(8,128)(2,1)S(1)} custom-call(bf16[64,1536]{1,0:T(8,128)(2,1)S(1)} %bitcast.28, bf16[64,1536]{1,0:T(8,128)(2,1)S(1)} %collective-permute-done.refs_1_, bf16[4096,1536]{1,0:T(8,128)(2,1)S(1)} %bitcast.9), custom_call_target="tpu_custom_call" | custom-call | flops 8000000000 | bytes 100000000 | tf_op jit(solution)/shard_map/pallas_call | solution.py:22
  10.1 1.1 %shard_map.79 = bf16[128,1024]{1,0:T(8,128)(2,1)S(1)} custom-call(bf16[64,1536]{1,0:T(8,128)(2,1)S(1)} %bitcast.29, bf16[64,1536]{1,0:T(8,128)(2,1)S(1)} %collective-permute-done.refs_1_, bf16[4096,1536]{1,0:T(8,128)(2,1)S(1)} %bitcast.10), custom_call_target="tpu_custom_call" | custom-call | flops 8000000000 | bytes 100000000 | tf_op jit(solution)/shard_map/pallas_call | solution.py:22
  11.8 1.1 %shard_map.80 = (f32[128,1024]{1,0:T(8,128)S(1)}, bf16[128,1024]{1,0:T(8,128)(2,1)S(1)}) custom-call(bf16[64,1536]{1,0:T(8,128)(2,1)S(1)} %bitcast.30, bf16[64,1536]{1,0:T(8,128)(2,1)S(1)} %collective-permute-done.refs_1_, bf16[4096,1536]{1,0:T(8,128)(2,1)S(1)} %bitcast.11, bf16[128,1024]{1,0:T(8,128)(2,1)S(1)} %collective-permute-done.1.refs_3_), custom_call_target="tpu_custom_call" | custom-call | flops 8000000000 | bytes 100000000 | tf_op jit(solution)/shard_map/pallas_call | solution.py:22
  12.9 1.7 %collective-permute-start.3 = (bf16[128,1024]{1,0:T(8,128)(2,1)S(1)}, bf16[128,1024]{1,0:T(8,128)(2,1)S(1)}, u32[]{:S(2)}, u32[]{:S(2)}) collective-permute-start(bf16[128,1024]{1,0:T(8,128)(2,1)S(1)} %get-tuple-element.60), channel_id=1, source_target_pairs={{0,2},{1,3},{2,0},{3,1},{4,6},{5,7},{6,4},{7,5},{8,10},{9,11},{10,... | collective-permute-start | bytes 786440 | tf_op jit(solution)/shard_map/ppermute | solution.py:274
  14.7 1.1 %shard_map.81 = (f32[128,1024]{1,0:T(8,128)S(1)}, bf16[128,1024]{1,0:T(8,128)(2,1)S(1)}) custom-call(bf16[64,1536]{1,0:T(8,128)(2,1)S(1)} %bitcast.31, bf16[64,1536]{1,0:T(8,128)(2,1)S(1)} %collective-permute-done.refs_1_, bf16[4096,1536]{1,0:T(8,128)(2,1)S(1)} %bitcast.12, bf16[128,1024]{1,0:T(8,128)(2,1)S(1)} %collective-permute-done.2.refs_3_), custom_call_target="tpu_custom_call" | custom-call | flops 8000000000 | bytes 100000000 | tf_op jit(solution)/shard_map/pallas_call | solution.py:22
  16.3 3.8 %collective-permute-start.7 = (bf16[2,64,1536]{2,1,0:T(8,128)(2,1)S(1)}, bf16[2,64,1536]{2,1,0:T(8,128)(2,1)S(1)}, u32[]{:S(2)}, u32[]{:S(2)}) collective-permute-start(bf16[2,64,1536]{2,1,0:T(8,128)(2,1)S(1)} %bitcast.34), channel_id=1, source_target_pairs={{0,24},{8,16},{16,8},{24,0},{1,25},{9,17},{17,9},{25,1},{2,26},{10... | collective-permute-start | bytes 1179656 | tf_op jit(solution)/shard_map/ppermute | solution.py:339
  20.1 2.1 %collective-permute-done.3.refs_1_ = bf16[128,1024]{1,0:T(8,128)(2,1)S(1)} collective-permute-done((bf16[128,1024]{1,0:T(8,128)(2,1)S(1)}, bf16[128,1024]{1,0:T(8,128)(2,1)S(1)}, u32[]{:S(2)}, u32[]{:S(2)}) %collective-permute-start.3) | collective-permute-done | bytes 262176 | tf_op jit(solution)/shard_map/ppermute | solution.py:274
  22.6 1.2 %shard_map.83.refs_0_ = f32[128,1536]{1,0:T(8,128)S(1)} custom-call(bf16[128,1024]{1,0:T(8,128)(2,1)S(1)} %shard_map.82.v.refs_4_, bf16[1536,4096]{1,0:T(8,128)(2,1)S(1)} %bitcast.19), custom_call_target="tpu_custom_call" | custom-call | flops 8000000000 | bytes 100000000 | tf_op jit(solution)/shard_map/pallas_call | solution.py:22
  24.0 1.2 %shard_map.84.refs_0_ = f32[128,1536]{1,0:T(8,128)S(1)} custom-call(bf16[128,1024]{1,0:T(8,128)(2,1)S(1)} %collective-permute-done.4.v.refs_6_, bf16[1536,4096]{1,0:T(8,128)(2,1)S(1)} %bitcast.20, f32[128,1536]{1,0:T(8,128)S(1)} %shard_map.83.refs_0_), custom_call_target="tpu_custom_call" | custom-call | flops 8000000000 | bytes 100000000 | tf_op jit(solution)/shard_map/pallas_call | solution.py:22
  25.2 1.7 %collective-permute-done.5.refs_1_ = bf16[128,1024]{1,0:T(8,128)(2,1)S(1)} collective-permute-done((bf16[128,1024]{1,0:T(8,128)(2,1)S(1)}, bf16[128,1024]{1,0:T(8,128)(2,1)S(1)}, u32[]{:S(2)}, u32[]{:S(2)}) %collective-permute-start.5) | collective-permute-done | bytes 262176 | tf_op jit(solution)/shard_map/ppermute | solution.py:274
  27.2 1.2 %shard_map.86.refs_0_ = f32[128,1536]{1,0:T(8,128)S(1)} custom-call(bf16[128,1024]{1,0:T(8,128)(2,1)S(1)} %shard_map.85.v.refs_8_, bf16[1536,4096]{1,0:T(8,128)(2,1)S(1)} %bitcast.21, f32[128,1536]{1,0:T(8,128)S(1)} %shard_map.84.refs_0_), custom_call_target="tpu_custom_call" | custom-call | flops 8000000000 | bytes 100000000 | tf_op jit(solution)/shard_map/pallas_call | solution.py:22
  28.7 1.2 %shard_map.87 = (f32[64,1536]{1,0:T(8,128)S(1)}, bf16[64,1536]{1,0:T(8,128)(2,1)S(1)}) custom-call(bf16[128,1024]{1,0:T(8,128)(2,1)S(1)} %collective-permute-done.6.v.refs_10_, bf16[1536,4096]{1,0:T(8,128)(2,1)S(1)} %bitcast.22, f32[128,1536]{1,0:T(8,128)S(1)} %shard_map.86.refs_0_), custom_call_target="tpu_custom_call" | custom-call | flops 8000000000 | bytes 100000000 | tf_op jit(solution)/shard_map/pallas_call | solution.py:22
  29.9 1.7 %collective-permute-start.8 = (bf16[64,1536]{1,0:T(8,128)(2,1)S(1)}, bf16[64,1536]{1,0:T(8,128)(2,1)S(1)}, u32[]{:S(2)}, u32[]{:S(2)}) collective-permute-start(bf16[64,1536]{1,0:T(8,128)(2,1)S(1)} %get-tuple-element.73), channel_id=1, source_target_pairs={{0,4},{4,0},{1,5},{5,1},{2,6},{6,2},{3,7},{7,3},{8,12},{12,8},{9,1... | collective-permute-start | bytes 589832 | tf_op jit(solution)/shard_map/ppermute | solution.py:274
  32.2 4.8 %collective-permute-done.8.refs_2_ = bf16[64,1536]{1,0:T(8,128)(2,1)S(1)} collective-permute-done((bf16[64,1536]{1,0:T(8,128)(2,1)S(1)}, bf16[64,1536]{1,0:T(8,128)(2,1)S(1)}, u32[]{:S(2)}, u32[]{:S(2)}) %collective-permute-start.8) | collective-permute-done | bytes 196640 | tf_op jit(solution)/shard_map/ppermute | solution.py:274
  37.9 1.1 %collective-permute-start.10 = (f32[8,128]{1,0:T(8,128)S(1)}, f32[8,128]{1,0:T(8,128)S(1)}, u32[]{:S(2)}, u32[]{:S(2)}) collective-permute-start(f32[8,128]{1,0:T(8,128)S(1)} %get-tuple-element.75.refs_3_.refs_7_.refs_4_), channel_id=1, source_target_pairs={{0,2},{1,3},{2,0},{3,1},{4,6},{5,7},{6,4},{7,5},{8,10},{9,11},{10,... | collective-permute-start | bytes 12296 | tf_op jit(solution)/shard_map/ppermute | solution.py:274
  39.2 1.2 %collective-permute-done.11.refs_6_.refs_10_.refs_7_ = f32[8,128]{1,0:T(8,128)S(1)} collective-permute-done((f32[8,128]{1,0:T(8,128)S(1)}, f32[8,128]{1,0:T(8,128)S(1)}, u32[]{:S(2)}, u32[]{:S(2)}) %collective-permute-start.11) | collective-permute-done | bytes 4128 | tf_op jit(solution)/shard_map/ppermute | solution.py:274
  40.3 1.2 %collective-permute-done.10.refs_5_.refs_9_.refs_6_ = f32[8,128]{1,0:T(8,128)S(1)} collective-permute-done((f32[8,128]{1,0:T(8,128)S(1)}, f32[8,128]{1,0:T(8,128)S(1)}, u32[]{:S(2)}, u32[]{:S(2)}) %collective-permute-start.10) | collective-permute-done | bytes 4128 | tf_op jit(solution)/shard_map/ppermute | solution.py:274
  42.0 1.3 %collective-permute-start.13 = (bf16[64,768]{1,0:T(8,128)(2,1)S(1)}, bf16[64,768]{1,0:T(8,128)(2,1)S(1)}, u32[]{:S(2)}, u32[]{:S(2)}) collective-permute-start(bf16[64,768]{1,0:T(8,128)(2,1)S(1)} %get-tuple-element.78), channel_id=1, source_target_pairs={{8,0},{12,4},{16,8},{20,12},{24,16},{28,20},{9,1},{13,5},{17,9},{2... | collective-permute-start | bytes 294920 | tf_op jit(solution)/shard_map/ppermute | solution.py:313
  43.3 1.3 %collective-permute-start.12 = (bf16[64,768]{1,0:T(8,128)(2,1)S(1)}, bf16[64,768]{1,0:T(8,128)(2,1)S(1)}, u32[]{:S(2)}, u32[]{:S(2)}) collective-permute-start(bf16[64,768]{1,0:T(8,128)(2,1)S(1)} %get-tuple-element.76), channel_id=1, source_target_pairs={{8,0},{12,4},{16,8},{20,12},{24,16},{28,20},{9,1},{13,5},{17,9},{2... | collective-permute-start | bytes 294920 | tf_op jit(solution)/shard_map/ppermute | solution.py:313
  44.6 1.5 %collective-permute-start.14 = (bf16[64,768]{1,0:T(8,128)(2,1)S(1)}, bf16[64,768]{1,0:T(8,128)(2,1)S(1)}, u32[]{:S(2)}, u32[]{:S(2)}) collective-permute-start(bf16[64,768]{1,0:T(8,128)(2,1)S(1)} %get-tuple-element.76), channel_id=1, source_target_pairs={{8,4},{12,0},{16,12},{20,8},{24,20},{28,16},{9,5},{13,1},{17,13},{... | collective-permute-start | bytes 294920 | tf_op jit(solution)/shard_map/ppermute | solution.py:313
  46.1 2.8 %collective-permute-done.13.refs_1_.refs_3_ = bf16[64,768]{1,0:T(8,128)(2,1)S(1)} collective-permute-done((bf16[64,768]{1,0:T(8,128)(2,1)S(1)}, bf16[64,768]{1,0:T(8,128)(2,1)S(1)}, u32[]{:S(2)}, u32[]{:S(2)}) %collective-permute-start.13) | collective-permute-done | bytes 98336 | tf_op jit(solution)/shard_map/ppermute | solution.py:313
  48.9 1.5 %collective-permute-start.15 = (bf16[64,768]{1,0:T(8,128)(2,1)S(1)}, bf16[64,768]{1,0:T(8,128)(2,1)S(1)}, u32[]{:S(2)}, u32[]{:S(2)}) collective-permute-start(bf16[64,768]{1,0:T(8,128)(2,1)S(1)} %collective-permute-done.13.refs_1_.refs_3_), channel_id=1, source_target_pairs={{0,4},{4,0},{1,5},{5,1},{2,6},{6,2},{3,7},{7,3},{8,12},{12,8},{9,1... | collective-permute-start | bytes 294920 | tf_op jit(solution)/shard_map/ppermute | solution.py:274
  50.3 0.8 collective-permute-done.12.refs_0_.refs_2_
  51.1 2.8 %collective-permute-done.14.refs_2_ = bf16[64,768]{1,0:T(8,128)(2,1)S(1)} collective-permute-done((bf16[64,768]{1,0:T(8,128)(2,1)S(1)}, bf16[64,768]{1,0:T(8,128)(2,1)S(1)}, u32[]{:S(2)}, u32[]{:S(2)}) %collective-permute-start.14) | collective-permute-done | bytes 98336 | tf_op jit(solution)/shard_map/ppermute | solution.py:313
  53.9 0.9 %collective-permute-done.15.refs_3_ = bf16[64,768]{1,0:T(8,128)(2,1)S(1)} collective-permute-done((bf16[64,768]{1,0:T(8,128)(2,1)S(1)}, bf16[64,768]{1,0:T(8,128)(2,1)S(1)}, u32[]{:S(2)}, u32[]{:S(2)}) %collective-permute-start.15) | collective-permute-done | bytes 98336 | tf_op jit(solution)/shard_map/ppermute | solution.py:274
  54.9 1.1 %shard_map.91 = bf16[128,1024]{1,0:T(8,128)(2,1)S(1)} custom-call(bf16[64,768]{1,0:T(8,128)(2,1)S(1)} %collective-permute-done.12.refs_0_.refs_2_, bf16[64,768]{1,0:T(8,128)(2,1)S(1)} %collective-permute-done.13.refs_1_.refs_3_, bf16[64,768]{1,0:T(8,128)(2,1)S(1)} %collective-permute-done.14.refs_2_, bf16[64,768]{1,0:T(8,128)(2,1)S(1)} %collective-permute-done.15.refs_3_, ...), custom_call_target="tpu_custom_call" | custom-call | flops 8000000000 | bytes 100000000 | tf_op jit(solution)/shard_map/pallas_call | solution.py:22
  56.1 1.2 %shard_map.92 = bf16[128,1024]{1,0:T(8,128)(2,1)S(1)} custom-call(bf16[64,768]{1,0:T(8,128)(2,1)S(1)} %collective-permute-done.12.refs_0_.refs_2_, bf16[64,768]{1,0:T(8,128)(2,1)S(1)} %collective-permute-done.13.refs_1_.refs_3_, bf16[64,768]{1,0:T(8,128)(2,1)S(1)} %collective-permute-done.14.refs_2_, bf16[64,768]{1,0:T(8,128)(2,1)S(1)} %collective-permute-done.15.refs_3_, ...), custom_call_target="tpu_custom_call" | custom-call | flops 8000000000 | bytes 100000000 | tf_op jit(solution)/shard_map/pallas_call | solution.py:22
  57.8 1.1 %shard_map.93 = (f32[128,1024]{1,0:T(8,128)S(1)}, bf16[128,1024]{1,0:T(8,128)(2,1)S(1)}) custom-call(bf16[64,768]{1,0:T(8,128)(2,1)S(1)} %collective-permute-done.12.refs_0_.refs_2_, bf16[64,768]{1,0:T(8,128)(2,1)S(1)} %collective-permute-done.13.refs_1_.refs_3_, bf16[64,768]{1,0:T(8,128)(2,1)S(1)} %collective-permute-done.14.refs_2_, ...), custom_call_target="tpu_custom_call" | custom-call | flops 8000000000 | bytes 100000000 | tf_op jit(solution)/shard_map/pallas_call | solution.py:22
  58.9 1.0 %collective-permute-start.18 = (bf16[128,1024]{1,0:T(8,128)(2,1)S(1)}, bf16[128,1024]{1,0:T(8,128)(2,1)S(1)}, u32[]{:S(2)}, u32[]{:S(2)}) collective-permute-start(bf16[128,1024]{1,0:T(8,128)(2,1)S(1)} %get-tuple-element.85), channel_id=1, source_target_pairs={{0,2},{1,3},{2,0},{3,1},{4,6},{5,7},{6,4},{7,5},{8,10},{9,11},{10,... | collective-permute-start | bytes 786440 | tf_op jit(solution)/shard_map/ppermute | solution.py:274
  59.9 1.1 %shard_map.94 = (f32[128,1024]{1,0:T(8,128)S(1)}, bf16[128,1024]{1,0:T(8,128)(2,1)S(1)}) custom-call(bf16[64,768]{1,0:T(8,128)(2,1)S(1)} %collective-permute-done.12.refs_0_.refs_2_, bf16[64,768]{1,0:T(8,128)(2,1)S(1)} %collective-permute-done.13.refs_1_.refs_3_, bf16[64,768]{1,0:T(8,128)(2,1)S(1)} %collective-permute-done.14.refs_2_, ...), custom_call_target="tpu_custom_call" | custom-call | flops 8000000000 | bytes 100000000 | tf_op jit(solution)/shard_map/pallas_call | solution.py:22
  61.1 0.7 collective-permute-start.22
  61.8 1.4 %collective-permute-start.23 = (bf16[64,1536]{1,0:T(8,128)(2,1)S(1)}, bf16[64,1536]{1,0:T(8,128)(2,1)S(1)}, u32[]{:S(2)}, u32[]{:S(2)}) collective-permute-start(bf16[64,1536]{1,0:T(8,128)(2,1)S(1)} %get-tuple-element.97.refs_2_), channel_id=1, source_target_pairs={{0,4},{4,0},{1,5},{5,1},{2,6},{6,2},{3,7},{7,3},{8,12},{12,8},{9,1... | collective-permute-start | bytes 589832 | tf_op jit(solution)/shard_map/ppermute | solution.py:274
  63.2 1.1 %collective-permute-start.20 = (bf16[128,1024]{1,0:T(8,128)(2,1)S(1)}, bf16[128,1024]{1,0:T(8,128)(2,1)S(1)}, u32[]{:S(2)}, u32[]{:S(2)}) collective-permute-start(bf16[128,1024]{1,0:T(8,128)(2,1)S(1)} %get-tuple-element.89), channel_id=1, source_target_pairs={{0,2},{1,3},{2,0},{3,1},{4,6},{5,7},{6,4},{7,5},{8,10},{9,11},{10,... | collective-permute-start | bytes 786440 | tf_op jit(solution)/shard_map/ppermute | solution.py:274
  64.3 3.9 %collective-permute-done.18.refs_1_ = bf16[128,1024]{1,0:T(8,128)(2,1)S(1)} collective-permute-done((bf16[128,1024]{1,0:T(8,128)(2,1)S(1)}, bf16[128,1024]{1,0:T(8,128)(2,1)S(1)}, u32[]{:S(2)}, u32[]{:S(2)}) %collective-permute-start.18) | collective-permute-done | bytes 262176 | tf_op jit(solution)/shard_map/ppermute | solution.py:274
  68.5 1.2 %shard_map.96.refs_0_ = f32[128,1536]{1,0:T(8,128)S(1)} custom-call(bf16[128,1024]{1,0:T(8,128)(2,1)S(1)} %shard_map.95.v.refs_5_, bf16[1536,4096]{1,0:T(8,128)(2,1)S(1)} %bitcast.23), custom_call_target="tpu_custom_call" | custom-call | flops 8000000000 | bytes 100000000 | tf_op jit(solution)/shard_map/pallas_call | solution.py:22
  70.0 1.2 %shard_map.97.refs_0_ = f32[128,1536]{1,0:T(8,128)S(1)} custom-call(bf16[128,1024]{1,0:T(8,128)(2,1)S(1)} %collective-permute-done.19.v.refs_7_, bf16[1536,4096]{1,0:T(8,128)(2,1)S(1)} %bitcast.24, f32[128,1536]{1,0:T(8,128)S(1)} %shard_map.96.refs_0_), custom_call_target="tpu_custom_call" | custom-call | flops 8000000000 | bytes 100000000 | tf_op jit(solution)/shard_map/pallas_call | solution.py:22
  71.2 1.7 %collective-permute-done.20.refs_1_ = bf16[128,1024]{1,0:T(8,128)(2,1)S(1)} collective-permute-done((bf16[128,1024]{1,0:T(8,128)(2,1)S(1)}, bf16[128,1024]{1,0:T(8,128)(2,1)S(1)}, u32[]{:S(2)}, u32[]{:S(2)}) %collective-permute-start.20) | collective-permute-done | bytes 262176 | tf_op jit(solution)/shard_map/ppermute | solution.py:274
  73.2 1.2 %shard_map.99.refs_0_ = f32[128,1536]{1,0:T(8,128)S(1)} custom-call(bf16[128,1024]{1,0:T(8,128)(2,1)S(1)} %shard_map.98.v.refs_9_, bf16[1536,4096]{1,0:T(8,128)(2,1)S(1)} %bitcast.25, f32[128,1536]{1,0:T(8,128)S(1)} %shard_map.97.refs_0_), custom_call_target="tpu_custom_call" | custom-call | flops 8000000000 | bytes 100000000 | tf_op jit(solution)/shard_map/pallas_call | solution.py:22
  74.7 1.2 %shard_map.100 = (f32[64,1536]{1,0:T(8,128)S(1)}, bf16[64,1536]{1,0:T(8,128)(2,1)S(1)}) custom-call(bf16[128,1024]{1,0:T(8,128)(2,1)S(1)} %collective-permute-done.21.v.refs_11_, bf16[1536,4096]{1,0:T(8,128)(2,1)S(1)} %bitcast.26, f32[128,1536]{1,0:T(8,128)S(1)} %shard_map.99.refs_0_), custom_call_target="tpu_custom_call" | custom-call | flops 8000000000 | bytes 100000000 | tf_op jit(solution)/shard_map/pallas_call | solution.py:22
  75.9 1.4 %collective-permute-start.24 = (bf16[64,1536]{1,0:T(8,128)(2,1)S(1)}, bf16[64,1536]{1,0:T(8,128)(2,1)S(1)}, u32[]{:S(2)}, u32[]{:S(2)}) collective-permute-start(bf16[64,1536]{1,0:T(8,128)(2,1)S(1)} %get-tuple-element.99), channel_id=1, source_target_pairs={{0,4},{4,0},{1,5},{5,1},{2,6},{6,2},{3,7},{7,3},{8,12},{12,8},{9,1... | collective-permute-start | bytes 589832 | tf_op jit(solution)/shard_map/ppermute | solution.py:274
  77.3 5.1 %shard_map.101 = bf16[1536,4096]{1,0:T(8,128)(2,1)} custom-call(bf16[64,1536]{1,0:T(8,128)(2,1)S(1)} %get-tuple-element.95.refs_0_, bf16[64,1536]{1,0:T(8,128)(2,1)S(1)} %collective-permute-done.22.refs_1_, bf16[64,1536]{1,0:T(8,128)(2,1)S(1)} %get-tuple-element.97.refs_2_, bf16[64,1536]{1,0:T(8,128)(2,1)S(1)} %collective-permute-done.23.refs_3_, ...), custom_call_target="tpu_custom_call" | custom-call | flops 8000000000 | bytes 100000000 | tf_op jit(solution)/shard_map/pallas_call | solution.py:239
  83.2 1.0 %collective-permute-start.26 = (f32[8,128]{1,0:T(8,128)S(1)}, f32[8,128]{1,0:T(8,128)S(1)}, u32[]{:S(2)}, u32[]{:S(2)}) collective-permute-start(f32[8,128]{1,0:T(8,128)S(1)} %get-tuple-element.101.refs_8_), channel_id=1, source_target_pairs={{0,2},{1,3},{2,0},{3,1},{4,6},{5,7},{6,4},{7,5},{8,10},{9,11},{10,... | collective-permute-start | bytes 12296 | tf_op jit(solution)/shard_map/ppermute | solution.py:274
  84.2 0.9 collective-permute-start.25
  85.0 1.2 %collective-permute-done.27.refs_11_ = f32[8,128]{1,0:T(8,128)S(1)} collective-permute-done((f32[8,128]{1,0:T(8,128)S(1)}, f32[8,128]{1,0:T(8,128)S(1)}, u32[]{:S(2)}, u32[]{:S(2)}) %collective-permute-start.27) | collective-permute-done | bytes 4128 | tf_op jit(solution)/shard_map/ppermute | solution.py:274
  86.9 1.1 %shard_map.103 = bf16[64,1536]{1,0:T(8,128)(2,1)} custom-call(f32[64,1536]{1,0:T(8,128)S(1)} %get-tuple-element.100.grad_ref, bf16[64,1536]{1,0:T(8,128)(2,1)S(1)} %get-tuple-element.70.refs_0_, bf16[64,1536]{1,0:T(8,128)(2,1)S(1)} %get-tuple-element.72.refs_1_, bf16[64,768]{1,0:T(8,128)(2,1)S(1)} %collective-permute-done.12.refs_0_.refs_2_, ...), custom_call_target="tpu_custom_call" | custom-call | flops 8000000000 | bytes 100000000 | tf_op jit(solution)/shard_map/pallas_call | solution.py:22
  (52 shorter events, 8.7 us)
Async XLA Ops:
  0.6 8.1 %collective-permute-start = (bf16[64,1536]{1,0:T(8,128)(2,1)}, bf16[64,1536]{1,0:T(8,128)(2,1)S(1)}, u32[]{:S(2)}, u32[]{:S(2)}) collective-permute-start(bf16[64,1536]{1,0:T(8,128)(2,1)} %bitcast.27), channel_id=1, source_target_pairs={{0,4},{4,0},{1,5},{5,1},{2,6},{6,2},{3,7},{7,3},{8,12},{12,8},{9,1... | collective-permute-start | bytes 589832 | tf_op jit(solution)/shard_map/ppermute | solution.py:274
  3.6 0.7 copy-start.3
  4.3 4.6 %copy-start.1 = (bf16[1,4096,1536]{2,1,0:T(8,128)(2,1)S(1)}, bf16[1,4096,1536]{2,1,0:T(8,128)(2,1)}, u32[]{:S(2)}) copy-start(bf16[1,4096,1536]{2,1,0:T(8,128)(2,1)} %param.10) | copy-start | bytes 37748740
  4.3 4.6 %copy-start.2 = (bf16[1,64,1536]{2,1,0:T(8,128)(2,1)S(1)}, bf16[1,64,1536]{2,1,0:T(8,128)(2,1)}, u32[]{:S(2)}) copy-start(bf16[1,64,1536]{2,1,0:T(8,128)(2,1)} %param.7) | copy-start | bytes 589828
  10.0 1.8 %collective-permute-start.1 = (bf16[128,1024]{1,0:T(8,128)(2,1)S(1)}, bf16[128,1024]{1,0:T(8,128)(2,1)S(1)}, u32[]{:S(2)}, u32[]{:S(2)}) collective-permute-start(bf16[128,1024]{1,0:T(8,128)(2,1)S(1)} %shard_map.78), channel_id=1, source_target_pairs={{0,1},{1,0},{2,3},{3,2},{4,5},{5,4},{6,7},{7,6},{8,9},{9,8},{10,11... | collective-permute-start | bytes 786440 | tf_op jit(solution)/shard_map/ppermute | solution.py:274
  11.2 3.4 %collective-permute-start.2 = (bf16[128,1024]{1,0:T(8,128)(2,1)S(1)}, bf16[128,1024]{1,0:T(8,128)(2,1)S(1)}, u32[]{:S(2)}, u32[]{:S(2)}) collective-permute-start(bf16[128,1024]{1,0:T(8,128)(2,1)S(1)} %shard_map.79), channel_id=1, source_target_pairs={{0,1},{1,0},{2,3},{3,2},{4,5},{5,4},{6,7},{7,6},{8,9},{9,8},{10,11... | collective-permute-start | bytes 786440 | tf_op jit(solution)/shard_map/ppermute | solution.py:274
  12.9 3.3 %copy-start.4 = (bf16[1,2,64,1536]{3,2,1,0:T(8,128)(2,1)S(1)}, bf16[1,2,64,1536]{3,2,1,0:T(8,128)(2,1)}, u32[]{:S(2)}) copy-start(bf16[1,2,64,1536]{3,2,1,0:T(8,128)(2,1)} %param.6) | copy-start | bytes 1179652
  12.9 9.2 %collective-permute-start.3 = (bf16[128,1024]{1,0:T(8,128)(2,1)S(1)}, bf16[128,1024]{1,0:T(8,128)(2,1)S(1)}, u32[]{:S(2)}, u32[]{:S(2)}) collective-permute-start(bf16[128,1024]{1,0:T(8,128)(2,1)S(1)} %get-tuple-element.60), channel_id=1, source_target_pairs={{0,2},{1,3},{2,0},{3,1},{4,6},{5,7},{6,4},{7,5},{8,10},{9,11},{10,... | collective-permute-start | bytes 786440 | tf_op jit(solution)/shard_map/ppermute | solution.py:274
  15.8 11.1 %collective-permute-start.5 = (bf16[128,1024]{1,0:T(8,128)(2,1)S(1)}, bf16[128,1024]{1,0:T(8,128)(2,1)S(1)}, u32[]{:S(2)}, u32[]{:S(2)}) collective-permute-start(bf16[128,1024]{1,0:T(8,128)(2,1)S(1)} %get-tuple-element.64), channel_id=1, source_target_pairs={{0,2},{1,3},{2,0},{3,1},{4,6},{5,7},{6,4},{7,5},{8,10},{9,11},{10,... | collective-permute-start | bytes 786440 | tf_op jit(solution)/shard_map/ppermute | solution.py:274
  16.3 6.3 %slice-start = ((s8[12582912]{0:T(1024)(128)(4,1)}), s8[4194304]{0:T(1024)(128)(4,1)S(1)}, s32[]{:S(2)}) async-start(s8[12582912]{0:T(1024)(128)(4,1)} %bitcast.17), calls=%async_computation | async-start | bytes 8388608
  16.3 6.3 %slice-start.1 = ((s8[12582912]{0:T(1024)(128)(4,1)}), s8[4194304]{0:T(1024)(128)(4,1)S(1)}, s32[]{:S(2)}) async-start(s8[12582912]{0:T(1024)(128)(4,1)} %bitcast.17), calls=%async_computation.1 | async-start | bytes 8388608
  16.3 6.3 %slice-start.2 = ((s8[12582912]{0:T(1024)(128)(4,1)}), s8[4194304]{0:T(1024)(128)(4,1)S(1)}, s32[]{:S(2)}) async-start(s8[12582912]{0:T(1024)(128)(4,1)} %bitcast.17), calls=%async_computation.2 | async-start | bytes 8388608
  16.3 15.3 %collective-permute-start.7 = (bf16[2,64,1536]{2,1,0:T(8,128)(2,1)S(1)}, bf16[2,64,1536]{2,1,0:T(8,128)(2,1)S(1)}, u32[]{:S(2)}, u32[]{:S(2)}) collective-permute-start(bf16[2,64,1536]{2,1,0:T(8,128)(2,1)S(1)} %bitcast.34), channel_id=1, source_target_pairs={{0,24},{8,16},{16,8},{24,0},{1,25},{9,17},{17,9},{25,1},{2,26},{10... | collective-permute-start | bytes 1179656 | tf_op jit(solution)/shard_map/ppermute | solution.py:339
  22.4 1.6 %collective-permute-start.4 = (bf16[128,1024]{1,0:T(8,128)(2,1)S(1)}, bf16[128,1024]{1,0:T(8,128)(2,1)S(1)}, u32[]{:S(2)}, u32[]{:S(2)}) collective-permute-start(bf16[128,1024]{1,0:T(8,128)(2,1)S(1)} %shard_map.82.v.refs_4_), channel_id=1, source_target_pairs={{0,1},{1,0},{2,3},{3,2},{4,5},{5,4},{6,7},{7,6},{8,9},{9,8},{10,11... | collective-permute-start | bytes 786440 | tf_op jit(solution)/shard_map/ppermute | solution.py:274
  27.1 1.6 %collective-permute-start.6 = (bf16[128,1024]{1,0:T(8,128)(2,1)S(1)}, bf16[128,1024]{1,0:T(8,128)(2,1)S(1)}, u32[]{:S(2)}, u32[]{:S(2)}) collective-permute-start(bf16[128,1024]{1,0:T(8,128)(2,1)S(1)} %shard_map.85.v.refs_8_), channel_id=1, source_target_pairs={{0,1},{1,0},{2,3},{3,2},{4,5},{5,4},{6,7},{7,6},{8,9},{9,8},{10,11... | collective-permute-start | bytes 786440 | tf_op jit(solution)/shard_map/ppermute | solution.py:274
  28.4 3.2 %copy-start = (s32[4,2]{0,1:T(2,128)S(1)}, s32[4,2]{0,1:T(2,128)}, u32[]{:S(2)}) copy-start(s32[4,2]{0,1:T(2,128)} %param.8) | copy-start | bytes 100
  29.9 7.0 %collective-permute-start.8 = (bf16[64,1536]{1,0:T(8,128)(2,1)S(1)}, bf16[64,1536]{1,0:T(8,128)(2,1)S(1)}, u32[]{:S(2)}, u32[]{:S(2)}) collective-permute-start(bf16[64,1536]{1,0:T(8,128)(2,1)S(1)} %get-tuple-element.73), channel_id=1, source_target_pairs={{0,4},{4,0},{1,5},{5,1},{2,6},{6,2},{3,7},{7,3},{8,12},{12,8},{9,1... | collective-permute-start | bytes 589832 | tf_op jit(solution)/shard_map/ppermute | solution.py:274
  37.3 3.0 %collective-permute-start.11 = (f32[8,128]{1,0:T(8,128)S(1)}, f32[8,128]{1,0:T(8,128)S(1)}, u32[]{:S(2)}, u32[]{:S(2)}) collective-permute-start(f32[8,128]{1,0:T(8,128)S(1)} %get-tuple-element.75.refs_3_.refs_7_.refs_4_), channel_id=1, source_target_pairs={{0,3},{1,2},{2,1},{3,0},{4,7},{5,6},{6,5},{7,4},{8,11},{9,10},{10,... | collective-permute-start | bytes 12296 | tf_op jit(solution)/shard_map/ppermute | solution.py:274
  37.9 3.6 %collective-permute-start.10 = (f32[8,128]{1,0:T(8,128)S(1)}, f32[8,128]{1,0:T(8,128)S(1)}, u32[]{:S(2)}, u32[]{:S(2)}) collective-permute-start(f32[8,128]{1,0:T(8,128)S(1)} %get-tuple-element.75.refs_3_.refs_7_.refs_4_), channel_id=1, source_target_pairs={{0,2},{1,3},{2,0},{3,1},{4,6},{5,7},{6,4},{7,5},{8,10},{9,11},{10,... | collective-permute-start | bytes 12296 | tf_op jit(solution)/shard_map/ppermute | solution.py:274
  39.0 2.5 %collective-permute-start.9 = (f32[8,128]{1,0:T(8,128)S(1)}, f32[8,128]{1,0:T(8,128)S(1)}, u32[]{:S(2)}, u32[]{:S(2)}) collective-permute-start(f32[8,128]{1,0:T(8,128)S(1)} %get-tuple-element.75.refs_3_.refs_7_.refs_4_), channel_id=1, source_target_pairs={{0,1},{1,0},{2,3},{3,2},{4,5},{5,4},{6,7},{7,6},{8,9},{9,8},{10,11... | collective-permute-start | bytes 12296 | tf_op jit(solution)/shard_map/ppermute | solution.py:274
  42.0 6.9 %collective-permute-start.13 = (bf16[64,768]{1,0:T(8,128)(2,1)S(1)}, bf16[64,768]{1,0:T(8,128)(2,1)S(1)}, u32[]{:S(2)}, u32[]{:S(2)}) collective-permute-start(bf16[64,768]{1,0:T(8,128)(2,1)S(1)} %get-tuple-element.78), channel_id=1, source_target_pairs={{8,0},{12,4},{16,8},{20,12},{24,16},{28,20},{9,1},{13,5},{17,9},{2... | collective-permute-start | bytes 294920 | tf_op jit(solution)/shard_map/ppermute | solution.py:313
  43.3 7.9 %collective-permute-start.12 = (bf16[64,768]{1,0:T(8,128)(2,1)S(1)}, bf16[64,768]{1,0:T(8,128)(2,1)S(1)}, u32[]{:S(2)}, u32[]{:S(2)}) collective-permute-start(bf16[64,768]{1,0:T(8,128)(2,1)S(1)} %get-tuple-element.76), channel_id=1, source_target_pairs={{8,0},{12,4},{16,8},{20,12},{24,16},{28,20},{9,1},{13,5},{17,9},{2... | collective-permute-start | bytes 294920 | tf_op jit(solution)/shard_map/ppermute | solution.py:313
  44.6 9.4 %collective-permute-start.14 = (bf16[64,768]{1,0:T(8,128)(2,1)S(1)}, bf16[64,768]{1,0:T(8,128)(2,1)S(1)}, u32[]{:S(2)}, u32[]{:S(2)}) collective-permute-start(bf16[64,768]{1,0:T(8,128)(2,1)S(1)} %get-tuple-element.76), channel_id=1, source_target_pairs={{8,4},{12,0},{16,12},{20,8},{24,20},{28,16},{9,5},{13,1},{17,13},{... | collective-permute-start | bytes 294920 | tf_op jit(solution)/shard_map/ppermute | solution.py:313
  48.9 6.0 %collective-permute-start.15 = (bf16[64,768]{1,0:T(8,128)(2,1)S(1)}, bf16[64,768]{1,0:T(8,128)(2,1)S(1)}, u32[]{:S(2)}, u32[]{:S(2)}) collective-permute-start(bf16[64,768]{1,0:T(8,128)(2,1)S(1)} %collective-permute-done.13.refs_1_.refs_3_), channel_id=1, source_target_pairs={{0,4},{4,0},{1,5},{5,1},{2,6},{6,2},{3,7},{7,3},{8,12},{12,8},{9,1... | collective-permute-start | bytes 294920 | tf_op jit(solution)/shard_map/ppermute | solution.py:274
  56.0 1.8 %collective-permute-start.16 = (bf16[128,1024]{1,0:T(8,128)(2,1)S(1)}, bf16[128,1024]{1,0:T(8,128)(2,1)S(1)}, u32[]{:S(2)}, u32[]{:S(2)}) collective-permute-start(bf16[128,1024]{1,0:T(8,128)(2,1)S(1)} %shard_map.91), channel_id=1, source_target_pairs={{0,1},{1,0},{2,3},{3,2},{4,5},{5,4},{6,7},{7,6},{8,9},{9,8},{10,11... | collective-permute-start | bytes 786440 | tf_op jit(solution)/shard_map/ppermute | solution.py:274
  57.3 2.7 %collective-permute-start.17 = (bf16[128,1024]{1,0:T(8,128)(2,1)S(1)}, bf16[128,1024]{1,0:T(8,128)(2,1)S(1)}, u32[]{:S(2)}, u32[]{:S(2)}) collective-permute-start(bf16[128,1024]{1,0:T(8,128)(2,1)S(1)} %shard_map.92), channel_id=1, source_target_pairs={{0,1},{1,0},{2,3},{3,2},{4,5},{5,4},{6,7},{7,6},{8,9},{9,8},{10,11... | collective-permute-start | bytes 786440 | tf_op jit(solution)/shard_map/ppermute | solution.py:274
  58.9 9.2 %collective-permute-start.18 = (bf16[128,1024]{1,0:T(8,128)(2,1)S(1)}, bf16[128,1024]{1,0:T(8,128)(2,1)S(1)}, u32[]{:S(2)}, u32[]{:S(2)}) collective-permute-start(bf16[128,1024]{1,0:T(8,128)(2,1)S(1)} %get-tuple-element.85), channel_id=1, source_target_pairs={{0,2},{1,3},{2,0},{3,1},{4,6},{5,7},{6,4},{7,5},{8,10},{9,11},{10,... | collective-permute-start | bytes 786440 | tf_op jit(solution)/shard_map/ppermute | solution.py:274
  61.1 16.2 %collective-permute-start.22 = (bf16[64,1536]{1,0:T(8,128)(2,1)S(1)}, bf16[64,1536]{1,0:T(8,128)(2,1)S(1)}, u32[]{:S(2)}, u32[]{:S(2)}) collective-permute-start(bf16[64,1536]{1,0:T(8,128)(2,1)S(1)} %get-tuple-element.95.refs_0_), channel_id=1, source_target_pairs={{0,4},{4,0},{1,5},{5,1},{2,6},{6,2},{3,7},{7,3},{8,12},{12,8},{9,1... | collective-permute-start | bytes 589832 | tf_op jit(solution)/shard_map/ppermute | solution.py:274
  61.8 15.5 %collective-permute-start.23 = (bf16[64,1536]{1,0:T(8,128)(2,1)S(1)}, bf16[64,1536]{1,0:T(8,128)(2,1)S(1)}, u32[]{:S(2)}, u32[]{:S(2)}) collective-permute-start(bf16[64,1536]{1,0:T(8,128)(2,1)S(1)} %get-tuple-element.97.refs_2_), channel_id=1, source_target_pairs={{0,4},{4,0},{1,5},{5,1},{2,6},{6,2},{3,7},{7,3},{8,12},{12,8},{9,1... | collective-permute-start | bytes 589832 | tf_op jit(solution)/shard_map/ppermute | solution.py:274
  63.2 9.7 %collective-permute-start.20 = (bf16[128,1024]{1,0:T(8,128)(2,1)S(1)}, bf16[128,1024]{1,0:T(8,128)(2,1)S(1)}, u32[]{:S(2)}, u32[]{:S(2)}) collective-permute-start(bf16[128,1024]{1,0:T(8,128)(2,1)S(1)} %get-tuple-element.89), channel_id=1, source_target_pairs={{0,2},{1,3},{2,0},{3,1},{4,6},{5,7},{6,4},{7,5},{8,10},{9,11},{10,... | collective-permute-start | bytes 786440 | tf_op jit(solution)/shard_map/ppermute | solution.py:274
  68.4 1.6 %collective-permute-start.19 = (bf16[128,1024]{1,0:T(8,128)(2,1)S(1)}, bf16[128,1024]{1,0:T(8,128)(2,1)S(1)}, u32[]{:S(2)}, u32[]{:S(2)}) collective-permute-start(bf16[128,1024]{1,0:T(8,128)(2,1)S(1)} %shard_map.95.v.refs_5_), channel_id=1, source_target_pairs={{0,1},{1,0},{2,3},{3,2},{4,5},{5,4},{6,7},{7,6},{8,9},{9,8},{10,11... | collective-permute-start | bytes 786440 | tf_op jit(solution)/shard_map/ppermute | solution.py:274
  73.1 1.6 %collective-permute-start.21 = (bf16[128,1024]{1,0:T(8,128)(2,1)S(1)}, bf16[128,1024]{1,0:T(8,128)(2,1)S(1)}, u32[]{:S(2)}, u32[]{:S(2)}) collective-permute-start(bf16[128,1024]{1,0:T(8,128)(2,1)S(1)} %shard_map.98.v.refs_9_), channel_id=1, source_target_pairs={{0,1},{1,0},{2,3},{3,2},{4,5},{5,4},{6,7},{7,6},{8,9},{9,8},{10,11... | collective-permute-start | bytes 786440 | tf_op jit(solution)/shard_map/ppermute | solution.py:274
  75.9 7.0 %collective-permute-start.24 = (bf16[64,1536]{1,0:T(8,128)(2,1)S(1)}, bf16[64,1536]{1,0:T(8,128)(2,1)S(1)}, u32[]{:S(2)}, u32[]{:S(2)}) collective-permute-start(bf16[64,1536]{1,0:T(8,128)(2,1)S(1)} %get-tuple-element.99), channel_id=1, source_target_pairs={{0,4},{4,0},{1,5},{5,1},{2,6},{6,2},{3,7},{7,3},{8,12},{12,8},{9,1... | collective-permute-start | bytes 589832 | tf_op jit(solution)/shard_map/ppermute | solution.py:274
  83.2 3.0 %collective-permute-start.27 = (f32[8,128]{1,0:T(8,128)S(1)}, f32[8,128]{1,0:T(8,128)S(1)}, u32[]{:S(2)}, u32[]{:S(2)}) collective-permute-start(f32[8,128]{1,0:T(8,128)S(1)} %get-tuple-element.101.refs_8_), channel_id=1, source_target_pairs={{0,3},{1,2},{2,1},{3,0},{4,7},{5,6},{6,5},{7,4},{8,11},{9,10},{10,... | collective-permute-start | bytes 12296 | tf_op jit(solution)/shard_map/ppermute | solution.py:274
  83.2 3.7 %collective-permute-start.26 = (f32[8,128]{1,0:T(8,128)S(1)}, f32[8,128]{1,0:T(8,128)S(1)}, u32[]{:S(2)}, u32[]{:S(2)}) collective-permute-start(f32[8,128]{1,0:T(8,128)S(1)} %get-tuple-element.101.refs_8_), channel_id=1, source_target_pairs={{0,2},{1,3},{2,0},{3,1},{4,6},{5,7},{6,4},{7,5},{8,10},{9,11},{10,... | collective-permute-start | bytes 12296 | tf_op jit(solution)/shard_map/ppermute | solution.py:274
  84.2 2.7 %collective-permute-start.25 = (f32[8,128]{1,0:T(8,128)S(1)}, f32[8,128]{1,0:T(8,128)S(1)}, u32[]{:S(2)}, u32[]{:S(2)}) collective-permute-start(f32[8,128]{1,0:T(8,128)S(1)} %get-tuple-element.101.refs_8_), channel_id=1, source_target_pairs={{0,1},{1,0},{2,3},{3,2},{4,5},{5,4},{6,7},{7,6},{8,9},{9,8},{10,11... | collective-permute-start | bytes 12296 | tf_op jit(solution)/shard_map/ppermute | solution.py:274

commit v7 on v6

--- a/solution.py
+++ b/solution.py
@@ -88,14 +88,15 @@
     return call(body, [shape((rows, size), BF16)], [kept, *received, mixing])
 
 
-def grad_normed_part(grads, w_value, other, offset, total=None, pieces=0):
-    (rows, size), width = grads.shape, w_value.shape[0]
+def grad_normed_part(grads, w_value, other, offset, total=None, pieces=0, span=None):
+    begin, end = span or (0, w_value.shape[0])
+    (rows, size), width = grads.shape, end - begin
 
     def body(v, w, *refs):
         start = half_start(w_value.shape[1], other, offset)
-        sums = lax.dot_general(v[...], w[:, pl.ds(start, size)], NT, preferred_element_type=F32)
+        sums = lax.dot_general(v[...], w[begin:end, pl.ds(start, size)], NT, preferred_element_type=F32)
         if total is not None:
-            sums = sums + refs[0][...]
+            sums = sums + refs[0][:, begin:end]
         if not pieces:
             refs[-1][...] = sums
             return
@@ -140,15 +141,21 @@
 
 
 def width_sums(keep, received, inputs, slot):
-    own, width = keep.shape
+    own, width = keep[0].shape[0], sum(k.shape[1] for k in keep)
+    count = len(keep)
     slots = len(inputs)
 
-    def body(keep_ref, *refs):
+    def body(*refs):
+        keeps, refs = refs[:count], refs[count:]
         ins, refs = refs[:slots], refs[slots:]
         grad_ref, stats = refs[-2:]
-        grad = keep_ref[...]
-        for r in refs[:-2]:
-            grad = grad + r[...].astype(F32)
+        parts = []
+        for k, ref in enumerate(keeps):
+            part = ref[...]
+            for r in refs[k:-2:count]:
+                part = part + r[...].astype(F32)
+            parts.append(part)
+        grad = jnp.concatenate(parts, axis=1)
         grad_ref[...] = grad
         floats = [r[...].astype(F32) for r in ins]
         columns = [jnp.sum(grad, axis=1, keepdims=True), jnp.sum(grad * floats[slot], axis=1, keepdims=True)]
@@ -158,7 +165,7 @@
         stats[...] = stacked(columns)
 
     outs = [shape((own, width), F32), shape((8, -(-own // 128) * 128), F32)]
-    return call(body, outs, [keep, *inputs, *received])
+    return call(body, outs, [*keep, *inputs, *received])
 
 
 def finish(grad, upstream, inputs, slot, input_stats, grad_stats, width, parts):
@@ -345,13 +352,18 @@
             theirs.append(flipped(mine[j], "dp", 1))
             for side, grads in enumerate((mine[j], theirs[j])):
                 end = j == final and side == 1
-                outs = run(grad_normed_part, grads, value_weight[0], side == 1, a, total, tensors if end else 0)
-                if end:
-                    keep, *sends = outs
-                else:
-                    total = outs[0]
+                if not end:
+                    total, = run(grad_normed_part, grads, value_weight[0], side == 1, a, total)
+        keep, sends = [], []
+        middle = part_width if last else part_width // 2
+        for span in ((0, middle), (middle, part_width))[: 1 if last else 2]:
+            kept_part, *sent = run(
+                grad_normed_part, theirs[-1], value_weight[0], True, chunks[-1][0], total, tensors, span
+            )
+            keep.append(kept_part)
+            sends.append(sent)
         values.append([mine, theirs])
-        received = [flipped(x, "tensor", t) for t, x in zip(others, sends, strict=True)]
+        received = [flipped(sent[t - 1], "tensor", t) for t in others for sent in sends]
         if slot == 0:
             inputs = run(ordered, store, slot_table.T)
         if last:

time: 88.2 us -> 88.3 us (level)
    ppermute x24 -> x25, starting transfers between devices: 19.2 us -> 19.6 us  [flipped(): lax.ppermute(array, axis, [(i, i ^ mask) for i in range(lax.axis_size(axi...]
    ppermute x24 -> x25, waiting for transfers between devices: 24.6 us -> 24.2 us  [flipped(): lax.ppermute(array, axis, [(i, i ^ mask) for i in range(lax.axis_size(axi...]
    pallas_call x26 -> x27, Pallas kernels: 23.1 us -> 23.2 us  [call(): pl.pallas_call(body, in_specs=[first_spec] + [VMEM] * (len(operands) - 1)...]
  transfers between devices with their start and end apart: 28 -> 29, of which waited for: 19 -> 20; matrix products, arithmetic and copies ran while one was open for 0% -> 0% of each run, Pallas kernels for 27% -> 27%
where the time goes in v7:
time: 88.3 us; the launch traced here: 88.1 us
  waiting for transfers between devices  30.6 us (35%)
  Pallas kernels  28.3 us (32%)
  starting transfers between devices  27.5 us (31%)
  between operations  0.98 us (1%)
    ppermute x25, waiting for transfers between devices, flipped(): lax.ppermute(array, axis, [(i, i ^ mask) for i in range(lax.axis_size(axi...  24.2 us
    pallas_call x27, Pallas kernels, call(): pl.pallas_call(body, in_specs=[first_spec] + [VMEM] * (len(operands) - 1)...  23.2 us
    ppermute x25, starting transfers between devices, flipped(): lax.ppermute(array, axis, [(i, i ^ mask) for i in range(lax.axis_size(axi...  19.6 us
    ppermute x3, waiting for transfers between devices, from_above(): lax.ppermute(array, ('section', 'tensor'), [(i * tensors + k, (i - 1) * t...  6.38 us
    pallas_call x1, Pallas kernels, value_grad(): pl.pallas_call(body, in_specs=[VMEM] * (blocks + len(flat)), out_specs=[A...  5.07 us
    ppermute x3, starting transfers between devices, from_above(): lax.ppermute(array, ('section', 'tensor'), [(i * tensors + k, (i - 1) * t...  4.06 us
    ppermute x1, starting transfers between devices, on_device(): lax.ppermute(after(parked[0], kept[-1][1]), 'section', [(i, sections - 1...  3.81 us
  transfers between devices with their start and end apart: 29, of which 20 were waited for; matrix products, arithmetic and copies ran while one was open for 0% of the time, Pallas kernels for 27%

profile of v7, /device:TPU:0, one launch (start us, length us, event | category | flops | bytes accessed | tf_op | source)
XLA Modules:
  0.0 88.1 jit_solution(1243380244093989718)
XLA Ops:
  0.6 3.0 %collective-permute-start = (bf16[64,1536]{1,0:T(8,128)(2,1)}, bf16[64,1536]{1,0:T(8,128)(2,1)S(1)}, u32[]{:S(2)}, u32[]{:S(2)}) collective-permute-start(bf16[64,1536]{1,0:T(8,128)(2,1)} %bitcast.28), channel_id=1, source_target_pairs={{0,4},{4,0},{1,5},{5,1},{2,6},{6,2},{3,7},{7,3},{8,12},{12,8},{9,1... | collective-permute-start | bytes 589832 | tf_op jit(solution)/shard_map/ppermute | solution.py:281
  4.3 1.0 %shard_map.77.refs_2_ = bf16[16,128,128]{2,1,0:T(8,128)(2,1)S(1)} custom-call(f32[1,32]{1,0:T(1,128)S(1)} %bitcast.34), custom_call_target="tpu_custom_call" | custom-call | flops 8000000000 | bytes 100000000 | tf_op jit(solution)/shard_map/pallas_call | solution.py:22
  5.3 3.5 %collective-permute-done.refs_1_ = bf16[64,1536]{1,0:T(8,128)(2,1)S(1)} collective-permute-done((bf16[64,1536]{1,0:T(8,128)(2,1)}, bf16[64,1536]{1,0:T(8,128)(2,1)S(1)}, u32[]{:S(2)}, u32[]{:S(2)}) %collective-permute-start) | collective-permute-done | bytes 196640 | tf_op jit(solution)/shard_map/ppermute | solution.py:281
  8.9 1.1 %shard_map.78 = bf16[128,1024]{1,0:T(8,128)(2,1)S(1)} custom-call(bf16[64,1536]{1,0:T(8,128)(2,1)S(1)} %bitcast.29, bf16[64,1536]{1,0:T(8,128)(2,1)S(1)} %collective-permute-done.refs_1_, bf16[4096,1536]{1,0:T(8,128)(2,1)S(1)} %bitcast.9), custom_call_target="tpu_custom_call" | custom-call | flops 8000000000 | bytes 100000000 | tf_op jit(solution)/shard_map/pallas_call | solution.py:22
  10.1 1.1 %shard_map.79 = bf16[128,1024]{1,0:T(8,128)(2,1)S(1)} custom-call(bf16[64,1536]{1,0:T(8,128)(2,1)S(1)} %bitcast.30, bf16[64,1536]{1,0:T(8,128)(2,1)S(1)} %collective-permute-done.refs_1_, bf16[4096,1536]{1,0:T(8,128)(2,1)S(1)} %bitcast.10), custom_call_target="tpu_custom_call" | custom-call | flops 8000000000 | bytes 100000000 | tf_op jit(solution)/shard_map/pallas_call | solution.py:22
  11.8 1.1 %shard_map.80 = (f32[128,1024]{1,0:T(8,128)S(1)}, bf16[128,1024]{1,0:T(8,128)(2,1)S(1)}) custom-call(bf16[64,1536]{1,0:T(8,128)(2,1)S(1)} %bitcast.31, bf16[64,1536]{1,0:T(8,128)(2,1)S(1)} %collective-permute-done.refs_1_, bf16[4096,1536]{1,0:T(8,128)(2,1)S(1)} %bitcast.11, bf16[128,1024]{1,0:T(8,128)(2,1)S(1)} %collective-permute-done.1.refs_3_), custom_call_target="tpu_custom_call" | custom-call | flops 8000000000 | bytes 100000000 | tf_op jit(solution)/shard_map/pallas_call | solution.py:22
  12.9 1.7 %collective-permute-start.3 = (bf16[128,1024]{1,0:T(8,128)(2,1)S(1)}, bf16[128,1024]{1,0:T(8,128)(2,1)S(1)}, u32[]{:S(2)}, u32[]{:S(2)}) collective-permute-start(bf16[128,1024]{1,0:T(8,128)(2,1)S(1)} %get-tuple-element.63), channel_id=1, source_target_pairs={{0,2},{1,3},{2,0},{3,1},{4,6},{5,7},{6,4},{7,5},{8,10},{9,11},{10,... | collective-permute-start | bytes 786440 | tf_op jit(solution)/shard_map/ppermute | solution.py:281
  14.7 1.1 %shard_map.81 = (f32[128,1024]{1,0:T(8,128)S(1)}, bf16[128,1024]{1,0:T(8,128)(2,1)S(1)}) custom-call(bf16[64,1536]{1,0:T(8,128)(2,1)S(1)} %bitcast.32, bf16[64,1536]{1,0:T(8,128)(2,1)S(1)} %collective-permute-done.refs_1_, bf16[4096,1536]{1,0:T(8,128)(2,1)S(1)} %bitcast.12, bf16[128,1024]{1,0:T(8,128)(2,1)S(1)} %collective-permute-done.2.refs_3_), custom_call_target="tpu_custom_call" | custom-call | flops 8000000000 | bytes 100000000 | tf_op jit(solution)/shard_map/pallas_call | solution.py:22
  16.3 3.8 %collective-permute-start.7 = (bf16[2,64,1536]{2,1,0:T(8,128)(2,1)S(1)}, bf16[2,64,1536]{2,1,0:T(8,128)(2,1)S(1)}, u32[]{:S(2)}, u32[]{:S(2)}) collective-permute-start(bf16[2,64,1536]{2,1,0:T(8,128)(2,1)S(1)} %bitcast.35), channel_id=1, source_target_pairs={{0,24},{8,16},{16,8},{24,0},{1,25},{9,17},{17,9},{25,1},{2,26},{10... | collective-permute-start | bytes 1179656 | tf_op jit(solution)/shard_map/ppermute | solution.py:346
  20.1 2.1 %collective-permute-done.3.refs_1_ = bf16[128,1024]{1,0:T(8,128)(2,1)S(1)} collective-permute-done((bf16[128,1024]{1,0:T(8,128)(2,1)S(1)}, bf16[128,1024]{1,0:T(8,128)(2,1)S(1)}, u32[]{:S(2)}, u32[]{:S(2)}) %collective-permute-start.3) | collective-permute-done | bytes 262176 | tf_op jit(solution)/shard_map/ppermute | solution.py:281
  22.6 1.2 %shard_map.83.refs_0_ = f32[128,1536]{1,0:T(8,128)S(1)} custom-call(bf16[128,1024]{1,0:T(8,128)(2,1)S(1)} %shard_map.82.v.refs_4_, bf16[1536,4096]{1,0:T(8,128)(2,1)S(1)} %bitcast.19), custom_call_target="tpu_custom_call" | custom-call | flops 8000000000 | bytes 100000000 | tf_op jit(solution)/shard_map/pallas_call | solution.py:22
  24.0 1.2 %shard_map.84.refs_0_ = f32[128,1536]{1,0:T(8,128)S(1)} custom-call(bf16[128,1024]{1,0:T(8,128)(2,1)S(1)} %collective-permute-done.4.v.refs_6_, bf16[1536,4096]{1,0:T(8,128)(2,1)S(1)} %bitcast.20, f32[128,1536]{1,0:T(8,128)S(1)} %shard_map.83.refs_0_), custom_call_target="tpu_custom_call" | custom-call | flops 8000000000 | bytes 100000000 | tf_op jit(solution)/shard_map/pallas_call | solution.py:22
  25.2 1.7 %collective-permute-done.5.refs_1_ = bf16[128,1024]{1,0:T(8,128)(2,1)S(1)} collective-permute-done((bf16[128,1024]{1,0:T(8,128)(2,1)S(1)}, bf16[128,1024]{1,0:T(8,128)(2,1)S(1)}, u32[]{:S(2)}, u32[]{:S(2)}) %collective-permute-start.5) | collective-permute-done | bytes 262176 | tf_op jit(solution)/shard_map/ppermute | solution.py:281
  27.2 1.2 %shard_map.86.refs_0_ = f32[128,1536]{1,0:T(8,128)S(1)} custom-call(bf16[128,1024]{1,0:T(8,128)(2,1)S(1)} %shard_map.85.v.refs_8_, bf16[1536,4096]{1,0:T(8,128)(2,1)S(1)} %bitcast.21, f32[128,1536]{1,0:T(8,128)S(1)} %shard_map.84.refs_0_), custom_call_target="tpu_custom_call" | custom-call | flops 8000000000 | bytes 100000000 | tf_op jit(solution)/shard_map/pallas_call | solution.py:22
  30.1 1.7 %collective-permute-start.9 = (bf16[64,768]{1,0:T(8,128)(2,1)S(1)}, bf16[64,768]{1,0:T(8,128)(2,1)S(1)}, u32[]{:S(2)}, u32[]{:S(2)}) collective-permute-start(bf16[64,768]{1,0:T(8,128)(2,1)S(1)} %get-tuple-element.79), channel_id=1, source_target_pairs={{0,4},{4,0},{1,5},{5,1},{2,6},{6,2},{3,7},{7,3},{8,12},{12,8},{9,1... | collective-permute-start | bytes 294920 | tf_op jit(solution)/shard_map/ppermute | solution.py:281
  32.8 3.0 %collective-permute-done.9.refs_5_ = bf16[64,768]{1,0:T(8,128)(2,1)S(1)} collective-permute-done((bf16[64,768]{1,0:T(8,128)(2,1)S(1)}, bf16[64,768]{1,0:T(8,128)(2,1)S(1)}, u32[]{:S(2)}, u32[]{:S(2)}) %collective-permute-start.9) | collective-permute-done | bytes 98336 | tf_op jit(solution)/shard_map/ppermute | solution.py:281
  35.8 1.3 %collective-permute-done.8.refs_4_ = bf16[64,768]{1,0:T(8,128)(2,1)S(1)} collective-permute-done((bf16[64,768]{1,0:T(8,128)(2,1)S(1)}, bf16[64,768]{1,0:T(8,128)(2,1)S(1)}, u32[]{:S(2)}, u32[]{:S(2)}) %collective-permute-start.8) | collective-permute-done | bytes 98336 | tf_op jit(solution)/shard_map/ppermute | solution.py:281
  38.0 1.1 %collective-permute-start.11 = (f32[8,128]{1,0:T(8,128)S(1)}, f32[8,128]{1,0:T(8,128)S(1)}, u32[]{:S(2)}, u32[]{:S(2)}) collective-permute-start(f32[8,128]{1,0:T(8,128)S(1)} %get-tuple-element.81.refs_3_.refs_7_.refs_4_), channel_id=1, source_target_pairs={{0,2},{1,3},{2,0},{3,1},{4,6},{5,7},{6,4},{7,5},{8,10},{9,11},{10,... | collective-permute-start | bytes 12296 | tf_op jit(solution)/shard_map/ppermute | solution.py:281
  39.3 1.2 %collective-permute-done.12.refs_6_.refs_10_.refs_7_ = f32[8,128]{1,0:T(8,128)S(1)} collective-permute-done((f32[8,128]{1,0:T(8,128)S(1)}, f32[8,128]{1,0:T(8,128)S(1)}, u32[]{:S(2)}, u32[]{:S(2)}) %collective-permute-start.12) | collective-permute-done | bytes 4128 | tf_op jit(solution)/shard_map/ppermute | solution.py:281
  40.4 1.2 %collective-permute-done.11.refs_5_.refs_9_.refs_6_ = f32[8,128]{1,0:T(8,128)S(1)} collective-permute-done((f32[8,128]{1,0:T(8,128)S(1)}, f32[8,128]{1,0:T(8,128)S(1)}, u32[]{:S(2)}, u32[]{:S(2)}) %collective-permute-start.11) | collective-permute-done | bytes 4128 | tf_op jit(solution)/shard_map/ppermute | solution.py:281
  42.1 1.3 %collective-permute-start.14 = (bf16[64,768]{1,0:T(8,128)(2,1)S(1)}, bf16[64,768]{1,0:T(8,128)(2,1)S(1)}, u32[]{:S(2)}, u32[]{:S(2)}) collective-permute-start(bf16[64,768]{1,0:T(8,128)(2,1)S(1)} %get-tuple-element.84), channel_id=1, source_target_pairs={{8,0},{12,4},{16,8},{20,12},{24,16},{28,20},{9,1},{13,5},{17,9},{2... | collective-permute-start | bytes 294920 | tf_op jit(solution)/shard_map/ppermute | solution.py:320
  43.4 1.3 %collective-permute-start.13 = (bf16[64,768]{1,0:T(8,128)(2,1)S(1)}, bf16[64,768]{1,0:T(8,128)(2,1)S(1)}, u32[]{:S(2)}, u32[]{:S(2)}) collective-permute-start(bf16[64,768]{1,0:T(8,128)(2,1)S(1)} %get-tuple-element.82), channel_id=1, source_target_pairs={{8,0},{12,4},{16,8},{20,12},{24,16},{28,20},{9,1},{13,5},{17,9},{2... | collective-permute-start | bytes 294920 | tf_op jit(solution)/shard_map/ppermute | solution.py:320
  44.7 1.5 %collective-permute-start.15 = (bf16[64,768]{1,0:T(8,128)(2,1)S(1)}, bf16[64,768]{1,0:T(8,128)(2,1)S(1)}, u32[]{:S(2)}, u32[]{:S(2)}) collective-permute-start(bf16[64,768]{1,0:T(8,128)(2,1)S(1)} %get-tuple-element.82), channel_id=1, source_target_pairs={{8,4},{12,0},{16,12},{20,8},{24,20},{28,16},{9,5},{13,1},{17,13},{... | collective-permute-start | bytes 294920 | tf_op jit(solution)/shard_map/ppermute | solution.py:320
  46.2 2.8 %collective-permute-done.14.refs_1_.refs_3_ = bf16[64,768]{1,0:T(8,128)(2,1)S(1)} collective-permute-done((bf16[64,768]{1,0:T(8,128)(2,1)S(1)}, bf16[64,768]{1,0:T(8,128)(2,1)S(1)}, u32[]{:S(2)}, u32[]{:S(2)}) %collective-permute-start.14) | collective-permute-done | bytes 98336 | tf_op jit(solution)/shard_map/ppermute | solution.py:320
  49.0 1.5 %collective-permute-start.16 = (bf16[64,768]{1,0:T(8,128)(2,1)S(1)}, bf16[64,768]{1,0:T(8,128)(2,1)S(1)}, u32[]{:S(2)}, u32[]{:S(2)}) collective-permute-start(bf16[64,768]{1,0:T(8,128)(2,1)S(1)} %collective-permute-done.14.refs_1_.refs_3_), channel_id=1, source_target_pairs={{0,4},{4,0},{1,5},{5,1},{2,6},{6,2},{3,7},{7,3},{8,12},{12,8},{9,1... | collective-permute-start | bytes 294920 | tf_op jit(solution)/shard_map/ppermute | solution.py:281
  50.5 0.8 collective-permute-done.13.refs_0_.refs_2_
  51.3 2.8 %collective-permute-done.15.refs_2_ = bf16[64,768]{1,0:T(8,128)(2,1)S(1)} collective-permute-done((bf16[64,768]{1,0:T(8,128)(2,1)S(1)}, bf16[64,768]{1,0:T(8,128)(2,1)S(1)}, u32[]{:S(2)}, u32[]{:S(2)}) %collective-permute-start.15) | collective-permute-done | bytes 98336 | tf_op jit(solution)/shard_map/ppermute | solution.py:320
  54.1 0.9 %collective-permute-done.16.refs_3_ = bf16[64,768]{1,0:T(8,128)(2,1)S(1)} collective-permute-done((bf16[64,768]{1,0:T(8,128)(2,1)S(1)}, bf16[64,768]{1,0:T(8,128)(2,1)S(1)}, u32[]{:S(2)}, u32[]{:S(2)}) %collective-permute-start.16) | collective-permute-done | bytes 98336 | tf_op jit(solution)/shard_map/ppermute | solution.py:281
  55.0 1.1 %shard_map.92 = bf16[128,1024]{1,0:T(8,128)(2,1)S(1)} custom-call(bf16[64,768]{1,0:T(8,128)(2,1)S(1)} %collective-permute-done.13.refs_0_.refs_2_, bf16[64,768]{1,0:T(8,128)(2,1)S(1)} %collective-permute-done.14.refs_1_.refs_3_, bf16[64,768]{1,0:T(8,128)(2,1)S(1)} %collective-permute-done.15.refs_2_, bf16[64,768]{1,0:T(8,128)(2,1)S(1)} %collective-permute-done.16.refs_3_, ...), custom_call_target="tpu_custom_call" | custom-call | flops 8000000000 | bytes 100000000 | tf_op jit(solution)/shard_map/pallas_call | solution.py:22
  56.2 1.2 %shard_map.93 = bf16[128,1024]{1,0:T(8,128)(2,1)S(1)} custom-call(bf16[64,768]{1,0:T(8,128)(2,1)S(1)} %collective-permute-done.13.refs_0_.refs_2_, bf16[64,768]{1,0:T(8,128)(2,1)S(1)} %collective-permute-done.14.refs_1_.refs_3_, bf16[64,768]{1,0:T(8,128)(2,1)S(1)} %collective-permute-done.15.refs_2_, bf16[64,768]{1,0:T(8,128)(2,1)S(1)} %collective-permute-done.16.refs_3_, ...), custom_call_target="tpu_custom_call" | custom-call | flops 8000000000 | bytes 100000000 | tf_op jit(solution)/shard_map/pallas_call | solution.py:22
  57.9 1.1 %shard_map.94 = (f32[128,1024]{1,0:T(8,128)S(1)}, bf16[128,1024]{1,0:T(8,128)(2,1)S(1)}) custom-call(bf16[64,768]{1,0:T(8,128)(2,1)S(1)} %collective-permute-done.13.refs_0_.refs_2_, bf16[64,768]{1,0:T(8,128)(2,1)S(1)} %collective-permute-done.14.refs_1_.refs_3_, bf16[64,768]{1,0:T(8,128)(2,1)S(1)} %collective-permute-done.15.refs_2_, ...), custom_call_target="tpu_custom_call" | custom-call | flops 8000000000 | bytes 100000000 | tf_op jit(solution)/shard_map/pallas_call | solution.py:22
  59.1 1.0 %collective-permute-start.19 = (bf16[128,1024]{1,0:T(8,128)(2,1)S(1)}, bf16[128,1024]{1,0:T(8,128)(2,1)S(1)}, u32[]{:S(2)}, u32[]{:S(2)}) collective-permute-start(bf16[128,1024]{1,0:T(8,128)(2,1)S(1)} %get-tuple-element.91), channel_id=1, source_target_pairs={{0,2},{1,3},{2,0},{3,1},{4,6},{5,7},{6,4},{7,5},{8,10},{9,11},{10,... | collective-permute-start | bytes 786440 | tf_op jit(solution)/shard_map/ppermute | solution.py:281
  60.1 1.1 %shard_map.95 = (f32[128,1024]{1,0:T(8,128)S(1)}, bf16[128,1024]{1,0:T(8,128)(2,1)S(1)}) custom-call(bf16[64,768]{1,0:T(8,128)(2,1)S(1)} %collective-permute-done.13.refs_0_.refs_2_, bf16[64,768]{1,0:T(8,128)(2,1)S(1)} %collective-permute-done.14.refs_1_.refs_3_, bf16[64,768]{1,0:T(8,128)(2,1)S(1)} %collective-permute-done.15.refs_2_, ...), custom_call_target="tpu_custom_call" | custom-call | flops 8000000000 | bytes 100000000 | tf_op jit(solution)/shard_map/pallas_call | solution.py:22
  61.2 0.7 collective-permute-start.23
  61.9 1.4 %collective-permute-start.24 = (bf16[64,1536]{1,0:T(8,128)(2,1)S(1)}, bf16[64,1536]{1,0:T(8,128)(2,1)S(1)}, u32[]{:S(2)}, u32[]{:S(2)}) collective-permute-start(bf16[64,1536]{1,0:T(8,128)(2,1)S(1)} %get-tuple-element.103.refs_2_), channel_id=1, source_target_pairs={{0,4},{4,0},{1,5},{5,1},{2,6},{6,2},{3,7},{7,3},{8,12},{12,8},{9,1... | collective-permute-start | bytes 589832 | tf_op jit(solution)/shard_map/ppermute | solution.py:281
  63.3 1.1 %collective-permute-start.21 = (bf16[128,1024]{1,0:T(8,128)(2,1)S(1)}, bf16[128,1024]{1,0:T(8,128)(2,1)S(1)}, u32[]{:S(2)}, u32[]{:S(2)}) collective-permute-start(bf16[128,1024]{1,0:T(8,128)(2,1)S(1)} %get-tuple-element.95), channel_id=1, source_target_pairs={{0,2},{1,3},{2,0},{3,1},{4,6},{5,7},{6,4},{7,5},{8,10},{9,11},{10,... | collective-permute-start | bytes 786440 | tf_op jit(solution)/shard_map/ppermute | solution.py:281
  64.4 3.9 %collective-permute-done.19.refs_1_ = bf16[128,1024]{1,0:T(8,128)(2,1)S(1)} collective-permute-done((bf16[128,1024]{1,0:T(8,128)(2,1)S(1)}, bf16[128,1024]{1,0:T(8,128)(2,1)S(1)}, u32[]{:S(2)}, u32[]{:S(2)}) %collective-permute-start.19) | collective-permute-done | bytes 262176 | tf_op jit(solution)/shard_map/ppermute | solution.py:281
  68.7 1.2 %shard_map.97.refs_0_ = f32[128,1536]{1,0:T(8,128)S(1)} custom-call(bf16[128,1024]{1,0:T(8,128)(2,1)S(1)} %shard_map.96.v.refs_5_, bf16[1536,4096]{1,0:T(8,128)(2,1)S(1)} %bitcast.24), custom_call_target="tpu_custom_call" | custom-call | flops 8000000000 | bytes 100000000 | tf_op jit(solution)/shard_map/pallas_call | solution.py:22
  70.2 1.2 %shard_map.98.refs_0_ = f32[128,1536]{1,0:T(8,128)S(1)} custom-call(bf16[128,1024]{1,0:T(8,128)(2,1)S(1)} %collective-permute-done.20.v.refs_7_, bf16[1536,4096]{1,0:T(8,128)(2,1)S(1)} %bitcast.25, f32[128,1536]{1,0:T(8,128)S(1)} %shard_map.97.refs_0_), custom_call_target="tpu_custom_call" | custom-call | flops 8000000000 | bytes 100000000 | tf_op jit(solution)/shard_map/pallas_call | solution.py:22
  71.3 1.7 %collective-permute-done.21.refs_1_ = bf16[128,1024]{1,0:T(8,128)(2,1)S(1)} collective-permute-done((bf16[128,1024]{1,0:T(8,128)(2,1)S(1)}, bf16[128,1024]{1,0:T(8,128)(2,1)S(1)}, u32[]{:S(2)}, u32[]{:S(2)}) %collective-permute-start.21) | collective-permute-done | bytes 262176 | tf_op jit(solution)/shard_map/ppermute | solution.py:281
  73.4 1.2 %shard_map.100.refs_0_ = f32[128,1536]{1,0:T(8,128)S(1)} custom-call(bf16[128,1024]{1,0:T(8,128)(2,1)S(1)} %shard_map.99.v.refs_9_, bf16[1536,4096]{1,0:T(8,128)(2,1)S(1)} %bitcast.26, f32[128,1536]{1,0:T(8,128)S(1)} %shard_map.98.refs_0_), custom_call_target="tpu_custom_call" | custom-call | flops 8000000000 | bytes 100000000 | tf_op jit(solution)/shard_map/pallas_call | solution.py:22
  74.9 1.2 %shard_map.101 = (f32[64,1536]{1,0:T(8,128)S(1)}, bf16[64,1536]{1,0:T(8,128)(2,1)S(1)}) custom-call(bf16[128,1024]{1,0:T(8,128)(2,1)S(1)} %collective-permute-done.22.v.refs_11_, bf16[1536,4096]{1,0:T(8,128)(2,1)S(1)} %bitcast.27, f32[128,1536]{1,0:T(8,128)S(1)} %shard_map.100.refs_0_), custom_call_target="tpu_custom_call" | custom-call | flops 8000000000 | bytes 100000000 | tf_op jit(solution)/shard_map/pallas_call | solution.py:22
  76.0 1.4 %collective-permute-start.25 = (bf16[64,1536]{1,0:T(8,128)(2,1)S(1)}, bf16[64,1536]{1,0:T(8,128)(2,1)S(1)}, u32[]{:S(2)}, u32[]{:S(2)}) collective-permute-start(bf16[64,1536]{1,0:T(8,128)(2,1)S(1)} %get-tuple-element.105), channel_id=1, source_target_pairs={{0,4},{4,0},{1,5},{5,1},{2,6},{6,2},{3,7},{7,3},{8,12},{12,8},{9,1... | collective-permute-start | bytes 589832 | tf_op jit(solution)/shard_map/ppermute | solution.py:281
  77.4 5.1 %shard_map.102 = bf16[1536,4096]{1,0:T(8,128)(2,1)} custom-call(bf16[64,1536]{1,0:T(8,128)(2,1)S(1)} %get-tuple-element.101.refs_0_, bf16[64,1536]{1,0:T(8,128)(2,1)S(1)} %collective-permute-done.23.refs_1_, bf16[64,1536]{1,0:T(8,128)(2,1)S(1)} %get-tuple-element.103.refs_2_, bf16[64,1536]{1,0:T(8,128)(2,1)S(1)} %collective-permute-done.24.refs_3_, ...), custom_call_target="tpu_custom_call" | custom-call | flops 8000000000 | bytes 100000000 | tf_op jit(solution)/shard_map/pallas_call | solution.py:246
  83.3 1.0 %collective-permute-start.27 = (f32[8,128]{1,0:T(8,128)S(1)}, f32[8,128]{1,0:T(8,128)S(1)}, u32[]{:S(2)}, u32[]{:S(2)}) collective-permute-start(f32[8,128]{1,0:T(8,128)S(1)} %get-tuple-element.107.refs_8_), channel_id=1, source_target_pairs={{0,2},{1,3},{2,0},{3,1},{4,6},{5,7},{6,4},{7,5},{8,10},{9,11},{10,... | collective-permute-start | bytes 12296 | tf_op jit(solution)/shard_map/ppermute | solution.py:281
  84.3 0.9 collective-permute-start.26
  85.2 1.2 %collective-permute-done.28.refs_11_ = f32[8,128]{1,0:T(8,128)S(1)} collective-permute-done((f32[8,128]{1,0:T(8,128)S(1)}, f32[8,128]{1,0:T(8,128)S(1)}, u32[]{:S(2)}, u32[]{:S(2)}) %collective-permute-start.28) | collective-permute-done | bytes 4128 | tf_op jit(solution)/shard_map/ppermute | solution.py:281
  87.0 1.1 %shard_map.104 = bf16[64,1536]{1,0:T(8,128)(2,1)} custom-call(f32[64,1536]{1,0:T(8,128)S(1)} %get-tuple-element.106.grad_ref, bf16[64,1536]{1,0:T(8,128)(2,1)S(1)} %get-tuple-element.75.refs_2_.refs_0_.refs_1_, bf16[64,1536]{1,0:T(8,128)(2,1)S(1)} %get-tuple-element.77.refs_3_.refs_1_.refs_2_, bf16[64,768]{1,0:T(8,128)(2,1)S(1)} %collective-permute-done.13.refs_0_.refs_2_, ...), custom_call_target="tpu_custom_call" | custom-call | flops 8000000000 | bytes 100000000 | tf_op jit(solution)/shard_map/pallas_call | solution.py:22
  (55 shorter events, 10.4 us)
Async XLA Ops:
  0.6 8.1 %collective-permute-start = (bf16[64,1536]{1,0:T(8,128)(2,1)}, bf16[64,1536]{1,0:T(8,128)(2,1)S(1)}, u32[]{:S(2)}, u32[]{:S(2)}) collective-permute-start(bf16[64,1536]{1,0:T(8,128)(2,1)} %bitcast.28), channel_id=1, source_target_pairs={{0,4},{4,0},{1,5},{5,1},{2,6},{6,2},{3,7},{7,3},{8,12},{12,8},{9,1... | collective-permute-start | bytes 589832 | tf_op jit(solution)/shard_map/ppermute | solution.py:281
  3.6 0.7 copy-start.3
  4.3 4.6 %copy-start.1 = (bf16[1,4096,1536]{2,1,0:T(8,128)(2,1)S(1)}, bf16[1,4096,1536]{2,1,0:T(8,128)(2,1)}, u32[]{:S(2)}) copy-start(bf16[1,4096,1536]{2,1,0:T(8,128)(2,1)} %param.10) | copy-start | bytes 37748740
  4.3 4.6 %copy-start.2 = (bf16[1,64,1536]{2,1,0:T(8,128)(2,1)S(1)}, bf16[1,64,1536]{2,1,0:T(8,128)(2,1)}, u32[]{:S(2)}) copy-start(bf16[1,64,1536]{2,1,0:T(8,128)(2,1)} %param.7) | copy-start | bytes 589828
  10.0 1.8 %collective-permute-start.1 = (bf16[128,1024]{1,0:T(8,128)(2,1)S(1)}, bf16[128,1024]{1,0:T(8,128)(2,1)S(1)}, u32[]{:S(2)}, u32[]{:S(2)}) collective-permute-start(bf16[128,1024]{1,0:T(8,128)(2,1)S(1)} %shard_map.78), channel_id=1, source_target_pairs={{0,1},{1,0},{2,3},{3,2},{4,5},{5,4},{6,7},{7,6},{8,9},{9,8},{10,11... | collective-permute-start | bytes 786440 | tf_op jit(solution)/shard_map/ppermute | solution.py:281
  11.2 3.4 %collective-permute-start.2 = (bf16[128,1024]{1,0:T(8,128)(2,1)S(1)}, bf16[128,1024]{1,0:T(8,128)(2,1)S(1)}, u32[]{:S(2)}, u32[]{:S(2)}) collective-permute-start(bf16[128,1024]{1,0:T(8,128)(2,1)S(1)} %shard_map.79), channel_id=1, source_target_pairs={{0,1},{1,0},{2,3},{3,2},{4,5},{5,4},{6,7},{7,6},{8,9},{9,8},{10,11... | collective-permute-start | bytes 786440 | tf_op jit(solution)/shard_map/ppermute | solution.py:281
  12.9 3.3 %copy-start.4 = (bf16[1,2,64,1536]{3,2,1,0:T(8,128)(2,1)S(1)}, bf16[1,2,64,1536]{3,2,1,0:T(8,128)(2,1)}, u32[]{:S(2)}) copy-start(bf16[1,2,64,1536]{3,2,1,0:T(8,128)(2,1)} %param.6) | copy-start | bytes 1179652
  12.9 9.2 %collective-permute-start.3 = (bf16[128,1024]{1,0:T(8,128)(2,1)S(1)}, bf16[128,1024]{1,0:T(8,128)(2,1)S(1)}, u32[]{:S(2)}, u32[]{:S(2)}) collective-permute-start(bf16[128,1024]{1,0:T(8,128)(2,1)S(1)} %get-tuple-element.63), channel_id=1, source_target_pairs={{0,2},{1,3},{2,0},{3,1},{4,6},{5,7},{6,4},{7,5},{8,10},{9,11},{10,... | collective-permute-start | bytes 786440 | tf_op jit(solution)/shard_map/ppermute | solution.py:281
  15.8 11.1 %collective-permute-start.5 = (bf16[128,1024]{1,0:T(8,128)(2,1)S(1)}, bf16[128,1024]{1,0:T(8,128)(2,1)S(1)}, u32[]{:S(2)}, u32[]{:S(2)}) collective-permute-start(bf16[128,1024]{1,0:T(8,128)(2,1)S(1)} %get-tuple-element.67), channel_id=1, source_target_pairs={{0,2},{1,3},{2,0},{3,1},{4,6},{5,7},{6,4},{7,5},{8,10},{9,11},{10,... | collective-permute-start | bytes 786440 | tf_op jit(solution)/shard_map/ppermute | solution.py:281
  16.3 6.3 %slice-start = ((s8[12582912]{0:T(1024)(128)(4,1)}), s8[4194304]{0:T(1024)(128)(4,1)S(1)}, s32[]{:S(2)}) async-start(s8[12582912]{0:T(1024)(128)(4,1)} %bitcast.17), calls=%async_computation | async-start | bytes 8388608
  16.3 6.3 %slice-start.1 = ((s8[12582912]{0:T(1024)(128)(4,1)}), s8[4194304]{0:T(1024)(128)(4,1)S(1)}, s32[]{:S(2)}) async-start(s8[12582912]{0:T(1024)(128)(4,1)} %bitcast.17), calls=%async_computation.1 | async-start | bytes 8388608
  16.3 6.3 %slice-start.2 = ((s8[12582912]{0:T(1024)(128)(4,1)}), s8[4194304]{0:T(1024)(128)(4,1)S(1)}, s32[]{:S(2)}) async-start(s8[12582912]{0:T(1024)(128)(4,1)} %bitcast.17), calls=%async_computation.2 | async-start | bytes 8388608
  16.3 15.9 %collective-permute-start.7 = (bf16[2,64,1536]{2,1,0:T(8,128)(2,1)S(1)}, bf16[2,64,1536]{2,1,0:T(8,128)(2,1)S(1)}, u32[]{:S(2)}, u32[]{:S(2)}) collective-permute-start(bf16[2,64,1536]{2,1,0:T(8,128)(2,1)S(1)} %bitcast.35), channel_id=1, source_target_pairs={{0,24},{8,16},{16,8},{24,0},{1,25},{9,17},{17,9},{25,1},{2,26},{10... | collective-permute-start | bytes 1179656 | tf_op jit(solution)/shard_map/ppermute | solution.py:346
  22.4 1.6 %collective-permute-start.4 = (bf16[128,1024]{1,0:T(8,128)(2,1)S(1)}, bf16[128,1024]{1,0:T(8,128)(2,1)S(1)}, u32[]{:S(2)}, u32[]{:S(2)}) collective-permute-start(bf16[128,1024]{1,0:T(8,128)(2,1)S(1)} %shard_map.82.v.refs_4_), channel_id=1, source_target_pairs={{0,1},{1,0},{2,3},{3,2},{4,5},{5,4},{6,7},{7,6},{8,9},{9,8},{10,11... | collective-permute-start | bytes 786440 | tf_op jit(solution)/shard_map/ppermute | solution.py:281
  27.1 1.6 %collective-permute-start.6 = (bf16[128,1024]{1,0:T(8,128)(2,1)S(1)}, bf16[128,1024]{1,0:T(8,128)(2,1)S(1)}, u32[]{:S(2)}, u32[]{:S(2)}) collective-permute-start(bf16[128,1024]{1,0:T(8,128)(2,1)S(1)} %shard_map.85.v.refs_8_), channel_id=1, source_target_pairs={{0,1},{1,0},{2,3},{3,2},{4,5},{5,4},{6,7},{7,6},{8,9},{9,8},{10,11... | collective-permute-start | bytes 786440 | tf_op jit(solution)/shard_map/ppermute | solution.py:281
  29.4 2.8 %copy-start = (s32[4,2]{0,1:T(2,128)S(1)}, s32[4,2]{0,1:T(2,128)}, u32[]{:S(2)}) copy-start(s32[4,2]{0,1:T(2,128)} %param.8) | copy-start | bytes 100
  30.1 5.7 %collective-permute-start.9 = (bf16[64,768]{1,0:T(8,128)(2,1)S(1)}, bf16[64,768]{1,0:T(8,128)(2,1)S(1)}, u32[]{:S(2)}, u32[]{:S(2)}) collective-permute-start(bf16[64,768]{1,0:T(8,128)(2,1)S(1)} %get-tuple-element.79), channel_id=1, source_target_pairs={{0,4},{4,0},{1,5},{5,1},{2,6},{6,2},{3,7},{7,3},{8,12},{12,8},{9,1... | collective-permute-start | bytes 294920 | tf_op jit(solution)/shard_map/ppermute | solution.py:281
  31.8 5.4 %collective-permute-start.8 = (bf16[64,768]{1,0:T(8,128)(2,1)S(1)}, bf16[64,768]{1,0:T(8,128)(2,1)S(1)}, u32[]{:S(2)}, u32[]{:S(2)}) collective-permute-start(bf16[64,768]{1,0:T(8,128)(2,1)S(1)} %get-tuple-element.78), channel_id=1, source_target_pairs={{0,4},{4,0},{1,5},{5,1},{2,6},{6,2},{3,7},{7,3},{8,12},{12,8},{9,1... | collective-permute-start | bytes 294920 | tf_op jit(solution)/shard_map/ppermute | solution.py:281
  37.4 3.0 %collective-permute-start.12 = (f32[8,128]{1,0:T(8,128)S(1)}, f32[8,128]{1,0:T(8,128)S(1)}, u32[]{:S(2)}, u32[]{:S(2)}) collective-permute-start(f32[8,128]{1,0:T(8,128)S(1)} %get-tuple-element.81.refs_3_.refs_7_.refs_4_), channel_id=1, source_target_pairs={{0,3},{1,2},{2,1},{3,0},{4,7},{5,6},{6,5},{7,4},{8,11},{9,10},{10,... | collective-permute-start | bytes 12296 | tf_op jit(solution)/shard_map/ppermute | solution.py:281
  38.0 3.6 %collective-permute-start.11 = (f32[8,128]{1,0:T(8,128)S(1)}, f32[8,128]{1,0:T(8,128)S(1)}, u32[]{:S(2)}, u32[]{:S(2)}) collective-permute-start(f32[8,128]{1,0:T(8,128)S(1)} %get-tuple-element.81.refs_3_.refs_7_.refs_4_), channel_id=1, source_target_pairs={{0,2},{1,3},{2,0},{3,1},{4,6},{5,7},{6,4},{7,5},{8,10},{9,11},{10,... | collective-permute-start | bytes 12296 | tf_op jit(solution)/shard_map/ppermute | solution.py:281
  39.1 2.5 %collective-permute-start.10 = (f32[8,128]{1,0:T(8,128)S(1)}, f32[8,128]{1,0:T(8,128)S(1)}, u32[]{:S(2)}, u32[]{:S(2)}) collective-permute-start(f32[8,128]{1,0:T(8,128)S(1)} %get-tuple-element.81.refs_3_.refs_7_.refs_4_), channel_id=1, source_target_pairs={{0,1},{1,0},{2,3},{3,2},{4,5},{5,4},{6,7},{7,6},{8,9},{9,8},{10,11... | collective-permute-start | bytes 12296 | tf_op jit(solution)/shard_map/ppermute | solution.py:281
  42.1 6.9 %collective-permute-start.14 = (bf16[64,768]{1,0:T(8,128)(2,1)S(1)}, bf16[64,768]{1,0:T(8,128)(2,1)S(1)}, u32[]{:S(2)}, u32[]{:S(2)}) collective-permute-start(bf16[64,768]{1,0:T(8,128)(2,1)S(1)} %get-tuple-element.84), channel_id=1, source_target_pairs={{8,0},{12,4},{16,8},{20,12},{24,16},{28,20},{9,1},{13,5},{17,9},{2... | collective-permute-start | bytes 294920 | tf_op jit(solution)/shard_map/ppermute | solution.py:320
  43.4 7.9 %collective-permute-start.13 = (bf16[64,768]{1,0:T(8,128)(2,1)S(1)}, bf16[64,768]{1,0:T(8,128)(2,1)S(1)}, u32[]{:S(2)}, u32[]{:S(2)}) collective-permute-start(bf16[64,768]{1,0:T(8,128)(2,1)S(1)} %get-tuple-element.82), channel_id=1, source_target_pairs={{8,0},{12,4},{16,8},{20,12},{24,16},{28,20},{9,1},{13,5},{17,9},{2... | collective-permute-start | bytes 294920 | tf_op jit(solution)/shard_map/ppermute | solution.py:320
  44.7 9.4 %collective-permute-start.15 = (bf16[64,768]{1,0:T(8,128)(2,1)S(1)}, bf16[64,768]{1,0:T(8,128)(2,1)S(1)}, u32[]{:S(2)}, u32[]{:S(2)}) collective-permute-start(bf16[64,768]{1,0:T(8,128)(2,1)S(1)} %get-tuple-element.82), channel_id=1, source_target_pairs={{8,4},{12,0},{16,12},{20,8},{24,20},{28,16},{9,5},{13,1},{17,13},{... | collective-permute-start | bytes 294920 | tf_op jit(solution)/shard_map/ppermute | solution.py:320
  49.0 6.0 %collective-permute-start.16 = (bf16[64,768]{1,0:T(8,128)(2,1)S(1)}, bf16[64,768]{1,0:T(8,128)(2,1)S(1)}, u32[]{:S(2)}, u32[]{:S(2)}) collective-permute-start(bf16[64,768]{1,0:T(8,128)(2,1)S(1)} %collective-permute-done.14.refs_1_.refs_3_), channel_id=1, source_target_pairs={{0,4},{4,0},{1,5},{5,1},{2,6},{6,2},{3,7},{7,3},{8,12},{12,8},{9,1... | collective-permute-start | bytes 294920 | tf_op jit(solution)/shard_map/ppermute | solution.py:281
  56.1 1.8 %collective-permute-start.17 = (bf16[128,1024]{1,0:T(8,128)(2,1)S(1)}, bf16[128,1024]{1,0:T(8,128)(2,1)S(1)}, u32[]{:S(2)}, u32[]{:S(2)}) collective-permute-start(bf16[128,1024]{1,0:T(8,128)(2,1)S(1)} %shard_map.92), channel_id=1, source_target_pairs={{0,1},{1,0},{2,3},{3,2},{4,5},{5,4},{6,7},{7,6},{8,9},{9,8},{10,11... | collective-permute-start | bytes 786440 | tf_op jit(solution)/shard_map/ppermute | solution.py:281
  57.4 2.7 %collective-permute-start.18 = (bf16[128,1024]{1,0:T(8,128)(2,1)S(1)}, bf16[128,1024]{1,0:T(8,128)(2,1)S(1)}, u32[]{:S(2)}, u32[]{:S(2)}) collective-permute-start(bf16[128,1024]{1,0:T(8,128)(2,1)S(1)} %shard_map.93), channel_id=1, source_target_pairs={{0,1},{1,0},{2,3},{3,2},{4,5},{5,4},{6,7},{7,6},{8,9},{9,8},{10,11... | collective-permute-start | bytes 786440 | tf_op jit(solution)/shard_map/ppermute | solution.py:281
  59.1 9.2 %collective-permute-start.19 = (bf16[128,1024]{1,0:T(8,128)(2,1)S(1)}, bf16[128,1024]{1,0:T(8,128)(2,1)S(1)}, u32[]{:S(2)}, u32[]{:S(2)}) collective-permute-start(bf16[128,1024]{1,0:T(8,128)(2,1)S(1)} %get-tuple-element.91), channel_id=1, source_target_pairs={{0,2},{1,3},{2,0},{3,1},{4,6},{5,7},{6,4},{7,5},{8,10},{9,11},{10,... | collective-permute-start | bytes 786440 | tf_op jit(solution)/shard_map/ppermute | solution.py:281
  61.2 16.2 %collective-permute-start.23 = (bf16[64,1536]{1,0:T(8,128)(2,1)S(1)}, bf16[64,1536]{1,0:T(8,128)(2,1)S(1)}, u32[]{:S(2)}, u32[]{:S(2)}) collective-permute-start(bf16[64,1536]{1,0:T(8,128)(2,1)S(1)} %get-tuple-element.101.refs_0_), channel_id=1, source_target_pairs={{0,4},{4,0},{1,5},{5,1},{2,6},{6,2},{3,7},{7,3},{8,12},{12,8},{9,1... | collective-permute-start | bytes 589832 | tf_op jit(solution)/shard_map/ppermute | solution.py:281
  61.9 15.5 %collective-permute-start.24 = (bf16[64,1536]{1,0:T(8,128)(2,1)S(1)}, bf16[64,1536]{1,0:T(8,128)(2,1)S(1)}, u32[]{:S(2)}, u32[]{:S(2)}) collective-permute-start(bf16[64,1536]{1,0:T(8,128)(2,1)S(1)} %get-tuple-element.103.refs_2_), channel_id=1, source_target_pairs={{0,4},{4,0},{1,5},{5,1},{2,6},{6,2},{3,7},{7,3},{8,12},{12,8},{9,1... | collective-permute-start | bytes 589832 | tf_op jit(solution)/shard_map/ppermute | solution.py:281
  63.3 9.7 %collective-permute-start.21 = (bf16[128,1024]{1,0:T(8,128)(2,1)S(1)}, bf16[128,1024]{1,0:T(8,128)(2,1)S(1)}, u32[]{:S(2)}, u32[]{:S(2)}) collective-permute-start(bf16[128,1024]{1,0:T(8,128)(2,1)S(1)} %get-tuple-element.95), channel_id=1, source_target_pairs={{0,2},{1,3},{2,0},{3,1},{4,6},{5,7},{6,4},{7,5},{8,10},{9,11},{10,... | collective-permute-start | bytes 786440 | tf_op jit(solution)/shard_map/ppermute | solution.py:281
  68.6 1.6 %collective-permute-start.20 = (bf16[128,1024]{1,0:T(8,128)(2,1)S(1)}, bf16[128,1024]{1,0:T(8,128)(2,1)S(1)}, u32[]{:S(2)}, u32[]{:S(2)}) collective-permute-start(bf16[128,1024]{1,0:T(8,128)(2,1)S(1)} %shard_map.96.v.refs_5_), channel_id=1, source_target_pairs={{0,1},{1,0},{2,3},{3,2},{4,5},{5,4},{6,7},{7,6},{8,9},{9,8},{10,11... | collective-permute-start | bytes 786440 | tf_op jit(solution)/shard_map/ppermute | solution.py:281
  73.3 1.6 %collective-permute-start.22 = (bf16[128,1024]{1,0:T(8,128)(2,1)S(1)}, bf16[128,1024]{1,0:T(8,128)(2,1)S(1)}, u32[]{:S(2)}, u32[]{:S(2)}) collective-permute-start(bf16[128,1024]{1,0:T(8,128)(2,1)S(1)} %shard_map.99.v.refs_9_), channel_id=1, source_target_pairs={{0,1},{1,0},{2,3},{3,2},{4,5},{5,4},{6,7},{7,6},{8,9},{9,8},{10,11... | collective-permute-start | bytes 786440 | tf_op jit(solution)/shard_map/ppermute | solution.py:281
  76.0 7.0 %collective-permute-start.25 = (bf16[64,1536]{1,0:T(8,128)(2,1)S(1)}, bf16[64,1536]{1,0:T(8,128)(2,1)S(1)}, u32[]{:S(2)}, u32[]{:S(2)}) collective-permute-start(bf16[64,1536]{1,0:T(8,128)(2,1)S(1)} %get-tuple-element.105), channel_id=1, source_target_pairs={{0,4},{4,0},{1,5},{5,1},{2,6},{6,2},{3,7},{7,3},{8,12},{12,8},{9,1... | collective-permute-start | bytes 589832 | tf_op jit(solution)/shard_map/ppermute | solution.py:281
  83.3 3.0 %collective-permute-start.28 = (f32[8,128]{1,0:T(8,128)S(1)}, f32[8,128]{1,0:T(8,128)S(1)}, u32[]{:S(2)}, u32[]{:S(2)}) collective-permute-start(f32[8,128]{1,0:T(8,128)S(1)} %get-tuple-element.107.refs_8_), channel_id=1, source_target_pairs={{0,3},{1,2},{2,1},{3,0},{4,7},{5,6},{6,5},{7,4},{8,11},{9,10},{10,... | collective-permute-start | bytes 12296 | tf_op jit(solution)/shard_map/ppermute | solution.py:281
  83.3 3.7 %collective-permute-start.27 = (f32[8,128]{1,0:T(8,128)S(1)}, f32[8,128]{1,0:T(8,128)S(1)}, u32[]{:S(2)}, u32[]{:S(2)}) collective-permute-start(f32[8,128]{1,0:T(8,128)S(1)} %get-tuple-element.107.refs_8_), channel_id=1, source_target_pairs={{0,2},{1,3},{2,0},{3,1},{4,6},{5,7},{6,4},{7,5},{8,10},{9,11},{10,... | collective-permute-start | bytes 12296 | tf_op jit(solution)/shard_map/ppermute | solution.py:281
  84.3 2.7 %collective-permute-start.26 = (f32[8,128]{1,0:T(8,128)S(1)}, f32[8,128]{1,0:T(8,128)S(1)}, u32[]{:S(2)}, u32[]{:S(2)}) collective-permute-start(f32[8,128]{1,0:T(8,128)S(1)} %get-tuple-element.107.refs_8_), channel_id=1, source_target_pairs={{0,1},{1,0},{2,3},{3,2},{4,5},{5,4},{6,7},{7,6},{8,9},{9,8},{10,11... | collective-permute-start | bytes 12296 | tf_op jit(solution)/shard_map/ppermute | solution.py:281
